TPU v7x, 32 devices: a whole 2x2x4 slice. The times are simulated.
32 devices in a mesh: groups: 2 (over y), tensor: 4 (over z), seq: 2 (over x), pipe: 2 (over core).
Axes of the slice: x: 2, y: 2, z: 4, core: 2. Of those that a mesh axis runs over, the one named last changes fastest.
Arguments:
- queries: bfloat16 [2048, 4096], P(('groups', 'seq', 'pipe'), 'tensor'), parts along dimension 0, may hold values from -20 to 20
- new_keys: bfloat16 [2048, 512], P(('groups', 'seq', 'pipe')), parts along dimension 0, may hold values from -6 to 6
- new_values: bfloat16 [2048, 512], P(('groups', 'seq', 'pipe')), parts along dimension 0, may hold values from -6 to 6
- key_cache: bfloat16 [4, 8192, 128], P(None, ('groups', 'seq', 'pipe')), parts along dimension 1, may hold values from -20 to 20
- value_cache: bfloat16 [4, 8192, 128], P(None, ('groups', 'seq', 'pipe')), parts along dimension 1, may hold values from -6 to 6
- prefix_len: int32 [8], P(('groups', 'seq', 'pipe')), parts along dimension 0, may hold values from 256 to 1024, as said below
- stretch_start: int32 [2], P('groups'), parts along dimension 0, may hold values from 4096 to 8191
- out_weight: bfloat16 [4096, 8192], P('tensor'), may hold values from -2 to 2
Outputs:
- out_values: bfloat16 [2048, 8192], P(('groups', 'seq', 'pipe'), 'tensor'), parts along dimension 0
- out_scales: float32 [2048, 64], P(('groups', 'seq', 'pipe'), 'tensor'), parts along dimension 0
There are 2 independent parts, one for each index of `groups`. A program takes and returns all parts, laid end to end along the dimension named above; an argument that names none is the same for every part. Nothing has to cross between parts.
Inputs may be any that keep to these rules, and one draw needn't show every extreme that they name: `prefix_len`: each shard's count is at least 256; some shard is full in every draw.
All inputs are finite; a program needn't handle non-finite values. Where the computation divides by a largest or mean magnitude, that divisor is 1e-20 or more.
Results may differ from a plain program's by a relative error of at most 0.029.
Values may be sent and summed in bfloat16 or wider, within the bound.
No kernel may reach another device: no remote copies, remote signals or barrier semaphores. Data moves between devices by JAX's collectives and lax.ppermute only.
A program may use at most 192 MiB of HBM per device.

v0:
```python
import math

import jax
import jax.numpy as jnp
from jax import lax
from jax.sharding import PartitionSpec as P

D = 8192
HD = 128
HQ = 32
KVH = 4
BLOCK = 128


def rotate(values, positions):
    half = values.shape[-1] // 2
    freq = 500000.0 ** (-(jnp.arange(half, dtype=jnp.float32) * 2.0 / values.shape[-1]))
    angle = positions.astype(jnp.float32)[:, None] * freq[None, :]
    cosine = jnp.cos(angle)[:, None, :]
    sine = jnp.sin(angle)[:, None, :]
    first = values[..., :half]
    second = values[..., half:]
    return jnp.concatenate(
        [first * cosine - second * sine, second * cosine + first * sine], axis=-1
    )


def attend(carry, query, keys, values, allowed):
    running, top, totals = carry
    factor = 1.0 / math.sqrt(HD)
    scores = jnp.einsum("kgrd,knd->kgrn", query, keys, preferred_element_type=jnp.float32) * factor
    scores = jnp.where(allowed, scores, -1e30)
    peak = jnp.maximum(top, jnp.max(scores, axis=3))
    weights = jnp.where(allowed, jnp.exp(scores - peak[..., None]), 0.0)
    shrink = jnp.exp(top - peak)
    totals = totals * shrink + jnp.sum(weights, axis=3)
    update = jnp.einsum(
        "kgrn,knd->kgrd", weights.astype(jnp.bfloat16), values, preferred_element_type=jnp.float32
    )
    running = running * shrink[..., None] + update
    return (running, peak, totals)


def local(
    queries, new_keys, new_values, key_cache, value_cache, prefix_len, stretch_start, out_weight
):
    row_count = queries.shape[0]
    heads_here = queries.shape[1] // HD
    group = HQ // KVH
    kv_count = max(1, heads_here // group)
    per_kv = heads_here // kv_count
    tensor_pos = lax.axis_index("tensor")
    kv_first = tensor_pos * heads_here // group
    shard_pos = lax.axis_index("seq") * lax.axis_size("pipe") + lax.axis_index("pipe")
    first_row = shard_pos * row_count
    positions = stretch_start[0] + first_row + jnp.arange(row_count, dtype=jnp.int32)
    query = rotate(
        queries.reshape(row_count, heads_here, HD).astype(jnp.float32), positions
    ).astype(jnp.bfloat16)
    query = jnp.transpose(query.reshape(row_count, kv_count, per_kv, HD), (1, 2, 0, 3))
    own_keys = lax.dynamic_slice_in_dim(new_keys, kv_first * HD, kv_count * HD, 1).reshape(
        row_count, kv_count, HD
    )
    own_keys = rotate(own_keys.astype(jnp.float32), positions).astype(jnp.bfloat16)
    stretch_keys = jnp.transpose(own_keys, (1, 0, 2))
    own_values = lax.dynamic_slice_in_dim(new_values, kv_first * HD, kv_count * HD, 1).reshape(
        row_count, kv_count, HD
    )
    stretch_values = jnp.transpose(own_values, (1, 0, 2))
    cache_keys = lax.dynamic_slice_in_dim(key_cache, kv_first, kv_count, 0)
    cache_values = lax.dynamic_slice_in_dim(value_cache, kv_first, kv_count, 0)
    cache_len = key_cache.shape[1]
    state_shape = (kv_count, per_kv, row_count)
    start_state = (
        jnp.zeros(state_shape + (HD,), jnp.float32),
        jnp.full(state_shape, -1e30, jnp.float32),
        jnp.zeros(state_shape, jnp.float32),
    )
    keys = lax.all_gather(cache_keys, ("seq", "pipe"), axis=1, tiled=True)
    values = lax.all_gather(cache_values, ("seq", "pipe"), axis=1, tiled=True)
    lengths = lax.all_gather(prefix_len.reshape(1, 1), ("seq", "pipe"), axis=1, tiled=True)
    slot_index = jnp.arange(cache_len, dtype=jnp.int32)
    live = slot_index[None, :] < lengths.reshape(-1)[:, None]
    allowed = live.reshape(1, -1)
    prefix_state = attend(start_state, query, keys, values, allowed)
    keys = lax.all_gather(stretch_keys, ("seq", "pipe"), axis=1, tiled=True)
    values = lax.all_gather(stretch_values, ("seq", "pipe"), axis=1, tiled=True)
    key_row = jnp.arange(keys.shape[1], dtype=jnp.int32)
    query_row = first_row + jnp.arange(row_count, dtype=jnp.int32)
    allowed = key_row[None, :] <= query_row[:, None]
    running, top, totals = attend(prefix_state, query, keys, values, allowed)
    attended = (running / totals[..., None]).astype(jnp.bfloat16)
    attended = jnp.transpose(attended, (2, 0, 1, 3)).reshape(row_count, heads_here * HD)
    block_count = D // BLOCK
    lanes = lax.axis_size("tensor")
    own_blocks = block_count // lanes
    partial_value = jnp.dot(attended, out_weight, preferred_element_type=jnp.float32)
    blocks = partial_value.reshape(row_count, block_count, BLOCK)
    scales = jnp.max(jnp.abs(blocks), axis=2) + 1e-06
    coded = lax.optimization_barrier((blocks / scales[..., None]).astype(jnp.bfloat16))
    coded_lanes = coded.reshape(row_count, lanes, own_blocks * BLOCK)
    scale_lanes = scales.reshape(row_count, lanes, own_blocks)
    values = lax.all_to_all(coded_lanes, "tensor", split_axis=1, concat_axis=1, tiled=True)
    weights = lax.all_to_all(
        scale_lanes.astype(jnp.bfloat16), "tensor", split_axis=1, concat_axis=1, tiled=True
    ).astype(scale_lanes.dtype)
    values = values.reshape(values.shape[0], lanes, own_blocks, BLOCK)
    summed = jnp.sum(values.astype(jnp.float32) * weights[..., None], axis=1)
    out_scales = jnp.max(jnp.abs(summed), axis=2) + 1e-06
    out_values = (
        (summed / out_scales[..., None]).astype(jnp.bfloat16).reshape(row_count, own_blocks * BLOCK)
    )
    return (out_values, out_scales)


def solution(mesh):
    return jax.shard_map(
        local,
        mesh=mesh,
        in_specs=(
            P(("groups", "seq", "pipe"), "tensor"),
            P(("groups", "seq", "pipe"), None),
            P(("groups", "seq", "pipe"), None),
            P(None, ("groups", "seq", "pipe"), None),
            P(None, ("groups", "seq", "pipe"), None),
            P(("groups", "seq", "pipe")),
            P("groups"),
            P("tensor", None),
        ),
        out_specs=(P(("groups", "seq", "pipe"), "tensor"), P(("groups", "seq", "pipe"), "tensor")),
        check_vma=False,
    )
```

profile of v0, /device:TPU:0, one launch (start us, length us, event | category | flops | bytes accessed | tf_op | source)
XLA Modules:
  0.0 257.8 jit_solution(6849841312130409522)
XLA Ops:
  7.2 1.1 copy-done
  9.2 1.0 constant_dynamic-slice_fusion.1
  11.8 1.2 copy.23
  14.1 1.2 dynamic-slice
  16.4 6.4 %all-reduce = s32[4]{0:T(128)S(1)} all-reduce(s32[4]{0:T(128)S(1)} %dynamic-update-slice), channel_id=2, replica_groups=mesh['groups'=2,'tensor'=4,'seq'=2,'pipe'=2] {'seq','pipe'}, use_global_device_ids=true, to_apply=%add | all-reduce | flops 4 | bytes 32
  22.9 1.2 multiply_cosine_fusion.1
  25.6 6.2 %all_gather.18 = bf16[1,1024,128]{2,1,0:T(8,128)(2,1)} all-gather(bf16[1,256,128]{2,1,0:T(8,128)(2,1)S(1)} %pad_maximum_fusion), channel_id=1, replica_groups=mesh['groups'=2,'tensor'=4,'seq'=2,'pipe'=2] {'seq','pipe'}, dimensions={1}, use_global_device_ids=true | all-gather | bytes 327680 | tf_op jit(solution)/shard_map/all_gather | solution.py:86
  33.1 6.5 %all-gather.1 = bf16[1024,128]{0,1:T(8,128)(2,1)} all-gather(bf16[256,128]{0,1:T(8,128)(2,1)S(1)} %copy.41), channel_id=3, replica_groups=mesh['groups'=2,'tensor'=4,'seq'=2,'pipe'=2] {'seq','pipe'}, dimensions={0}, use_global_device_ids=true | all-gather | bytes 327680 | tf_op jit(solution)/shard_map/all_gather | solution.py:87
  39.6 22.4 %copy.36 = bf16[8192,1024]{1,0:T(8,128)(2,1)} copy(bf16[8192,1024]{0,1:T(8,128)(2,1)} %bitcast.76) | data formatting | bytes 33554432 | tf_op jit(solution)/shard_map/dot_general | solution.py:97
  62.0 1.2 fusion.30
  63.2 6.0 %fusion.7 = (f32[8,256]{1,0:T(8,128)S(1)}, f32[8,256,1024]{2,1,0:T(8,128)}) fusion(pred[256,1024]{1,0:T(8,128)(4,1)S(1)} %iota_compare_fusion, bf16[1,1024,128]{2,1,0:T(8,128)(2,1)} %all_gather.18, bf16[256,1,8,64]{3,0,2,1:T(8,128)(2,1)S(1)} %get-tuple-element.7, bf16[256,1,8,64]{3,0,2,1:T(8,128)(2,1)S(1)} %get-tuple-element.6), kind=kOutput, calls=%fused_computation.13 | convolution fusion | flops 544208896 | bytes 9445376 | tf_op jit(solution)/shard_map/kgrd,knd->kgrn/dot_general | solution.py:31
  69.2 14.7 %fusion = (f32[8,256]{1,0:T(8,128)S(1)}, f32[8,256,4096]{2,1,0:T(8,128)}) fusion(pred[4096]{0:T(1024)(128)(4,1)S(1)} %bitcast.79, bf16[1,4096,128]{2,1,0:T(8,128)(2,1)} %all-gather.5.cloned.1.call-done, bf16[256,1,8,64]{3,0,2,1:T(8,128)(2,1)S(1)} %get-tuple-element.7, bf16[256,1,8,64]{3,0,2,1:T(8,128)(2,1)S(1)} %get-tuple-element.6), kind=kOutput, calls=%fused_computation.2 | convolution fusion | flops 2173696000 | bytes 35139584 | tf_op jit(solution)/shard_map/kgrd,knd->kgrn/dot_general | solution.py:31
  83.9 15.8 %fusion.1 = f32[8,256]{1,0:T(8,128)S(1)} fusion(f32[8,256,4096]{2,1,0:T(8,128)} %get-tuple-element.20, f32[8,256]{1,0:T(8,128)S(1)} %get-tuple-element.16, pred[4096]{0:T(1024)(128)(4,1)S(1)} %bitcast.80), kind=kLoop, calls=%fused_computation.3 | loop fusion | flops 41940992 | bytes 33574912 | tf_op jit(solution)/shard_map/reduce_sum | solution.py:36
  99.8 2.5 fusion.8
  102.4 2.4 fusion.10
  104.8 15.0 %divide_convert_fusion.1 = bf16[8,256,128]{1,2,0:T(8,128)(2,1)S(1)} fusion(f32[8,256,128]{1,2,0:T(8,128)S(1)} %fusion.10, bf16[1,4096,128]{1,2,0:T(8,128)(2,1)} %all-gather.7.cloned.1.call-done, f32[8,256,4096]{2,1,0:T(8,128)} %get-tuple-element.20, f32[8,256]{1,0:T(8,128)S(1)} %get-tuple-element.16, pred[4096]{0:T(1024)(128)(4,1)S(1)} %bitcast.81, ...), kind=kOutput, calls=%fused_computation.27 | convolution fusion | flops 2190737408 | bytes 36212736 | tf_op jit(solution)/shard_map/kgrn,knd->kgrd/dot_general | solution.py:37
  119.8 13.5 %abs_reduce_fusion = (f32[256,64]{0,1:T(8,128)S(1)}, f32[256,64,128]{0,2,1:T(8,128)}) fusion(bf16[256,1024,1]{0,1,2:T(8,128)(2,1)S(1)} %bitcast.82, bf16[64,128,1024]{2,1,0:T(8,128)(2,1)} %bitcast.77), kind=kOutput, calls=%fused_computation.10 | convolution fusion | flops 4299145216 | bytes 25755648 | tf_op jit(solution)/shard_map/dot_general | solution.py:97
  133.9 4.9 %all-to-all-start.1 = ((bf16[256,4,16]{0,2,1:T(8,128)(2,1)}), bf16[256,4,16]{0,2,1:T(8,128)(2,1)S(1)}, u32[]{:S(2)}, u32[]{:S(2)}) async-start(bf16[256,4,16]{0,2,1:T(8,128)(2,1)} %bitcast.27), calls=%async_computation.1 | async-start | bytes 65536 | tf_op jit(solution)/shard_map/all_to_all | solution.py:104
  138.7 6.6 %divide_convert_fusion = bf16[256,64,128]{0,2,1:T(8,128)(2,1)} fusion(f32[256,64,128]{0,2,1:T(8,128)} %get-tuple-element.24, f32[256,64]{0,1:T(8,128)S(1)} %get-tuple-element.13), kind=kLoop, calls=%fused_computation.9 | loop fusion | flops 4194304 | bytes 12648448 | tf_op jit(solution)/shard_map/convert_element_type | solution.py:100
  145.3 5.1 %all-to-all-start = ((bf16[256,4,2048]{0,2,1:T(8,128)(2,1)}), bf16[256,4,2048]{0,2,1:T(8,128)(2,1)}, u32[]{:S(2)}, u32[]{:S(2)}) async-start(bf16[256,4,2048]{0,2,1:T(8,128)(2,1)} %bitcast.75), calls=%async_computation | async-start | bytes 8388608 | tf_op jit(solution)/shard_map/all_to_all | solution.py:103
  150.4 93.5 %all-to-all-done = bf16[256,4,2048]{0,2,1:T(8,128)(2,1)} async-done(((bf16[256,4,2048]{0,2,1:T(8,128)(2,1)}), bf16[256,4,2048]{0,2,1:T(8,128)(2,1)}, u32[]{:S(2)}, u32[]{:S(2)}) %all-to-all-start) | async-done | bytes 4194336 | tf_op jit(solution)/shard_map/all_to_all | solution.py:103
  243.9 3.3 %fusion.6 = f32[256,2048]{0,1:T(8,128)S(1)} fusion(bf16[256,4,2048]{0,2,1:T(8,128)(2,1)} %all-to-all-done, f32[256,4,16]{0,2,1:T(8,128)S(1)} %convert_element_type.85), kind=kLoop, calls=%fused_computation.8 | loop fusion | flops 5767168 | bytes 6356992 | tf_op jit(solution)/shard_map/reduce_sum | solution.py:108
  247.5 1.2 fusion.13
  248.7 2.3 copy.32
  (42 shorter events, 7.1 us)
Async XLA Ops:
  7.2 1.2 copy-start
  7.2 62.0 %all-gather.5.cloned.1.call-start = ((), (), s32[]{:S(2)}) async-start(), calls=%async_computation.2 | async-start | bytes 1310720 | tf_op jit(solution)/shard_map/all_gather | solution.py:79
  9.1 95.6 %all-gather.7.cloned.1.call-start = ((), (), s32[]{:S(2)}) async-start(), calls=%async_computation.3 | async-start | bytes 1310720 | tf_op jit(solution)/shard_map/all_gather | solution.py:80
  83.9 15.8 %copy-start.2 = (f32[8,256,1024]{2,1,0:T(8,128)S(1)}, f32[8,256,1024]{2,1,0:T(8,128)}, u32[]{:S(2)}) copy-start(f32[8,256,1024]{2,1,0:T(8,128)} %get-tuple-element.22) | copy-start | bytes 25165828
  99.8 2.6 %copy-start.3 = (bf16[1024,128]{0,1:T(8,128)(2,1)S(1)}, bf16[1024,128]{0,1:T(8,128)(2,1)}, u32[]{:S(2)}) copy-start(bf16[1024,128]{0,1:T(8,128)(2,1)} %all-gather.1) | copy-start | bytes 786436
  133.9 11.5 %all-to-all-start.1 = ((bf16[256,4,16]{0,2,1:T(8,128)(2,1)}), bf16[256,4,16]{0,2,1:T(8,128)(2,1)S(1)}, u32[]{:S(2)}, u32[]{:S(2)}) async-start(bf16[256,4,16]{0,2,1:T(8,128)(2,1)} %bitcast.27), calls=%async_computation.1 | async-start | bytes 65536 | tf_op jit(solution)/shard_map/all_to_all | solution.py:104
  145.3 98.6 %all-to-all-start = ((bf16[256,4,2048]{0,2,1:T(8,128)(2,1)}), bf16[256,4,2048]{0,2,1:T(8,128)(2,1)}, u32[]{:S(2)}, u32[]{:S(2)}) async-start(bf16[256,4,2048]{0,2,1:T(8,128)(2,1)} %bitcast.75), calls=%async_computation | async-start | bytes 8388608 | tf_op jit(solution)/shard_map/all_to_all | solution.py:103
  150.4 100.5 %copy-start.1 = (bf16[4,1024,128]{2,1,0:T(8,128)(2,1)S(1)}, bf16[4,1024,128]{2,1,0:T(8,128)(2,1)}, u32[]{:S(2)}) copy-start(bf16[4,1024,128]{2,1,0:T(8,128)(2,1)} %param.11) | copy-start | bytes 3145732
  247.5 3.4 %copy-start.4 = (f32[256,16]{0,1:T(8,128)}, f32[256,16]{0,1:T(8,128)S(1)}, u32[]{:S(2)}) copy-start(f32[256,16]{0,1:T(8,128)S(1)} %copy.31) | copy-start | bytes 49156
Sparse Core Ops, SparseCore 0:
  10.1 19.4 all-gather.4
  31.2 16.7 all-gather.6
where the time goes:
time: 259 us; the launch traced here: 258 us
  waiting for transfers between devices  93.5 us (36%)
  matrix products  51.5 us (20%)
  other arithmetic  34.4 us (13%)
  local copies, waits for them, and re-layouts  33.6 us (13%)
  blocking collectives  19.1 us (7%)
  between operations  15.6 us (6%)
  starting transfers between devices  10 us (4%)
    all_to_all x1, waiting for transfers between devices, local(): lax.all_to_all(coded_lanes, 'tensor', split_axis=1, concat_axis=1, tiled=...  93.5 us
    dot_general x1, local copies, waits for them, and re-layouts, local(): jnp.dot(attended, out_weight, preferred_element_type=jnp.float32)  22.4 us
    dot_general x2, matrix products, attend(): jnp.einsum('kgrd,knd->kgrn', query, keys, preferred_element_type=jnp.floa...  20.7 us
    reduce_sum x2, other arithmetic, attend(): totals = totals * shrink + jnp.sum(weights, axis=3)  18.4 us
    dot_general x2, matrix products, attend(): jnp.einsum('kgrn,knd->kgrd', weights.astype(jnp.bfloat16), values, prefer...  17.4 us
    dot_general x1, matrix products, local(): jnp.dot(attended, out_weight, preferred_element_type=jnp.float32)  13.5 us
    unnamed x21, local copies, waits for them, and re-layouts  8.42 us
    convert_element_type x1, other arithmetic, local(): (blocks / scales[..., None]).astype(jnp.bfloat16)  6.58 us
  transfers between devices with their start and end apart: 4, of which 1 were waited for; matrix products, arithmetic and copies ran while one was open for 32% of the time, Pallas kernels for 0%

commit v1 on v0

v1 whole, which is shorter than its diff:
```python
import functools
import math

import jax
import jax.numpy as jnp
from jax import lax
from jax.experimental import pallas as pl
from jax.experimental.pallas import tpu as pltpu
from jax.sharding import PartitionSpec as P

D = 8192
HD = 128
HQ = 32
KVH = 4
BLOCK = 128
LEN_ROWS = 16
LOW = 32
NEG = -1e30
VMEM_LIMIT = 48 * 1024 * 1024
F32 = jnp.float32
BF16 = jnp.bfloat16
NT = (((1,), (1,)), ((), ()))


def params(steps=1):
    return pltpu.CompilerParams(
        dimension_semantics=("arbitrary",) * steps, vmem_limit_bytes=VMEM_LIMIT
    )


def cost(flops, nbytes, transcendentals=0):
    return pl.CostEstimate(
        flops=int(flops), bytes_accessed=int(nbytes), transcendentals=int(transcendentals)
    )


def rotated(x, cosine, sine):
    return x * cosine + pltpu.roll(x, HD // 2, 1) * sine


def pack_first_kernel(info_ref, k_ref, v_ref, out_ref):
    half = k_ref.shape[1]
    out_ref[0, :half] = k_ref[0]
    out_ref[1, :half] = v_ref[0]
    live = info_ref[1]
    high = (live // LOW).astype(F32)
    low = (live % LOW).astype(F32)
    out_ref[0, half:] = jnp.full((LEN_ROWS, HD), high, F32).astype(BF16)
    out_ref[1, half:] = jnp.full((LEN_ROWS, HD), low, F32).astype(BF16)


def pack_first(info, key_cache, value_cache):
    half = key_cache.shape[1] // 2
    spec = pl.BlockSpec((1, half, HD), lambda i, info: (info[0], 0, 0))
    return pl.pallas_call(
        pack_first_kernel,
        out_shape=jax.ShapeDtypeStruct((2, half + LEN_ROWS, HD), BF16),
        grid_spec=pltpu.PrefetchScalarGridSpec(
            num_scalar_prefetch=1,
            grid=(1,),
            in_specs=[spec, spec],
            out_specs=pl.BlockSpec((2, half + LEN_ROWS, HD), lambda i, info: (0, 0, 0)),
        ),
        compiler_params=params(),
        cost_estimate=cost(0, 4 * half * HD * 2),
        name="pack_first",
    )(info, key_cache, value_cache)


def pack_second_kernel(info_ref, k_ref, v_ref, nk_ref, nv_ref, cos_ref, sin_ref, out_ref):
    half = k_ref.shape[1]
    out_ref[0, :half] = k_ref[0]
    out_ref[1, :half] = v_ref[0]
    out_ref[0, half:] = rotated(nk_ref[...].astype(F32), cos_ref[...], sin_ref[...]).astype(BF16)
    out_ref[1, half:] = nv_ref[...]


def pack_second(info, key_cache, value_cache, new_keys, new_values, cosine, sine):
    half = key_cache.shape[1] // 2
    rows = new_keys.shape[0]
    cache_spec = pl.BlockSpec((1, half, HD), lambda i, info: (info[0], 1, 0))
    new_spec = pl.BlockSpec((rows, HD), lambda i, info: (0, info[0]))
    table_spec = pl.BlockSpec((rows, HD), lambda i, info: (0, 0))
    return pl.pallas_call(
        pack_second_kernel,
        out_shape=jax.ShapeDtypeStruct((2, half + rows, HD), BF16),
        grid_spec=pltpu.PrefetchScalarGridSpec(
            num_scalar_prefetch=1,
            grid=(1,),
            in_specs=[cache_spec, cache_spec, new_spec, new_spec, table_spec, table_spec],
            out_specs=pl.BlockSpec((2, half + rows, HD), lambda i, info: (0, 0, 0)),
        ),
        compiler_params=params(),
        cost_estimate=cost(0, 4 * (half + rows) * HD * 2),
        name="pack_second",
    )(info, key_cache, value_cache, new_keys, new_values, cosine, sine)


def rope_kernel(q_ref, cos_ref, sin_ref, out_ref):
    factor = math.log2(math.e) / math.sqrt(HD)
    cosine = cos_ref[...] * factor
    sine = sin_ref[...] * factor
    for head in range(q_ref.shape[1] // HD):
        at = slice(head * HD, (head + 1) * HD)
        out_ref[:, at] = rotated(q_ref[:, at].astype(F32), cosine, sine).astype(BF16)


def rope_queries(queries, cosine, sine):
    return pl.pallas_call(
        rope_kernel,
        out_shape=jax.ShapeDtypeStruct(queries.shape, BF16),
        compiler_params=pltpu.CompilerParams(vmem_limit_bytes=VMEM_LIMIT),
        cost_estimate=cost(queries.size * 4, queries.size * 4),
        name="rope_queries",
    )(queries, cosine, sine)


def lane_max(x):
    parts = [x[:, i : i + HD] for i in range(0, x.shape[1], HD)]
    return functools.reduce(jnp.maximum, parts)


def lane_sum(x):
    parts = [x[:, i : i + HD] for i in range(0, x.shape[1], HD)]
    return functools.reduce(jnp.add, parts)


def attend_kernel(plan, lens, first, last, heads_per_step, n_kv, offs_ref, *refs):
    q_ref = refs[0]
    kv_refs = refs[1 : 1 + n_kv]
    refs = refs[1 + n_kv :]
    if not first:
        acc_in, top_in, sum_in = refs[:3]
        refs = refs[3:]
    rows = q_ref.shape[0]
    masks = []
    for array, begin, count, kind, argument in plan:
        if kind == "live":
            ref = kv_refs[lens[array]]
            at = ref.shape[1] - LEN_ROWS
            live = ref[0, at : at + 8, :].astype(F32) * LOW + ref[1, at : at + 8, :].astype(F32)
            live = live[:1, :]
            slot = lax.broadcasted_iota(jnp.int32, (1, HD), 1).astype(F32)
            pieces = [
                jnp.where(slot + float(argument + i) < live, 0.0, NEG)
                for i in range(0, count, HD)
            ]
            masks.append(jnp.concatenate(pieces, axis=1))
        else:
            row = lax.broadcasted_iota(jnp.int32, (rows, count), 0)
            column = lax.broadcasted_iota(jnp.int32, (rows, count), 1)
            masks.append(jnp.where(column <= row + offs_ref[argument], 0.0, NEG))
    for head in range(heads_per_step):
        at = slice(head * HD, (head + 1) * HD)
        query = q_ref[:, at]
        scores = []
        for (array, begin, count, kind, argument), mask in zip(plan, masks):
            keys = kv_refs[array][0, begin : begin + count, :]
            scores.append(lax.dot_general(query, keys, NT, preferred_element_type=F32) + mask)
        peak = functools.reduce(jnp.maximum, [lane_max(x) for x in scores])
        peak = jnp.max(peak, axis=1, keepdims=True)
        if not first:
            before = top_in[:, at]
            peak = jnp.maximum(before, peak)
            shrink = jnp.exp2(before - peak)
        else:
            peak = jnp.broadcast_to(peak, (rows, HD))
        total = None
        out = None
        for (array, begin, count, kind, argument), score in zip(plan, scores):
            weights = jnp.exp2(score - peak[:, :1])
            part = lane_sum(weights)
            total = part if total is None else total + part
            values = kv_refs[array][1, begin : begin + count, :]
            update = jnp.dot(weights.astype(BF16), values, preferred_element_type=F32)
            out = update if out is None else out + update
        if not first:
            total = total + sum_in[:, at] * shrink
            out = out + acc_in[:, at] * shrink
        if last:
            denominator = jnp.sum(total, axis=1, keepdims=True)
            refs[0][:, at] = (out / denominator).astype(BF16)
        else:
            refs[0][:, at] = out
            refs[1][:, at] = peak
            refs[2][:, at] = total


def attend(name, query, arrays, plan, lens, offs, state, last, heads_per_step=2):
    rows, width = query.shape
    heads_per_step = min(heads_per_step, width // HD)
    first = state is None
    block = pl.BlockSpec((rows, heads_per_step * HD), lambda i, offs: (0, i))
    in_specs = [block]
    for array in arrays:
        in_specs.append(pl.BlockSpec(array.shape, lambda i, offs: (0, 0, 0)))
    state = () if first else state
    in_specs += [block] * len(state)
    if last:
        out_shape = jax.ShapeDtypeStruct((rows, width), BF16)
        out_specs = block
    else:
        out_shape = (jax.ShapeDtypeStruct((rows, width), F32),) * 3
        out_specs = (block,) * 3
    keys = sum(p[2] for p in plan)
    return pl.pallas_call(
        functools.partial(
            attend_kernel, plan, lens, first, last, heads_per_step, len(arrays)
        ),
        out_shape=out_shape,
        grid_spec=pltpu.PrefetchScalarGridSpec(
            num_scalar_prefetch=1,
            grid=(width // (heads_per_step * HD),),
            in_specs=in_specs,
            out_specs=out_specs,
        ),
        compiler_params=params(),
        cost_estimate=cost(
            8 * rows * width * keys, rows * width * 14 + keys * HD * 4, rows * (width // HD) * keys
        ),
        name=name,
    )(offs, query, *arrays, *state)


def project_kernel(order_ref, x_ref, w_ref, out_ref):
    out_ref[0] = jnp.dot(x_ref[...], w_ref[...], preferred_element_type=F32).astype(BF16)


def project(name, order, begin, count, attended, out_weight, chunk, tile=1024):
    rows, depth = attended.shape
    tile = min(tile, chunk)
    per = chunk // tile
    return pl.pallas_call(
        project_kernel,
        out_shape=jax.ShapeDtypeStruct((count, rows, chunk), BF16),
        grid_spec=pltpu.PrefetchScalarGridSpec(
            num_scalar_prefetch=1,
            grid=(count, per),
            in_specs=[
                pl.BlockSpec((rows, depth), lambda i, j, order: (0, 0)),
                pl.BlockSpec((depth, tile), lambda i, j, order: (0, order[begin + i] * per + j)),
            ],
            out_specs=pl.BlockSpec((1, rows, tile), lambda i, j, order: (i, 0, j)),
        ),
        compiler_params=params(2),
        cost_estimate=cost(2 * rows * depth * chunk * count, depth * chunk * count * 2),
        name=name,
    )(order, attended, out_weight)


def finish_kernel(parts, out_ref, scale_ref):
    rows, columns = out_ref.shape
    blocks = columns // BLOCK
    lane = lax.broadcasted_iota(jnp.int32, (rows, blocks), 1)
    scales = jnp.zeros((rows, blocks), F32)
    for block in range(blocks):
        at = slice(block * BLOCK, (block + 1) * BLOCK)
        total = functools.reduce(jnp.add, [part[:, at].astype(F32) for part in parts])
        scale = jnp.max(jnp.abs(total), axis=1, keepdims=True) + 1e-06
        out_ref[:, at] = (total / scale).astype(BF16)
        scales = jnp.where(lane == block, scale, scales)
    scale_ref[...] = scales


def finish(parts, tile=64):
    rows, columns = parts[0].shape
    tile = min(tile, rows)
    spec = pl.BlockSpec((tile, columns), lambda i: (i, 0))

    def kernel(*refs):
        finish_kernel(refs[: len(parts)], refs[-2], refs[-1])

    return pl.pallas_call(
        kernel,
        out_shape=(
            jax.ShapeDtypeStruct((rows, columns), BF16),
            jax.ShapeDtypeStruct((rows, columns // BLOCK), F32),
        ),
        grid=(rows // tile,),
        in_specs=[spec] * len(parts),
        out_specs=(spec, pl.BlockSpec((tile, columns // BLOCK), lambda i: (i, 0))),
        compiler_params=params(),
        cost_estimate=cost(rows * columns * 6, rows * columns * 2 * (len(parts) + 1)),
        name="finish",
    )(*parts)


def after(value, *others):
    return lax.optimization_barrier((value, *others))[0]


def added(a, b):
    return (a.astype(F32) + b.astype(F32)).astype(BF16)


def local(
    queries, new_keys, new_values, key_cache, value_cache, prefix_len, stretch_start, out_weight
):
    rows = queries.shape[0]
    heads_here = queries.shape[1] // HD
    group = HQ // KVH
    tensor_pos = lax.axis_index("tensor")
    lanes = lax.axis_size("tensor")
    n_seq, n_pipe = lax.axis_size("seq"), lax.axis_size("pipe")
    shards = n_seq * n_pipe
    assert heads_here <= group
    half = key_cache.shape[1] // 2
    kv_head = tensor_pos * heads_here // group
    me = lax.axis_index("seq") * n_pipe + lax.axis_index("pipe")
    info = jnp.stack([kv_head.astype(jnp.int32), prefix_len[0]])

    positions = stretch_start[0] + me * rows + jnp.arange(rows, dtype=jnp.int32)
    lane = jnp.arange(HD)
    freq = 500000.0 ** (-((lane % (HD // 2)).astype(F32) * 2.0 / HD))
    angle = positions.astype(F32)[:, None] * freq[None, :]
    cosine = jnp.cos(angle)
    sine = jnp.sin(angle) * jnp.where(lane < HD // 2, -1.0, 1.0)[None, :]

    own_a = pack_first(info, key_cache, value_cache)
    own_b = pack_second(info, key_cache, value_cache, new_keys, new_values, cosine, sine)
    query = rope_queries(queries, cosine, sine)

    def whole_plan(a, b, off):
        return [
            (a, 0, half, "live", 0),
            (b, 0, half, "live", half),
            (b, half, rows, "rows", off),
        ]

    if n_seq == 2 and n_pipe == 2:
        swap = [(0, 1), (1, 0)]
        far_a = lax.ppermute(own_a, "seq", swap)
        near_a = lax.ppermute(own_a, "pipe", swap)
        far_b = lax.ppermute(own_b, "seq", swap)
        near_b = lax.ppermute(own_b, "pipe", swap)
        cross_a = lax.ppermute(far_a, "pipe", swap)
        cross_b = lax.ppermute(far_b, "pipe", swap)
        offs = (me - jnp.stack([me, me ^ 1, me ^ 2, me ^ 3])).astype(jnp.int32) * rows
        state = attend(
            "attend_own", query, [own_a, own_b], whole_plan(0, 1, 0), {0: 0, 1: 0}, offs, None, False
        )
        state = attend(
            "attend_near", query, [near_a, near_b], whole_plan(0, 1, 1), {0: 0, 1: 0}, offs, state, False
        )
        state = attend(
            "attend_far_a",
            query,
            [far_a, cross_a],
            [(0, 0, half, "live", 0), (1, 0, half, "live", 0)],
            {0: 0, 1: 1},
            offs,
            state,
            False,
        )
        tail_a, tail_c = far_a[:, half:], cross_a[:, half:]
        attended = attend(
            "attend_far_b",
            query,
            [far_b, cross_b, tail_a, tail_c],
            [
                (0, 0, half, "live", half),
                (0, half, rows, "rows", 2),
                (1, 0, half, "live", half),
                (1, half, rows, "rows", 3),
            ],
            {0: 2, 1: 3},
            offs,
            state,
            True,
        )
    else:
        all_a = lax.all_gather(own_a, ("seq", "pipe"), axis=0)
        all_b = lax.all_gather(own_b, ("seq", "pipe"), axis=0)
        offs = (me - jnp.arange(shards)).astype(jnp.int32) * rows
        state = None
        for shard in range(shards):
            state = attend(
                "attend",
                query,
                [all_a[shard], all_b[shard]],
                whole_plan(0, 1, shard),
                {0: 0, 1: 0},
                offs,
                state,
                shard == shards - 1,
            )
        attended = state

    columns = D // lanes
    if lanes == 4:
        step = jnp.arange(4, dtype=jnp.int32)
        order = jnp.where(tensor_pos < 2, 3 - step, step)
        inward = [(0, 1), (3, 2)]
        middle = [(1, 2), (2, 1)]
        outward = [(1, 0), (2, 3)]
        p0 = project("project_0", order, 0, 1, attended, out_weight, columns)[0]
        rest = project("project_rest", order, 1, 3, attended, out_weight, columns)
        p1, p2, p3 = rest[0], rest[1], rest[2]
        cut = rows // 2
        halves = [slice(0, cut), slice(cut, rows)]
        e1 = [lax.ppermute(p0[h], "tensor", inward) for h in halves]
        e2, o1, e3, o2, f = [], [], [], [], []
        for i, h in enumerate(halves):
            e2.append(lax.ppermute(after(p1[h], e1[i]), "tensor", inward))
            o1.append(lax.ppermute(added(p0[h], e1[i]), "tensor", middle))
        for i, h in enumerate(halves):
            e3.append(lax.ppermute(after(p2[h], e2[i]), "tensor", inward))
            o2.append(lax.ppermute(added(p1[h], e2[i]), "tensor", middle))
            f.append(lax.ppermute(added(p3[h], o1[i]), "tensor", outward))
        outer = (tensor_pos == 0) | (tensor_pos == 3)
        values, scales = [], []
        for i, h in enumerate(halves):
            zero = jnp.zeros_like(e3[i])
            parts = [
                jnp.where(outer, p3[h], p2[h]),
                jnp.where(outer, f[i], e3[i]),
                jnp.where(outer, zero, o2[i]),
            ]
            v, s = finish(parts)
            values.append(v)
            scales.append(s)
        return jnp.concatenate(values, axis=0), jnp.concatenate(scales, axis=0)
    order = jnp.arange(lanes, dtype=jnp.int32)
    partial = project("project_all", order, 0, lanes, attended, out_weight, columns)
    total = lax.psum_scatter(partial, "tensor", scatter_dimension=0, tiled=True)[0]
    return tuple(finish([total]))


def solution(mesh):
    return jax.shard_map(
        local,
        mesh=mesh,
        in_specs=(
            P(("groups", "seq", "pipe"), "tensor"),
            P(("groups", "seq", "pipe"), None),
            P(("groups", "seq", "pipe"), None),
            P(None, ("groups", "seq", "pipe"), None),
            P(None, ("groups", "seq", "pipe"), None),
            P(("groups", "seq", "pipe")),
            P("groups"),
            P("tensor", None),
        ),
        out_specs=(P(("groups", "seq", "pipe"), "tensor"), P(("groups", "seq", "pipe"), "tensor")),
        check_vma=False,
    )
```

time: 259 us -> 139 us (0.54)
  waiting for transfers between devices: 93.5 us -> 27.7 us
  matrix products: 51.5 us -> 0 us
  Pallas kernels: 0 us -> 45.7 us
  starting transfers between devices: 10 us -> 44.4 us
  other arithmetic: 34.4 us -> 6.78 us
  local copies, waits for them, and re-layouts: 33.6 us -> 10.3 us
  blocking collectives: 19.1 us -> 0 us
  between operations: 15.6 us -> 2.29 us
    all_to_all x2 -> x0, waiting for transfers between devices: 93.5 us -> none  [the longest x1 93.5 us: local(): lax.all_to_all(coded_lanes, 'tensor', split_axis=1, concat_axis=1, tiled=...]
    dot_general x5 -> x0, matrix products: 51.5 us -> none  [the longest x2 20.7 us: attend(): jnp.einsum('kgrd,knd->kgrn', query, keys, preferred_element_type=jnp.floa...]
    pallas_call x0 -> x11, Pallas kernels: none -> 45.7 us  [the longest x4 30.8 us: attend(): pl.pallas_call(functools.partial(attend_kernel, plan, lens, first, last,...]
    ppermute x0 -> x18, starting transfers between devices: none -> 44.4 us  [the longest x2 16.9 us: local(): e3.append(lax.ppermute(after(p2[h], e2[i]), 'tensor', inward))]
    ppermute x0 -> x18, waiting for transfers between devices: none -> 27.7 us  [the longest x2 7.88 us: local(): e1 = [lax.ppermute(p0[h], 'tensor', inward) for h in halves]]
    dot_general x1 -> x0, local copies, waits for them, and re-layouts: 22.4 us -> none  [local(): jnp.dot(attended, out_weight, preferred_element_type=jnp.float32)]
    reduce_sum x3 -> x0, other arithmetic: 21.6 us -> none  [the longest x2 18.4 us: attend(): totals = totals * shrink + jnp.sum(weights, axis=3)]
    all_gather x2 -> x0, blocking collectives: 12.8 us -> none  [the longest x1 6.52 us: local(): values = lax.all_gather(stretch_values, ('seq', 'pipe'), axis=1, tiled=True)]
  transfers between devices with their start and end apart: 4 -> 18, of which waited for: 1 -> 8; matrix products, arithmetic and copies ran while one was open for 32% -> 5% of each run, Pallas kernels for 0% -> 24%
where the time goes in v1:
time: 139 us; the launch traced here: 137 us
  Pallas kernels  45.7 us (33%)
  starting transfers between devices  44.4 us (32%)
  waiting for transfers between devices  27.7 us (20%)
  local copies, waits for them, and re-layouts  10.3 us (7%)
  other arithmetic  6.78 us (5%)
  between operations  2.29 us (2%)
    pallas_call x4, Pallas kernels, attend(): pl.pallas_call(functools.partial(attend_kernel, plan, lens, first, last,...  30.8 us
    ppermute x2, starting transfers between devices, local(): e3.append(lax.ppermute(after(p2[h], e2[i]), 'tensor', inward))  16.9 us
    ppermute x2, starting transfers between devices, local(): e2.append(lax.ppermute(after(p1[h], e1[i]), 'tensor', inward))  13.3 us
    pallas_call x2, Pallas kernels, project(): pl.pallas_call(project_kernel, out_shape=jax.ShapeDtypeStruct((count, row...  12.3 us
    unnamed x24, local copies, waits for them, and re-layouts  8.27 us
    ppermute x2, waiting for transfers between devices, local(): e1 = [lax.ppermute(p0[h], 'tensor', inward) for h in halves]  7.88 us
    ppermute x2, waiting for transfers between devices, local(): f.append(lax.ppermute(added(p3[h], o1[i]), 'tensor', outward))  7.45 us
    ppermute x2, waiting for transfers between devices, local(): e2.append(lax.ppermute(after(p1[h], e1[i]), 'tensor', inward))  7.14 us
  transfers between devices with their start and end apart: 18, of which 8 were waited for; matrix products, arithmetic and copies ran while one was open for 5% of the time, Pallas kernels for 24%

profile of v1, /device:TPU:0, one launch (start us, length us, event | category | flops | bytes accessed | tf_op | source)
XLA Modules:
  0.0 137.1 jit_solution(3288798483828828123)
XLA Ops:
  1.4 1.2 copy-done
  2.6 1.2 copy-done.2
  4.9 2.6 %collective-permute-start.2 = (bf16[2,528,128]{2,1,0:T(8,128)(2,1)S(1)}, bf16[2,528,128]{2,1,0:T(8,128)(2,1)}, u32[]{:S(2)}, u32[]{:S(2)}) collective-permute-start(bf16[2,528,128]{2,1,0:T(8,128)(2,1)S(1)} %pack_first.1.refs_1_), channel_id=1, source_target_pairs={{0,2},{2,0},{1,3},{3,1},{4,6},{6,4},{5,7},{7,5},{8,10},{10,8},{9,1... | collective-permute-start | bytes 811016 | tf_op jit(solution)/shard_map/ppermute | solution.py:332
  12.2 6.3 %attend_own.1 = (f32[256,1024]{1,0:T(8,128)S(1)}, f32[256,1024]{1,0:T(8,128)S(1)}, f32[256,1024]{1,0:T(8,128)S(1)}) custom-call(s32[4]{0:T(128)S(1)} %fusion.5.offs_ref, bf16[256,1024]{1,0:T(8,128)(2,1)S(1)} %rope_queries.1.refs_0_, bf16[2,528,128]{2,1,0:T(8,128)(2,1)S(1)} %pack_first.1.refs_1_, bf16[2,768,128]{2,1,0:T(8,128)(2,1)S(1)} %pack_second.1.refs_2_), custom_call_target="tpu_custom_call" | custom-call | flops 2684354560 | bytes 4325376 | tf_op jit(solution)/shard_map/attend_own/pallas_call | solution.py:206
  21.3 1.7 %collective-permute-done.refs_1_ = bf16[2,768,128]{2,1,0:T(8,128)(2,1)S(1)} collective-permute-done((bf16[2,768,128]{2,1,0:T(8,128)(2,1)S(1)}, bf16[2,768,128]{2,1,0:T(8,128)(2,1)S(1)}, u32[]{:S(2)}, u32[]{:S(2)}) %collective-permute-start) | collective-permute-done | bytes 393248 | tf_op jit(solution)/shard_map/ppermute | solution.py:334
  23.0 8.6 %attend_near.1 = (f32[256,1024]{1,0:T(8,128)S(1)}, f32[256,1024]{1,0:T(8,128)S(1)}, f32[256,1024]{1,0:T(8,128)S(1)}) custom-call(s32[4]{0:T(128)S(1)} %fusion.5.offs_ref, bf16[256,1024]{1,0:T(8,128)(2,1)S(1)} %rope_queries.1.refs_0_, bf16[2,528,128]{2,1,0:T(8,128)(2,1)} %collective-permute-done.4.refs_1_, ...), custom_call_target="tpu_custom_call" | custom-call | flops 2684354560 | bytes 4325376 | tf_op jit(solution)/shard_map/attend_near/pallas_call | solution.py:206
  33.6 7.5 %attend_far_a.1 = (f32[256,1024]{1,0:T(8,128)S(1)}, f32[256,1024]{1,0:T(8,128)S(1)}, f32[256,1024]{1,0:T(8,128)S(1)}) custom-call(s32[4]{0:T(128)S(1)} %fusion.5.offs_ref, bf16[256,1024]{1,0:T(8,128)(2,1)S(1)} %rope_queries.1.refs_0_, bf16[2,528,128]{2,1,0:T(8,128)(2,1)} %collective-permute-done.2.refs_1_, ...), custom_call_target="tpu_custom_call" | custom-call | flops 2147483648 | bytes 4194304 | tf_op jit(solution)/shard_map/attend_far_a/pallas_call | solution.py:206
  41.1 8.4 %attend_far_b.1.x_ref = bf16[256,1024]{1,0:T(8,128)(2,1)S(1)} custom-call(s32[4]{0:T(128)S(1)} %fusion.5.offs_ref, bf16[256,1024]{1,0:T(8,128)(2,1)S(1)} %rope_queries.1.refs_0_, bf16[2,768,128]{2,1,0:T(8,128)(2,1)S(1)} %collective-permute-done.refs_1_, bf16[2,768,128]{2,1,0:T(8,128)(2,1)S(1)} %collective-permute-done.1.refs_2_, ...), custom_call_target="tpu_custom_call" | custom-call | flops 3221225472 | bytes 4456448 | tf_op jit(solution)/shard_map/attend_far_b/pallas_call | solution.py:206
  49.5 3.6 %project_0.1 = bf16[1,256,2048]{2,1,0:T(8,128)(2,1)S(1)} custom-call(s32[4]{0:T(128)S(1)} %broadcast_select_fusion.6.order_ref, bf16[256,1024]{1,0:T(8,128)(2,1)S(1)} %attend_far_b.1.x_ref, bf16[1024,8192]{1,0:T(8,128)(2,1)} %w_ref.3), custom_call_target="tpu_custom_call" | custom-call | flops 1073741824 | bytes 4194304 | tf_op jit(solution)/shard_map/project_0/pallas_call | solution.py:233
  53.3 3.8 %collective-permute-start.6 = (bf16[128,2048]{1,0:T(8,128)(2,1)S(1)}, bf16[128,2048]{1,0:T(8,128)(2,1)S(1)}, u32[]{:S(2)}, u32[]{:S(2)}) collective-permute-start(bf16[128,2048]{1,0:T(8,128)(2,1)S(1)} %get-tuple-element.50), channel_id=1, source_target_pairs={{0,4},{12,8},{1,5},{13,9},{2,6},{14,10},{3,7},{15,11},{16,20},{28,... | collective-permute-start | bytes 1572872 | tf_op jit(solution)/shard_map/ppermute | solution.py:401
  57.1 1.3 collective-permute-start.12
  58.4 8.7 %project_rest.1 = bf16[3,256,2048]{2,1,0:T(8,128)(2,1)S(1)} custom-call(s32[4]{0:T(128)S(1)} %broadcast_select_fusion.6.order_ref, bf16[256,1024]{1,0:T(8,128)(2,1)S(1)} %attend_far_b.1.x_ref, bf16[1024,8192]{1,0:T(8,128)(2,1)} %w_ref.3), custom_call_target="tpu_custom_call" | custom-call | flops 3221225472 | bytes 12582912 | tf_op jit(solution)/shard_map/project_rest/pallas_call | solution.py:233
  69.3 4.4 %collective-permute-start.9 = (bf16[128,2048]{1,0:T(8,128)(2,1)S(1)}, bf16[128,2048]{1,0:T(8,128)(2,1)S(1)}, u32[]{:S(2)}, u32[]{:S(2)}) collective-permute-start(bf16[128,2048]{1,0:T(8,128)(2,1)S(1)} %get-tuple-element.28), channel_id=1, source_target_pairs={{0,4},{12,8},{1,5},{13,9},{2,6},{14,10},{3,7},{15,11},{16,20},{28,... | collective-permute-start | bytes 1572872 | tf_op jit(solution)/shard_map/ppermute | solution.py:404
  73.7 6.8 %collective-permute-done.12 = bf16[128,2048]{1,0:T(8,128)(2,1)S(1)} collective-permute-done((bf16[128,2048]{1,0:T(8,128)(2,1)S(1)}, bf16[128,2048]{1,0:T(8,128)(2,1)S(1)}, u32[]{:S(2)}, u32[]{:S(2)}) %collective-permute-start.12) | collective-permute-done | bytes 524320 | tf_op jit(solution)/shard_map/ppermute | solution.py:401
  82.3 8.9 %collective-permute-start.15 = (bf16[128,2048]{1,0:T(8,128)(2,1)S(1)}, bf16[128,2048]{1,0:T(8,128)(2,1)S(1)}, u32[]{:S(2)}, u32[]{:S(2)}) collective-permute-start(bf16[128,2048]{1,0:T(8,128)(2,1)S(1)} %get-tuple-element.31), channel_id=1, source_target_pairs={{0,4},{12,8},{1,5},{13,9},{2,6},{14,10},{3,7},{15,11},{16,20},{28,... | collective-permute-start | bytes 1572872 | tf_op jit(solution)/shard_map/ppermute | solution.py:404
  91.7 5.2 %collective-permute-start.10 = (bf16[128,2048]{1,0:T(8,128)(2,1)}, bf16[128,2048]{1,0:T(8,128)(2,1)}, u32[]{:S(2)}, u32[]{:S(2)}) collective-permute-start(bf16[128,2048]{1,0:T(8,128)(2,1)} %get-tuple-element.29), channel_id=1, source_target_pairs={{0,4},{12,8},{1,5},{13,9},{2,6},{14,10},{3,7},{15,11},{16,20},{28,... | collective-permute-start | bytes 1572872 | tf_op jit(solution)/shard_map/ppermute | solution.py:407
  96.9 6.6 %collective-permute-done.15 = bf16[128,2048]{1,0:T(8,128)(2,1)S(1)} collective-permute-done((bf16[128,2048]{1,0:T(8,128)(2,1)S(1)}, bf16[128,2048]{1,0:T(8,128)(2,1)S(1)}, u32[]{:S(2)}, u32[]{:S(2)}) %collective-permute-start.15) | collective-permute-done | bytes 524320 | tf_op jit(solution)/shard_map/ppermute | solution.py:404
  103.5 1.9 %add_convert_fusion.3 = (bf16[128,2048]{1,0:T(8,128)(2,1)}, bf16[128,2048]{1,0:T(8,128)(2,1)}, bf16[128,2048]{1,0:T(8,128)(2,1)}, bf16[128,2048]{1,0:T(8,128)(2,1)}) fusion(bf16[128,2048]{1,0:T(8,128)(2,1)S(1)} %collective-permute-done.9, bf16[3,256,2048]{2,1,0:T(8,128)(2,1)S(1)} %project_rest.1, bf16[128,2048]{1,0:T(8,128)(2,1)S(1)} %collective-permute-done.15, ...), kind=kLoop, calls=%fused_computation.4 | loop fusion | flops 4194304 | bytes 6291456 | tf_op jit(solution)/shard_map/convert_element_type | solution.py:293
  105.4 1.3 collective-permute-start.8
  108.3 11.7 %collective-permute-start.16 = (bf16[128,2048]{1,0:T(8,128)(2,1)}, bf16[128,2048]{1,0:T(8,128)(2,1)S(1)}, u32[]{:S(2)}, u32[]{:S(2)}) collective-permute-start(bf16[128,2048]{1,0:T(8,128)(2,1)} %get-tuple-element.32), channel_id=1, source_target_pairs={{0,4},{12,8},{1,5},{13,9},{2,6},{14,10},{3,7},{15,11},{16,20},{28,... | collective-permute-start | bytes 1572872 | tf_op jit(solution)/shard_map/ppermute | solution.py:407
  120.0 1.3 collective-permute-start.14
  122.1 2.5 %collective-permute-done.8 = bf16[128,2048]{1,0:T(8,128)(2,1)} collective-permute-done((bf16[128,2048]{1,0:T(8,128)(2,1)}, bf16[128,2048]{1,0:T(8,128)(2,1)}, u32[]{:S(2)}, u32[]{:S(2)}) %collective-permute-start.8) | collective-permute-done | bytes 524320 | tf_op jit(solution)/shard_map/ppermute | solution.py:409
  126.4 3.5 %collective-permute-done.16 = bf16[128,2048]{1,0:T(8,128)(2,1)S(1)} collective-permute-done((bf16[128,2048]{1,0:T(8,128)(2,1)}, bf16[128,2048]{1,0:T(8,128)(2,1)S(1)}, u32[]{:S(2)}, u32[]{:S(2)}) %collective-permute-start.16) | collective-permute-done | bytes 524320 | tf_op jit(solution)/shard_map/ppermute | solution.py:407
  129.8 5.0 %collective-permute-done.14 = bf16[128,2048]{1,0:T(8,128)(2,1)S(1)} collective-permute-done((bf16[128,2048]{1,0:T(8,128)(2,1)}, bf16[128,2048]{1,0:T(8,128)(2,1)S(1)}, u32[]{:S(2)}, u32[]{:S(2)}) %collective-permute-start.14) | collective-permute-done | bytes 524320 | tf_op jit(solution)/shard_map/ppermute | solution.py:409
  (68 shorter events, 21.0 us)
Async XLA Ops:
  1.4 1.2 copy-start
  2.6 1.2 copy-start.2
  3.8 4.9 %copy-start.1 = (bf16[4,1024,128]{2,1,0:T(8,128)(2,1)S(1)}, bf16[4,1024,128]{2,1,0:T(8,128)(2,1)}, u32[]{:S(2)}) copy-start(bf16[4,1024,128]{2,1,0:T(8,128)(2,1)} %k_ref.3) | copy-start | bytes 3145732
  3.8 4.9 %copy-start.3 = (bf16[4,1024,128]{2,1,0:T(8,128)(2,1)S(1)}, bf16[4,1024,128]{2,1,0:T(8,128)(2,1)}, u32[]{:S(2)}) copy-start(bf16[4,1024,128]{2,1,0:T(8,128)(2,1)} %v_ref.3) | copy-start | bytes 3145732
  3.8 8.0 %copy-start.5 = (bf16[256,1024]{1,0:T(8,128)(2,1)S(1)}, bf16[256,1024]{1,0:T(8,128)(2,1)}, u32[]{:S(2)}) copy-start(bf16[256,1024]{1,0:T(8,128)(2,1)} %q_ref.1) | copy-start | bytes 1572868
  4.4 18.6 %collective-permute-start.4 = (bf16[2,528,128]{2,1,0:T(8,128)(2,1)S(1)}, bf16[2,528,128]{2,1,0:T(8,128)(2,1)}, u32[]{:S(2)}, u32[]{:S(2)}) collective-permute-start(bf16[2,528,128]{2,1,0:T(8,128)(2,1)S(1)} %pack_first.1.refs_1_), channel_id=1, source_target_pairs={{0,1},{1,0},{2,3},{3,2},{4,5},{5,4},{6,7},{7,6},{8,9},{9,8},{10,11... | collective-permute-start | bytes 811016 | tf_op jit(solution)/shard_map/ppermute | solution.py:333
  4.9 15.6 %collective-permute-start.2 = (bf16[2,528,128]{2,1,0:T(8,128)(2,1)S(1)}, bf16[2,528,128]{2,1,0:T(8,128)(2,1)}, u32[]{:S(2)}, u32[]{:S(2)}) collective-permute-start(bf16[2,528,128]{2,1,0:T(8,128)(2,1)S(1)} %pack_first.1.refs_1_), channel_id=1, source_target_pairs={{0,2},{2,0},{1,3},{3,1},{4,6},{6,4},{5,7},{7,5},{8,10},{10,8},{9,1... | collective-permute-start | bytes 811016 | tf_op jit(solution)/shard_map/ppermute | solution.py:332
  11.3 11.7 %collective-permute-start.5 = (bf16[2,768,128]{2,1,0:T(8,128)(2,1)S(1)}, bf16[2,768,128]{2,1,0:T(8,128)(2,1)S(1)}, u32[]{:S(2)}, u32[]{:S(2)}) collective-permute-start(bf16[2,768,128]{2,1,0:T(8,128)(2,1)S(1)} %pack_second.1.refs_2_), channel_id=1, source_target_pairs={{0,1},{1,0},{2,3},{3,2},{4,5},{5,4},{6,7},{7,6},{8,9},{9,8},{10,11... | collective-permute-start | bytes 1179656 | tf_op jit(solution)/shard_map/ppermute | solution.py:335
  11.5 11.5 %collective-permute-start = (bf16[2,768,128]{2,1,0:T(8,128)(2,1)S(1)}, bf16[2,768,128]{2,1,0:T(8,128)(2,1)S(1)}, u32[]{:S(2)}, u32[]{:S(2)}) collective-permute-start(bf16[2,768,128]{2,1,0:T(8,128)(2,1)S(1)} %pack_second.1.refs_2_), channel_id=1, source_target_pairs={{0,2},{2,0},{1,3},{3,1},{4,6},{6,4},{5,7},{7,5},{8,10},{10,8},{9,1... | collective-permute-start | bytes 1179656 | tf_op jit(solution)/shard_map/ppermute | solution.py:334
  20.5 13.1 %collective-permute-start.3 = (bf16[2,528,128]{2,1,0:T(8,128)(2,1)}, bf16[2,528,128]{2,1,0:T(8,128)(2,1)S(1)}, u32[]{:S(2)}, u32[]{:S(2)}) collective-permute-start(bf16[2,528,128]{2,1,0:T(8,128)(2,1)} %collective-permute-done.2.refs_1_), channel_id=1, source_target_pairs={{0,1},{1,0},{2,3},{3,2},{4,5},{5,4},{6,7},{7,6},{8,9},{9,8},{10,11... | collective-permute-start | bytes 811016 | tf_op jit(solution)/shard_map/ppermute | solution.py:336
  23.0 18.1 %collective-permute-start.1 = (bf16[2,768,128]{2,1,0:T(8,128)(2,1)S(1)}, bf16[2,768,128]{2,1,0:T(8,128)(2,1)S(1)}, u32[]{:S(2)}, u32[]{:S(2)}) collective-permute-start(bf16[2,768,128]{2,1,0:T(8,128)(2,1)S(1)} %collective-permute-done.refs_1_), channel_id=1, source_target_pairs={{0,1},{1,0},{2,3},{3,2},{4,5},{5,4},{6,7},{7,6},{8,9},{9,8},{10,11... | collective-permute-start | bytes 1179656 | tf_op jit(solution)/shard_map/ppermute | solution.py:337
  53.3 16.0 %collective-permute-start.6 = (bf16[128,2048]{1,0:T(8,128)(2,1)S(1)}, bf16[128,2048]{1,0:T(8,128)(2,1)S(1)}, u32[]{:S(2)}, u32[]{:S(2)}) collective-permute-start(bf16[128,2048]{1,0:T(8,128)(2,1)S(1)} %get-tuple-element.50), channel_id=1, source_target_pairs={{0,4},{12,8},{1,5},{13,9},{2,6},{14,10},{3,7},{15,11},{16,20},{28,... | collective-permute-start | bytes 1572872 | tf_op jit(solution)/shard_map/ppermute | solution.py:401
  57.1 23.4 %collective-permute-start.12 = (bf16[128,2048]{1,0:T(8,128)(2,1)S(1)}, bf16[128,2048]{1,0:T(8,128)(2,1)S(1)}, u32[]{:S(2)}, u32[]{:S(2)}) collective-permute-start(bf16[128,2048]{1,0:T(8,128)(2,1)S(1)} %get-tuple-element.51), channel_id=1, source_target_pairs={{0,4},{12,8},{1,5},{13,9},{2,6},{14,10},{3,7},{15,11},{16,20},{28,... | collective-permute-start | bytes 1572872 | tf_op jit(solution)/shard_map/ppermute | solution.py:401
  69.3 22.5 %collective-permute-start.9 = (bf16[128,2048]{1,0:T(8,128)(2,1)S(1)}, bf16[128,2048]{1,0:T(8,128)(2,1)S(1)}, u32[]{:S(2)}, u32[]{:S(2)}) collective-permute-start(bf16[128,2048]{1,0:T(8,128)(2,1)S(1)} %get-tuple-element.28), channel_id=1, source_target_pairs={{0,4},{12,8},{1,5},{13,9},{2,6},{14,10},{3,7},{15,11},{16,20},{28,... | collective-permute-start | bytes 1572872 | tf_op jit(solution)/shard_map/ppermute | solution.py:404
  80.9 16.0 %collective-permute-start.13 = (bf16[128,2048]{1,0:T(8,128)(2,1)S(1)}, bf16[128,2048]{1,0:T(8,128)(2,1)S(1)}, u32[]{:S(2)}, u32[]{:S(2)}) collective-permute-start(bf16[128,2048]{1,0:T(8,128)(2,1)S(1)} %get-tuple-element.49), channel_id=1, source_target_pairs={{4,8},{8,4},{5,9},{9,5},{6,10},{10,6},{7,11},{11,7},{20,24},{24,20... | collective-permute-start | bytes 1572872 | tf_op jit(solution)/shard_map/ppermute | solution.py:405
  81.6 15.3 %collective-permute-start.7 = (bf16[128,2048]{1,0:T(8,128)(2,1)S(1)}, bf16[128,2048]{1,0:T(8,128)(2,1)S(1)}, u32[]{:S(2)}, u32[]{:S(2)}) collective-permute-start(bf16[128,2048]{1,0:T(8,128)(2,1)S(1)} %get-tuple-element.48), channel_id=1, source_target_pairs={{4,8},{8,4},{5,9},{9,5},{6,10},{10,6},{7,11},{11,7},{20,24},{24,20... | collective-permute-start | bytes 1572872 | tf_op jit(solution)/shard_map/ppermute | solution.py:405
  82.3 21.2 %collective-permute-start.15 = (bf16[128,2048]{1,0:T(8,128)(2,1)S(1)}, bf16[128,2048]{1,0:T(8,128)(2,1)S(1)}, u32[]{:S(2)}, u32[]{:S(2)}) collective-permute-start(bf16[128,2048]{1,0:T(8,128)(2,1)S(1)} %get-tuple-element.31), channel_id=1, source_target_pairs={{0,4},{12,8},{1,5},{13,9},{2,6},{14,10},{3,7},{15,11},{16,20},{28,... | collective-permute-start | bytes 1572872 | tf_op jit(solution)/shard_map/ppermute | solution.py:404
  91.7 29.5 %collective-permute-start.10 = (bf16[128,2048]{1,0:T(8,128)(2,1)}, bf16[128,2048]{1,0:T(8,128)(2,1)}, u32[]{:S(2)}, u32[]{:S(2)}) collective-permute-start(bf16[128,2048]{1,0:T(8,128)(2,1)} %get-tuple-element.29), channel_id=1, source_target_pairs={{0,4},{12,8},{1,5},{13,9},{2,6},{14,10},{3,7},{15,11},{16,20},{28,... | collective-permute-start | bytes 1572872 | tf_op jit(solution)/shard_map/ppermute | solution.py:407
  105.4 19.2 %collective-permute-start.8 = (bf16[128,2048]{1,0:T(8,128)(2,1)}, bf16[128,2048]{1,0:T(8,128)(2,1)}, u32[]{:S(2)}, u32[]{:S(2)}) collective-permute-start(bf16[128,2048]{1,0:T(8,128)(2,1)} %get-tuple-element.41), channel_id=1, source_target_pairs={{4,0},{8,12},{5,1},{9,13},{6,2},{10,14},{7,3},{11,15},{20,16},{24,... | collective-permute-start | bytes 1572872 | tf_op jit(solution)/shard_map/ppermute | solution.py:409
  106.7 19.0 %collective-permute-start.11 = (bf16[128,2048]{1,0:T(8,128)(2,1)}, bf16[128,2048]{1,0:T(8,128)(2,1)S(1)}, u32[]{:S(2)}, u32[]{:S(2)}) collective-permute-start(bf16[128,2048]{1,0:T(8,128)(2,1)} %get-tuple-element.38), channel_id=1, source_target_pairs={{4,8},{8,4},{5,9},{9,5},{6,10},{10,6},{7,11},{11,7},{20,24},{24,20... | collective-permute-start | bytes 1572872 | tf_op jit(solution)/shard_map/ppermute | solution.py:408
  108.3 21.6 %collective-permute-start.16 = (bf16[128,2048]{1,0:T(8,128)(2,1)}, bf16[128,2048]{1,0:T(8,128)(2,1)S(1)}, u32[]{:S(2)}, u32[]{:S(2)}) collective-permute-start(bf16[128,2048]{1,0:T(8,128)(2,1)} %get-tuple-element.32), channel_id=1, source_target_pairs={{0,4},{12,8},{1,5},{13,9},{2,6},{14,10},{3,7},{15,11},{16,20},{28,... | collective-permute-start | bytes 1572872 | tf_op jit(solution)/shard_map/ppermute | solution.py:407
  120.0 14.9 %collective-permute-start.14 = (bf16[128,2048]{1,0:T(8,128)(2,1)}, bf16[128,2048]{1,0:T(8,128)(2,1)S(1)}, u32[]{:S(2)}, u32[]{:S(2)}) collective-permute-start(bf16[128,2048]{1,0:T(8,128)(2,1)} %get-tuple-element.40), channel_id=1, source_target_pairs={{4,0},{8,12},{5,1},{9,13},{6,2},{10,14},{7,3},{11,15},{20,16},{24,... | collective-permute-start | bytes 1572872 | tf_op jit(solution)/shard_map/ppermute | solution.py:409
  121.3 13.6 %copy-start.4 = (bf16[128,2048]{1,0:T(8,128)(2,1)S(1)}, bf16[128,2048]{1,0:T(8,128)(2,1)}, u32[]{:S(2)}) copy-start(bf16[128,2048]{1,0:T(8,128)(2,1)} %get-tuple-element.47.refs_0_) | copy-start | bytes 1572868
  121.3 5.0 %collective-permute-start.17 = (bf16[128,2048]{1,0:T(8,128)(2,1)}, bf16[128,2048]{1,0:T(8,128)(2,1)S(1)}, u32[]{:S(2)}, u32[]{:S(2)}) collective-permute-start(bf16[128,2048]{1,0:T(8,128)(2,1)} %get-tuple-element.39), channel_id=1, source_target_pairs={{4,8},{8,4},{5,9},{9,5},{6,10},{10,6},{7,11},{11,7},{20,24},{24,20... | collective-permute-start | bytes 1572872 | tf_op jit(solution)/shard_map/ppermute | solution.py:408
  (6 other events, 5.8 us)

commit v2 on v1

v2 whole, which is shorter than its diff:
```python
import functools
import math

import jax
import jax.numpy as jnp
from jax import lax
from jax.experimental import pallas as pl
from jax.experimental.pallas import tpu as pltpu
from jax.sharding import PartitionSpec as P

D = 8192
HD = 128
HQ = 32
KVH = 4
BLOCK = 128
LEN_ROWS = 16
LOW = 32
NEG = -1e30
VMEM_LIMIT = 24 * 1024 * 1024
F32 = jnp.float32
BF16 = jnp.bfloat16
NT = (((1,), (1,)), ((), ()))


SMEM = pl.BlockSpec(memory_space=pltpu.SMEM)
VMEM = pl.BlockSpec(memory_space=pltpu.VMEM)
HBM = pl.BlockSpec(memory_space=pltpu.HBM)
PARAMS = pltpu.CompilerParams(vmem_limit_bytes=VMEM_LIMIT)


def cost(flops, nbytes, transcendentals=0):
    return pl.CostEstimate(
        flops=int(flops), bytes_accessed=int(nbytes), transcendentals=int(transcendentals)
    )


def rotated(x, cosine, sine):
    return x * cosine + pltpu.roll(x, HD // 2, 1) * sine


def pack_first_kernel(info_ref, k_ref, v_ref, out_ref, sems):
    count = out_ref.shape[1] - LEN_ROWS
    head = info_ref[0]
    copies = [
        pltpu.make_async_copy(
            ref.at[head, pl.ds(0, count)], out_ref.at[at, pl.ds(0, count)], sems.at[at]
        )
        for at, ref in enumerate((k_ref, v_ref))
    ]
    for copy in copies:
        copy.start()
    live = info_ref[1]
    high = (live // LOW).astype(F32)
    low = (live % LOW).astype(F32)
    out_ref[0, count:] = jnp.full((LEN_ROWS, HD), high, F32).astype(BF16)
    out_ref[1, count:] = jnp.full((LEN_ROWS, HD), low, F32).astype(BF16)
    for copy in copies:
        copy.wait()


def pack_first(info, key_cache, value_cache, count):
    return pl.pallas_call(
        pack_first_kernel,
        out_shape=jax.ShapeDtypeStruct((2, count + LEN_ROWS, HD), BF16),
        in_specs=[SMEM, HBM, HBM],
        out_specs=VMEM,
        scratch_shapes=[pltpu.SemaphoreType.DMA((2,))],
        compiler_params=PARAMS,
        cost_estimate=cost(0, 4 * count * HD * 2),
        name="pack_first",
    )(info, key_cache, value_cache)


def pack_second_kernel(
    first, info_ref, k_ref, v_ref, nk_ref, nv_ref, cos_ref, sin_ref, out_ref, raw, sems
):
    rows = raw.shape[0]
    count = out_ref.shape[1] - rows
    head = info_ref[0]
    columns = pl.ds(pl.multiple_of(head * HD, HD), HD)
    copies = [
        pltpu.make_async_copy(nk_ref.at[:, columns], raw, sems.at[0]),
        pltpu.make_async_copy(nv_ref.at[:, columns], out_ref.at[1, pl.ds(count, rows)], sems.at[1]),
        pltpu.make_async_copy(
            k_ref.at[head, pl.ds(first, count)], out_ref.at[0, pl.ds(0, count)], sems.at[2]
        ),
        pltpu.make_async_copy(
            v_ref.at[head, pl.ds(first, count)], out_ref.at[1, pl.ds(0, count)], sems.at[3]
        ),
    ]
    for copy in copies:
        copy.start()
    copies[0].wait()
    out_ref[0, count:] = rotated(raw[...].astype(F32), cos_ref[...], sin_ref[...]).astype(BF16)
    for copy in copies[1:]:
        copy.wait()


def pack_second(info, key_cache, value_cache, new_keys, new_values, cosine, sine, first):
    rows = new_keys.shape[0]
    size = key_cache.shape[1] - first + rows
    return pl.pallas_call(
        functools.partial(pack_second_kernel, first),
        out_shape=jax.ShapeDtypeStruct((2, size, HD), BF16),
        in_specs=[SMEM, HBM, HBM, HBM, HBM, VMEM, VMEM],
        out_specs=VMEM,
        scratch_shapes=[pltpu.VMEM((rows, HD), BF16), pltpu.SemaphoreType.DMA((4,))],
        compiler_params=PARAMS,
        cost_estimate=cost(0, 4 * size * HD * 2),
        name="pack_second",
    )(info, key_cache, value_cache, new_keys, new_values, cosine, sine)


def rope_kernel(q_ref, cos_ref, sin_ref, out_ref):
    factor = math.log2(math.e) / math.sqrt(HD)
    cosine = cos_ref[...] * factor
    sine = sin_ref[...] * factor
    for head in range(q_ref.shape[1] // HD):
        at = slice(head * HD, (head + 1) * HD)
        out_ref[:, at] = rotated(q_ref[:, at].astype(F32), cosine, sine).astype(BF16)


def rope_queries(queries, cosine, sine):
    return pl.pallas_call(
        rope_kernel,
        out_shape=jax.ShapeDtypeStruct(queries.shape, BF16),
        compiler_params=PARAMS,
        cost_estimate=cost(queries.size * 4, queries.size * 4),
        name="rope_queries",
    )(queries, cosine, sine)


def lane_max(x):
    parts = [x[:, i : i + HD] for i in range(0, x.shape[1], HD)]
    return functools.reduce(jnp.maximum, parts)


def lane_sum(x):
    parts = [x[:, i : i + HD] for i in range(0, x.shape[1], HD)]
    return functools.reduce(jnp.add, parts)


def attend_kernel(plan, lens, first, last, n_kv, offs_ref, q_ref, *refs):
    kv_refs = refs[:n_kv]
    refs = refs[n_kv:]
    if not first:
        acc_in, stats_in = refs[:2]
        refs = refs[2:]
    rows = q_ref.shape[0]
    heads = q_ref.shape[1] // HD
    masks = []
    for array, begin, count, kind, argument in plan:
        if kind == "live":
            ref = kv_refs[lens[array]]
            at = ref.shape[1] - LEN_ROWS
            live = ref[0, at:, :].astype(F32) * LOW + ref[1, at:, :].astype(F32)
            live = live[:1, :]
            slot = lax.broadcasted_iota(jnp.int32, (1, HD), 1).astype(F32)
            pieces = [
                jnp.where(slot + float(argument + i) < live, 0.0, NEG)
                for i in range(0, count, HD)
            ]
            masks.append(jnp.concatenate(pieces, axis=1))
        else:
            row = lax.broadcasted_iota(jnp.int32, (rows, count), 0)
            column = lax.broadcasted_iota(jnp.int32, (rows, count), 1)
            masks.append(jnp.where(column <= row + offs_ref[argument], 0.0, NEG))

    def score(head):
        query = q_ref[:, head * HD : (head + 1) * HD]
        scores = []
        for (array, begin, count, kind, argument), mask in zip(plan, masks):
            keys = kv_refs[array][0, begin : begin + count, :]
            scores.append(lax.dot_general(query, keys, NT, preferred_element_type=F32) + mask)
        return scores

    lane = lax.broadcasted_iota(jnp.int32, (rows, HD), 1)
    stats = jnp.zeros((rows, HD), F32)
    following = score(0)
    for head in range(heads):
        scores = following
        if head + 1 < heads:
            following = score(head + 1)
        at = slice(head * HD, (head + 1) * HD)
        peak = functools.reduce(jnp.maximum, [lane_max(x) for x in scores])
        peak = jnp.max(peak, axis=1, keepdims=True)
        if not first:
            before = stats_in[:, head : head + 1]
            peak = jnp.maximum(before, peak)
            shrink = jnp.exp2(before - peak)
        total = None
        out = None
        for (array, begin, count, kind, argument), part in zip(plan, scores):
            weights = jnp.exp2(part - peak)
            subtotal = lane_sum(weights)
            total = subtotal if total is None else total + subtotal
            values = kv_refs[array][1, begin : begin + count, :]
            update = jnp.dot(weights.astype(BF16), values, preferred_element_type=F32)
            out = update if out is None else out + update
        total = jnp.sum(total, axis=1, keepdims=True)
        if not first:
            total = total + stats_in[:, HD // 2 + head : HD // 2 + head + 1] * shrink
            out = out + acc_in[:, at] * shrink
        if last:
            refs[0][:, at] = (out / total).astype(BF16)
        else:
            refs[0][:, at] = out
            stats = jnp.where(lane == head, peak, stats)
            stats = jnp.where(lane == HD // 2 + head, total, stats)
    if not last:
        refs[1][...] = stats


def attend(name, query, arrays, plan, lens, offs, state, last):
    rows, width = query.shape
    first = state is None
    state = () if first else state
    if last:
        out_shape = jax.ShapeDtypeStruct((rows, width), BF16)
        out_specs = VMEM
    else:
        out_shape = (
            jax.ShapeDtypeStruct((rows, width), F32),
            jax.ShapeDtypeStruct((rows, HD), F32),
        )
        out_specs = (VMEM, VMEM)
    keys = sum(p[2] for p in plan)
    return pl.pallas_call(
        functools.partial(attend_kernel, plan, lens, first, last, len(arrays)),
        out_shape=out_shape,
        in_specs=[SMEM] + [VMEM] * (1 + len(arrays) + len(state)),
        out_specs=out_specs,
        compiler_params=PARAMS,
        cost_estimate=cost(
            8 * rows * width * keys, rows * width * 8 + keys * HD * 4, rows * (width // HD) * keys
        ),
        name=name,
    )(offs, query, *arrays, *state)


def project_kernel(order_ref, x_ref, w_ref, *out_refs):
    out = jnp.dot(x_ref[...], w_ref[...], preferred_element_type=F32).astype(BF16)
    rows = out_refs[0].shape[0]
    for i, ref in enumerate(out_refs):
        ref[...] = out[i * rows : (i + 1) * rows]


def project(name, order, at, attended, out_weight, chunk, halves, tile=512):
    rows, depth = attended.shape
    tile = min(tile, chunk)
    per = chunk // tile
    cut = rows // halves
    return pl.pallas_call(
        project_kernel,
        out_shape=(jax.ShapeDtypeStruct((cut, chunk), BF16),) * halves,
        grid_spec=pltpu.PrefetchScalarGridSpec(
            num_scalar_prefetch=1,
            grid=(per,),
            in_specs=[
                pl.BlockSpec((rows, depth), lambda j, order: (0, 0)),
                pl.BlockSpec((depth, tile), lambda j, order: (0, order[at] * per + j)),
            ],
            out_specs=(pl.BlockSpec((cut, tile), lambda j, order: (0, j)),) * halves,
        ),
        compiler_params=PARAMS,
        cost_estimate=cost(2 * rows * depth * chunk, depth * chunk * 2),
        name=name,
    )(order, attended, out_weight)


def add_kernel(a_ref, b_ref, out_ref):
    out_ref[...] = (a_ref[...].astype(F32) + b_ref[...].astype(F32)).astype(BF16)


def added(name, a, b):
    return pl.pallas_call(
        add_kernel,
        out_shape=jax.ShapeDtypeStruct(a.shape, BF16),
        in_specs=[VMEM, VMEM],
        out_specs=VMEM,
        compiler_params=PARAMS,
        cost_estimate=cost(a.size, a.size * 6),
        name=name,
    )(a, b)


def finish(name, flag, either, parts, begin, rows_all, into=None):
    rows, columns = parts[0].shape
    blocks = columns // BLOCK
    n_either, n_parts = len(either), len(parts)

    def kernel(flag_ref, *refs):
        out_ref, scale_ref = refs[-2:]
        chosen = flag_ref[0] == 1
        lane = lax.broadcasted_iota(jnp.int32, (rows, blocks), 1)
        scales = jnp.zeros((rows, blocks), F32)
        for block in range(blocks):
            at = slice(block * BLOCK, (block + 1) * BLOCK)
            terms = [ref[:, at].astype(F32) for ref in refs[: n_either + n_parts]]
            if n_either:
                terms = [jnp.where(chosen, terms[0], terms[1])] + terms[2:]
            total = functools.reduce(jnp.add, terms)
            scale = jnp.max(jnp.abs(total), axis=1, keepdims=True) + 1e-06
            out_ref[:, at] = (total / scale).astype(BF16)
            scales = jnp.where(lane == block, scale, scales)
        scale_ref[...] = scales

    whole = pl.BlockSpec((rows, columns), lambda i: (0, 0))
    into = () if into is None else into
    n = n_either + n_parts
    return pl.pallas_call(
        kernel,
        out_shape=(
            jax.ShapeDtypeStruct((rows_all, columns), BF16),
            jax.ShapeDtypeStruct((rows_all, blocks), F32),
        ),
        grid=(1,),
        in_specs=[SMEM] + [whole] * n + [pl.BlockSpec(memory_space=pl.ANY)] * len(into),
        out_specs=(
            pl.BlockSpec((rows, columns), lambda i: (begin // rows, 0)),
            pl.BlockSpec((rows, blocks), lambda i: (begin // rows, 0)),
        ),
        input_output_aliases={n + 1: 0, n + 2: 1} if into else {},
        compiler_params=PARAMS,
        cost_estimate=cost(rows * columns * 6, rows * columns * 2 * (n + 1)),
        name=name,
    )(flag, *either, *parts, *into)


def local(
    queries, new_keys, new_values, key_cache, value_cache, prefix_len, stretch_start, out_weight
):
    rows = queries.shape[0]
    heads_here = queries.shape[1] // HD
    group = HQ // KVH
    tensor_pos = lax.axis_index("tensor")
    lanes = lax.axis_size("tensor")
    n_seq, n_pipe = lax.axis_size("seq"), lax.axis_size("pipe")
    shards = n_seq * n_pipe
    assert heads_here <= group
    slots = key_cache.shape[1]
    split = slots * 3 // 4
    kv_head = tensor_pos * heads_here // group
    me = lax.axis_index("seq") * n_pipe + lax.axis_index("pipe")
    info = jnp.stack([kv_head.astype(jnp.int32), prefix_len[0]])

    positions = stretch_start[0] + me * rows + jnp.arange(rows, dtype=jnp.int32)
    lane = jnp.arange(HD)
    freq = 500000.0 ** (-((lane % (HD // 2)).astype(F32) * 2.0 / HD))
    angle = positions.astype(F32)[:, None] * freq[None, :]
    cosine = jnp.cos(angle)
    sine = jnp.sin(angle) * jnp.where(lane < HD // 2, -1.0, 1.0)[None, :]

    own_a = pack_first(info, key_cache, value_cache, split)
    own_b = pack_second(info, key_cache, value_cache, new_keys, new_values, cosine, sine, split)
    query = rope_queries(queries, cosine, sine)

    def whole_plan(off):
        return [
            (0, 0, split, "live", 0),
            (1, 0, slots - split, "live", split),
            (1, slots - split, rows, "rows", off),
        ]

    lens = {0: 0, 1: 0}
    if n_seq == 2 and n_pipe == 2:
        swap = [(0, 1), (1, 0)]
        far_a = lax.ppermute(own_a, "seq", swap)
        near_a = lax.ppermute(own_a, "pipe", swap)
        far_b = lax.ppermute(own_b, "seq", swap)
        near_b = lax.ppermute(own_b, "pipe", swap)
        cross_a = lax.ppermute(far_a, "pipe", swap)
        cross_b = lax.ppermute(far_b, "pipe", swap)
        offs = (me - jnp.stack([me, me ^ 1, me ^ 2, me ^ 3])).astype(jnp.int32) * rows
        state = attend("attend_own", query, [own_a, own_b], whole_plan(0), lens, offs, None, False)
        state = attend(
            "attend_near", query, [near_a, near_b], whole_plan(1), lens, offs, state, False
        )
        state = attend(
            "attend_far_a",
            query,
            [far_a, cross_a],
            [(0, 0, split, "live", 0), (1, 0, split, "live", 0)],
            {0: 0, 1: 1},
            offs,
            state,
            False,
        )
        attended = attend(
            "attend_far_b",
            query,
            [far_b, cross_b, far_a[:, split:], cross_a[:, split:]],
            [
                (0, 0, slots - split, "live", split),
                (0, slots - split, rows, "rows", 2),
                (1, 0, slots - split, "live", split),
                (1, slots - split, rows, "rows", 3),
            ],
            {0: 2, 1: 3},
            offs,
            state,
            True,
        )
    else:
        all_a = lax.all_gather(own_a, ("seq", "pipe"), axis=0)
        all_b = lax.all_gather(own_b, ("seq", "pipe"), axis=0)
        offs = (me - jnp.arange(shards)).astype(jnp.int32) * rows
        state = None
        for shard in range(shards):
            arrays = [all_a[shard], all_b[shard]]
            state = attend(
                "attend", query, arrays, whole_plan(shard), lens, offs, state, shard == shards - 1
            )
        attended = state

    columns = D // lanes
    flag = ((tensor_pos == 0) | (tensor_pos == lanes - 1)).astype(jnp.int32).reshape(1)
    if lanes == 4:
        step = jnp.arange(4, dtype=jnp.int32)
        order = jnp.where(tensor_pos < 2, 3 - step, step)
        inward = [(0, 1), (3, 2)]
        middle = [(1, 2), (2, 1)]
        outward = [(1, 0), (2, 3)]
        part = [project(f"project_{k}", order, k, attended, out_weight, columns, 2) for k in range(4)]
        come = [[lax.ppermute(p, "tensor", inward) for p in part[k]] for k in range(3)]
        done = None
        for i in range(2):
            across = lax.ppermute(added(f"add_0{i}", part[0][i], come[0][i]), "tensor", middle)
            second = lax.ppermute(added(f"add_1{i}", part[1][i], come[1][i]), "tensor", middle)
            back = lax.ppermute(added(f"add_3{i}", part[3][i], across), "tensor", outward)
            done = finish(
                f"finish_{i}",
                flag,
                [part[3][i], part[2][i]],
                [come[2][i], second, back],
                i * (rows // 2),
                rows,
                done,
            )
        return tuple(done)
    order = jnp.arange(lanes, dtype=jnp.int32)
    partial = [
        project(f"project_{k}", order, k, attended, out_weight, columns, 1)[0] for k in range(lanes)
    ]
    total = lax.psum_scatter(jnp.stack(partial), "tensor", scatter_dimension=0, tiled=True)[0]
    return tuple(finish("finish", flag, [], [total], 0, rows))


def solution(mesh):
    return jax.shard_map(
        local,
        mesh=mesh,
        in_specs=(
            P(("groups", "seq", "pipe"), "tensor"),
            P(("groups", "seq", "pipe"), None),
            P(("groups", "seq", "pipe"), None),
            P(None, ("groups", "seq", "pipe"), None),
            P(None, ("groups", "seq", "pipe"), None),
            P(("groups", "seq", "pipe")),
            P("groups"),
            P("tensor", None),
        ),
        out_specs=(P(("groups", "seq", "pipe"), "tensor"), P(("groups", "seq", "pipe"), "tensor")),
        check_vma=False,
    )
```

time: 139 us -> 132 us (0.950)
  starting transfers between devices: 44.4 us -> 31.6 us
  local copies, waits for them, and re-layouts: 10.3 us -> 19.4 us
  waiting for transfers between devices: 27.7 us -> 34.8 us
  other arithmetic: 6.78 us -> 0.71 us
  Pallas kernels: 45.7 us -> 41.9 us
    ppermute x12, starting transfers between devices: 40.7 us -> 27.7 us  [the longest x6 20.8 us: local(): lax.ppermute(p, 'tensor', inward)]
    unnamed x24 -> x36, local copies, waits for them, and re-layouts: 8.27 us -> 18.7 us
    pallas_call x4, Pallas kernels: 30.8 us -> 21.4 us  [attend(): pl.pallas_call(functools.partial(attend_kernel, plan, lens, first, last,...]
    ppermute x12, waiting for transfers between devices: 25.9 us -> 33 us  [the longest x6 28.3 us: local(): lax.ppermute(p, 'tensor', inward)]
    pallas_call x6 -> x14, Pallas kernels: 14.5 us -> 20.2 us  [the longest x4 12 us: project(): pl.pallas_call(project_kernel, out_shape=(jax.ShapeDtypeStruct((cut, chun...]
    convert_element_type x2 -> x0, other arithmetic: 2.26 us -> none  [added(): return (a.astype(F32) + b.astype(F32)).astype(BF16)]
    select_n x5 -> x0, other arithmetic: 2.15 us -> none  [the longest x2 1.16 us: local(): jnp.where(outer, f[i], e3[i])]
    slice x4 -> x2, local copies, waits for them, and re-layouts: 1.93 us -> 0.01 us  [the longest x1 0.01 us: local(): cross_a[:, split:]]
  transfers between devices with their start and end apart: 18 -> 18, of which waited for: 8 -> 8; matrix products, arithmetic and copies ran while one was open for 5% -> 0% of each run, Pallas kernels for 24% -> 23%
where the time goes in v2:
time: 132 us; the launch traced here: 131 us
  Pallas kernels  41.9 us (32%)
  waiting for transfers between devices  34.8 us (26%)
  starting transfers between devices  31.6 us (24%)
  local copies, waits for them, and re-layouts  19.4 us (15%)
  between operations  2.32 us (2%)
    ppermute x6, waiting for transfers between devices, local(): lax.ppermute(p, 'tensor', inward)  28.3 us
    pallas_call x4, Pallas kernels, attend(): pl.pallas_call(functools.partial(attend_kernel, plan, lens, first, last,...  21.4 us
    ppermute x6, starting transfers between devices, local(): lax.ppermute(p, 'tensor', inward)  20.8 us
    unnamed x36, local copies, waits for them, and re-layouts  18.7 us
    pallas_call x4, Pallas kernels, project(): pl.pallas_call(project_kernel, out_shape=(jax.ShapeDtypeStruct((cut, chun...  12 us
    pallas_call x2, Pallas kernels, finish(): pl.pallas_call(kernel, out_shape=(jax.ShapeDtypeStruct((rows_all, columns...  5.54 us
    ppermute x2, waiting for transfers between devices, local(): lax.ppermute(added(f'add_3{i}', part[3][i], across), 'tensor', outward)  4.68 us
    ppermute x2, starting transfers between devices, local(): lax.ppermute(added(f'add_1{i}', part[1][i], come[1][i]), 'tensor', middle)  2.95 us
  transfers between devices with their start and end apart: 18, of which 8 were waited for; matrix products, arithmetic and copies ran while one was open for 0% of the time, Pallas kernels for 23%

profile of v2, /device:TPU:0, one launch (start us, length us, event | category | flops | bytes accessed | tf_op | source)
XLA Modules:
  0.0 130.7 jit_solution(5829912676044830976)
XLA Ops:
  5.4 2.6 %collective-permute-start.2 = (bf16[2,784,128]{2,1,0:T(8,128)(2,1)S(1)}, bf16[2,784,128]{2,1,0:T(8,128)(2,1)S(1)}, u32[]{:S(2)}, u32[]{:S(2)}) collective-permute-start(bf16[2,784,128]{2,1,0:T(8,128)(2,1)S(1)} %pack_first.1.refs_0_), channel_id=1, source_target_pairs={{0,2},{2,0},{1,3},{3,1},{4,6},{6,4},{5,7},{7,5},{8,10},{10,8},{9,1... | collective-permute-start | bytes 1204232 | tf_op jit(solution)/shard_map/ppermute | solution.py:368
  16.4 1.6 %collective-permute-done.2.refs_0_ = bf16[2,784,128]{2,1,0:T(8,128)(2,1)S(1)} collective-permute-done((bf16[2,784,128]{2,1,0:T(8,128)(2,1)S(1)}, bf16[2,784,128]{2,1,0:T(8,128)(2,1)S(1)}, u32[]{:S(2)}, u32[]{:S(2)}) %collective-permute-start.2) | collective-permute-done | bytes 401440 | tf_op jit(solution)/shard_map/ppermute | solution.py:368
  18.1 4.3 %attend_own.1 = (f32[256,1024]{1,0:T(8,128)S(1)}, f32[256,128]{1,0:T(8,128)S(1)}) custom-call(s32[4]{0:T(128)S(1)} %fusion.5.offs_ref, bf16[256,1024]{1,0:T(8,128)(2,1)S(1)} %rope_queries.1.q_ref, bf16[2,784,128]{2,1,0:T(8,128)(2,1)S(1)} %pack_first.1.refs_0_, bf16[2,512,128]{2,1,0:T(8,128)(2,1)S(1)} %pack_second.1.refs_1_), custom_call_target="tpu_custom_call" | custom-call | flops 2684354560 | bytes 2752512 | tf_op jit(solution)/shard_map/attend_own/pallas_call | solution.py:228
  25.1 5.6 %attend_near.1 = (f32[256,1024]{1,0:T(8,128)S(1)}, f32[256,128]{1,0:T(8,128)S(1)}) custom-call(s32[4]{0:T(128)S(1)} %fusion.5.offs_ref, bf16[256,1024]{1,0:T(8,128)(2,1)S(1)} %rope_queries.1.q_ref, bf16[2,784,128]{2,1,0:T(8,128)(2,1)S(1)} %collective-permute-done.4.refs_0_, bf16[2,512,128]{2,1,0:T(8,128)(2,1)S(1)} %collective-permute-done.5.refs_1_, ...), custom_call_target="tpu_custom_call" | custom-call | flops 2684354560 | bytes 2752512 | tf_op jit(solution)/shard_map/attend_near/pallas_call | solution.py:228
  30.7 6.0 %attend_far_a.1 = (f32[256,1024]{1,0:T(8,128)S(1)}, f32[256,128]{1,0:T(8,128)S(1)}) custom-call(s32[4]{0:T(128)S(1)} %fusion.5.offs_ref, bf16[256,1024]{1,0:T(8,128)(2,1)S(1)} %rope_queries.1.q_ref, bf16[2,784,128]{2,1,0:T(8,128)(2,1)S(1)} %collective-permute-done.2.refs_0_, bf16[2,784,128]{2,1,0:T(8,128)(2,1)S(1)} %collective-permute-done.3.refs_1_, ...), custom_call_target="tpu_custom_call" | custom-call | flops 3221225472 | bytes 2883584 | tf_op jit(solution)/shard_map/attend_far_a/pallas_call | solution.py:228
  36.7 5.5 %attend_far_b.1.x_ref = bf16[256,1024]{1,0:T(8,128)(2,1)S(1)} custom-call(s32[4]{0:T(128)S(1)} %fusion.5.offs_ref, bf16[256,1024]{1,0:T(8,128)(2,1)S(1)} %rope_queries.1.q_ref, bf16[2,512,128]{2,1,0:T(8,128)(2,1)S(1)} %collective-permute-done.refs_0_, bf16[2,512,128]{2,1,0:T(8,128)(2,1)S(1)} %collective-permute-done.1.refs_1_, ...), custom_call_target="tpu_custom_call" | custom-call | flops 2147483648 | bytes 2621440 | tf_op jit(solution)/shard_map/attend_far_b/pallas_call | solution.py:228
  42.2 5.8 %copy-done = bf16[1024,8192]{1,0:T(8,128)(2,1)S(1)} copy-done((bf16[1024,8192]{1,0:T(8,128)(2,1)S(1)}, bf16[1024,8192]{1,0:T(8,128)(2,1)}, u32[]{:S(2)}) %copy-start) | copy-done | bytes 16777240
  48.0 2.8 %project_0.1 = (bf16[128,2048]{1,0:T(8,128)(2,1)S(1)}, bf16[128,2048]{1,0:T(8,128)(2,1)S(1)}) custom-call(s32[4]{0:T(128)S(1)} %broadcast_select_fusion.order_ref, bf16[256,1024]{1,0:T(8,128)(2,1)S(1)} %attend_far_b.1.x_ref, bf16[1024,8192]{1,0:T(8,128)(2,1)S(1)} %copy-done), custom_call_target="tpu_custom_call" | custom-call | flops 1073741824 | bytes 4194304 | tf_op jit(solution)/shard_map/project_0/pallas_call | solution.py:253
  50.8 4.0 %collective-permute-start.15 = (bf16[128,2048]{1,0:T(8,128)(2,1)S(1)}, bf16[128,2048]{1,0:T(8,128)(2,1)S(1)}, u32[]{:S(2)}, u32[]{:S(2)}) collective-permute-start(bf16[128,2048]{1,0:T(8,128)(2,1)S(1)} %get-tuple-element.31.a_ref), channel_id=1, source_target_pairs={{0,4},{12,8},{1,5},{13,9},{2,6},{14,10},{3,7},{15,11},{16,20},{28,... | collective-permute-start | bytes 1572872 | tf_op jit(solution)/shard_map/ppermute | solution.py:425
  54.9 1.7 %collective-permute-start.9 = (bf16[128,2048]{1,0:T(8,128)(2,1)S(1)}, bf16[128,2048]{1,0:T(8,128)(2,1)S(1)}, u32[]{:S(2)}, u32[]{:S(2)}) collective-permute-start(bf16[128,2048]{1,0:T(8,128)(2,1)S(1)} %get-tuple-element.27.a_ref), channel_id=1, source_target_pairs={{0,4},{12,8},{1,5},{13,9},{2,6},{14,10},{3,7},{15,11},{16,20},{28,... | collective-permute-start | bytes 1572872 | tf_op jit(solution)/shard_map/ppermute | solution.py:425
  56.6 2.8 %project_1.1 = (bf16[128,2048]{1,0:T(8,128)(2,1)S(1)}, bf16[128,2048]{1,0:T(8,128)(2,1)S(1)}) custom-call(s32[4]{0:T(128)S(1)} %broadcast_select_fusion.order_ref, bf16[256,1024]{1,0:T(8,128)(2,1)S(1)} %attend_far_b.1.x_ref, bf16[1024,8192]{1,0:T(8,128)(2,1)S(1)} %copy-done), custom_call_target="tpu_custom_call" | custom-call | flops 1073741824 | bytes 4194304 | tf_op jit(solution)/shard_map/project_1/pallas_call | solution.py:253
  62.1 5.0 %collective-permute-done.15.b_ref = bf16[128,2048]{1,0:T(8,128)(2,1)S(1)} collective-permute-done((bf16[128,2048]{1,0:T(8,128)(2,1)S(1)}, bf16[128,2048]{1,0:T(8,128)(2,1)S(1)}, u32[]{:S(2)}, u32[]{:S(2)}) %collective-permute-start.15) | collective-permute-done | bytes 524320 | tf_op jit(solution)/shard_map/ppermute | solution.py:425
  67.9 10.4 %collective-permute-done.9.b_ref = bf16[128,2048]{1,0:T(8,128)(2,1)S(1)} collective-permute-done((bf16[128,2048]{1,0:T(8,128)(2,1)S(1)}, bf16[128,2048]{1,0:T(8,128)(2,1)S(1)}, u32[]{:S(2)}, u32[]{:S(2)}) %collective-permute-start.9) | collective-permute-done | bytes 524320 | tf_op jit(solution)/shard_map/ppermute | solution.py:425
  79.2 3.5 %project_2.1 = (bf16[128,2048]{1,0:T(8,128)(2,1)S(1)}, bf16[128,2048]{1,0:T(8,128)(2,1)}) custom-call(s32[4]{0:T(128)S(1)} %broadcast_select_fusion.order_ref, bf16[256,1024]{1,0:T(8,128)(2,1)S(1)} %attend_far_b.1.x_ref, bf16[1024,8192]{1,0:T(8,128)(2,1)S(1)} %bitcast.9), custom_call_target="tpu_custom_call" | custom-call | flops 1073741824 | bytes 4194304 | tf_op jit(solution)/shard_map/project_2/pallas_call | solution.py:253
  82.7 7.2 %collective-permute-start.12 = (bf16[128,2048]{1,0:T(8,128)(2,1)S(1)}, bf16[128,2048]{1,0:T(8,128)(2,1)S(1)}, u32[]{:S(2)}, u32[]{:S(2)}) collective-permute-start(bf16[128,2048]{1,0:T(8,128)(2,1)S(1)} %get-tuple-element.29.refs_1_), channel_id=1, source_target_pairs={{0,4},{12,8},{1,5},{13,9},{2,6},{14,10},{3,7},{15,11},{16,20},{28,... | collective-permute-start | bytes 1572872 | tf_op jit(solution)/shard_map/ppermute | solution.py:425
  90.0 2.8 %project_3.1 = (bf16[128,2048]{1,0:T(8,128)(2,1)S(1)}, bf16[128,2048]{1,0:T(8,128)(2,1)S(1)}) custom-call(s32[4]{0:T(128)S(1)} %broadcast_select_fusion.order_ref, bf16[256,1024]{1,0:T(8,128)(2,1)S(1)} %attend_far_b.1.x_ref, bf16[1024,8192]{1,0:T(8,128)(2,1)S(1)} %bitcast.9), custom_call_target="tpu_custom_call" | custom-call | flops 1073741824 | bytes 4194304 | tf_op jit(solution)/shard_map/project_3/pallas_call | solution.py:253
  95.8 5.0 %collective-permute-done.7.b_ref = bf16[128,2048]{1,0:T(8,128)(2,1)S(1)} collective-permute-done((bf16[128,2048]{1,0:T(8,128)(2,1)S(1)}, bf16[128,2048]{1,0:T(8,128)(2,1)S(1)}, u32[]{:S(2)}, u32[]{:S(2)}) %collective-permute-start.7) | collective-permute-done | bytes 524320 | tf_op jit(solution)/shard_map/ppermute | solution.py:425
  100.8 5.2 %collective-permute-start.6 = (bf16[128,2048]{1,0:T(8,128)(2,1)}, bf16[128,2048]{1,0:T(8,128)(2,1)}, u32[]{:S(2)}, u32[]{:S(2)}) collective-permute-start(bf16[128,2048]{1,0:T(8,128)(2,1)} %get-tuple-element.25.refs_1_), channel_id=1, source_target_pairs={{0,4},{12,8},{1,5},{13,9},{2,6},{14,10},{3,7},{15,11},{16,20},{28,... | collective-permute-start | bytes 1572872 | tf_op jit(solution)/shard_map/ppermute | solution.py:425
  106.2 1.5 %collective-permute-start.8 = (bf16[128,2048]{1,0:T(8,128)(2,1)S(1)}, bf16[128,2048]{1,0:T(8,128)(2,1)}, u32[]{:S(2)}, u32[]{:S(2)}) collective-permute-start(bf16[128,2048]{1,0:T(8,128)(2,1)S(1)} %add_11.1), channel_id=1, source_target_pairs={{4,8},{8,4},{5,9},{9,5},{6,10},{10,6},{7,11},{11,7},{20,24},{24,20... | collective-permute-start | bytes 1572872 | tf_op jit(solution)/shard_map/ppermute | solution.py:429
  107.8 4.3 %collective-permute-done.12.refs_2_ = bf16[128,2048]{1,0:T(8,128)(2,1)S(1)} collective-permute-done((bf16[128,2048]{1,0:T(8,128)(2,1)S(1)}, bf16[128,2048]{1,0:T(8,128)(2,1)S(1)}, u32[]{:S(2)}, u32[]{:S(2)}) %collective-permute-start.12) | collective-permute-done | bytes 524320 | tf_op jit(solution)/shard_map/ppermute | solution.py:425
  116.3 2.6 %finish_0.1 = (bf16[256,2048]{1,0:T(8,128)(2,1)}, f32[256,16]{1,0:T(8,128)S(1)}) custom-call(s32[1]{0:T(128)} %bitcast.flag_ref, bf16[128,2048]{1,0:T(8,128)(2,1)S(1)} %get-tuple-element.28.a_ref.refs_0_, bf16[128,2048]{1,0:T(8,128)(2,1)S(1)} %copy-done.7, bf16[128,2048]{1,0:T(8,128)(2,1)S(1)} %copy-done.9, ...), custom_call_target="tpu_custom_call" | custom-call | flops 1572864 | bytes 3145728 | tf_op jit(solution)/shard_map/finish_0/pallas_call | solution.py:311
  118.9 3.6 %collective-permute-done.6.refs_2_ = bf16[128,2048]{1,0:T(8,128)(2,1)} collective-permute-done((bf16[128,2048]{1,0:T(8,128)(2,1)}, bf16[128,2048]{1,0:T(8,128)(2,1)}, u32[]{:S(2)}, u32[]{:S(2)}) %collective-permute-start.6) | collective-permute-done | bytes 524320 | tf_op jit(solution)/shard_map/ppermute | solution.py:425
  122.5 4.7 %collective-permute-done.11.refs_4_ = bf16[128,2048]{1,0:T(8,128)(2,1)} collective-permute-done((bf16[128,2048]{1,0:T(8,128)(2,1)S(1)}, bf16[128,2048]{1,0:T(8,128)(2,1)}, u32[]{:S(2)}, u32[]{:S(2)}) %collective-permute-start.11) | collective-permute-done | bytes 524320 | tf_op jit(solution)/shard_map/ppermute | solution.py:430
  127.1 2.9 %finish_1.1 = (bf16[256,2048]{1,0:T(8,128)(2,1)}, f32[256,16]{1,0:T(8,128)S(1)}) custom-call(s32[1]{0:T(128)} %bitcast.flag_ref, bf16[128,2048]{1,0:T(8,128)(2,1)S(1)} %get-tuple-element.24.a_ref.refs_0_, bf16[128,2048]{1,0:T(8,128)(2,1)} %get-tuple-element.25.refs_1_, ...), custom_call_target="tpu_custom_call", output_to_operand_aliasing={{0}: (6, {}), {1}: (7, {})} | custom-call | flops 1572864 | bytes 3145728 | tf_op jit(solution)/shard_map/finish_1/pallas_call | solution.py:311
  (77 shorter events, 27.0 us)
Async XLA Ops:
  4.9 19.0 %collective-permute-start.4 = (bf16[2,784,128]{2,1,0:T(8,128)(2,1)S(1)}, bf16[2,784,128]{2,1,0:T(8,128)(2,1)S(1)}, u32[]{:S(2)}, u32[]{:S(2)}) collective-permute-start(bf16[2,784,128]{2,1,0:T(8,128)(2,1)S(1)} %pack_first.1.refs_0_), channel_id=1, source_target_pairs={{0,1},{1,0},{2,3},{3,2},{4,5},{5,4},{6,7},{7,6},{8,9},{9,8},{10,11... | collective-permute-start | bytes 1204232 | tf_op jit(solution)/shard_map/ppermute | solution.py:369
  5.4 12.6 %collective-permute-start.2 = (bf16[2,784,128]{2,1,0:T(8,128)(2,1)S(1)}, bf16[2,784,128]{2,1,0:T(8,128)(2,1)S(1)}, u32[]{:S(2)}, u32[]{:S(2)}) collective-permute-start(bf16[2,784,128]{2,1,0:T(8,128)(2,1)S(1)} %pack_first.1.refs_0_), channel_id=1, source_target_pairs={{0,2},{2,0},{1,3},{3,1},{4,6},{6,4},{5,7},{7,5},{8,10},{10,8},{9,1... | collective-permute-start | bytes 1204232 | tf_op jit(solution)/shard_map/ppermute | solution.py:368
  14.4 9.4 %collective-permute-start.5 = (bf16[2,512,128]{2,1,0:T(8,128)(2,1)S(1)}, bf16[2,512,128]{2,1,0:T(8,128)(2,1)S(1)}, u32[]{:S(2)}, u32[]{:S(2)}) collective-permute-start(bf16[2,512,128]{2,1,0:T(8,128)(2,1)S(1)} %pack_second.1.refs_1_), channel_id=1, source_target_pairs={{0,1},{1,0},{2,3},{3,2},{4,5},{5,4},{6,7},{7,6},{8,9},{9,8},{10,11... | collective-permute-start | bytes 786440 | tf_op jit(solution)/shard_map/ppermute | solution.py:371
  14.7 8.8 %collective-permute-start = (bf16[2,512,128]{2,1,0:T(8,128)(2,1)S(1)}, bf16[2,512,128]{2,1,0:T(8,128)(2,1)S(1)}, u32[]{:S(2)}, u32[]{:S(2)}) collective-permute-start(bf16[2,512,128]{2,1,0:T(8,128)(2,1)S(1)} %pack_second.1.refs_1_), channel_id=1, source_target_pairs={{0,2},{2,0},{1,3},{3,1},{4,6},{6,4},{5,7},{7,5},{8,10},{10,8},{9,1... | collective-permute-start | bytes 786440 | tf_op jit(solution)/shard_map/ppermute | solution.py:370
  18.1 12.6 %collective-permute-start.3 = (bf16[2,784,128]{2,1,0:T(8,128)(2,1)S(1)}, bf16[2,784,128]{2,1,0:T(8,128)(2,1)S(1)}, u32[]{:S(2)}, u32[]{:S(2)}) collective-permute-start(bf16[2,784,128]{2,1,0:T(8,128)(2,1)S(1)} %collective-permute-done.2.refs_0_), channel_id=1, source_target_pairs={{0,1},{1,0},{2,3},{3,2},{4,5},{5,4},{6,7},{7,6},{8,9},{9,8},{10,11... | collective-permute-start | bytes 1204232 | tf_op jit(solution)/shard_map/ppermute | solution.py:372
  23.5 13.2 %collective-permute-start.1 = (bf16[2,512,128]{2,1,0:T(8,128)(2,1)S(1)}, bf16[2,512,128]{2,1,0:T(8,128)(2,1)S(1)}, u32[]{:S(2)}, u32[]{:S(2)}) collective-permute-start(bf16[2,512,128]{2,1,0:T(8,128)(2,1)S(1)} %collective-permute-done.refs_0_), channel_id=1, source_target_pairs={{0,1},{1,0},{2,3},{3,2},{4,5},{5,4},{6,7},{7,6},{8,9},{9,8},{10,11... | collective-permute-start | bytes 786440 | tf_op jit(solution)/shard_map/ppermute | solution.py:373
  42.2 5.8 %copy-start = (bf16[1024,8192]{1,0:T(8,128)(2,1)S(1)}, bf16[1024,8192]{1,0:T(8,128)(2,1)}, u32[]{:S(2)}) copy-start(bf16[1024,8192]{1,0:T(8,128)(2,1)} %w_ref.7) | copy-start | bytes 50331652
  48.0 31.2 %slice-start = ((s8[16777216]{0:T(1024)(128)(4,1)}), s8[4194304]{0:T(1024)(128)(4,1)S(1)}, s32[]{:S(2)}) async-start(s8[16777216]{0:T(1024)(128)(4,1)} %bitcast.8), calls=%async_computation | async-start | bytes 8388608
  48.0 31.2 %slice-start.1 = ((s8[16777216]{0:T(1024)(128)(4,1)}), s8[4194304]{0:T(1024)(128)(4,1)S(1)}, s32[]{:S(2)}) async-start(s8[16777216]{0:T(1024)(128)(4,1)} %bitcast.8), calls=%async_computation.1 | async-start | bytes 8388608
  50.8 16.3 %collective-permute-start.15 = (bf16[128,2048]{1,0:T(8,128)(2,1)S(1)}, bf16[128,2048]{1,0:T(8,128)(2,1)S(1)}, u32[]{:S(2)}, u32[]{:S(2)}) collective-permute-start(bf16[128,2048]{1,0:T(8,128)(2,1)S(1)} %get-tuple-element.31.a_ref), channel_id=1, source_target_pairs={{0,4},{12,8},{1,5},{13,9},{2,6},{14,10},{3,7},{15,11},{16,20},{28,... | collective-permute-start | bytes 1572872 | tf_op jit(solution)/shard_map/ppermute | solution.py:425
  54.9 24.3 %slice-start.2 = ((s8[16777216]{0:T(1024)(128)(4,1)}), s8[4194304]{0:T(1024)(128)(4,1)S(1)}, s32[]{:S(2)}) async-start(s8[16777216]{0:T(1024)(128)(4,1)} %bitcast.8), calls=%async_computation.2 | async-start | bytes 8388608
  54.9 24.3 %slice-start.3 = ((s8[16777216]{0:T(1024)(128)(4,1)}), s8[4194304]{0:T(1024)(128)(4,1)S(1)}, s32[]{:S(2)}) async-start(s8[16777216]{0:T(1024)(128)(4,1)} %bitcast.8), calls=%async_computation.3 | async-start | bytes 8388608
  54.9 23.5 %collective-permute-start.9 = (bf16[128,2048]{1,0:T(8,128)(2,1)S(1)}, bf16[128,2048]{1,0:T(8,128)(2,1)S(1)}, u32[]{:S(2)}, u32[]{:S(2)}) collective-permute-start(bf16[128,2048]{1,0:T(8,128)(2,1)S(1)} %get-tuple-element.27.a_ref), channel_id=1, source_target_pairs={{0,4},{12,8},{1,5},{13,9},{2,6},{14,10},{3,7},{15,11},{16,20},{28,... | collective-permute-start | bytes 1572872 | tf_op jit(solution)/shard_map/ppermute | solution.py:425
  59.4 33.4 %collective-permute-start.13 = (bf16[128,2048]{1,0:T(8,128)(2,1)S(1)}, bf16[128,2048]{1,0:T(8,128)(2,1)S(1)}, u32[]{:S(2)}, u32[]{:S(2)}) collective-permute-start(bf16[128,2048]{1,0:T(8,128)(2,1)S(1)} %get-tuple-element.30.a_ref), channel_id=1, source_target_pairs={{0,4},{12,8},{1,5},{13,9},{2,6},{14,10},{3,7},{15,11},{16,20},{28,... | collective-permute-start | bytes 1572872 | tf_op jit(solution)/shard_map/ppermute | solution.py:425
  60.8 40.1 %collective-permute-start.7 = (bf16[128,2048]{1,0:T(8,128)(2,1)S(1)}, bf16[128,2048]{1,0:T(8,128)(2,1)S(1)}, u32[]{:S(2)}, u32[]{:S(2)}) collective-permute-start(bf16[128,2048]{1,0:T(8,128)(2,1)S(1)} %get-tuple-element.26.a_ref), channel_id=1, source_target_pairs={{0,4},{12,8},{1,5},{13,9},{2,6},{14,10},{3,7},{15,11},{16,20},{28,... | collective-permute-start | bytes 1572872 | tf_op jit(solution)/shard_map/ppermute | solution.py:425
  67.2 27.1 %collective-permute-start.16 = (bf16[128,2048]{1,0:T(8,128)(2,1)S(1)}, bf16[128,2048]{1,0:T(8,128)(2,1)S(1)}, u32[]{:S(2)}, u32[]{:S(2)}) collective-permute-start(bf16[128,2048]{1,0:T(8,128)(2,1)S(1)} %add_00.1), channel_id=1, source_target_pairs={{4,8},{8,4},{5,9},{9,5},{6,10},{10,6},{7,11},{11,7},{20,24},{24,20... | collective-permute-start | bytes 1572872 | tf_op jit(solution)/shard_map/ppermute | solution.py:428
  78.5 27.7 %collective-permute-start.10 = (bf16[128,2048]{1,0:T(8,128)(2,1)S(1)}, bf16[128,2048]{1,0:T(8,128)(2,1)S(1)}, u32[]{:S(2)}, u32[]{:S(2)}) collective-permute-start(bf16[128,2048]{1,0:T(8,128)(2,1)S(1)} %add_01.1), channel_id=1, source_target_pairs={{4,8},{8,4},{5,9},{9,5},{6,10},{10,6},{7,11},{11,7},{20,24},{24,20... | collective-permute-start | bytes 1572872 | tf_op jit(solution)/shard_map/ppermute | solution.py:428
  82.7 25.0 %copy-start.6 = (bf16[128,2048]{1,0:T(8,128)(2,1)}, bf16[128,2048]{1,0:T(8,128)(2,1)S(1)}, u32[]{:S(2)}) copy-start(bf16[128,2048]{1,0:T(8,128)(2,1)S(1)} %get-tuple-element.29.refs_1_) | copy-start | bytes 1572868
  82.7 29.3 %collective-permute-start.12 = (bf16[128,2048]{1,0:T(8,128)(2,1)S(1)}, bf16[128,2048]{1,0:T(8,128)(2,1)S(1)}, u32[]{:S(2)}, u32[]{:S(2)}) collective-permute-start(bf16[128,2048]{1,0:T(8,128)(2,1)S(1)} %get-tuple-element.29.refs_1_), channel_id=1, source_target_pairs={{0,4},{12,8},{1,5},{13,9},{2,6},{14,10},{3,7},{15,11},{16,20},{28,... | collective-permute-start | bytes 1572872 | tf_op jit(solution)/shard_map/ppermute | solution.py:425
  92.9 21.2 %collective-permute-start.14 = (bf16[128,2048]{1,0:T(8,128)(2,1)S(1)}, bf16[128,2048]{1,0:T(8,128)(2,1)}, u32[]{:S(2)}, u32[]{:S(2)}) collective-permute-start(bf16[128,2048]{1,0:T(8,128)(2,1)S(1)} %add_10.1), channel_id=1, source_target_pairs={{4,8},{8,4},{5,9},{9,5},{6,10},{10,6},{7,11},{11,7},{20,24},{24,20... | collective-permute-start | bytes 1572872 | tf_op jit(solution)/shard_map/ppermute | solution.py:429
  94.5 19.7 %collective-permute-start.17 = (bf16[128,2048]{1,0:T(8,128)(2,1)S(1)}, bf16[128,2048]{1,0:T(8,128)(2,1)}, u32[]{:S(2)}, u32[]{:S(2)}) collective-permute-start(bf16[128,2048]{1,0:T(8,128)(2,1)S(1)} %add_30.1), channel_id=1, source_target_pairs={{4,0},{8,12},{5,1},{9,13},{6,2},{10,14},{7,3},{11,15},{20,16},{24,... | collective-permute-start | bytes 1572872 | tf_op jit(solution)/shard_map/ppermute | solution.py:430
  100.8 21.6 %collective-permute-start.6 = (bf16[128,2048]{1,0:T(8,128)(2,1)}, bf16[128,2048]{1,0:T(8,128)(2,1)}, u32[]{:S(2)}, u32[]{:S(2)}) collective-permute-start(bf16[128,2048]{1,0:T(8,128)(2,1)} %get-tuple-element.25.refs_1_), channel_id=1, source_target_pairs={{0,4},{12,8},{1,5},{13,9},{2,6},{14,10},{3,7},{15,11},{16,20},{28,... | collective-permute-start | bytes 1572872 | tf_op jit(solution)/shard_map/ppermute | solution.py:425
  106.2 16.3 %collective-permute-start.8 = (bf16[128,2048]{1,0:T(8,128)(2,1)S(1)}, bf16[128,2048]{1,0:T(8,128)(2,1)}, u32[]{:S(2)}, u32[]{:S(2)}) collective-permute-start(bf16[128,2048]{1,0:T(8,128)(2,1)S(1)} %add_11.1), channel_id=1, source_target_pairs={{4,8},{8,4},{5,9},{9,5},{6,10},{10,6},{7,11},{11,7},{20,24},{24,20... | collective-permute-start | bytes 1572872 | tf_op jit(solution)/shard_map/ppermute | solution.py:429
  112.9 14.3 %collective-permute-start.11 = (bf16[128,2048]{1,0:T(8,128)(2,1)S(1)}, bf16[128,2048]{1,0:T(8,128)(2,1)}, u32[]{:S(2)}, u32[]{:S(2)}) collective-permute-start(bf16[128,2048]{1,0:T(8,128)(2,1)S(1)} %add_31.1), channel_id=1, source_target_pairs={{4,0},{8,12},{5,1},{9,13},{6,2},{10,14},{7,3},{11,15},{20,16},{24,... | collective-permute-start | bytes 1572872 | tf_op jit(solution)/shard_map/ppermute | solution.py:430
  (12 other events, 12.9 us)

commit v3 on v2

v3 whole, which is shorter than its diff:
```python
import functools
import math

import jax
import jax.numpy as jnp
from jax import lax
from jax.experimental import pallas as pl
from jax.experimental.pallas import tpu as pltpu
from jax.sharding import PartitionSpec as P

D = 8192
HD = 128
HQ = 32
KVH = 4
BLOCK = 128
LEN_ROWS = 16
LOW = 32
NEG = -1e30
VMEM_LIMIT = 48 * 1024 * 1024
VMEM_MOST = 60 * 1024 * 1024
F32 = jnp.float32
BF16 = jnp.bfloat16
NT = (((1,), (1,)), ((), ()))


SMEM = pl.BlockSpec(memory_space=pltpu.SMEM)
VMEM = pl.BlockSpec(memory_space=pltpu.VMEM)
HBM = pl.BlockSpec(memory_space=pltpu.HBM)
PARAMS = pltpu.CompilerParams(vmem_limit_bytes=VMEM_LIMIT)
PARAMS_MOST = pltpu.CompilerParams(vmem_limit_bytes=VMEM_MOST)


def cost(flops, nbytes, transcendentals=0):
    return pl.CostEstimate(
        flops=int(flops), bytes_accessed=int(nbytes), transcendentals=int(transcendentals)
    )


def rotated(x, cosine, sine):
    return x * cosine + pltpu.roll(x, HD // 2, 1) * sine


def pack_first_kernel(info_ref, k_ref, v_ref, out_ref, sems):
    count = out_ref.shape[1] - LEN_ROWS
    head = info_ref[0]
    copies = [
        pltpu.make_async_copy(
            ref.at[head, pl.ds(0, count)], out_ref.at[at, pl.ds(0, count)], sems.at[at]
        )
        for at, ref in enumerate((k_ref, v_ref))
    ]
    for copy in copies:
        copy.start()
    live = info_ref[1]
    high = (live // LOW).astype(F32)
    low = (live % LOW).astype(F32)
    out_ref[0, count:] = jnp.full((LEN_ROWS, HD), high, F32).astype(BF16)
    out_ref[1, count:] = jnp.full((LEN_ROWS, HD), low, F32).astype(BF16)
    for copy in copies:
        copy.wait()


def pack_first(info, key_cache, value_cache, count):
    return pl.pallas_call(
        pack_first_kernel,
        out_shape=jax.ShapeDtypeStruct((2, count + LEN_ROWS, HD), BF16),
        in_specs=[SMEM, HBM, HBM],
        out_specs=VMEM,
        scratch_shapes=[pltpu.SemaphoreType.DMA((2,))],
        compiler_params=PARAMS_MOST,
        cost_estimate=cost(0, 4 * count * HD * 2),
        name="pack_first",
    )(info, key_cache, value_cache)


def pack_second_kernel(
    first, info_ref, k_ref, v_ref, nk_ref, nv_ref, cos_ref, sin_ref, out_ref, raw, sems
):
    rows = raw.shape[0]
    count = out_ref.shape[1] - rows
    head = info_ref[0]
    columns = pl.ds(pl.multiple_of(head * HD, HD), HD)
    copies = [
        pltpu.make_async_copy(nk_ref.at[:, columns], raw, sems.at[0]),
        pltpu.make_async_copy(nv_ref.at[:, columns], out_ref.at[1, pl.ds(count, rows)], sems.at[1]),
        pltpu.make_async_copy(
            k_ref.at[head, pl.ds(first, count)], out_ref.at[0, pl.ds(0, count)], sems.at[2]
        ),
        pltpu.make_async_copy(
            v_ref.at[head, pl.ds(first, count)], out_ref.at[1, pl.ds(0, count)], sems.at[3]
        ),
    ]
    for copy in copies:
        copy.start()
    copies[0].wait()
    out_ref[0, count:] = rotated(raw[...].astype(F32), cos_ref[...], sin_ref[...]).astype(BF16)
    for copy in copies[1:]:
        copy.wait()


def pack_second(info, key_cache, value_cache, new_keys, new_values, cosine, sine, first):
    rows = new_keys.shape[0]
    size = key_cache.shape[1] - first + rows
    return pl.pallas_call(
        functools.partial(pack_second_kernel, first),
        out_shape=jax.ShapeDtypeStruct((2, size, HD), BF16),
        in_specs=[SMEM, HBM, HBM, HBM, HBM, VMEM, VMEM],
        out_specs=VMEM,
        scratch_shapes=[pltpu.VMEM((rows, HD), BF16), pltpu.SemaphoreType.DMA((4,))],
        compiler_params=PARAMS_MOST,
        cost_estimate=cost(0, 4 * size * HD * 2),
        name="pack_second",
    )(info, key_cache, value_cache, new_keys, new_values, cosine, sine)


def lane_max(x):
    parts = [x[:, i : i + HD] for i in range(0, x.shape[1], HD)]
    return functools.reduce(jnp.maximum, parts)


def lane_sum(x):
    parts = [x[:, i : i + HD] for i in range(0, x.shape[1], HD)]
    return functools.reduce(jnp.add, parts)


def attend_kernel(plan, lens, first, last, chunk, span, n_kv, offs_ref, q_ref, *refs):
    kv_refs = refs[:n_kv]
    refs = refs[n_kv:]
    begin_row, rows = span
    at_rows = slice(begin_row, begin_row + rows)
    if first:
        cos_ref, sin_ref, acc_out, stats_out, query_out, raw, sem = refs
        copy = pltpu.make_async_copy(q_ref, raw, sem)
        copy.start()
        heads = q_ref.shape[1] // HD
    else:
        acc_in, stats_in = refs[:2]
        refs = refs[2:]
        heads = q_ref.shape[1] // HD
        if chunk:
            w_ref, attended_out, part_out, w_held, sem = refs
            columns = pl.ds(pl.multiple_of(offs_ref[offs_ref.shape[0] - 1] * chunk, chunk), chunk)
            copy = pltpu.make_async_copy(w_ref.at[:, columns], w_held, sem)
            copy.start()
        elif last:
            (attended_out,) = refs
        else:
            acc_out, stats_out = refs
    masks = []
    for array, begin, count, kind, argument in plan:
        if kind == "live":
            ref = kv_refs[lens[array]]
            at = ref.shape[1] - LEN_ROWS
            live = ref[0, at:, :].astype(F32) * LOW + ref[1, at:, :].astype(F32)
            live = live[:1, :]
            slot = lax.broadcasted_iota(jnp.int32, (1, HD), 1).astype(F32)
            pieces = [
                jnp.where(slot + float(argument + i) < live, 0.0, NEG)
                for i in range(0, count, HD)
            ]
            masks.append(jnp.concatenate(pieces, axis=1))
        else:
            row = lax.broadcasted_iota(jnp.int32, (rows, count), 0) + begin_row
            column = lax.broadcasted_iota(jnp.int32, (rows, count), 1)
            masks.append(jnp.where(column <= row + offs_ref[argument], 0.0, NEG))
    if first:
        factor = math.log2(math.e) / math.sqrt(HD)
        cosine = cos_ref[...] * factor
        sine = sin_ref[...] * factor
        copy.wait()
        for head in range(heads):
            at = slice(head * HD, (head + 1) * HD)
            query_out[:, at] = rotated(raw[:, at].astype(F32), cosine, sine).astype(BF16)
        q_ref = query_out

    def score(head):
        query = q_ref[at_rows, head * HD : (head + 1) * HD]
        scores = []
        for (array, begin, count, kind, argument), mask in zip(plan, masks):
            keys = kv_refs[array][0, begin : begin + count, :]
            scores.append(lax.dot_general(query, keys, NT, preferred_element_type=F32) + mask)
        return scores

    lane = lax.broadcasted_iota(jnp.int32, (rows, HD), 1)
    stats = jnp.zeros((rows, HD), F32)
    following = score(0)
    for head in range(heads):
        scores = following
        if head + 1 < heads:
            following = score(head + 1)
        at = slice(head * HD, (head + 1) * HD)
        peak = functools.reduce(jnp.maximum, [lane_max(x) for x in scores])
        peak = jnp.max(peak, axis=1, keepdims=True)
        if not first:
            before = stats_in[at_rows, head : head + 1]
            peak = jnp.maximum(before, peak)
            shrink = jnp.exp2(before - peak)
        total = None
        out = None
        for (array, begin, count, kind, argument), part in zip(plan, scores):
            weights = jnp.exp2(part - peak)
            subtotal = lane_sum(weights)
            total = subtotal if total is None else total + subtotal
            values = kv_refs[array][1, begin : begin + count, :]
            update = jnp.dot(weights.astype(BF16), values, preferred_element_type=F32)
            out = update if out is None else out + update
        total = jnp.sum(total, axis=1, keepdims=True)
        if not first:
            total = total + stats_in[at_rows, HD // 2 + head : HD // 2 + head + 1] * shrink
            out = out + acc_in[at_rows, at] * shrink
        if last:
            attended_out[:, at] = (out / total).astype(BF16)
        else:
            acc_out[:, at] = out
            stats = jnp.where(lane == head, peak, stats)
            stats = jnp.where(lane == HD // 2 + head, total, stats)
    if not last:
        stats_out[...] = stats
    if chunk:
        copy.wait()
        tile = 512
        for i in range(0, chunk, tile):
            part_out[:, i : i + tile] = jnp.dot(
                attended_out[...], w_held[:, i : i + tile], preferred_element_type=F32
            ).astype(BF16)


def attend(name, query, arrays, plan, lens, offs, state, last, tables=None, weight=None, chunk=0, span=None):
    rows, width = query.shape
    first = state is None
    span = (0, rows) if span is None else span
    operands = [offs, query, *arrays]
    in_specs = [SMEM, HBM if first else VMEM] + [VMEM] * len(arrays)
    scratch = []
    if first:
        operands += tables
        in_specs += [VMEM] * 2
        scratch = [pltpu.VMEM((rows, width), BF16), pltpu.SemaphoreType.DMA]
    else:
        operands += state
        in_specs += [VMEM] * 2
    if last:
        out_shape = [jax.ShapeDtypeStruct((span[1], width), BF16)]
        if chunk:
            operands.append(weight)
            in_specs.append(HBM)
            out_shape.append(jax.ShapeDtypeStruct((span[1], chunk), BF16))
            scratch = [pltpu.VMEM((width, chunk), BF16), pltpu.SemaphoreType.DMA]
    else:
        out_shape = [
            jax.ShapeDtypeStruct((rows, width), F32),
            jax.ShapeDtypeStruct((rows, HD), F32),
        ]
        if first:
            out_shape.append(jax.ShapeDtypeStruct((rows, width), BF16))
    keys = sum(p[2] for p in plan)
    return pl.pallas_call(
        functools.partial(attend_kernel, plan, lens, first, last, chunk, span, len(arrays)),
        out_shape=out_shape,
        in_specs=in_specs,
        out_specs=[VMEM] * len(out_shape),
        scratch_shapes=scratch,
        compiler_params=PARAMS,
        cost_estimate=cost(
            span[1] * width * keys // 2, rows * width, span[1] * (width // HD) * keys // 8
        ),
        name=name,
    )(*operands)


def project_kernel(pieces, order_ref, *refs):
    w_ref = refs[pieces]
    for x_ref, out_ref in zip(refs[:pieces], refs[pieces + 1 :]):
        out_ref[...] = jnp.dot(x_ref[...], w_ref[...], preferred_element_type=F32).astype(BF16)


def project(name, order, at, attended, out_weight, chunk, tile=512):
    cut, depth = attended[0].shape
    pieces = len(attended)
    tile = min(tile, chunk)
    per = chunk // tile
    return pl.pallas_call(
        functools.partial(project_kernel, pieces),
        out_shape=(jax.ShapeDtypeStruct((cut, chunk), BF16),) * pieces,
        grid_spec=pltpu.PrefetchScalarGridSpec(
            num_scalar_prefetch=1,
            grid=(per,),
            in_specs=[pl.BlockSpec((cut, depth), lambda j, order: (0, 0))] * pieces
            + [pl.BlockSpec((depth, tile), lambda j, order: (0, order[at] * per + j))],
            out_specs=(pl.BlockSpec((cut, tile), lambda j, order: (0, j)),) * pieces,
        ),
        compiler_params=PARAMS,
        cost_estimate=cost(2 * pieces * cut * depth * chunk, depth * chunk * 2),
        name=name,
    )(order, *attended, out_weight)


def add_kernel(a_ref, b_ref, out_ref):
    out_ref[...] = (a_ref[...].astype(F32) + b_ref[...].astype(F32)).astype(BF16)


def added(name, a, b):
    return pl.pallas_call(
        add_kernel,
        out_shape=jax.ShapeDtypeStruct(a.shape, BF16),
        in_specs=[VMEM, VMEM],
        out_specs=VMEM,
        compiler_params=PARAMS,
        cost_estimate=cost(a.size, a.size * 6),
        name=name,
    )(a, b)


def finish(name, flag, parts, begin, rows_all, into=None):
    rows, columns = parts[0].shape
    blocks = columns // BLOCK
    steps = 2 if blocks % 16 == 0 else 1
    per = blocks // steps
    count = len(parts)
    flags = () if flag is None else (flag,)

    def kernel(*refs):
        if flags:
            chosen = refs[0][0] == 1
            refs = refs[1:]
        out_ref, scale_ref = refs[-2:]
        lane = lax.broadcasted_iota(jnp.int32, (rows, HD), 1)
        scales = jnp.zeros((rows, HD), F32)
        for block in range(per):
            at = slice(block * BLOCK, (block + 1) * BLOCK)
            terms = [ref[:, at].astype(F32) for ref in refs[:count]]
            if flags:
                terms = [jnp.where(chosen, terms[0], terms[1])] + terms[2:]
            total = functools.reduce(jnp.add, terms)
            scale = jnp.max(jnp.abs(total), axis=1, keepdims=True) + 1e-06
            out_ref[:, at] = (total / scale).astype(BF16)
            scales = jnp.where(lane == block, scale, scales)
        scale_ref[...] = scales.T[:per]

    part_spec = pl.BlockSpec((rows, columns // steps), lambda i: (0, i))
    into = () if into is None else into
    return pl.pallas_call(
        kernel,
        out_shape=(
            jax.ShapeDtypeStruct((rows_all, columns), BF16),
            jax.ShapeDtypeStruct((blocks, rows_all), F32),
        ),
        grid=(steps,),
        in_specs=[SMEM] * len(flags) + [part_spec] * count + [pl.BlockSpec(memory_space=pl.ANY)] * len(into),
        out_specs=(
            pl.BlockSpec((rows, columns // steps), lambda i: (begin // rows, i)),
            pl.BlockSpec((per, rows), lambda i: (i, begin // rows)),
        ),
        input_output_aliases={len(flags) + count: 0, len(flags) + count + 1: 1} if into else {},
        compiler_params=PARAMS,
        cost_estimate=cost(rows * columns * 6, rows * columns * 2 * (count + 1)),
        name=name,
    )(*flags, *parts, *into)


def after(value, *others):
    return lax.optimization_barrier((value, *others))[0]


def local(
    queries, new_keys, new_values, key_cache, value_cache, prefix_len, stretch_start, out_weight
):
    rows = queries.shape[0]
    heads_here = queries.shape[1] // HD
    group = HQ // KVH
    tensor_pos = lax.axis_index("tensor")
    lanes = lax.axis_size("tensor")
    n_seq, n_pipe = lax.axis_size("seq"), lax.axis_size("pipe")
    shards = n_seq * n_pipe
    assert heads_here <= group
    slots = key_cache.shape[1]
    split = slots * 3 // 4
    kv_head = tensor_pos * heads_here // group
    me = lax.axis_index("seq") * n_pipe + lax.axis_index("pipe")
    info = jnp.stack([kv_head.astype(jnp.int32), prefix_len[0]])

    positions = stretch_start[0] + me * rows + jnp.arange(rows, dtype=jnp.int32)
    lane = jnp.arange(HD)
    freq = 500000.0 ** (-((lane % (HD // 2)).astype(F32) * 2.0 / HD))
    angle = positions.astype(F32)[:, None] * freq[None, :]
    cosine = jnp.cos(angle)
    sine = jnp.sin(angle) * jnp.where(lane < HD // 2, -1.0, 1.0)[None, :]

    own_a = pack_first(info, key_cache, value_cache, split)
    own_b = pack_second(info, key_cache, value_cache, new_keys, new_values, cosine, sine, split)
    tables = [cosine, sine]
    columns = D // lanes
    step = jnp.arange(lanes, dtype=jnp.int32)

    def whole_plan(at, off):
        return [
            (at, 0, split, "live", 0),
            (at + 1, 0, slots - split, "live", split),
            (at + 1, slots - split, rows, "rows", off),
        ]

    if n_seq == 2 and n_pipe == 2 and lanes == 4:
        order = jnp.where(tensor_pos < 2, 3 - step, step)
        flag = ((tensor_pos == 0) | (tensor_pos == lanes - 1)).astype(jnp.int32).reshape(1)
        inward = [(0, 1), (3, 2)]
        middle = [(1, 2), (2, 1)]
        outward = [(1, 0), (2, 3)]
        swap = [(0, 1), (1, 0)]
        far_a = lax.ppermute(own_a, "seq", swap)
        near_a = lax.ppermute(own_a, "pipe", swap)
        far_b = lax.ppermute(own_b, "seq", swap)
        near_b = lax.ppermute(own_b, "pipe", swap)
        offs = (me - jnp.stack([me, me ^ 1, me ^ 2, me ^ 3])).astype(jnp.int32) * rows
        offs = jnp.concatenate([offs, order[:1]])
        acc, stats, query = attend(
            "attend_near",
            queries,
            [own_a, own_b, near_a, near_b],
            whole_plan(0, 0) + whole_plan(2, 1),
            {0: 0, 1: 0, 2: 2, 3: 2},
            offs,
            None,
            False,
            tables,
        )
        cross_a = lax.ppermute(after(far_a, stats), "pipe", swap)
        cross_b = lax.ppermute(after(far_b, stats), "pipe", swap)
        acc, stats = attend(
            "attend_far_a",
            query,
            [far_a, cross_a],
            [(0, 0, split, "live", 0), (1, 0, split, "live", 0)],
            {0: 0, 1: 1},
            offs,
            (acc, stats),
            False,
        )
        cut = rows // 2
        attended, first_part, come = [], [], [[], [], []]
        for i in range(2):
            x, p = attend(
                f"attend_far_b{i}",
                query,
                [far_b, cross_b, far_a[:, split:], cross_a[:, split:]],
                [
                    (0, 0, slots - split, "live", split),
                    (0, slots - split, rows, "rows", 2),
                    (1, 0, slots - split, "live", split),
                    (1, slots - split, rows, "rows", 3),
                ],
                {0: 2, 1: 3},
                offs,
                (acc, stats) if i == 0 else (acc, after(stats, first_part[0])),
                True,
                weight=out_weight,
                chunk=columns,
                span=(i * cut, cut),
            )
            attended.append(x)
            first_part.append(p)
            come[0].append(lax.ppermute(p, "tensor", inward))
        part = [first_part]
        for k in range(1, 4):
            part.append(project(f"project_{k}", order, k, attended, out_weight, columns))
            if k < 3:
                come[k] = [lax.ppermute(p, "tensor", inward) for p in part[k]]
        done = None
        for i in range(2):
            across = lax.ppermute(added(f"add_0{i}", part[0][i], come[0][i]), "tensor", middle)
            second = lax.ppermute(added(f"add_1{i}", part[1][i], come[1][i]), "tensor", middle)
            back = lax.ppermute(added(f"add_3{i}", part[3][i], across), "tensor", outward)
            parts = [part[3][i], part[2][i], come[2][i], second, back]
            done = finish(f"finish_{i}", flag, parts, i * cut, rows, done)
        return done[0], done[1].T
    all_a = lax.all_gather(own_a, ("seq", "pipe"), axis=0)
    all_b = lax.all_gather(own_b, ("seq", "pipe"), axis=0)
    offs = (me - jnp.arange(shards)).astype(jnp.int32) * rows
    state = None
    query = queries
    for shard in range(shards):
        arrays = [all_a[shard], all_b[shard]]
        state = attend(
            "attend",
            query,
            arrays,
            whole_plan(0, shard),
            {0: 0, 1: 0},
            offs,
            state,
            shard == shards - 1,
            tables,
        )
        if shard == 0:
            query = state[2]
            state = state[:2]
    partial = [
        project(f"project_{k}", step, k, state[:1], out_weight, columns)[0] for k in range(lanes)
    ]
    total = lax.psum_scatter(jnp.stack(partial), "tensor", scatter_dimension=0, tiled=True)[0]
    values, scales = finish("finish", None, [total], 0, rows)
    return values, scales.T


def solution(mesh):
    return jax.shard_map(
        local,
        mesh=mesh,
        in_specs=(
            P(("groups", "seq", "pipe"), "tensor"),
            P(("groups", "seq", "pipe"), None),
            P(("groups", "seq", "pipe"), None),
            P(None, ("groups", "seq", "pipe"), None),
            P(None, ("groups", "seq", "pipe"), None),
            P(("groups", "seq", "pipe")),
            P("groups"),
            P("tensor", None),
        ),
        out_specs=(P(("groups", "seq", "pipe"), "tensor"), P(("groups", "seq", "pipe"), "tensor")),
        check_vma=False,
    )
```

time: 132 us -> 121 us (0.917)
  local copies, waits for them, and re-layouts: 19.4 us -> 7.68 us
  Pallas kernels: 41.9 us -> 52.3 us
  waiting for transfers between devices: 34.8 us -> 24.6 us
  other arithmetic: 0.71 us -> 2.09 us
    unnamed x36 -> x18, local copies, waits for them, and re-layouts: 18.7 us -> 7.68 us
    ppermute x8, waiting for transfers between devices: 28.3 us -> 18.7 us  [the longest x4 9.73 us: local(): come[k] = [lax.ppermute(p, 'tensor', inward) for p in part[k]]]
    pallas_call x4, Pallas kernels: 21.4 us -> 27 us  [attend(): pl.pallas_call(functools.partial(attend_kernel, plan, lens, first, last,...]
    pallas_call x5 -> x3, Pallas kernels: 12.3 us -> 14.4 us  [project(): pl.pallas_call(functools.partial(project_kernel, pieces), out_shape=(jax....]
    pallas_call x1, Pallas kernels: 0.87 us -> 2.64 us  [pack_second(): pl.pallas_call(functools.partial(pack_second_kernel, first), out_shape=ja...]
    ppermute x1, waiting for transfers between devices: 1.64 us -> 0.01 us  [local(): far_a = lax.ppermute(own_a, 'seq', swap)]
    pallas_call x1, Pallas kernels: 1.08 us -> 2.45 us  [pack_first(): pl.pallas_call(pack_first_kernel, out_shape=jax.ShapeDtypeStruct((2, coun...]
  transfers between devices with their start and end apart: 18 -> 18, of which waited for: 8 -> 7; matrix products, arithmetic and copies ran while one was open for 0% -> 1% of each run, Pallas kernels for 23% -> 34%
where the time goes in v3:
time: 121 us; the launch traced here: 120 us
  Pallas kernels  52.3 us (43%)
  starting transfers between devices  30.9 us (26%)
  waiting for transfers between devices  24.6 us (20%)
  local copies, waits for them, and re-layouts  7.68 us (6%)
  between operations  2.21 us (2%)
  other arithmetic  2.09 us (2%)
    pallas_call x4, Pallas kernels, attend(): pl.pallas_call(functools.partial(attend_kernel, plan, lens, first, last,...  27 us
    ppermute x4, starting transfers between devices, local(): come[k] = [lax.ppermute(p, 'tensor', inward) for p in part[k]]  15 us
    pallas_call x3, Pallas kernels, project(): pl.pallas_call(functools.partial(project_kernel, pieces), out_shape=(jax....  14.4 us
    ppermute x4, waiting for transfers between devices, local(): come[k] = [lax.ppermute(p, 'tensor', inward) for p in part[k]]  9.73 us
    ppermute x2, waiting for transfers between devices, local(): come[0].append(lax.ppermute(p, 'tensor', inward))  7.72 us
    unnamed x18, local copies, waits for them, and re-layouts  7.68 us
    pallas_call x2, Pallas kernels, finish(): pl.pallas_call(kernel, out_shape=(jax.ShapeDtypeStruct((rows_all, columns...  5.1 us
    ppermute x2, waiting for transfers between devices, local(): lax.ppermute(added(f'add_3{i}', part[3][i], across), 'tensor', outward)  4.84 us
  transfers between devices with their start and end apart: 18, of which 7 were waited for; matrix products, arithmetic and copies ran while one was open for 1% of the time, Pallas kernels for 34%

profile of v3, /device:TPU:0, one launch (start us, length us, event | category | flops | bytes accessed | tf_op | source)
XLA Modules:
  0.0 119.8 jit_solution(4607610645973178132)
XLA Ops:
  1.9 2.5 %pack_first.1.refs_0_ = bf16[2,784,128]{2,1,0:T(8,128)(2,1)} custom-call(s32[2]{0:T(128)} %pad_add_fusion.1.info_ref, bf16[4,1024,128]{2,1,0:T(8,128)(2,1)} %k_ref.3, bf16[4,1024,128]{2,1,0:T(8,128)(2,1)} %v_ref.3), custom_call_target="tpu_custom_call" | custom-call | bytes 786432 | tf_op jit(solution)/shard_map/pack_first/pallas_call | solution.py:64
  4.9 2.6 %collective-permute-start.4 = (bf16[2,784,128]{2,1,0:T(8,128)(2,1)}, bf16[2,784,128]{2,1,0:T(8,128)(2,1)S(1)}, u32[]{:S(2)}, u32[]{:S(2)}) collective-permute-start(bf16[2,784,128]{2,1,0:T(8,128)(2,1)} %pack_first.1.refs_0_), channel_id=1, source_target_pairs={{0,2},{2,0},{1,3},{3,1},{4,6},{6,4},{5,7},{7,5},{8,10},{10,8},{9,1... | collective-permute-start | bytes 1204232 | tf_op jit(solution)/shard_map/ppermute | solution.py:409
  9.4 2.6 %pack_second.1.refs_1_ = bf16[2,512,128]{2,1,0:T(8,128)(2,1)} custom-call(s32[2]{0:T(128)} %pad_add_fusion.1.info_ref, bf16[4,1024,128]{2,1,0:T(8,128)(2,1)} %k_ref.3, bf16[4,1024,128]{2,1,0:T(8,128)(2,1)} %v_ref.3, bf16[256,512]{1,0:T(8,128)(2,1)} %nk_ref.1, bf16[256,512]{1,0:T(8,128)(2,1)} %nv_ref.1, f32[256,128]{1,0:T(8,128)} %get-tuple-element.47.cos_ref.refs_4_, ...), custom_call_target="tpu_custom_call" | custom-call | bytes 524288 | tf_op jit(solution)/shard_map/pack_second/pallas_call | solution.py:104
  18.7 8.4 %attend_near.1 = (f32[256,1024]{1,0:T(8,128)S(1)}, f32[256,128]{1,0:T(8,128)S(1)}, bf16[256,1024]{1,0:T(8,128)(2,1)S(1)}) custom-call(s32[5]{0:T(128)S(1)} %pad_add_fusion.offs_ref, bf16[256,1024]{1,0:T(8,128)(2,1)S(1)} %copy-done.4, bf16[2,784,128]{2,1,0:T(8,128)(2,1)S(1)} %copy-done, bf16[2,512,128]{2,1,0:T(8,128)(2,1)S(1)} %copy-done.3, ...), custom_call_target="tpu_custom_call" | custom-call | flops 335544320 | bytes 262144 | tf_op jit(solution)/shard_map/attend_near/pallas_call | solution.py:257
  28.9 5.8 %attend_far_a.1 = (f32[256,1024]{1,0:T(8,128)S(1)}, f32[256,128]{1,0:T(8,128)S(1)}) custom-call(s32[5]{0:T(128)S(1)} %pad_add_fusion.offs_ref, bf16[256,1024]{1,0:T(8,128)(2,1)S(1)} %get-tuple-element.24.q_ref, bf16[2,784,128]{2,1,0:T(8,128)(2,1)S(1)} %collective-permute-done.4.refs_0_, bf16[2,784,128]{2,1,0:T(8,128)(2,1)S(1)} %collective-permute-done.5.refs_1_, ...), custom_call_target="tpu_custom_call" | custom-call | flops 201326592 | bytes 262144 | tf_op jit(solution)/shard_map/attend_far_a/pallas_call | solution.py:257
  34.7 6.4 %attend_far_b0.1 = (bf16[128,1024]{1,0:T(8,128)(2,1)S(1)}, bf16[128,2048]{1,0:T(8,128)(2,1)S(1)}) custom-call(s32[5]{0:T(128)S(1)} %pad_add_fusion.offs_ref, bf16[256,1024]{1,0:T(8,128)(2,1)S(1)} %get-tuple-element.24.q_ref, bf16[2,512,128]{2,1,0:T(8,128)(2,1)S(1)} %collective-permute-done.2.refs_0_, ...), custom_call_target="tpu_custom_call" | custom-call | flops 67108864 | bytes 262144 | tf_op jit(solution)/shard_map/attend_far_b0/pallas_call | solution.py:257
  41.1 3.5 %collective-permute-start.15 = (bf16[128,2048]{1,0:T(8,128)(2,1)S(1)}, bf16[128,2048]{1,0:T(8,128)(2,1)S(1)}, u32[]{:S(2)}, u32[]{:S(2)}) collective-permute-start(bf16[128,2048]{1,0:T(8,128)(2,1)S(1)} %get-tuple-element.32.a_ref), channel_id=1, source_target_pairs={{0,4},{12,8},{1,5},{13,9},{2,6},{14,10},{3,7},{15,11},{16,20},{28,... | collective-permute-start | bytes 1572872 | tf_op jit(solution)/shard_map/ppermute | solution.py:461
  44.6 6.4 %attend_far_b1.1 = (bf16[128,1024]{1,0:T(8,128)(2,1)S(1)}, bf16[128,2048]{1,0:T(8,128)(2,1)S(1)}) custom-call(s32[5]{0:T(128)S(1)} %pad_add_fusion.offs_ref, bf16[256,1024]{1,0:T(8,128)(2,1)S(1)} %get-tuple-element.24.q_ref, bf16[2,512,128]{2,1,0:T(8,128)(2,1)S(1)} %collective-permute-done.2.refs_0_, ...), custom_call_target="tpu_custom_call" | custom-call | flops 67108864 | bytes 262144 | tf_op jit(solution)/shard_map/attend_far_b1/pallas_call | solution.py:257
  51.0 1.3 %collective-permute-start.9 = (bf16[128,2048]{1,0:T(8,128)(2,1)S(1)}, bf16[128,2048]{1,0:T(8,128)(2,1)S(1)}, u32[]{:S(2)}, u32[]{:S(2)}) collective-permute-start(bf16[128,2048]{1,0:T(8,128)(2,1)S(1)} %get-tuple-element.38.a_ref), channel_id=1, source_target_pairs={{0,4},{12,8},{1,5},{13,9},{2,6},{14,10},{3,7},{15,11},{16,20},{28,... | collective-permute-start | bytes 1572872 | tf_op jit(solution)/shard_map/ppermute | solution.py:461
  52.3 4.5 %project_1.1 = (bf16[128,2048]{1,0:T(8,128)(2,1)S(1)}, bf16[128,2048]{1,0:T(8,128)(2,1)S(1)}) custom-call(s32[4]{0:T(128)S(1)} %broadcast_select_fusion.order_ref, bf16[128,1024]{1,0:T(8,128)(2,1)S(1)} %get-tuple-element.31.refs_0_, bf16[128,1024]{1,0:T(8,128)(2,1)S(1)} %get-tuple-element.34.refs_1_, bf16[1024,8192]{1,0:T(8,128)(2,1)} %refs_2_.5), custom_call_target="tpu_custom_call" | custom-call | flops 1073741824 | bytes 4194304 | tf_op jit(solution)/shard_map/project_1/pallas_call | solution.py:282
  56.9 1.3 %collective-permute-start.13 = (bf16[128,2048]{1,0:T(8,128)(2,1)S(1)}, bf16[128,2048]{1,0:T(8,128)(2,1)S(1)}, u32[]{:S(2)}, u32[]{:S(2)}) collective-permute-start(bf16[128,2048]{1,0:T(8,128)(2,1)S(1)} %get-tuple-element.41.a_ref), channel_id=1, source_target_pairs={{0,4},{12,8},{1,5},{13,9},{2,6},{14,10},{3,7},{15,11},{16,20},{28,... | collective-permute-start | bytes 1572872 | tf_op jit(solution)/shard_map/ppermute | solution.py:466
  60.4 7.7 %collective-permute-done.9.b_ref = bf16[128,2048]{1,0:T(8,128)(2,1)S(1)} collective-permute-done((bf16[128,2048]{1,0:T(8,128)(2,1)S(1)}, bf16[128,2048]{1,0:T(8,128)(2,1)S(1)}, u32[]{:S(2)}, u32[]{:S(2)}) %collective-permute-start.9) | collective-permute-done | bytes 524320 | tf_op jit(solution)/shard_map/ppermute | solution.py:461
  68.9 5.3 %project_2.1 = (bf16[128,2048]{1,0:T(8,128)(2,1)S(1)}, bf16[128,2048]{1,0:T(8,128)(2,1)}) custom-call(s32[4]{0:T(128)S(1)} %broadcast_select_fusion.order_ref, bf16[128,1024]{1,0:T(8,128)(2,1)S(1)} %get-tuple-element.31.refs_0_, bf16[128,1024]{1,0:T(8,128)(2,1)S(1)} %get-tuple-element.34.refs_1_, bf16[1024,8192]{1,0:T(8,128)(2,1)} %refs_2_.5), custom_call_target="tpu_custom_call" | custom-call | flops 1073741824 | bytes 4194304 | tf_op jit(solution)/shard_map/project_2/pallas_call | solution.py:282
  74.2 7.2 %collective-permute-start.12 = (bf16[128,2048]{1,0:T(8,128)(2,1)S(1)}, bf16[128,2048]{1,0:T(8,128)(2,1)S(1)}, u32[]{:S(2)}, u32[]{:S(2)}) collective-permute-start(bf16[128,2048]{1,0:T(8,128)(2,1)S(1)} %get-tuple-element.40.refs_2_), channel_id=1, source_target_pairs={{0,4},{12,8},{1,5},{13,9},{2,6},{14,10},{3,7},{15,11},{16,20},{28,... | collective-permute-start | bytes 1572872 | tf_op jit(solution)/shard_map/ppermute | solution.py:466
  81.5 4.5 %project_3.1 = (bf16[128,2048]{1,0:T(8,128)(2,1)S(1)}, bf16[128,2048]{1,0:T(8,128)(2,1)S(1)}) custom-call(s32[4]{0:T(128)S(1)} %broadcast_select_fusion.order_ref, bf16[128,1024]{1,0:T(8,128)(2,1)S(1)} %get-tuple-element.31.refs_0_, bf16[128,1024]{1,0:T(8,128)(2,1)S(1)} %get-tuple-element.34.refs_1_, bf16[1024,8192]{1,0:T(8,128)(2,1)} %refs_2_.5), custom_call_target="tpu_custom_call" | custom-call | flops 1073741824 | bytes 4194304 | tf_op jit(solution)/shard_map/project_3/pallas_call | solution.py:282
  86.1 1.5 %collective-permute-start.14 = (bf16[128,2048]{1,0:T(8,128)(2,1)S(1)}, bf16[128,2048]{1,0:T(8,128)(2,1)}, u32[]{:S(2)}, u32[]{:S(2)}) collective-permute-start(bf16[128,2048]{1,0:T(8,128)(2,1)S(1)} %add_10.1), channel_id=1, source_target_pairs={{4,8},{8,4},{5,9},{9,5},{6,10},{10,6},{7,11},{11,7},{20,24},{24,20... | collective-permute-start | bytes 1572872 | tf_op jit(solution)/shard_map/ppermute | solution.py:470
  89.0 1.5 %collective-permute-done.7.b_ref = bf16[128,2048]{1,0:T(8,128)(2,1)S(1)} collective-permute-done((bf16[128,2048]{1,0:T(8,128)(2,1)S(1)}, bf16[128,2048]{1,0:T(8,128)(2,1)S(1)}, u32[]{:S(2)}, u32[]{:S(2)}) %collective-permute-start.7) | collective-permute-done | bytes 524320 | tf_op jit(solution)/shard_map/ppermute | solution.py:466
  90.5 5.2 %collective-permute-start.6 = (bf16[128,2048]{1,0:T(8,128)(2,1)}, bf16[128,2048]{1,0:T(8,128)(2,1)}, u32[]{:S(2)}, u32[]{:S(2)}) collective-permute-start(bf16[128,2048]{1,0:T(8,128)(2,1)} %get-tuple-element.36.refs_2_), channel_id=1, source_target_pairs={{0,4},{12,8},{1,5},{13,9},{2,6},{14,10},{3,7},{15,11},{16,20},{28,... | collective-permute-start | bytes 1572872 | tf_op jit(solution)/shard_map/ppermute | solution.py:466
  95.9 1.5 %collective-permute-start.8 = (bf16[128,2048]{1,0:T(8,128)(2,1)S(1)}, bf16[128,2048]{1,0:T(8,128)(2,1)}, u32[]{:S(2)}, u32[]{:S(2)}) collective-permute-start(bf16[128,2048]{1,0:T(8,128)(2,1)S(1)} %add_11.1), channel_id=1, source_target_pairs={{4,8},{8,4},{5,9},{9,5},{6,10},{10,6},{7,11},{11,7},{20,24},{24,20... | collective-permute-start | bytes 1572872 | tf_op jit(solution)/shard_map/ppermute | solution.py:470
  97.5 4.3 %collective-permute-done.12.refs_3_ = bf16[128,2048]{1,0:T(8,128)(2,1)S(1)} collective-permute-done((bf16[128,2048]{1,0:T(8,128)(2,1)S(1)}, bf16[128,2048]{1,0:T(8,128)(2,1)S(1)}, u32[]{:S(2)}, u32[]{:S(2)}) %collective-permute-start.12) | collective-permute-done | bytes 524320 | tf_op jit(solution)/shard_map/ppermute | solution.py:466
  106.0 2.5 %finish_0.1 = (bf16[256,2048]{1,0:T(8,128)(2,1)}, f32[16,256]{1,0:T(8,128)}) custom-call(s32[1]{0:T(128)} %bitcast.refs_0_, bf16[128,2048]{1,0:T(8,128)(2,1)S(1)} %get-tuple-element.39.a_ref.refs_1_, bf16[128,2048]{1,0:T(8,128)(2,1)S(1)} %copy-done.6, bf16[128,2048]{1,0:T(8,128)(2,1)S(1)} %copy-done.8, bf16[128,2048]{1,0:T(8,128)(2,1)} %collective-permute-done.14.refs_4_, ...), custom_call_target="tpu_custom_call" | custom-call | flops 1572864 | bytes 3145728 | tf_op jit(solution)/shard_map/finish_0/pallas_call | solution.py:342
  108.5 3.9 %collective-permute-done.6.refs_3_ = bf16[128,2048]{1,0:T(8,128)(2,1)} collective-permute-done((bf16[128,2048]{1,0:T(8,128)(2,1)}, bf16[128,2048]{1,0:T(8,128)(2,1)}, u32[]{:S(2)}, u32[]{:S(2)}) %collective-permute-start.6) | collective-permute-done | bytes 524320 | tf_op jit(solution)/shard_map/ppermute | solution.py:466
  112.3 4.8 %collective-permute-done.11.refs_5_ = bf16[128,2048]{1,0:T(8,128)(2,1)} collective-permute-done((bf16[128,2048]{1,0:T(8,128)(2,1)S(1)}, bf16[128,2048]{1,0:T(8,128)(2,1)}, u32[]{:S(2)}, u32[]{:S(2)}) %collective-permute-start.11) | collective-permute-done | bytes 524320 | tf_op jit(solution)/shard_map/ppermute | solution.py:471
  117.2 2.6 %finish_1.1 = (bf16[256,2048]{1,0:T(8,128)(2,1)}, f32[16,256]{1,0:T(8,128)}) custom-call(s32[1]{0:T(128)} %bitcast.refs_0_, bf16[128,2048]{1,0:T(8,128)(2,1)S(1)} %get-tuple-element.35.a_ref.refs_1_, bf16[128,2048]{1,0:T(8,128)(2,1)} %get-tuple-element.36.refs_2_, ...), custom_call_target="tpu_custom_call", output_to_operand_aliasing={{0}: (6, {}), {1}: (7, {})} | custom-call | flops 1572864 | bytes 3145728 | tf_op jit(solution)/shard_map/finish_1/pallas_call | solution.py:342
  (56 shorter events, 19.7 us)
Async XLA Ops:
  4.4 9.5 %collective-permute-start = (bf16[2,784,128]{2,1,0:T(8,128)(2,1)}, bf16[2,784,128]{2,1,0:T(8,128)(2,1)S(1)}, u32[]{:S(2)}, u32[]{:S(2)}) collective-permute-start(bf16[2,784,128]{2,1,0:T(8,128)(2,1)} %pack_first.1.refs_0_), channel_id=1, source_target_pairs={{0,1},{1,0},{2,3},{3,2},{4,5},{5,4},{6,7},{7,6},{8,9},{9,8},{10,11... | collective-permute-start | bytes 1204232 | tf_op jit(solution)/shard_map/ppermute | solution.py:410
  4.9 22.2 %collective-permute-start.4 = (bf16[2,784,128]{2,1,0:T(8,128)(2,1)}, bf16[2,784,128]{2,1,0:T(8,128)(2,1)S(1)}, u32[]{:S(2)}, u32[]{:S(2)}) collective-permute-start(bf16[2,784,128]{2,1,0:T(8,128)(2,1)} %pack_first.1.refs_0_), channel_id=1, source_target_pairs={{0,2},{2,0},{1,3},{3,1},{4,6},{6,4},{5,7},{7,5},{8,10},{10,8},{9,1... | collective-permute-start | bytes 1204232 | tf_op jit(solution)/shard_map/ppermute | solution.py:409
  12.0 1.8 %collective-permute-start.1 = (bf16[2,512,128]{2,1,0:T(8,128)(2,1)}, bf16[2,512,128]{2,1,0:T(8,128)(2,1)S(1)}, u32[]{:S(2)}, u32[]{:S(2)}) collective-permute-start(bf16[2,512,128]{2,1,0:T(8,128)(2,1)} %pack_second.1.refs_1_), channel_id=1, source_target_pairs={{0,1},{1,0},{2,3},{3,2},{4,5},{5,4},{6,7},{7,6},{8,9},{9,8},{10,11... | collective-permute-start | bytes 786440 | tf_op jit(solution)/shard_map/ppermute | solution.py:412
  12.3 15.1 %collective-permute-start.2 = (bf16[2,512,128]{2,1,0:T(8,128)(2,1)}, bf16[2,512,128]{2,1,0:T(8,128)(2,1)S(1)}, u32[]{:S(2)}, u32[]{:S(2)}) collective-permute-start(bf16[2,512,128]{2,1,0:T(8,128)(2,1)} %pack_second.1.refs_1_), channel_id=1, source_target_pairs={{0,2},{2,0},{1,3},{3,1},{4,6},{6,4},{5,7},{7,5},{8,10},{10,8},{9,1... | collective-permute-start | bytes 786440 | tf_op jit(solution)/shard_map/ppermute | solution.py:411
  13.9 1.0 copy-start
  16.7 0.9 copy-start.3
  17.6 1.0 copy-start.4
  27.1 1.8 %collective-permute-start.5 = (bf16[2,784,128]{2,1,0:T(8,128)(2,1)S(1)}, bf16[2,784,128]{2,1,0:T(8,128)(2,1)S(1)}, u32[]{:S(2)}, u32[]{:S(2)}) collective-permute-start(bf16[2,784,128]{2,1,0:T(8,128)(2,1)S(1)} %collective-permute-done.4.refs_0_), channel_id=1, source_target_pairs={{0,1},{1,0},{2,3},{3,2},{4,5},{5,4},{6,7},{7,6},{8,9},{9,8},{10,11... | collective-permute-start | bytes 1204232 | tf_op jit(solution)/shard_map/ppermute | solution.py:426
  27.3 7.3 %collective-permute-start.3 = (bf16[2,512,128]{2,1,0:T(8,128)(2,1)S(1)}, bf16[2,512,128]{2,1,0:T(8,128)(2,1)S(1)}, u32[]{:S(2)}, u32[]{:S(2)}) collective-permute-start(bf16[2,512,128]{2,1,0:T(8,128)(2,1)S(1)} %collective-permute-done.2.refs_0_), channel_id=1, source_target_pairs={{0,1},{1,0},{2,3},{3,2},{4,5},{5,4},{6,7},{7,6},{8,9},{9,8},{10,11... | collective-permute-start | bytes 786440 | tf_op jit(solution)/shard_map/ppermute | solution.py:427
  41.1 18.4 %collective-permute-start.15 = (bf16[128,2048]{1,0:T(8,128)(2,1)S(1)}, bf16[128,2048]{1,0:T(8,128)(2,1)S(1)}, u32[]{:S(2)}, u32[]{:S(2)}) collective-permute-start(bf16[128,2048]{1,0:T(8,128)(2,1)S(1)} %get-tuple-element.32.a_ref), channel_id=1, source_target_pairs={{0,4},{12,8},{1,5},{13,9},{2,6},{14,10},{3,7},{15,11},{16,20},{28,... | collective-permute-start | bytes 1572872 | tf_op jit(solution)/shard_map/ppermute | solution.py:461
  51.0 17.1 %collective-permute-start.9 = (bf16[128,2048]{1,0:T(8,128)(2,1)S(1)}, bf16[128,2048]{1,0:T(8,128)(2,1)S(1)}, u32[]{:S(2)}, u32[]{:S(2)}) collective-permute-start(bf16[128,2048]{1,0:T(8,128)(2,1)S(1)} %get-tuple-element.38.a_ref), channel_id=1, source_target_pairs={{0,4},{12,8},{1,5},{13,9},{2,6},{14,10},{3,7},{15,11},{16,20},{28,... | collective-permute-start | bytes 1572872 | tf_op jit(solution)/shard_map/ppermute | solution.py:461
  56.9 29.1 %collective-permute-start.13 = (bf16[128,2048]{1,0:T(8,128)(2,1)S(1)}, bf16[128,2048]{1,0:T(8,128)(2,1)S(1)}, u32[]{:S(2)}, u32[]{:S(2)}) collective-permute-start(bf16[128,2048]{1,0:T(8,128)(2,1)S(1)} %get-tuple-element.41.a_ref), channel_id=1, source_target_pairs={{0,4},{12,8},{1,5},{13,9},{2,6},{14,10},{3,7},{15,11},{16,20},{28,... | collective-permute-start | bytes 1572872 | tf_op jit(solution)/shard_map/ppermute | solution.py:466
  58.2 32.4 %collective-permute-start.7 = (bf16[128,2048]{1,0:T(8,128)(2,1)S(1)}, bf16[128,2048]{1,0:T(8,128)(2,1)S(1)}, u32[]{:S(2)}, u32[]{:S(2)}) collective-permute-start(bf16[128,2048]{1,0:T(8,128)(2,1)S(1)} %get-tuple-element.37.a_ref), channel_id=1, source_target_pairs={{0,4},{12,8},{1,5},{13,9},{2,6},{14,10},{3,7},{15,11},{16,20},{28,... | collective-permute-start | bytes 1572872 | tf_op jit(solution)/shard_map/ppermute | solution.py:466
  59.7 27.9 %collective-permute-start.16 = (bf16[128,2048]{1,0:T(8,128)(2,1)S(1)}, bf16[128,2048]{1,0:T(8,128)(2,1)S(1)}, u32[]{:S(2)}, u32[]{:S(2)}) collective-permute-start(bf16[128,2048]{1,0:T(8,128)(2,1)S(1)} %add_00.1), channel_id=1, source_target_pairs={{4,8},{8,4},{5,9},{9,5},{6,10},{10,6},{7,11},{11,7},{20,24},{24,20... | collective-permute-start | bytes 1572872 | tf_op jit(solution)/shard_map/ppermute | solution.py:469
  68.2 27.7 %collective-permute-start.10 = (bf16[128,2048]{1,0:T(8,128)(2,1)S(1)}, bf16[128,2048]{1,0:T(8,128)(2,1)S(1)}, u32[]{:S(2)}, u32[]{:S(2)}) collective-permute-start(bf16[128,2048]{1,0:T(8,128)(2,1)S(1)} %add_01.1), channel_id=1, source_target_pairs={{4,8},{8,4},{5,9},{9,5},{6,10},{10,6},{7,11},{11,7},{20,24},{24,20... | collective-permute-start | bytes 1572872 | tf_op jit(solution)/shard_map/ppermute | solution.py:469
  74.2 23.2 %copy-start.5 = (bf16[128,2048]{1,0:T(8,128)(2,1)}, bf16[128,2048]{1,0:T(8,128)(2,1)S(1)}, u32[]{:S(2)}) copy-start(bf16[128,2048]{1,0:T(8,128)(2,1)S(1)} %get-tuple-element.40.refs_2_) | copy-start | bytes 1572868
  74.2 27.5 %collective-permute-start.12 = (bf16[128,2048]{1,0:T(8,128)(2,1)S(1)}, bf16[128,2048]{1,0:T(8,128)(2,1)S(1)}, u32[]{:S(2)}, u32[]{:S(2)}) collective-permute-start(bf16[128,2048]{1,0:T(8,128)(2,1)S(1)} %get-tuple-element.40.refs_2_), channel_id=1, source_target_pairs={{0,4},{12,8},{1,5},{13,9},{2,6},{14,10},{3,7},{15,11},{16,20},{28,... | collective-permute-start | bytes 1572872 | tf_op jit(solution)/shard_map/ppermute | solution.py:466
  86.1 17.8 %collective-permute-start.14 = (bf16[128,2048]{1,0:T(8,128)(2,1)S(1)}, bf16[128,2048]{1,0:T(8,128)(2,1)}, u32[]{:S(2)}, u32[]{:S(2)}) collective-permute-start(bf16[128,2048]{1,0:T(8,128)(2,1)S(1)} %add_10.1), channel_id=1, source_target_pairs={{4,8},{8,4},{5,9},{9,5},{6,10},{10,6},{7,11},{11,7},{20,24},{24,20... | collective-permute-start | bytes 1572872 | tf_op jit(solution)/shard_map/ppermute | solution.py:470
  87.7 16.2 %collective-permute-start.17 = (bf16[128,2048]{1,0:T(8,128)(2,1)S(1)}, bf16[128,2048]{1,0:T(8,128)(2,1)}, u32[]{:S(2)}, u32[]{:S(2)}) collective-permute-start(bf16[128,2048]{1,0:T(8,128)(2,1)S(1)} %add_30.1), channel_id=1, source_target_pairs={{4,0},{8,12},{5,1},{9,13},{6,2},{10,14},{7,3},{11,15},{20,16},{24,... | collective-permute-start | bytes 1572872 | tf_op jit(solution)/shard_map/ppermute | solution.py:471
  90.5 21.8 %collective-permute-start.6 = (bf16[128,2048]{1,0:T(8,128)(2,1)}, bf16[128,2048]{1,0:T(8,128)(2,1)}, u32[]{:S(2)}, u32[]{:S(2)}) collective-permute-start(bf16[128,2048]{1,0:T(8,128)(2,1)} %get-tuple-element.36.refs_2_), channel_id=1, source_target_pairs={{0,4},{12,8},{1,5},{13,9},{2,6},{14,10},{3,7},{15,11},{16,20},{28,... | collective-permute-start | bytes 1572872 | tf_op jit(solution)/shard_map/ppermute | solution.py:466
  95.9 16.5 %collective-permute-start.8 = (bf16[128,2048]{1,0:T(8,128)(2,1)S(1)}, bf16[128,2048]{1,0:T(8,128)(2,1)}, u32[]{:S(2)}, u32[]{:S(2)}) collective-permute-start(bf16[128,2048]{1,0:T(8,128)(2,1)S(1)} %add_11.1), channel_id=1, source_target_pairs={{4,8},{8,4},{5,9},{9,5},{6,10},{10,6},{7,11},{11,7},{20,24},{24,20... | collective-permute-start | bytes 1572872 | tf_op jit(solution)/shard_map/ppermute | solution.py:470
  102.6 14.6 %collective-permute-start.11 = (bf16[128,2048]{1,0:T(8,128)(2,1)S(1)}, bf16[128,2048]{1,0:T(8,128)(2,1)}, u32[]{:S(2)}, u32[]{:S(2)}) collective-permute-start(bf16[128,2048]{1,0:T(8,128)(2,1)S(1)} %add_31.1), channel_id=1, source_target_pairs={{4,0},{8,12},{5,1},{9,13},{6,2},{10,14},{7,3},{11,15},{20,16},{24,... | collective-permute-start | bytes 1572872 | tf_op jit(solution)/shard_map/ppermute | solution.py:471
  103.9 1.0 copy-start.6
  104.9 1.0 copy-start.8
  (3 other events, 2.6 us)

commit v4 on v3

v4 whole, which is shorter than its diff:
```python
import functools
import math

import jax
import jax.numpy as jnp
from jax import lax
from jax.experimental import pallas as pl
from jax.experimental.pallas import tpu as pltpu
from jax.sharding import PartitionSpec as P

D = 8192
HD = 128
HQ = 32
KVH = 4
BLOCK = 128
LEN_ROWS = 16
LOW = 32
NEG = -1e30
VMEM_LIMIT = 48 * 1024 * 1024
VMEM_MOST = 60 * 1024 * 1024
F32 = jnp.float32
BF16 = jnp.bfloat16
NT = (((1,), (1,)), ((), ()))


SMEM = pl.BlockSpec(memory_space=pltpu.SMEM)
VMEM = pl.BlockSpec(memory_space=pltpu.VMEM)
HBM = pl.BlockSpec(memory_space=pltpu.HBM)
PARAMS = pltpu.CompilerParams(vmem_limit_bytes=VMEM_LIMIT)
PARAMS_MOST = pltpu.CompilerParams(vmem_limit_bytes=VMEM_MOST)


def cost(flops, nbytes, transcendentals=0):
    return pl.CostEstimate(
        flops=int(flops), bytes_accessed=int(nbytes), transcendentals=int(transcendentals)
    )


def rotated(x, cosine, sine):
    return x * cosine + pltpu.roll(x, HD // 2, 1) * sine


def pack_kernel(per_kv_head, heads_here, len_ref, k_ref, v_ref, nk_ref, nv_ref, out_ref, live_rows, sems):
    slots, rows = k_ref.shape[1], nk_ref.shape[0]
    head = lax.axis_index("tensor") * heads_here // per_kv_head
    columns = pl.ds(pl.multiple_of(head * HD, HD), HD)
    copies = []
    for i, (cache, new) in enumerate(((k_ref, nk_ref), (v_ref, nv_ref))):
        copies.append((cache.at[head], out_ref.at[i, pl.ds(0, slots)]))
        copies.append((new.at[:, columns], out_ref.at[i, pl.ds(slots, rows)]))
    copies.append((live_rows, out_ref.at[:, pl.ds(slots + rows, LEN_ROWS)]))
    copies = [pltpu.make_async_copy(*pair, sems.at[i]) for i, pair in enumerate(copies)]
    for copy in copies[:-1]:
        copy.start()
    live = len_ref[0]
    live_rows[0] = jnp.full((LEN_ROWS, HD), (live // LOW).astype(F32), F32).astype(BF16)
    live_rows[1] = jnp.full((LEN_ROWS, HD), (live % LOW).astype(F32), F32).astype(BF16)
    copies[-1].start()
    for copy in copies:
        copy.wait()


def pack(prefix_len, key_cache, value_cache, new_keys, new_values, heads_here):
    size = key_cache.shape[1] + new_keys.shape[0] + LEN_ROWS
    return pl.pallas_call(
        functools.partial(pack_kernel, HQ // KVH, heads_here),
        out_shape=jax.ShapeDtypeStruct((2, size, HD), BF16),
        in_specs=[SMEM, HBM, HBM, HBM, HBM],
        out_specs=HBM,
        scratch_shapes=[pltpu.VMEM((2, LEN_ROWS, HD), BF16), pltpu.SemaphoreType.DMA((5,))],
        compiler_params=PARAMS_MOST,
        cost_estimate=cost(0, 4 * size * HD * 2),
        name="pack",
    )(prefix_len, key_cache, value_cache, new_keys, new_values)


def lane_max(x):
    parts = [x[:, i : i + HD] for i in range(0, x.shape[1], HD)]
    return functools.reduce(jnp.maximum, parts)


def lane_sum(x):
    parts = [x[:, i : i + HD] for i in range(0, x.shape[1], HD)]
    return functools.reduce(jnp.add, parts)


def attend_kernel(first, last, chunk, slots, shards_at, place_ref, q_ref, cos_ref, sin_ref, *refs):
    n = len(shards_at)
    kv_refs = refs[:n]
    refs = refs[n:]
    rows = q_ref.shape[0]
    heads = q_ref.shape[1] // HD
    me = place_ref[0]
    if first:
        acc_out, stats_out, query_out, raw, sem = refs
        copy = pltpu.make_async_copy(q_ref, raw, sem)
        copy.start()
    else:
        acc_in, stats_in = refs[:2]
        refs = refs[2:]
        if chunk:
            w_ref, attended_out, part_a, part_b, w_held, sem = refs
            columns = pl.ds(pl.multiple_of(place_ref[1] * chunk, chunk), chunk)
            copy = pltpu.make_async_copy(w_ref.at[:, columns], w_held, sem)
            copy.start()
        elif last:
            (attended_out,) = refs
        else:
            acc_out, stats_out = refs
    row = lax.broadcasted_iota(jnp.int32, (rows, rows), 0)
    column = lax.broadcasted_iota(jnp.int32, (rows, rows), 1)
    slot = lax.broadcasted_iota(jnp.int32, (1, HD), 1).astype(F32)
    segments = []
    for ref, at in zip(kv_refs, shards_at):
        shard = place_ref[2 + at]
        high = ref[0, slots + rows :, :].astype(F32)
        live = (high * LOW + ref[1, slots + rows :, :].astype(F32))[:1, :]
        pieces = [jnp.where(slot + float(i) < live, 0.0, NEG) for i in range(0, slots, HD)]
        segments.append((ref, None, 0, slots, jnp.concatenate(pieces, axis=1)))
        table = pl.ds(pl.multiple_of(shard * rows, rows), rows)
        keys = rotated(ref[0, slots : slots + rows, :].astype(F32), cos_ref[table], sin_ref[table])
        mask = jnp.where(column <= row + (me - shard) * rows, 0.0, NEG)
        segments.append((ref, keys.astype(BF16), slots, rows, mask))
    if first:
        factor = math.log2(math.e) / math.sqrt(HD)
        table = pl.ds(pl.multiple_of(me * rows, rows), rows)
        cosine = cos_ref[table] * factor
        sine = sin_ref[table] * factor
        copy.wait()
        for head in range(heads):
            at = slice(head * HD, (head + 1) * HD)
            query_out[:, at] = rotated(raw[:, at].astype(F32), cosine, sine).astype(BF16)
        q_ref = query_out

    def score(head):
        query = q_ref[:, head * HD : (head + 1) * HD]
        scores = []
        for ref, keys, begin, count, mask in segments:
            keys = ref[0, begin : begin + count, :] if keys is None else keys
            scores.append(lax.dot_general(query, keys, NT, preferred_element_type=F32) + mask)
        return scores

    lane = lax.broadcasted_iota(jnp.int32, (rows, HD), 1)
    stats = jnp.zeros((rows, HD), F32)
    following = score(0)
    for head in range(heads):
        scores = following
        if head + 1 < heads:
            following = score(head + 1)
        at = slice(head * HD, (head + 1) * HD)
        peak = functools.reduce(jnp.maximum, [lane_max(x) for x in scores])
        peak = jnp.max(peak, axis=1, keepdims=True)
        if not first:
            before = stats_in[:, head : head + 1]
            peak = jnp.maximum(before, peak)
            shrink = jnp.exp2(before - peak)
        total = None
        out = None
        for (ref, keys, begin, count, mask), part in zip(segments, scores):
            weights = jnp.exp2(part - peak)
            subtotal = lane_sum(weights)
            total = subtotal if total is None else total + subtotal
            values = ref[1, begin : begin + count, :]
            update = jnp.dot(weights.astype(BF16), values, preferred_element_type=F32)
            out = update if out is None else out + update
        total = jnp.sum(total, axis=1, keepdims=True)
        if not first:
            total = total + stats_in[:, HD // 2 + head : HD // 2 + head + 1] * shrink
            out = out + acc_in[:, at] * shrink
        if last:
            attended_out[:, at] = (out / total).astype(BF16)
        else:
            acc_out[:, at] = out
            stats = jnp.where(lane == head, peak, stats)
            stats = jnp.where(lane == HD // 2 + head, total, stats)
    if not last:
        stats_out[...] = stats
    if chunk:
        copy.wait()
        tile = 512
        cut = rows // 2
        for i in range(0, chunk, tile):
            part = jnp.dot(attended_out[...], w_held[:, i : i + tile], preferred_element_type=F32)
            part_a[:, i : i + tile] = part[:cut].astype(BF16)
            part_b[:, i : i + tile] = part[cut:].astype(BF16)


def attend(name, place, query, tables, arrays, shards_at, state, last, weight=None, chunk=0):
    rows, width = query.shape
    slots = arrays[0].shape[1] - rows - LEN_ROWS
    first = state is None
    operands = [place, query, *tables, *arrays]
    in_specs = [SMEM, HBM if first else VMEM] + [VMEM] * (2 + len(arrays))
    scratch = []
    if first:
        scratch = [pltpu.VMEM((rows, width), BF16), pltpu.SemaphoreType.DMA]
    else:
        operands += state
        in_specs += [VMEM] * 2
    if last:
        out_shape = [jax.ShapeDtypeStruct((rows, width), BF16)]
        if chunk:
            operands.append(weight)
            in_specs.append(HBM)
            out_shape += [jax.ShapeDtypeStruct((rows // 2, chunk), BF16)] * 2
            scratch = [pltpu.VMEM((width, chunk), BF16), pltpu.SemaphoreType.DMA]
    else:
        out_shape = [
            jax.ShapeDtypeStruct((rows, width), F32),
            jax.ShapeDtypeStruct((rows, HD), F32),
        ]
        if first:
            out_shape.append(jax.ShapeDtypeStruct((rows, width), BF16))
    keys = len(arrays) * (slots + rows)
    return pl.pallas_call(
        functools.partial(attend_kernel, first, last, chunk, slots, shards_at),
        out_shape=out_shape,
        in_specs=in_specs,
        out_specs=[VMEM] * len(out_shape),
        scratch_shapes=scratch,
        compiler_params=PARAMS,
        cost_estimate=cost(
            rows * width * keys // 2, rows * width, rows * (width // HD) * keys // 8
        ),
        name=name,
    )(*operands)


def project_kernel(order_ref, x_ref, w_ref, *out_refs):
    out = jnp.dot(x_ref[...], w_ref[...], preferred_element_type=F32)
    cut = out_refs[0].shape[0]
    for i, ref in enumerate(out_refs):
        ref[...] = out[i * cut : (i + 1) * cut].astype(BF16)


def project(name, order, at, attended, out_weight, chunk, pieces, tile=512):
    rows, depth = attended.shape
    cut = rows // pieces
    tile = min(tile, chunk)
    per = chunk // tile
    return pl.pallas_call(
        project_kernel,
        out_shape=(jax.ShapeDtypeStruct((cut, chunk), BF16),) * pieces,
        grid_spec=pltpu.PrefetchScalarGridSpec(
            num_scalar_prefetch=1,
            grid=(per,),
            in_specs=[
                pl.BlockSpec((rows, depth), lambda j, order: (0, 0)),
                pl.BlockSpec((depth, tile), lambda j, order: (0, order[at] * per + j)),
            ],
            out_specs=(pl.BlockSpec((cut, tile), lambda j, order: (0, j)),) * pieces,
        ),
        compiler_params=PARAMS,
        cost_estimate=cost(2 * rows * depth * chunk, depth * chunk * 2),
        name=name,
    )(order, attended, out_weight)


def add_kernel(a_ref, b_ref, out_ref):
    out_ref[...] = (a_ref[...].astype(F32) + b_ref[...].astype(F32)).astype(BF16)


def added(name, a, b):
    return pl.pallas_call(
        add_kernel,
        out_shape=jax.ShapeDtypeStruct(a.shape, BF16),
        in_specs=[VMEM, VMEM],
        out_specs=VMEM,
        compiler_params=PARAMS,
        cost_estimate=cost(a.size, a.size * 6),
        name=name,
    )(a, b)


def finish(name, flag, parts, begin, rows_all, into=None):
    rows, columns = parts[0].shape
    blocks = columns // BLOCK
    steps = 2 if blocks % 16 == 0 else 1
    per = blocks // steps
    count = len(parts)
    flags = () if flag is None else (flag,)

    def kernel(*refs):
        if flags:
            chosen = refs[0][0] == 1
            refs = refs[1:]
        out_ref, scale_ref = refs[-2:]
        lane = lax.broadcasted_iota(jnp.int32, (rows, HD), 1)
        scales = jnp.zeros((rows, HD), F32)
        for block in range(per):
            at = slice(block * BLOCK, (block + 1) * BLOCK)
            terms = [ref[:, at].astype(F32) for ref in refs[:count]]
            if flags:
                terms = [jnp.where(chosen, terms[0], terms[1])] + terms[2:]
            total = functools.reduce(jnp.add, terms)
            scale = jnp.max(jnp.abs(total), axis=1, keepdims=True) + 1e-06
            out_ref[:, at] = (total / scale).astype(BF16)
            scales = jnp.where(lane == block, scale, scales)
        scale_ref[...] = scales.T[:per]

    part_spec = pl.BlockSpec((rows, columns // steps), lambda i: (0, i))
    into = () if into is None else into
    return pl.pallas_call(
        kernel,
        out_shape=(
            jax.ShapeDtypeStruct((rows_all, columns), BF16),
            jax.ShapeDtypeStruct((blocks, rows_all), F32),
        ),
        grid=(steps,),
        in_specs=[SMEM] * len(flags) + [part_spec] * count + [pl.BlockSpec(memory_space=pl.ANY)] * len(into),
        out_specs=(
            pl.BlockSpec((rows, columns // steps), lambda i: (begin // rows, i)),
            pl.BlockSpec((per, rows), lambda i: (i, begin // rows)),
        ),
        input_output_aliases={len(flags) + count: 0, len(flags) + count + 1: 1} if into else {},
        compiler_params=PARAMS,
        cost_estimate=cost(rows * columns * 6, rows * columns * 2 * (count + 1)),
        name=name,
    )(*flags, *parts, *into)


def after(value, *others):
    return lax.optimization_barrier((value, *others))[0]


def local(
    queries, new_keys, new_values, key_cache, value_cache, prefix_len, stretch_start, out_weight
):
    rows = queries.shape[0]
    heads_here = queries.shape[1] // HD
    group = HQ // KVH
    tensor_pos = lax.axis_index("tensor")
    lanes = lax.axis_size("tensor")
    n_seq, n_pipe = lax.axis_size("seq"), lax.axis_size("pipe")
    shards = n_seq * n_pipe
    assert heads_here <= group
    me = lax.axis_index("seq") * n_pipe + lax.axis_index("pipe")
    own = pack(prefix_len, key_cache, value_cache, new_keys, new_values, heads_here)

    positions = stretch_start[0] + jnp.arange(shards * rows, dtype=jnp.int32)
    lane = jnp.arange(HD)
    freq = 500000.0 ** (-((lane % (HD // 2)).astype(F32) * 2.0 / HD))
    angle = positions.astype(F32)[:, None] * freq[None, :]
    tables = [jnp.cos(angle), jnp.sin(angle) * jnp.where(lane < HD // 2, -1.0, 1.0)[None, :]]

    columns = D // lanes
    step = jnp.arange(lanes, dtype=jnp.int32)
    if n_seq == 2 and n_pipe == 2 and lanes == 4:
        order = jnp.where(tensor_pos < 2, 3 - step, step)
        flag = ((tensor_pos == 0) | (tensor_pos == lanes - 1)).astype(jnp.int32).reshape(1)
        inward = [(0, 1), (3, 2)]
        middle = [(1, 2), (2, 1)]
        outward = [(1, 0), (2, 3)]
        swap = [(0, 1), (1, 0)]
        far = lax.ppermute(own, "seq", swap)
        near = lax.ppermute(own, "pipe", swap)
        place = jnp.stack([me, order[0], me, me ^ 1, me ^ 2, me ^ 3]).astype(jnp.int32)
        acc, stats, query = attend(
            "attend_near", place, queries, tables, [own, near], (0, 1), None, False
        )
        far = after(far, stats)
        cross = lax.ppermute(far, "pipe", swap)
        acc, stats = attend(
            "attend_far", place, query, tables, [far], (2,), (acc, stats), False
        )
        attended, *first_part = attend(
            "attend_cross",
            place,
            query,
            tables,
            [cross],
            (3,),
            (acc, stats),
            True,
            weight=out_weight,
            chunk=columns,
        )
        part = [first_part]
        for k in range(1, 4):
            part.append(project(f"project_{k}", order, k, attended, out_weight, columns, 2))
        come = [[lax.ppermute(p, "tensor", inward) for p in part[k]] for k in range(3)]
        cut = rows // 2
        done = None
        for i in range(2):
            across = lax.ppermute(added(f"add_0{i}", part[0][i], come[0][i]), "tensor", middle)
            second = lax.ppermute(added(f"add_1{i}", part[1][i], come[1][i]), "tensor", middle)
            back = lax.ppermute(added(f"add_3{i}", part[3][i], across), "tensor", outward)
            parts = [part[3][i], part[2][i], come[2][i], second, back]
            done = finish(f"finish_{i}", flag, parts, i * cut, rows, done)
        return done[0], done[1].T
    every = lax.all_gather(own, ("seq", "pipe"), axis=0)
    place = jnp.concatenate([jnp.stack([me, me]), jnp.arange(shards)]).astype(jnp.int32)
    state = None
    query = queries
    for shard in range(shards):
        state = attend(
            "attend", place, query, tables, [every[shard]], (shard,), state, shard == shards - 1
        )
        if shard == 0:
            query = state[2]
            state = state[:2]
    partial = [
        project(f"project_{k}", step, k, state[0], out_weight, columns, 1)[0] for k in range(lanes)
    ]
    total = lax.psum_scatter(jnp.stack(partial), "tensor", scatter_dimension=0, tiled=True)[0]
    values, scales = finish("finish", None, [total], 0, rows)
    return values, scales.T


def solution(mesh):
    return jax.shard_map(
        local,
        mesh=mesh,
        in_specs=(
            P(("groups", "seq", "pipe"), "tensor"),
            P(("groups", "seq", "pipe"), None),
            P(("groups", "seq", "pipe"), None),
            P(None, ("groups", "seq", "pipe"), None),
            P(None, ("groups", "seq", "pipe"), None),
            P(("groups", "seq", "pipe")),
            P("groups"),
            P("tensor", None),
        ),
        out_specs=(P(("groups", "seq", "pipe"), "tensor"), P(("groups", "seq", "pipe"), "tensor")),
        check_vma=False,
    )
```

time: 121 us -> 134 us (1.11)
  Pallas kernels: 52.3 us -> 62.7 us
  waiting for transfers between devices: 24.6 us -> 31.5 us
  local copies, waits for them, and re-layouts: 7.68 us -> 5.14 us
    pallas_call x9 -> x7, Pallas kernels: 46.4 us -> 56.8 us  [the longest x3 21.6 us: attend(): pl.pallas_call(functools.partial(attend_kernel, first, last, chunk, slots...]
    ppermute x12 -> x9, waiting for transfers between devices: 19.8 us -> 26.3 us  [the longest x6 24.3 us: local(): lax.ppermute(p, 'tensor', inward)]
    unnamed x18 -> x12, local copies, waits for them, and re-layouts: 7.68 us -> 5.02 us
    ppermute x12 -> x9, starting transfers between devices: 24 us -> 23.2 us  [the longest x6 20.1 us: local(): lax.ppermute(p, 'tensor', inward)]
  transfers between devices with their start and end apart: 18 -> 15, of which waited for: 7 -> 7; matrix products, arithmetic and copies ran while one was open for 1% -> 2% of each run, Pallas kernels for 34% -> 24%
where the time goes in v4:
time: 134 us
  Pallas kernels  62.7 us (47%)
  waiting for transfers between devices  31.5 us (24%)
  starting transfers between devices  30.1 us (22%)
  local copies, waits for them, and re-layouts  5.14 us (4%)
  between operations  2.18 us (2%)
  other arithmetic  1.92 us (1%)
    ppermute x6, waiting for transfers between devices, local(): lax.ppermute(p, 'tensor', inward)  24.3 us
    pallas_call x3, Pallas kernels, attend(): pl.pallas_call(functools.partial(attend_kernel, first, last, chunk, slots...  21.6 us
    pallas_call x1, Pallas kernels, pack(): pl.pallas_call(functools.partial(pack_kernel, HQ // KVH, heads_here), out...  21 us
    ppermute x6, starting transfers between devices, local(): lax.ppermute(p, 'tensor', inward)  20.1 us
    pallas_call x3, Pallas kernels, project(): pl.pallas_call(project_kernel, out_shape=(jax.ShapeDtypeStruct((cut, chun...  14.2 us
    ppermute x2, waiting for transfers between devices, local(): lax.ppermute(added(f'add_3{i}', part[3][i], across), 'tensor', outward)  5.24 us
    pallas_call x2, Pallas kernels, finish(): pl.pallas_call(kernel, out_shape=(jax.ShapeDtypeStruct((rows_all, columns...  5.1 us
    unnamed x12, local copies, waits for them, and re-layouts  5.02 us
  transfers between devices with their start and end apart: 15, of which 7 were waited for; matrix products, arithmetic and copies ran while one was open for 2% of the time, Pallas kernels for 24%

profile of v4, /device:TPU:0, one launch (start us, length us, event | category | flops | bytes accessed | tf_op | source)
XLA Modules:
  0.0 133.6 jit_solution(4309415532507801909)
XLA Ops:
  1.3 21.0 %pack.1.refs_0_ = bf16[2,1296,128]{2,1,0:T(8,128)(2,1)} custom-call(s32[1]{0:T(128)S(6)} %copy.14.len_ref, bf16[4,1024,128]{2,1,0:T(8,128)(2,1)} %k_ref.1, bf16[4,1024,128]{2,1,0:T(8,128)(2,1)} %v_ref.1, bf16[256,512]{1,0:T(8,128)(2,1)} %nk_ref.1, bf16[256,512]{1,0:T(8,128)(2,1)} %nv_ref.1), custom_call_target="tpu_custom_call" | custom-call | bytes 1327104 | tf_op jit(solution)/shard_map/pack/pallas_call | solution.py:65
  22.8 2.6 %collective-permute-start.1 = (bf16[2,1296,128]{2,1,0:T(8,128)(2,1)}, bf16[2,1296,128]{2,1,0:T(8,128)(2,1)S(1)}, u32[]{:S(2)}, u32[]{:S(2)}) collective-permute-start(bf16[2,1296,128]{2,1,0:T(8,128)(2,1)} %pack.1.refs_0_), channel_id=1, source_target_pairs={{0,2},{2,0},{1,3},{3,1},{4,6},{6,4},{5,7},{7,5},{8,10},{10,8},{9,1... | collective-permute-start | bytes 1990664 | tf_op jit(solution)/shard_map/ppermute | solution.py:355
  26.2 1.9 %fusion = (f32[1024,128]{1,0:T(8,128)S(1)}, f32[1024,128]{1,0:T(8,128)S(1)}) fusion(f32[128]{0:T(128)S(1)} %get-tuple-element.42, f32[128]{0:T(128)S(1)} %get-tuple-element.43, f32[1024]{0:T(1024)S(1)} %add_convert_fusion), kind=kLoop, calls=%fused_computation.2 | loop fusion | flops 262144 | bytes 1053696 | tf_op jit(solution)/shard_map/mul | solution.py:344
  30.2 8.9 %attend_near.1 = (f32[256,1024]{1,0:T(8,128)S(1)}, f32[256,128]{1,0:T(8,128)S(1)}, bf16[256,1024]{1,0:T(8,128)(2,1)S(1)}) custom-call(s32[6]{0:T(128)S(1)} %stack.20.place_ref, bf16[256,1024]{1,0:T(8,128)(2,1)S(1)} %copy-done.1, f32[1024,128]{1,0:T(8,128)S(1)} %get-tuple-element.41.cos_ref, f32[1024,128]{1,0:T(8,128)S(1)} %get-tuple-element.40.sin_ref, ...), custom_call_target="tpu_custom_call" | custom-call | flops 335544320 | bytes 262144 | tf_op jit(solution)/shard_map/attend_near/pallas_call | solution.py:215
  39.1 2.0 %collective-permute-done.1.refs_0_ = bf16[2,1296,128]{2,1,0:T(8,128)(2,1)S(1)} collective-permute-done((bf16[2,1296,128]{2,1,0:T(8,128)(2,1)}, bf16[2,1296,128]{2,1,0:T(8,128)(2,1)S(1)}, u32[]{:S(2)}, u32[]{:S(2)}) %collective-permute-start.1) | collective-permute-done | bytes 663584 | tf_op jit(solution)/shard_map/ppermute | solution.py:355
  41.1 5.8 %attend_far.1 = (f32[256,1024]{1,0:T(8,128)S(1)}, f32[256,128]{1,0:T(8,128)S(1)}) custom-call(s32[6]{0:T(128)S(1)} %stack.20.place_ref, bf16[256,1024]{1,0:T(8,128)(2,1)S(1)} %get-tuple-element.21.q_ref, f32[1024,128]{1,0:T(8,128)S(1)} %get-tuple-element.41.cos_ref, f32[1024,128]{1,0:T(8,128)S(1)} %get-tuple-element.40.sin_ref, ...), custom_call_target="tpu_custom_call" | custom-call | flops 167772160 | bytes 262144 | tf_op jit(solution)/shard_map/attend_far/pallas_call | solution.py:215
  46.9 7.0 %attend_cross.1 = (bf16[256,1024]{1,0:T(8,128)(2,1)S(1)}, bf16[128,2048]{1,0:T(8,128)(2,1)S(1)}, bf16[128,2048]{1,0:T(8,128)(2,1)S(1)}) custom-call(s32[6]{0:T(128)S(1)} %stack.20.place_ref, bf16[256,1024]{1,0:T(8,128)(2,1)S(1)} %get-tuple-element.21.q_ref, f32[1024,128]{1,0:T(8,128)S(1)} %get-tuple-element.41.cos_ref, ...), custom_call_target="tpu_custom_call" | custom-call | flops 167772160 | bytes 262144 | tf_op jit(solution)/shard_map/attend_cross/pallas_call | solution.py:215
  53.9 3.8 %collective-permute-start.12 = (bf16[128,2048]{1,0:T(8,128)(2,1)S(1)}, bf16[128,2048]{1,0:T(8,128)(2,1)S(1)}, u32[]{:S(2)}, u32[]{:S(2)}) collective-permute-start(bf16[128,2048]{1,0:T(8,128)(2,1)S(1)} %get-tuple-element.35.a_ref), channel_id=1, source_target_pairs={{0,4},{12,8},{1,5},{13,9},{2,6},{14,10},{3,7},{15,11},{16,20},{28,... | collective-permute-start | bytes 1572872 | tf_op jit(solution)/shard_map/ppermute | solution.py:381
  57.6 1.3 collective-permute-start.6
  59.0 4.5 %project_1.1 = (bf16[128,2048]{1,0:T(8,128)(2,1)S(1)}, bf16[128,2048]{1,0:T(8,128)(2,1)S(1)}) custom-call(s32[4]{0:T(128)S(1)} %broadcast_select_fusion.order_ref, bf16[256,1024]{1,0:T(8,128)(2,1)S(1)} %get-tuple-element.27.x_ref, bf16[1024,8192]{1,0:T(8,128)(2,1)} %w_ref.5), custom_call_target="tpu_custom_call" | custom-call | flops 1073741824 | bytes 4194304 | tf_op jit(solution)/shard_map/project_1/pallas_call | solution.py:241
  66.1 3.7 %collective-permute-done.12.b_ref = bf16[128,2048]{1,0:T(8,128)(2,1)S(1)} collective-permute-done((bf16[128,2048]{1,0:T(8,128)(2,1)S(1)}, bf16[128,2048]{1,0:T(8,128)(2,1)S(1)}, u32[]{:S(2)}, u32[]{:S(2)}) %collective-permute-start.12) | collective-permute-done | bytes 524320 | tf_op jit(solution)/shard_map/ppermute | solution.py:381
  70.7 10.4 %collective-permute-done.6.b_ref = bf16[128,2048]{1,0:T(8,128)(2,1)S(1)} collective-permute-done((bf16[128,2048]{1,0:T(8,128)(2,1)S(1)}, bf16[128,2048]{1,0:T(8,128)(2,1)S(1)}, u32[]{:S(2)}, u32[]{:S(2)}) %collective-permute-start.6) | collective-permute-done | bytes 524320 | tf_op jit(solution)/shard_map/ppermute | solution.py:381
  81.9 5.3 %project_2.1 = (bf16[128,2048]{1,0:T(8,128)(2,1)S(1)}, bf16[128,2048]{1,0:T(8,128)(2,1)}) custom-call(s32[4]{0:T(128)S(1)} %broadcast_select_fusion.order_ref, bf16[256,1024]{1,0:T(8,128)(2,1)S(1)} %get-tuple-element.27.x_ref, bf16[1024,8192]{1,0:T(8,128)(2,1)} %w_ref.5), custom_call_target="tpu_custom_call" | custom-call | flops 1073741824 | bytes 4194304 | tf_op jit(solution)/shard_map/project_2/pallas_call | solution.py:241
  87.2 7.2 %collective-permute-start.9 = (bf16[128,2048]{1,0:T(8,128)(2,1)S(1)}, bf16[128,2048]{1,0:T(8,128)(2,1)S(1)}, u32[]{:S(2)}, u32[]{:S(2)}) collective-permute-start(bf16[128,2048]{1,0:T(8,128)(2,1)S(1)} %get-tuple-element.33.refs_2_), channel_id=1, source_target_pairs={{0,4},{12,8},{1,5},{13,9},{2,6},{14,10},{3,7},{15,11},{16,20},{28,... | collective-permute-start | bytes 1572872 | tf_op jit(solution)/shard_map/ppermute | solution.py:381
  94.4 4.5 %project_3.1 = (bf16[128,2048]{1,0:T(8,128)(2,1)S(1)}, bf16[128,2048]{1,0:T(8,128)(2,1)S(1)}) custom-call(s32[4]{0:T(128)S(1)} %broadcast_select_fusion.order_ref, bf16[256,1024]{1,0:T(8,128)(2,1)S(1)} %get-tuple-element.27.x_ref, bf16[1024,8192]{1,0:T(8,128)(2,1)} %w_ref.5), custom_call_target="tpu_custom_call" | custom-call | flops 1073741824 | bytes 4194304 | tf_op jit(solution)/shard_map/project_3/pallas_call | solution.py:241
  99.0 1.5 %collective-permute-start.11 = (bf16[128,2048]{1,0:T(8,128)(2,1)S(1)}, bf16[128,2048]{1,0:T(8,128)(2,1)}, u32[]{:S(2)}, u32[]{:S(2)}) collective-permute-start(bf16[128,2048]{1,0:T(8,128)(2,1)S(1)} %add_10.1), channel_id=1, source_target_pairs={{4,8},{8,4},{5,9},{9,5},{6,10},{10,6},{7,11},{11,7},{20,24},{24,20... | collective-permute-start | bytes 1572872 | tf_op jit(solution)/shard_map/ppermute | solution.py:386
  101.9 1.6 %collective-permute-done.4.b_ref = bf16[128,2048]{1,0:T(8,128)(2,1)S(1)} collective-permute-done((bf16[128,2048]{1,0:T(8,128)(2,1)S(1)}, bf16[128,2048]{1,0:T(8,128)(2,1)S(1)}, u32[]{:S(2)}, u32[]{:S(2)}) %collective-permute-start.4) | collective-permute-done | bytes 524320 | tf_op jit(solution)/shard_map/ppermute | solution.py:381
  103.5 5.2 %collective-permute-start.3 = (bf16[128,2048]{1,0:T(8,128)(2,1)}, bf16[128,2048]{1,0:T(8,128)(2,1)}, u32[]{:S(2)}, u32[]{:S(2)}) collective-permute-start(bf16[128,2048]{1,0:T(8,128)(2,1)} %get-tuple-element.29.refs_2_), channel_id=1, source_target_pairs={{0,4},{12,8},{1,5},{13,9},{2,6},{14,10},{3,7},{15,11},{16,20},{28,... | collective-permute-start | bytes 1572872 | tf_op jit(solution)/shard_map/ppermute | solution.py:381
  108.9 1.5 %collective-permute-start.5 = (bf16[128,2048]{1,0:T(8,128)(2,1)S(1)}, bf16[128,2048]{1,0:T(8,128)(2,1)}, u32[]{:S(2)}, u32[]{:S(2)}) collective-permute-start(bf16[128,2048]{1,0:T(8,128)(2,1)S(1)} %add_11.1), channel_id=1, source_target_pairs={{4,8},{8,4},{5,9},{9,5},{6,10},{10,6},{7,11},{11,7},{20,24},{24,20... | collective-permute-start | bytes 1572872 | tf_op jit(solution)/shard_map/ppermute | solution.py:386
  110.5 4.3 %collective-permute-done.9.refs_3_ = bf16[128,2048]{1,0:T(8,128)(2,1)S(1)} collective-permute-done((bf16[128,2048]{1,0:T(8,128)(2,1)S(1)}, bf16[128,2048]{1,0:T(8,128)(2,1)S(1)}, u32[]{:S(2)}, u32[]{:S(2)}) %collective-permute-start.9) | collective-permute-done | bytes 524320 | tf_op jit(solution)/shard_map/ppermute | solution.py:381
  119.0 2.5 %finish_0.1 = (bf16[256,2048]{1,0:T(8,128)(2,1)}, f32[16,256]{1,0:T(8,128)}) custom-call(s32[1]{0:T(128)} %bitcast.refs_0_, bf16[128,2048]{1,0:T(8,128)(2,1)S(1)} %get-tuple-element.32.a_ref.refs_1_, bf16[128,2048]{1,0:T(8,128)(2,1)S(1)} %copy-done.3, bf16[128,2048]{1,0:T(8,128)(2,1)S(1)} %copy-done.5, bf16[128,2048]{1,0:T(8,128)(2,1)} %collective-permute-done.11.refs_4_, ...), custom_call_target="tpu_custom_call" | custom-call | flops 1572864 | bytes 3145728 | tf_op jit(solution)/shard_map/finish_0/pallas_call | solution.py:303
  121.5 4.2 %collective-permute-done.3.refs_3_ = bf16[128,2048]{1,0:T(8,128)(2,1)} collective-permute-done((bf16[128,2048]{1,0:T(8,128)(2,1)}, bf16[128,2048]{1,0:T(8,128)(2,1)}, u32[]{:S(2)}, u32[]{:S(2)}) %collective-permute-start.3) | collective-permute-done | bytes 524320 | tf_op jit(solution)/shard_map/ppermute | solution.py:381
  125.7 5.2 %collective-permute-done.8.refs_5_ = bf16[128,2048]{1,0:T(8,128)(2,1)} collective-permute-done((bf16[128,2048]{1,0:T(8,128)(2,1)S(1)}, bf16[128,2048]{1,0:T(8,128)(2,1)}, u32[]{:S(2)}, u32[]{:S(2)}) %collective-permute-start.8) | collective-permute-done | bytes 524320 | tf_op jit(solution)/shard_map/ppermute | solution.py:387
  131.0 2.6 %finish_1.1 = (bf16[256,2048]{1,0:T(8,128)(2,1)}, f32[16,256]{1,0:T(8,128)}) custom-call(s32[1]{0:T(128)} %bitcast.refs_0_, bf16[128,2048]{1,0:T(8,128)(2,1)S(1)} %get-tuple-element.28.a_ref.refs_1_, bf16[128,2048]{1,0:T(8,128)(2,1)} %get-tuple-element.29.refs_2_, ...), custom_call_target="tpu_custom_call", output_to_operand_aliasing={{0}: (6, {}), {1}: (7, {})} | custom-call | flops 1572864 | bytes 3145728 | tf_op jit(solution)/shard_map/finish_1/pallas_call | solution.py:303
  (38 shorter events, 13.0 us)
Async XLA Ops:
  22.3 5.8 %collective-permute-start = (bf16[2,1296,128]{2,1,0:T(8,128)(2,1)}, bf16[2,1296,128]{2,1,0:T(8,128)(2,1)S(1)}, u32[]{:S(2)}, u32[]{:S(2)}) collective-permute-start(bf16[2,1296,128]{2,1,0:T(8,128)(2,1)} %pack.1.refs_0_), channel_id=1, source_target_pairs={{0,1},{1,0},{2,3},{3,2},{4,5},{5,4},{6,7},{7,6},{8,9},{9,8},{10,11... | collective-permute-start | bytes 1990664 | tf_op jit(solution)/shard_map/ppermute | solution.py:356
  22.8 18.3 %collective-permute-start.1 = (bf16[2,1296,128]{2,1,0:T(8,128)(2,1)}, bf16[2,1296,128]{2,1,0:T(8,128)(2,1)S(1)}, u32[]{:S(2)}, u32[]{:S(2)}) collective-permute-start(bf16[2,1296,128]{2,1,0:T(8,128)(2,1)} %pack.1.refs_0_), channel_id=1, source_target_pairs={{0,2},{2,0},{1,3},{3,1},{4,6},{6,4},{5,7},{7,5},{8,10},{10,8},{9,1... | collective-permute-start | bytes 1990664 | tf_op jit(solution)/shard_map/ppermute | solution.py:355
  28.1 1.1 copy-start
  29.2 1.0 copy-start.1
  41.1 5.8 %collective-permute-start.2 = (bf16[2,1296,128]{2,1,0:T(8,128)(2,1)S(1)}, bf16[2,1296,128]{2,1,0:T(8,128)(2,1)S(1)}, u32[]{:S(2)}, u32[]{:S(2)}) collective-permute-start(bf16[2,1296,128]{2,1,0:T(8,128)(2,1)S(1)} %collective-permute-done.1.refs_0_), channel_id=1, source_target_pairs={{0,1},{1,0},{2,3},{3,2},{4,5},{5,4},{6,7},{7,6},{8,9},{9,8},{10,11... | collective-permute-start | bytes 1990664 | tf_op jit(solution)/shard_map/ppermute | solution.py:362
  53.9 16.0 %collective-permute-start.12 = (bf16[128,2048]{1,0:T(8,128)(2,1)S(1)}, bf16[128,2048]{1,0:T(8,128)(2,1)S(1)}, u32[]{:S(2)}, u32[]{:S(2)}) collective-permute-start(bf16[128,2048]{1,0:T(8,128)(2,1)S(1)} %get-tuple-element.35.a_ref), channel_id=1, source_target_pairs={{0,4},{12,8},{1,5},{13,9},{2,6},{14,10},{3,7},{15,11},{16,20},{28,... | collective-permute-start | bytes 1572872 | tf_op jit(solution)/shard_map/ppermute | solution.py:381
  57.6 23.4 %collective-permute-start.6 = (bf16[128,2048]{1,0:T(8,128)(2,1)S(1)}, bf16[128,2048]{1,0:T(8,128)(2,1)S(1)}, u32[]{:S(2)}, u32[]{:S(2)}) collective-permute-start(bf16[128,2048]{1,0:T(8,128)(2,1)S(1)} %get-tuple-element.31.a_ref), channel_id=1, source_target_pairs={{0,4},{12,8},{1,5},{13,9},{2,6},{14,10},{3,7},{15,11},{16,20},{28,... | collective-permute-start | bytes 1572872 | tf_op jit(solution)/shard_map/ppermute | solution.py:381
  63.5 35.4 %collective-permute-start.10 = (bf16[128,2048]{1,0:T(8,128)(2,1)S(1)}, bf16[128,2048]{1,0:T(8,128)(2,1)S(1)}, u32[]{:S(2)}, u32[]{:S(2)}) collective-permute-start(bf16[128,2048]{1,0:T(8,128)(2,1)S(1)} %get-tuple-element.34.a_ref), channel_id=1, source_target_pairs={{0,4},{12,8},{1,5},{13,9},{2,6},{14,10},{3,7},{15,11},{16,20},{28,... | collective-permute-start | bytes 1572872 | tf_op jit(solution)/shard_map/ppermute | solution.py:381
  64.8 38.8 %collective-permute-start.4 = (bf16[128,2048]{1,0:T(8,128)(2,1)S(1)}, bf16[128,2048]{1,0:T(8,128)(2,1)S(1)}, u32[]{:S(2)}, u32[]{:S(2)}) collective-permute-start(bf16[128,2048]{1,0:T(8,128)(2,1)S(1)} %get-tuple-element.30.a_ref), channel_id=1, source_target_pairs={{0,4},{12,8},{1,5},{13,9},{2,6},{14,10},{3,7},{15,11},{16,20},{28,... | collective-permute-start | bytes 1572872 | tf_op jit(solution)/shard_map/ppermute | solution.py:381
  70.0 30.5 %collective-permute-start.13 = (bf16[128,2048]{1,0:T(8,128)(2,1)S(1)}, bf16[128,2048]{1,0:T(8,128)(2,1)S(1)}, u32[]{:S(2)}, u32[]{:S(2)}) collective-permute-start(bf16[128,2048]{1,0:T(8,128)(2,1)S(1)} %add_00.1), channel_id=1, source_target_pairs={{4,8},{8,4},{5,9},{9,5},{6,10},{10,6},{7,11},{11,7},{20,24},{24,20... | collective-permute-start | bytes 1572872 | tf_op jit(solution)/shard_map/ppermute | solution.py:385
  81.2 27.7 %collective-permute-start.7 = (bf16[128,2048]{1,0:T(8,128)(2,1)S(1)}, bf16[128,2048]{1,0:T(8,128)(2,1)S(1)}, u32[]{:S(2)}, u32[]{:S(2)}) collective-permute-start(bf16[128,2048]{1,0:T(8,128)(2,1)S(1)} %add_01.1), channel_id=1, source_target_pairs={{4,8},{8,4},{5,9},{9,5},{6,10},{10,6},{7,11},{11,7},{20,24},{24,20... | collective-permute-start | bytes 1572872 | tf_op jit(solution)/shard_map/ppermute | solution.py:385
  87.2 23.3 %copy-start.2 = (bf16[128,2048]{1,0:T(8,128)(2,1)}, bf16[128,2048]{1,0:T(8,128)(2,1)S(1)}, u32[]{:S(2)}) copy-start(bf16[128,2048]{1,0:T(8,128)(2,1)S(1)} %get-tuple-element.33.refs_2_) | copy-start | bytes 1572868
  87.2 27.6 %collective-permute-start.9 = (bf16[128,2048]{1,0:T(8,128)(2,1)S(1)}, bf16[128,2048]{1,0:T(8,128)(2,1)S(1)}, u32[]{:S(2)}, u32[]{:S(2)}) collective-permute-start(bf16[128,2048]{1,0:T(8,128)(2,1)S(1)} %get-tuple-element.33.refs_2_), channel_id=1, source_target_pairs={{0,4},{12,8},{1,5},{13,9},{2,6},{14,10},{3,7},{15,11},{16,20},{28,... | collective-permute-start | bytes 1572872 | tf_op jit(solution)/shard_map/ppermute | solution.py:381
  99.0 17.9 %collective-permute-start.11 = (bf16[128,2048]{1,0:T(8,128)(2,1)S(1)}, bf16[128,2048]{1,0:T(8,128)(2,1)}, u32[]{:S(2)}, u32[]{:S(2)}) collective-permute-start(bf16[128,2048]{1,0:T(8,128)(2,1)S(1)} %add_10.1), channel_id=1, source_target_pairs={{4,8},{8,4},{5,9},{9,5},{6,10},{10,6},{7,11},{11,7},{20,24},{24,20... | collective-permute-start | bytes 1572872 | tf_op jit(solution)/shard_map/ppermute | solution.py:386
  100.6 16.3 %collective-permute-start.14 = (bf16[128,2048]{1,0:T(8,128)(2,1)S(1)}, bf16[128,2048]{1,0:T(8,128)(2,1)}, u32[]{:S(2)}, u32[]{:S(2)}) collective-permute-start(bf16[128,2048]{1,0:T(8,128)(2,1)S(1)} %add_30.1), channel_id=1, source_target_pairs={{4,0},{8,12},{5,1},{9,13},{6,2},{10,14},{7,3},{11,15},{20,16},{24,... | collective-permute-start | bytes 1572872 | tf_op jit(solution)/shard_map/ppermute | solution.py:387
  103.5 22.2 %collective-permute-start.3 = (bf16[128,2048]{1,0:T(8,128)(2,1)}, bf16[128,2048]{1,0:T(8,128)(2,1)}, u32[]{:S(2)}, u32[]{:S(2)}) collective-permute-start(bf16[128,2048]{1,0:T(8,128)(2,1)} %get-tuple-element.29.refs_2_), channel_id=1, source_target_pairs={{0,4},{12,8},{1,5},{13,9},{2,6},{14,10},{3,7},{15,11},{16,20},{28,... | collective-permute-start | bytes 1572872 | tf_op jit(solution)/shard_map/ppermute | solution.py:381
  108.9 16.9 %collective-permute-start.5 = (bf16[128,2048]{1,0:T(8,128)(2,1)S(1)}, bf16[128,2048]{1,0:T(8,128)(2,1)}, u32[]{:S(2)}, u32[]{:S(2)}) collective-permute-start(bf16[128,2048]{1,0:T(8,128)(2,1)S(1)} %add_11.1), channel_id=1, source_target_pairs={{4,8},{8,4},{5,9},{9,5},{6,10},{10,6},{7,11},{11,7},{20,24},{24,20... | collective-permute-start | bytes 1572872 | tf_op jit(solution)/shard_map/ppermute | solution.py:386
  114.8 0.8 copy-start.4
  115.6 15.4 %collective-permute-start.8 = (bf16[128,2048]{1,0:T(8,128)(2,1)S(1)}, bf16[128,2048]{1,0:T(8,128)(2,1)}, u32[]{:S(2)}, u32[]{:S(2)}) collective-permute-start(bf16[128,2048]{1,0:T(8,128)(2,1)S(1)} %add_31.1), channel_id=1, source_target_pairs={{4,0},{8,12},{5,1},{9,13},{6,2},{10,14},{7,3},{11,15},{20,16},{24,... | collective-permute-start | bytes 1572872 | tf_op jit(solution)/shard_map/ppermute | solution.py:387
  116.9 1.0 copy-start.3
  118.0 1.0 copy-start.5

commit v5 on v4

--- a/solution.py
+++ b/solution.py
@@ -15,6 +15,7 @@
 BLOCK = 128
 LEN_ROWS = 16
 LOW = 32
+W_COPIES = 8
 NEG = -1e30
 VMEM_LIMIT = 48 * 1024 * 1024
 VMEM_MOST = 60 * 1024 * 1024
@@ -40,7 +41,7 @@
     return x * cosine + pltpu.roll(x, HD // 2, 1) * sine
 
 
-def pack_kernel(per_kv_head, heads_here, len_ref, k_ref, v_ref, nk_ref, nv_ref, out_ref, live_rows, sems):
+def pack_kernel(per_kv_head, heads_here, len_ref, k_ref, v_ref, nk_ref, nv_ref, out_ref, sems):
     slots, rows = k_ref.shape[1], nk_ref.shape[0]
     head = lax.axis_index("tensor") * heads_here // per_kv_head
     columns = pl.ds(pl.multiple_of(head * HD, HD), HD)
@@ -48,14 +49,13 @@
     for i, (cache, new) in enumerate(((k_ref, nk_ref), (v_ref, nv_ref))):
         copies.append((cache.at[head], out_ref.at[i, pl.ds(0, slots)]))
         copies.append((new.at[:, columns], out_ref.at[i, pl.ds(slots, rows)]))
-    copies.append((live_rows, out_ref.at[:, pl.ds(slots + rows, LEN_ROWS)]))
     copies = [pltpu.make_async_copy(*pair, sems.at[i]) for i, pair in enumerate(copies)]
-    for copy in copies[:-1]:
+    for copy in copies:
         copy.start()
     live = len_ref[0]
-    live_rows[0] = jnp.full((LEN_ROWS, HD), (live // LOW).astype(F32), F32).astype(BF16)
-    live_rows[1] = jnp.full((LEN_ROWS, HD), (live % LOW).astype(F32), F32).astype(BF16)
-    copies[-1].start()
+    for i, part in enumerate((live // LOW, live % LOW)):
+        part = jnp.full((LEN_ROWS, HD), part.astype(F32), F32).astype(BF16)
+        out_ref[i, slots + rows :] = part
     for copy in copies:
         copy.wait()
 
@@ -66,8 +66,8 @@
         functools.partial(pack_kernel, HQ // KVH, heads_here),
         out_shape=jax.ShapeDtypeStruct((2, size, HD), BF16),
         in_specs=[SMEM, HBM, HBM, HBM, HBM],
-        out_specs=HBM,
-        scratch_shapes=[pltpu.VMEM((2, LEN_ROWS, HD), BF16), pltpu.SemaphoreType.DMA((5,))],
+        out_specs=VMEM,
+        scratch_shapes=[pltpu.SemaphoreType.DMA((4,))],
         compiler_params=PARAMS_MOST,
         cost_estimate=cost(0, 4 * size * HD * 2),
         name="pack",
@@ -84,12 +84,17 @@
     return functools.reduce(jnp.add, parts)
 
 
-def attend_kernel(first, last, chunk, slots, shards_at, place_ref, q_ref, cos_ref, sin_ref, *refs):
+def attend_kernel(
+    first, last, chunk, slots, shards_at, span, held, place_ref, q_ref, cos_ref, sin_ref, *refs
+):
     n = len(shards_at)
     kv_refs = refs[:n]
     refs = refs[n:]
     rows = q_ref.shape[0]
     heads = q_ref.shape[1] // HD
+    begin_row, n_rows = span
+    at_rows = slice(begin_row, begin_row + n_rows)
+    at_held = slice(held, held + n_rows)
     me = place_ref[0]
     if first:
         acc_out, stats_out, query_out, raw, sem = refs
@@ -99,16 +104,20 @@
         acc_in, stats_in = refs[:2]
         refs = refs[2:]
         if chunk:
-            w_ref, attended_out, part_a, part_b, w_held, sem = refs
+            w_ref, attended_out, part_out, w_held, sems = refs
             columns = pl.ds(pl.multiple_of(place_ref[1] * chunk, chunk), chunk)
-            copy = pltpu.make_async_copy(w_ref.at[:, columns], w_held, sem)
-            copy.start()
+            depth = w_ref.shape[0] // W_COPIES
+            copies = []
+            for i in range(W_COPIES):
+                at = pl.ds(i * depth, depth)
+                copies.append(pltpu.make_async_copy(w_ref.at[at, columns], w_held.at[at], sems.at[i]))
+                copies[i].start()
         elif last:
             (attended_out,) = refs
         else:
             acc_out, stats_out = refs
-    row = lax.broadcasted_iota(jnp.int32, (rows, rows), 0)
-    column = lax.broadcasted_iota(jnp.int32, (rows, rows), 1)
+    row = lax.broadcasted_iota(jnp.int32, (n_rows, rows), 0) + begin_row
+    column = lax.broadcasted_iota(jnp.int32, (n_rows, rows), 1)
     slot = lax.broadcasted_iota(jnp.int32, (1, HD), 1).astype(F32)
     segments = []
     for ref, at in zip(kv_refs, shards_at):
@@ -133,15 +142,15 @@
         q_ref = query_out
 
     def score(head):
-        query = q_ref[:, head * HD : (head + 1) * HD]
+        query = q_ref[at_rows, head * HD : (head + 1) * HD]
         scores = []
         for ref, keys, begin, count, mask in segments:
             keys = ref[0, begin : begin + count, :] if keys is None else keys
             scores.append(lax.dot_general(query, keys, NT, preferred_element_type=F32) + mask)
         return scores
 
-    lane = lax.broadcasted_iota(jnp.int32, (rows, HD), 1)
-    stats = jnp.zeros((rows, HD), F32)
+    lane = lax.broadcasted_iota(jnp.int32, (n_rows, HD), 1)
+    stats = jnp.zeros((n_rows, HD), F32)
     following = score(0)
     for head in range(heads):
         scores = following
@@ -151,7 +160,7 @@
         peak = functools.reduce(jnp.maximum, [lane_max(x) for x in scores])
         peak = jnp.max(peak, axis=1, keepdims=True)
         if not first:
-            before = stats_in[:, head : head + 1]
+            before = stats_in[at_held, head : head + 1]
             peak = jnp.maximum(before, peak)
             shrink = jnp.exp2(before - peak)
         total = None
@@ -165,8 +174,8 @@
             out = update if out is None else out + update
         total = jnp.sum(total, axis=1, keepdims=True)
         if not first:
-            total = total + stats_in[:, HD // 2 + head : HD // 2 + head + 1] * shrink
-            out = out + acc_in[:, at] * shrink
+            total = total + stats_in[at_held, HD // 2 + head : HD // 2 + head + 1] * shrink
+            out = out + acc_in[at_held, at] * shrink
         if last:
             attended_out[:, at] = (out / total).astype(BF16)
         else:
@@ -176,18 +185,20 @@
     if not last:
         stats_out[...] = stats
     if chunk:
-        copy.wait()
+        for copy in copies:
+            copy.wait()
         tile = 512
-        cut = rows // 2
         for i in range(0, chunk, tile):
             part = jnp.dot(attended_out[...], w_held[:, i : i + tile], preferred_element_type=F32)
-            part_a[:, i : i + tile] = part[:cut].astype(BF16)
-            part_b[:, i : i + tile] = part[cut:].astype(BF16)
-
-
-def attend(name, place, query, tables, arrays, shards_at, state, last, weight=None, chunk=0):
+            part_out[:, i : i + tile] = part.astype(BF16)
+
+
+def attend(
+    name, place, query, tables, arrays, shards_at, state, last, weight=None, chunk=0, span=None, held=0
+):
     rows, width = query.shape
     slots = arrays[0].shape[1] - rows - LEN_ROWS
+    span = (0, rows) if span is None else span
     first = state is None
     operands = [place, query, *tables, *arrays]
     in_specs = [SMEM, HBM if first else VMEM] + [VMEM] * (2 + len(arrays))
@@ -198,22 +209,22 @@
         operands += state
         in_specs += [VMEM] * 2
     if last:
-        out_shape = [jax.ShapeDtypeStruct((rows, width), BF16)]
+        out_shape = [jax.ShapeDtypeStruct((span[1], width), BF16)]
         if chunk:
             operands.append(weight)
             in_specs.append(HBM)
-            out_shape += [jax.ShapeDtypeStruct((rows // 2, chunk), BF16)] * 2
-            scratch = [pltpu.VMEM((width, chunk), BF16), pltpu.SemaphoreType.DMA]
+            out_shape.append(jax.ShapeDtypeStruct((span[1], chunk), BF16))
+            scratch = [pltpu.VMEM((width, chunk), BF16), pltpu.SemaphoreType.DMA((W_COPIES,))]
     else:
         out_shape = [
-            jax.ShapeDtypeStruct((rows, width), F32),
-            jax.ShapeDtypeStruct((rows, HD), F32),
+            jax.ShapeDtypeStruct((span[1], width), F32),
+            jax.ShapeDtypeStruct((span[1], HD), F32),
         ]
         if first:
             out_shape.append(jax.ShapeDtypeStruct((rows, width), BF16))
     keys = len(arrays) * (slots + rows)
     return pl.pallas_call(
-        functools.partial(attend_kernel, first, last, chunk, slots, shards_at),
+        functools.partial(attend_kernel, first, last, chunk, slots, shards_at, span, held),
         out_shape=out_shape,
         in_specs=in_specs,
         out_specs=[VMEM] * len(out_shape),
@@ -226,34 +237,33 @@
     )(*operands)
 
 
-def project_kernel(order_ref, x_ref, w_ref, *out_refs):
-    out = jnp.dot(x_ref[...], w_ref[...], preferred_element_type=F32)
-    cut = out_refs[0].shape[0]
-    for i, ref in enumerate(out_refs):
+def project_kernel(pieces, order_ref, *refs):
+    x = jnp.concatenate([ref[...] for ref in refs[:pieces]], axis=0)
+    out = jnp.dot(x, refs[pieces][...], preferred_element_type=F32)
+    cut = refs[0].shape[0]
+    for i, ref in enumerate(refs[pieces + 1 :]):
         ref[...] = out[i * cut : (i + 1) * cut].astype(BF16)
 
 
-def project(name, order, at, attended, out_weight, chunk, pieces, tile=512):
-    rows, depth = attended.shape
-    cut = rows // pieces
+def project(name, order, at, attended, out_weight, chunk, tile=512):
+    cut, depth = attended[0].shape
+    pieces = len(attended)
     tile = min(tile, chunk)
     per = chunk // tile
     return pl.pallas_call(
-        project_kernel,
+        functools.partial(project_kernel, pieces),
         out_shape=(jax.ShapeDtypeStruct((cut, chunk), BF16),) * pieces,
         grid_spec=pltpu.PrefetchScalarGridSpec(
             num_scalar_prefetch=1,
             grid=(per,),
-            in_specs=[
-                pl.BlockSpec((rows, depth), lambda j, order: (0, 0)),
-                pl.BlockSpec((depth, tile), lambda j, order: (0, order[at] * per + j)),
-            ],
+            in_specs=[pl.BlockSpec((cut, depth), lambda j, order: (0, 0))] * pieces
+            + [pl.BlockSpec((depth, tile), lambda j, order: (0, order[at] * per + j))],
             out_specs=(pl.BlockSpec((cut, tile), lambda j, order: (0, j)),) * pieces,
         ),
         compiler_params=PARAMS,
-        cost_estimate=cost(2 * rows * depth * chunk, depth * chunk * 2),
+        cost_estimate=cost(2 * pieces * cut * depth * chunk, depth * chunk * 2),
         name=name,
-    )(order, attended, out_weight)
+    )(order, *attended, out_weight)
 
 
 def add_kernel(a_ref, b_ref, out_ref):
@@ -360,26 +370,42 @@
         )
         far = after(far, stats)
         cross = lax.ppermute(far, "pipe", swap)
-        acc, stats = attend(
-            "attend_far", place, query, tables, [far], (2,), (acc, stats), False
+        cut = rows // 2
+        state = attend(
+            "attend_far", place, query, tables, [far], (2,), (acc, stats), False, span=(0, cut)
         )
-        attended, *first_part = attend(
+        attended, first_part = [None, None], [None, None]
+        attended[0], first_part[0] = attend(
             "attend_cross",
             place,
             query,
             tables,
             [cross],
             (3,),
-            (acc, stats),
+            tuple(state),
             True,
             weight=out_weight,
             chunk=columns,
+            span=(0, cut),
+        )
+        attended[1], first_part[1] = attend(
+            "attend_rest",
+            place,
+            query,
+            tables,
+            [far, cross],
+            (2, 3),
+            (acc, after(stats, first_part[0])),
+            True,
+            weight=out_weight,
+            chunk=columns,
+            span=(cut, cut),
+            held=cut,
         )
         part = [first_part]
         for k in range(1, 4):
-            part.append(project(f"project_{k}", order, k, attended, out_weight, columns, 2))
+            part.append(project(f"project_{k}", order, k, attended, out_weight, columns))
         come = [[lax.ppermute(p, "tensor", inward) for p in part[k]] for k in range(3)]
-        cut = rows // 2
         done = None
         for i in range(2):
             across = lax.ppermute(added(f"add_0{i}", part[0][i], come[0][i]), "tensor", middle)
@@ -400,7 +426,7 @@
             query = state[2]
             state = state[:2]
     partial = [
-        project(f"project_{k}", step, k, state[0], out_weight, columns, 1)[0] for k in range(lanes)
+        project(f"project_{k}", step, k, state[:1], out_weight, columns)[0] for k in range(lanes)
     ]
     total = lax.psum_scatter(jnp.stack(partial), "tensor", scatter_dimension=0, tiled=True)[0]
     values, scales = finish("finish", None, [total], 0, rows)

time: 134 us -> 113 us (0.84)
  Pallas kernels: 62.7 us -> 49.1 us
  waiting for transfers between devices: 31.5 us -> 23.8 us
    pallas_call x1, Pallas kernels: 21 us -> 1.95 us  [pack(): pl.pallas_call(functools.partial(pack_kernel, HQ // KVH, heads_here), out...]
    ppermute x6, waiting for transfers between devices: 24.3 us -> 16.6 us  [local(): lax.ppermute(p, 'tensor', inward)]
    pallas_call x3 -> x4, Pallas kernels: 21.6 us -> 27.1 us  [attend(): pl.pallas_call(functools.partial(attend_kernel, first, last, chunk, slots...]
  transfers between devices with their start and end apart: 15 -> 15, of which waited for: 7 -> 6; matrix products, arithmetic and copies ran while one was open for 2% -> 2% of each run, Pallas kernels for 24% -> 33%
where the time goes in v5:
time: 113 us; the launch traced here: 112 us
  Pallas kernels  49.1 us (43%)
  starting transfers between devices  30.2 us (27%)
  waiting for transfers between devices  23.8 us (21%)
  local copies, waits for them, and re-layouts  5.14 us (5%)
  between operations  2.2 us (2%)
  other arithmetic  1.92 us (2%)
    pallas_call x4, Pallas kernels, attend(): pl.pallas_call(functools.partial(attend_kernel, first, last, chunk, slots...  27.1 us
    ppermute x6, starting transfers between devices, local(): lax.ppermute(p, 'tensor', inward)  20.2 us
    ppermute x6, waiting for transfers between devices, local(): lax.ppermute(p, 'tensor', inward)  16.6 us
    pallas_call x3, Pallas kernels, project(): pl.pallas_call(functools.partial(project_kernel, pieces), out_shape=(jax....  14.2 us
    ppermute x2, waiting for transfers between devices, local(): lax.ppermute(added(f'add_3{i}', part[3][i], across), 'tensor', outward)  5.22 us
    pallas_call x2, Pallas kernels, finish(): pl.pallas_call(kernel, out_shape=(jax.ShapeDtypeStruct((rows_all, columns...  5.1 us
    unnamed x12, local copies, waits for them, and re-layouts  5.02 us
    ppermute x2, starting transfers between devices, local(): lax.ppermute(added(f'add_1{i}', part[1][i], come[1][i]), 'tensor', middle)  2.96 us
  transfers between devices with their start and end apart: 15, of which 6 were waited for; matrix products, arithmetic and copies ran while one was open for 2% of the time, Pallas kernels for 33%

profile of v5, /device:TPU:0, one launch (start us, length us, event | category | flops | bytes accessed | tf_op | source)
XLA Modules:
  0.0 112.4 jit_solution(10580806509295949937)
XLA Ops:
  1.3 2.0 %pack.1.refs_0_ = bf16[2,1296,128]{2,1,0:T(8,128)(2,1)} custom-call(s32[1]{0:T(128)S(6)} %copy.14.len_ref, bf16[4,1024,128]{2,1,0:T(8,128)(2,1)} %k_ref.1, bf16[4,1024,128]{2,1,0:T(8,128)(2,1)} %v_ref.1, bf16[256,512]{1,0:T(8,128)(2,1)} %nk_ref.1, bf16[256,512]{1,0:T(8,128)(2,1)} %nv_ref.1), custom_call_target="tpu_custom_call" | custom-call | bytes 1327104 | tf_op jit(solution)/shard_map/pack/pallas_call | solution.py:65
  3.8 2.6 %collective-permute-start.1 = (bf16[2,1296,128]{2,1,0:T(8,128)(2,1)}, bf16[2,1296,128]{2,1,0:T(8,128)(2,1)S(1)}, u32[]{:S(2)}, u32[]{:S(2)}) collective-permute-start(bf16[2,1296,128]{2,1,0:T(8,128)(2,1)} %pack.1.refs_0_), channel_id=1, source_target_pairs={{0,2},{2,0},{1,3},{3,1},{4,6},{6,4},{5,7},{7,5},{8,10},{10,8},{9,1... | collective-permute-start | bytes 1990664 | tf_op jit(solution)/shard_map/ppermute | solution.py:365
  7.1 1.9 %fusion = (f32[1024,128]{1,0:T(8,128)S(1)}, f32[1024,128]{1,0:T(8,128)S(1)}) fusion(f32[128]{0:T(128)S(1)} %get-tuple-element.46, f32[128]{0:T(128)S(1)} %get-tuple-element.47, f32[1024]{0:T(1024)S(1)} %add_convert_fusion), kind=kLoop, calls=%fused_computation.2 | loop fusion | flops 262144 | bytes 1053696 | tf_op jit(solution)/shard_map/mul | solution.py:354
  11.2 8.8 %attend_near.1 = (f32[256,1024]{1,0:T(8,128)S(1)}, f32[256,128]{1,0:T(8,128)S(1)}, bf16[256,1024]{1,0:T(8,128)(2,1)S(1)}) custom-call(s32[6]{0:T(128)S(1)} %stack.20.place_ref, bf16[256,1024]{1,0:T(8,128)(2,1)S(1)} %copy-done.1, f32[1024,128]{1,0:T(8,128)S(1)} %get-tuple-element.45.cos_ref, f32[1024,128]{1,0:T(8,128)S(1)} %get-tuple-element.44.sin_ref, ...), custom_call_target="tpu_custom_call" | custom-call | flops 335544320 | bytes 262144 | tf_op jit(solution)/shard_map/attend_near/pallas_call | solution.py:226
  20.0 2.0 %collective-permute-done.1.refs_0_ = bf16[2,1296,128]{2,1,0:T(8,128)(2,1)S(1)} collective-permute-done((bf16[2,1296,128]{2,1,0:T(8,128)(2,1)}, bf16[2,1296,128]{2,1,0:T(8,128)(2,1)S(1)}, u32[]{:S(2)}, u32[]{:S(2)}) %collective-permute-start.1) | collective-permute-done | bytes 663584 | tf_op jit(solution)/shard_map/ppermute | solution.py:365
  22.0 3.7 %attend_far.1 = (f32[128,1024]{1,0:T(8,128)S(1)}, f32[128,128]{1,0:T(8,128)S(1)}) custom-call(s32[6]{0:T(128)S(1)} %stack.20.place_ref, bf16[256,1024]{1,0:T(8,128)(2,1)S(1)} %get-tuple-element.23.q_ref, f32[1024,128]{1,0:T(8,128)S(1)} %get-tuple-element.45.cos_ref, f32[1024,128]{1,0:T(8,128)S(1)} %get-tuple-element.44.sin_ref, ...), custom_call_target="tpu_custom_call" | custom-call | flops 167772160 | bytes 262144 | tf_op jit(solution)/shard_map/attend_far/pallas_call | solution.py:226
  25.7 6.9 %attend_cross.1 = (bf16[128,1024]{1,0:T(8,128)(2,1)S(1)}, bf16[128,2048]{1,0:T(8,128)(2,1)S(1)}) custom-call(s32[6]{0:T(128)S(1)} %stack.20.place_ref, bf16[256,1024]{1,0:T(8,128)(2,1)S(1)} %get-tuple-element.23.q_ref, f32[1024,128]{1,0:T(8,128)S(1)} %get-tuple-element.45.cos_ref, f32[1024,128]{1,0:T(8,128)S(1)} %get-tuple-element.44.sin_ref, ...), custom_call_target="tpu_custom_call" | custom-call | flops 167772160 | bytes 262144 | tf_op jit(solution)/shard_map/attend_cross/pallas_call | solution.py:226
  32.6 3.8 %collective-permute-start.12 = (bf16[128,2048]{1,0:T(8,128)(2,1)S(1)}, bf16[128,2048]{1,0:T(8,128)(2,1)S(1)}, u32[]{:S(2)}, u32[]{:S(2)}) collective-permute-start(bf16[128,2048]{1,0:T(8,128)(2,1)S(1)} %get-tuple-element.30.a_ref), channel_id=1, source_target_pairs={{0,4},{12,8},{1,5},{13,9},{2,6},{14,10},{3,7},{15,11},{16,20},{28,... | collective-permute-start | bytes 1572872 | tf_op jit(solution)/shard_map/ppermute | solution.py:408
  36.5 7.7 %attend_rest.1 = (bf16[128,1024]{1,0:T(8,128)(2,1)S(1)}, bf16[128,2048]{1,0:T(8,128)(2,1)S(1)}) custom-call(s32[6]{0:T(128)S(1)} %stack.20.place_ref, bf16[256,1024]{1,0:T(8,128)(2,1)S(1)} %get-tuple-element.23.q_ref, f32[1024,128]{1,0:T(8,128)S(1)} %get-tuple-element.45.cos_ref, f32[1024,128]{1,0:T(8,128)S(1)} %get-tuple-element.44.sin_ref, ...), custom_call_target="tpu_custom_call" | custom-call | flops 335544320 | bytes 262144 | tf_op jit(solution)/shard_map/attend_rest/pallas_call | solution.py:226
  45.4 4.5 %project_1.1 = (bf16[128,2048]{1,0:T(8,128)(2,1)S(1)}, bf16[128,2048]{1,0:T(8,128)(2,1)S(1)}) custom-call(s32[4]{0:T(128)S(1)} %broadcast_select_fusion.order_ref, bf16[128,1024]{1,0:T(8,128)(2,1)S(1)} %get-tuple-element.29.refs_0_, bf16[128,1024]{1,0:T(8,128)(2,1)S(1)} %get-tuple-element.32.refs_1_, bf16[1024,8192]{1,0:T(8,128)(2,1)} %refs_2_.5), custom_call_target="tpu_custom_call" | custom-call | flops 1073741824 | bytes 4194304 | tf_op jit(solution)/shard_map/project_1/pallas_call | solution.py:253
  49.9 1.3 %collective-permute-start.10 = (bf16[128,2048]{1,0:T(8,128)(2,1)S(1)}, bf16[128,2048]{1,0:T(8,128)(2,1)S(1)}, u32[]{:S(2)}, u32[]{:S(2)}) collective-permute-start(bf16[128,2048]{1,0:T(8,128)(2,1)S(1)} %get-tuple-element.39.a_ref), channel_id=1, source_target_pairs={{0,4},{12,8},{1,5},{13,9},{2,6},{14,10},{3,7},{15,11},{16,20},{28,... | collective-permute-start | bytes 1572872 | tf_op jit(solution)/shard_map/ppermute | solution.py:408
  53.4 6.5 %collective-permute-done.6.b_ref = bf16[128,2048]{1,0:T(8,128)(2,1)S(1)} collective-permute-done((bf16[128,2048]{1,0:T(8,128)(2,1)S(1)}, bf16[128,2048]{1,0:T(8,128)(2,1)S(1)}, u32[]{:S(2)}, u32[]{:S(2)}) %collective-permute-start.6) | collective-permute-done | bytes 524320 | tf_op jit(solution)/shard_map/ppermute | solution.py:408
  60.7 5.3 %project_2.1 = (bf16[128,2048]{1,0:T(8,128)(2,1)S(1)}, bf16[128,2048]{1,0:T(8,128)(2,1)}) custom-call(s32[4]{0:T(128)S(1)} %broadcast_select_fusion.order_ref, bf16[128,1024]{1,0:T(8,128)(2,1)S(1)} %get-tuple-element.29.refs_0_, bf16[128,1024]{1,0:T(8,128)(2,1)S(1)} %get-tuple-element.32.refs_1_, bf16[1024,8192]{1,0:T(8,128)(2,1)} %refs_2_.5), custom_call_target="tpu_custom_call" | custom-call | flops 1073741824 | bytes 4194304 | tf_op jit(solution)/shard_map/project_2/pallas_call | solution.py:253
  66.0 7.2 %collective-permute-start.9 = (bf16[128,2048]{1,0:T(8,128)(2,1)S(1)}, bf16[128,2048]{1,0:T(8,128)(2,1)S(1)}, u32[]{:S(2)}, u32[]{:S(2)}) collective-permute-start(bf16[128,2048]{1,0:T(8,128)(2,1)S(1)} %get-tuple-element.38.refs_2_), channel_id=1, source_target_pairs={{0,4},{12,8},{1,5},{13,9},{2,6},{14,10},{3,7},{15,11},{16,20},{28,... | collective-permute-start | bytes 1572872 | tf_op jit(solution)/shard_map/ppermute | solution.py:408
  73.2 4.5 %project_3.1 = (bf16[128,2048]{1,0:T(8,128)(2,1)S(1)}, bf16[128,2048]{1,0:T(8,128)(2,1)S(1)}) custom-call(s32[4]{0:T(128)S(1)} %broadcast_select_fusion.order_ref, bf16[128,1024]{1,0:T(8,128)(2,1)S(1)} %get-tuple-element.29.refs_0_, bf16[128,1024]{1,0:T(8,128)(2,1)S(1)} %get-tuple-element.32.refs_1_, bf16[1024,8192]{1,0:T(8,128)(2,1)} %refs_2_.5), custom_call_target="tpu_custom_call" | custom-call | flops 1073741824 | bytes 4194304 | tf_op jit(solution)/shard_map/project_3/pallas_call | solution.py:253
  77.8 1.5 %collective-permute-start.11 = (bf16[128,2048]{1,0:T(8,128)(2,1)S(1)}, bf16[128,2048]{1,0:T(8,128)(2,1)}, u32[]{:S(2)}, u32[]{:S(2)}) collective-permute-start(bf16[128,2048]{1,0:T(8,128)(2,1)S(1)} %add_10.1), channel_id=1, source_target_pairs={{4,8},{8,4},{5,9},{9,5},{6,10},{10,6},{7,11},{11,7},{20,24},{24,20... | collective-permute-start | bytes 1572872 | tf_op jit(solution)/shard_map/ppermute | solution.py:412
  80.7 1.6 %collective-permute-done.4.b_ref = bf16[128,2048]{1,0:T(8,128)(2,1)S(1)} collective-permute-done((bf16[128,2048]{1,0:T(8,128)(2,1)S(1)}, bf16[128,2048]{1,0:T(8,128)(2,1)S(1)}, u32[]{:S(2)}, u32[]{:S(2)}) %collective-permute-start.4) | collective-permute-done | bytes 524320 | tf_op jit(solution)/shard_map/ppermute | solution.py:408
  82.3 5.2 %collective-permute-start.3 = (bf16[128,2048]{1,0:T(8,128)(2,1)}, bf16[128,2048]{1,0:T(8,128)(2,1)}, u32[]{:S(2)}, u32[]{:S(2)}) collective-permute-start(bf16[128,2048]{1,0:T(8,128)(2,1)} %get-tuple-element.34.refs_2_), channel_id=1, source_target_pairs={{0,4},{12,8},{1,5},{13,9},{2,6},{14,10},{3,7},{15,11},{16,20},{28,... | collective-permute-start | bytes 1572872 | tf_op jit(solution)/shard_map/ppermute | solution.py:408
  87.7 1.5 %collective-permute-start.5 = (bf16[128,2048]{1,0:T(8,128)(2,1)S(1)}, bf16[128,2048]{1,0:T(8,128)(2,1)}, u32[]{:S(2)}, u32[]{:S(2)}) collective-permute-start(bf16[128,2048]{1,0:T(8,128)(2,1)S(1)} %add_11.1), channel_id=1, source_target_pairs={{4,8},{8,4},{5,9},{9,5},{6,10},{10,6},{7,11},{11,7},{20,24},{24,20... | collective-permute-start | bytes 1572872 | tf_op jit(solution)/shard_map/ppermute | solution.py:412
  89.3 4.3 %collective-permute-done.9.refs_3_ = bf16[128,2048]{1,0:T(8,128)(2,1)S(1)} collective-permute-done((bf16[128,2048]{1,0:T(8,128)(2,1)S(1)}, bf16[128,2048]{1,0:T(8,128)(2,1)S(1)}, u32[]{:S(2)}, u32[]{:S(2)}) %collective-permute-start.9) | collective-permute-done | bytes 524320 | tf_op jit(solution)/shard_map/ppermute | solution.py:408
  97.8 2.5 %finish_0.1 = (bf16[256,2048]{1,0:T(8,128)(2,1)}, f32[16,256]{1,0:T(8,128)}) custom-call(s32[1]{0:T(128)} %bitcast.refs_0_, bf16[128,2048]{1,0:T(8,128)(2,1)S(1)} %get-tuple-element.37.a_ref.refs_1_, bf16[128,2048]{1,0:T(8,128)(2,1)S(1)} %copy-done.3, bf16[128,2048]{1,0:T(8,128)(2,1)S(1)} %copy-done.5, bf16[128,2048]{1,0:T(8,128)(2,1)} %collective-permute-done.11.refs_4_, ...), custom_call_target="tpu_custom_call" | custom-call | flops 1572864 | bytes 3145728 | tf_op jit(solution)/shard_map/finish_0/pallas_call | solution.py:313
  100.3 4.2 %collective-permute-done.3.refs_3_ = bf16[128,2048]{1,0:T(8,128)(2,1)} collective-permute-done((bf16[128,2048]{1,0:T(8,128)(2,1)}, bf16[128,2048]{1,0:T(8,128)(2,1)}, u32[]{:S(2)}, u32[]{:S(2)}) %collective-permute-start.3) | collective-permute-done | bytes 524320 | tf_op jit(solution)/shard_map/ppermute | solution.py:408
  104.5 5.2 %collective-permute-done.8.refs_5_ = bf16[128,2048]{1,0:T(8,128)(2,1)} collective-permute-done((bf16[128,2048]{1,0:T(8,128)(2,1)S(1)}, bf16[128,2048]{1,0:T(8,128)(2,1)}, u32[]{:S(2)}, u32[]{:S(2)}) %collective-permute-start.8) | collective-permute-done | bytes 524320 | tf_op jit(solution)/shard_map/ppermute | solution.py:413
  109.7 2.6 %finish_1.1 = (bf16[256,2048]{1,0:T(8,128)(2,1)}, f32[16,256]{1,0:T(8,128)}) custom-call(s32[1]{0:T(128)} %bitcast.refs_0_, bf16[128,2048]{1,0:T(8,128)(2,1)S(1)} %get-tuple-element.33.a_ref.refs_1_, bf16[128,2048]{1,0:T(8,128)(2,1)} %get-tuple-element.34.refs_2_, ...), custom_call_target="tpu_custom_call", output_to_operand_aliasing={{0}: (6, {}), {1}: (7, {})} | custom-call | flops 1572864 | bytes 3145728 | tf_op jit(solution)/shard_map/finish_1/pallas_call | solution.py:313
  (39 shorter events, 13.1 us)
Async XLA Ops:
  3.2 5.8 %collective-permute-start = (bf16[2,1296,128]{2,1,0:T(8,128)(2,1)}, bf16[2,1296,128]{2,1,0:T(8,128)(2,1)S(1)}, u32[]{:S(2)}, u32[]{:S(2)}) collective-permute-start(bf16[2,1296,128]{2,1,0:T(8,128)(2,1)} %pack.1.refs_0_), channel_id=1, source_target_pairs={{0,1},{1,0},{2,3},{3,2},{4,5},{5,4},{6,7},{7,6},{8,9},{9,8},{10,11... | collective-permute-start | bytes 1990664 | tf_op jit(solution)/shard_map/ppermute | solution.py:366
  3.8 18.3 %collective-permute-start.1 = (bf16[2,1296,128]{2,1,0:T(8,128)(2,1)}, bf16[2,1296,128]{2,1,0:T(8,128)(2,1)S(1)}, u32[]{:S(2)}, u32[]{:S(2)}) collective-permute-start(bf16[2,1296,128]{2,1,0:T(8,128)(2,1)} %pack.1.refs_0_), channel_id=1, source_target_pairs={{0,2},{2,0},{1,3},{3,1},{4,6},{6,4},{5,7},{7,5},{8,10},{10,8},{9,1... | collective-permute-start | bytes 1990664 | tf_op jit(solution)/shard_map/ppermute | solution.py:365
  9.0 1.1 copy-start
  10.1 1.0 copy-start.1
  22.0 3.7 %collective-permute-start.2 = (bf16[2,1296,128]{2,1,0:T(8,128)(2,1)S(1)}, bf16[2,1296,128]{2,1,0:T(8,128)(2,1)S(1)}, u32[]{:S(2)}, u32[]{:S(2)}) collective-permute-start(bf16[2,1296,128]{2,1,0:T(8,128)(2,1)S(1)} %collective-permute-done.1.refs_0_), channel_id=1, source_target_pairs={{0,1},{1,0},{2,3},{3,2},{4,5},{5,4},{6,7},{7,6},{8,9},{9,8},{10,11... | collective-permute-start | bytes 1990664 | tf_op jit(solution)/shard_map/ppermute | solution.py:372
  32.6 19.9 %collective-permute-start.12 = (bf16[128,2048]{1,0:T(8,128)(2,1)S(1)}, bf16[128,2048]{1,0:T(8,128)(2,1)S(1)}, u32[]{:S(2)}, u32[]{:S(2)}) collective-permute-start(bf16[128,2048]{1,0:T(8,128)(2,1)S(1)} %get-tuple-element.30.a_ref), channel_id=1, source_target_pairs={{0,4},{12,8},{1,5},{13,9},{2,6},{14,10},{3,7},{15,11},{16,20},{28,... | collective-permute-start | bytes 1572872 | tf_op jit(solution)/shard_map/ppermute | solution.py:408
  44.1 15.8 %collective-permute-start.6 = (bf16[128,2048]{1,0:T(8,128)(2,1)S(1)}, bf16[128,2048]{1,0:T(8,128)(2,1)S(1)}, u32[]{:S(2)}, u32[]{:S(2)}) collective-permute-start(bf16[128,2048]{1,0:T(8,128)(2,1)S(1)} %get-tuple-element.36.a_ref), channel_id=1, source_target_pairs={{0,4},{12,8},{1,5},{13,9},{2,6},{14,10},{3,7},{15,11},{16,20},{28,... | collective-permute-start | bytes 1572872 | tf_op jit(solution)/shard_map/ppermute | solution.py:408
  49.9 27.8 %collective-permute-start.10 = (bf16[128,2048]{1,0:T(8,128)(2,1)S(1)}, bf16[128,2048]{1,0:T(8,128)(2,1)S(1)}, u32[]{:S(2)}, u32[]{:S(2)}) collective-permute-start(bf16[128,2048]{1,0:T(8,128)(2,1)S(1)} %get-tuple-element.39.a_ref), channel_id=1, source_target_pairs={{0,4},{12,8},{1,5},{13,9},{2,6},{14,10},{3,7},{15,11},{16,20},{28,... | collective-permute-start | bytes 1572872 | tf_op jit(solution)/shard_map/ppermute | solution.py:408
  51.2 31.1 %collective-permute-start.4 = (bf16[128,2048]{1,0:T(8,128)(2,1)S(1)}, bf16[128,2048]{1,0:T(8,128)(2,1)S(1)}, u32[]{:S(2)}, u32[]{:S(2)}) collective-permute-start(bf16[128,2048]{1,0:T(8,128)(2,1)S(1)} %get-tuple-element.35.a_ref), channel_id=1, source_target_pairs={{0,4},{12,8},{1,5},{13,9},{2,6},{14,10},{3,7},{15,11},{16,20},{28,... | collective-permute-start | bytes 1572872 | tf_op jit(solution)/shard_map/ppermute | solution.py:408
  52.7 26.6 %collective-permute-start.13 = (bf16[128,2048]{1,0:T(8,128)(2,1)S(1)}, bf16[128,2048]{1,0:T(8,128)(2,1)S(1)}, u32[]{:S(2)}, u32[]{:S(2)}) collective-permute-start(bf16[128,2048]{1,0:T(8,128)(2,1)S(1)} %add_00.1), channel_id=1, source_target_pairs={{4,8},{8,4},{5,9},{9,5},{6,10},{10,6},{7,11},{11,7},{20,24},{24,20... | collective-permute-start | bytes 1572872 | tf_op jit(solution)/shard_map/ppermute | solution.py:411
  60.0 27.7 %collective-permute-start.7 = (bf16[128,2048]{1,0:T(8,128)(2,1)S(1)}, bf16[128,2048]{1,0:T(8,128)(2,1)S(1)}, u32[]{:S(2)}, u32[]{:S(2)}) collective-permute-start(bf16[128,2048]{1,0:T(8,128)(2,1)S(1)} %add_01.1), channel_id=1, source_target_pairs={{4,8},{8,4},{5,9},{9,5},{6,10},{10,6},{7,11},{11,7},{20,24},{24,20... | collective-permute-start | bytes 1572872 | tf_op jit(solution)/shard_map/ppermute | solution.py:411
  66.0 23.3 %copy-start.2 = (bf16[128,2048]{1,0:T(8,128)(2,1)}, bf16[128,2048]{1,0:T(8,128)(2,1)S(1)}, u32[]{:S(2)}) copy-start(bf16[128,2048]{1,0:T(8,128)(2,1)S(1)} %get-tuple-element.38.refs_2_) | copy-start | bytes 1572868
  66.0 27.6 %collective-permute-start.9 = (bf16[128,2048]{1,0:T(8,128)(2,1)S(1)}, bf16[128,2048]{1,0:T(8,128)(2,1)S(1)}, u32[]{:S(2)}, u32[]{:S(2)}) collective-permute-start(bf16[128,2048]{1,0:T(8,128)(2,1)S(1)} %get-tuple-element.38.refs_2_), channel_id=1, source_target_pairs={{0,4},{12,8},{1,5},{13,9},{2,6},{14,10},{3,7},{15,11},{16,20},{28,... | collective-permute-start | bytes 1572872 | tf_op jit(solution)/shard_map/ppermute | solution.py:408
  77.8 17.9 %collective-permute-start.11 = (bf16[128,2048]{1,0:T(8,128)(2,1)S(1)}, bf16[128,2048]{1,0:T(8,128)(2,1)}, u32[]{:S(2)}, u32[]{:S(2)}) collective-permute-start(bf16[128,2048]{1,0:T(8,128)(2,1)S(1)} %add_10.1), channel_id=1, source_target_pairs={{4,8},{8,4},{5,9},{9,5},{6,10},{10,6},{7,11},{11,7},{20,24},{24,20... | collective-permute-start | bytes 1572872 | tf_op jit(solution)/shard_map/ppermute | solution.py:412
  79.4 16.3 %collective-permute-start.14 = (bf16[128,2048]{1,0:T(8,128)(2,1)S(1)}, bf16[128,2048]{1,0:T(8,128)(2,1)}, u32[]{:S(2)}, u32[]{:S(2)}) collective-permute-start(bf16[128,2048]{1,0:T(8,128)(2,1)S(1)} %add_30.1), channel_id=1, source_target_pairs={{4,0},{8,12},{5,1},{9,13},{6,2},{10,14},{7,3},{11,15},{20,16},{24,... | collective-permute-start | bytes 1572872 | tf_op jit(solution)/shard_map/ppermute | solution.py:413
  82.3 22.2 %collective-permute-start.3 = (bf16[128,2048]{1,0:T(8,128)(2,1)}, bf16[128,2048]{1,0:T(8,128)(2,1)}, u32[]{:S(2)}, u32[]{:S(2)}) collective-permute-start(bf16[128,2048]{1,0:T(8,128)(2,1)} %get-tuple-element.34.refs_2_), channel_id=1, source_target_pairs={{0,4},{12,8},{1,5},{13,9},{2,6},{14,10},{3,7},{15,11},{16,20},{28,... | collective-permute-start | bytes 1572872 | tf_op jit(solution)/shard_map/ppermute | solution.py:408
  87.7 16.8 %collective-permute-start.5 = (bf16[128,2048]{1,0:T(8,128)(2,1)S(1)}, bf16[128,2048]{1,0:T(8,128)(2,1)}, u32[]{:S(2)}, u32[]{:S(2)}) collective-permute-start(bf16[128,2048]{1,0:T(8,128)(2,1)S(1)} %add_11.1), channel_id=1, source_target_pairs={{4,8},{8,4},{5,9},{9,5},{6,10},{10,6},{7,11},{11,7},{20,24},{24,20... | collective-permute-start | bytes 1572872 | tf_op jit(solution)/shard_map/ppermute | solution.py:412
  93.6 0.8 copy-start.4
  94.4 15.4 %collective-permute-start.8 = (bf16[128,2048]{1,0:T(8,128)(2,1)S(1)}, bf16[128,2048]{1,0:T(8,128)(2,1)}, u32[]{:S(2)}, u32[]{:S(2)}) collective-permute-start(bf16[128,2048]{1,0:T(8,128)(2,1)S(1)} %add_31.1), channel_id=1, source_target_pairs={{4,0},{8,12},{5,1},{9,13},{6,2},{10,14},{7,3},{11,15},{20,16},{24,... | collective-permute-start | bytes 1572872 | tf_op jit(solution)/shard_map/ppermute | solution.py:413
  95.7 1.0 copy-start.3
  96.8 1.0 copy-start.5

commit v6 on v5

--- a/solution.py
+++ b/solution.py
@@ -17,7 +17,7 @@
 LOW = 32
 W_COPIES = 8
 NEG = -1e30
-VMEM_LIMIT = 48 * 1024 * 1024
+VMEM_LIMIT = 44 * 1024 * 1024
 VMEM_MOST = 60 * 1024 * 1024
 F32 = jnp.float32
 BF16 = jnp.bfloat16
@@ -28,6 +28,7 @@
 VMEM = pl.BlockSpec(memory_space=pltpu.VMEM)
 HBM = pl.BlockSpec(memory_space=pltpu.HBM)
 PARAMS = pltpu.CompilerParams(vmem_limit_bytes=VMEM_LIMIT)
+PARAMS_LESS = pltpu.CompilerParams(vmem_limit_bytes=28 * 1024 * 1024)
 PARAMS_MOST = pltpu.CompilerParams(vmem_limit_bytes=VMEM_MOST)
 
 
@@ -97,21 +98,26 @@
     at_held = slice(held, held + n_rows)
     me = place_ref[0]
     if first:
-        acc_out, stats_out, query_out, raw, sem = refs
-        copy = pltpu.make_async_copy(q_ref, raw, sem)
-        copy.start()
-    else:
-        acc_in, stats_in = refs[:2]
-        refs = refs[2:]
         if chunk:
-            w_ref, attended_out, part_out, w_held, sems = refs
+            w_ref, acc_out, stats_out, query_out, w_held, raw, sem, sems = refs
             columns = pl.ds(pl.multiple_of(place_ref[1] * chunk, chunk), chunk)
             depth = w_ref.shape[0] // W_COPIES
             copies = []
             for i in range(W_COPIES):
                 at = pl.ds(i * depth, depth)
                 copies.append(pltpu.make_async_copy(w_ref.at[at, columns], w_held.at[at], sems.at[i]))
-                copies[i].start()
+        else:
+            acc_out, stats_out, query_out, raw, sem = refs
+            copies = []
+        copy = pltpu.make_async_copy(q_ref, raw, sem)
+        copy.start()
+        for other in copies:
+            other.start()
+    else:
+        acc_in, stats_in = refs[:2]
+        refs = refs[2:]
+        if chunk:
+            w_held, attended_out, part_out = refs
         elif last:
             (attended_out,) = refs
         else:
@@ -184,9 +190,10 @@
             stats = jnp.where(lane == HD // 2 + head, total, stats)
     if not last:
         stats_out[...] = stats
-    if chunk:
-        for copy in copies:
-            copy.wait()
+    if first:
+        for other in copies:
+            other.wait()
+    elif chunk:
         tile = 512
         for i in range(0, chunk, tile):
             part = jnp.dot(attended_out[...], w_held[:, i : i + tile], preferred_element_type=F32)
@@ -208,13 +215,13 @@
     else:
         operands += state
         in_specs += [VMEM] * 2
+    if chunk:
+        operands.append(weight)
+        in_specs.append(HBM if first else VMEM)
     if last:
         out_shape = [jax.ShapeDtypeStruct((span[1], width), BF16)]
         if chunk:
-            operands.append(weight)
-            in_specs.append(HBM)
             out_shape.append(jax.ShapeDtypeStruct((span[1], chunk), BF16))
-            scratch = [pltpu.VMEM((width, chunk), BF16), pltpu.SemaphoreType.DMA((W_COPIES,))]
     else:
         out_shape = [
             jax.ShapeDtypeStruct((span[1], width), F32),
@@ -222,6 +229,9 @@
         ]
         if first:
             out_shape.append(jax.ShapeDtypeStruct((rows, width), BF16))
+            if chunk:
+                out_shape.append(jax.ShapeDtypeStruct((width, chunk), BF16))
+                scratch.append(pltpu.SemaphoreType.DMA((W_COPIES,)))
     keys = len(arrays) * (slots + rows)
     return pl.pallas_call(
         functools.partial(attend_kernel, first, last, chunk, slots, shards_at, span, held),
@@ -229,7 +239,7 @@
         in_specs=in_specs,
         out_specs=[VMEM] * len(out_shape),
         scratch_shapes=scratch,
-        compiler_params=PARAMS,
+        compiler_params=PARAMS if first else PARAMS_LESS,
         cost_estimate=cost(
             rows * width * keys // 2, rows * width, rows * (width // HD) * keys // 8
         ),
@@ -276,7 +286,7 @@
         out_shape=jax.ShapeDtypeStruct(a.shape, BF16),
         in_specs=[VMEM, VMEM],
         out_specs=VMEM,
-        compiler_params=PARAMS,
+        compiler_params=PARAMS_LESS,
         cost_estimate=cost(a.size, a.size * 6),
         name=name,
     )(a, b)
@@ -323,7 +333,7 @@
             pl.BlockSpec((per, rows), lambda i: (i, begin // rows)),
         ),
         input_output_aliases={len(flags) + count: 0, len(flags) + count + 1: 1} if into else {},
-        compiler_params=PARAMS,
+        compiler_params=PARAMS_LESS,
         cost_estimate=cost(rows * columns * 6, rows * columns * 2 * (count + 1)),
         name=name,
     )(*flags, *parts, *into)
@@ -365,8 +375,17 @@
         far = lax.ppermute(own, "seq", swap)
         near = lax.ppermute(own, "pipe", swap)
         place = jnp.stack([me, order[0], me, me ^ 1, me ^ 2, me ^ 3]).astype(jnp.int32)
-        acc, stats, query = attend(
-            "attend_near", place, queries, tables, [own, near], (0, 1), None, False
+        acc, stats, query, w_held = attend(
+            "attend_near",
+            place,
+            queries,
+            tables,
+            [own, near],
+            (0, 1),
+            None,
+            False,
+            weight=out_weight,
+            chunk=columns,
         )
         far = after(far, stats)
         cross = lax.ppermute(far, "pipe", swap)
@@ -384,7 +403,7 @@
             (3,),
             tuple(state),
             True,
-            weight=out_weight,
+            weight=w_held,
             chunk=columns,
             span=(0, cut),
         )
@@ -397,7 +416,7 @@
             (2, 3),
             (acc, after(stats, first_part[0])),
             True,
-            weight=out_weight,
+            weight=w_held,
             chunk=columns,
             span=(cut, cut),
             held=cut,
@@ -405,10 +424,17 @@
         part = [first_part]
         for k in range(1, 4):
             part.append(project(f"project_{k}", order, k, attended, out_weight, columns))
-        come = [[lax.ppermute(p, "tensor", inward) for p in part[k]] for k in range(3)]
+        come = [[None, None] for k in range(3)]
+        for i in range(2):
+            come[0][i] = lax.ppermute(part[0][i], "tensor", inward)
+        part[1] = [part[1][0], after(part[1][1], come[0][0])]
+        for k in (1, 2):
+            come[k] = [lax.ppermute(p, "tensor", inward) for p in part[k]]
         done = None
+        previous = attended[1]
         for i in range(2):
-            across = lax.ppermute(added(f"add_0{i}", part[0][i], come[0][i]), "tensor", middle)
+            previous = added(f"add_0{i}", part[0][i], after(come[0][i], previous))
+            across = lax.ppermute(previous, "tensor", middle)
             second = lax.ppermute(added(f"add_1{i}", part[1][i], come[1][i]), "tensor", middle)
             back = lax.ppermute(added(f"add_3{i}", part[3][i], across), "tensor", outward)
             parts = [part[3][i], part[2][i], come[2][i], second, back]

time: 113 us -> 111 us (0.982)
  Pallas kernels: 49.1 us -> 45.1 us
  waiting for transfers between devices: 23.8 us -> 25.1 us
    pallas_call x4, Pallas kernels: 27.1 us -> 23.1 us  [attend(): pl.pallas_call(functools.partial(attend_kernel, first, last, chunk, slots...]
    ppermute x8, waiting for transfers between devices: 16.6 us -> 17.9 us  [the longest x2 9.81 us: local(): come[0][i] = lax.ppermute(part[0][i], 'tensor', inward)]
  transfers between devices with their start and end apart: 15 -> 15, of which waited for: 6 -> 6; matrix products, arithmetic and copies ran while one was open for 2% -> 2% of each run, Pallas kernels for 33% -> 32%
where the time goes in v6:
time: 111 us; the launch traced here: 110 us
  Pallas kernels  45.1 us (41%)
  starting transfers between devices  30.9 us (28%)
  waiting for transfers between devices  25.1 us (23%)
  local copies, waits for them, and re-layouts  5.14 us (5%)
  between operations  2.2 us (2%)
  other arithmetic  1.92 us (2%)
    pallas_call x4, Pallas kernels, attend(): pl.pallas_call(functools.partial(attend_kernel, first, last, chunk, slots...  23.1 us
    ppermute x4, starting transfers between devices, local(): come[k] = [lax.ppermute(p, 'tensor', inward) for p in part[k]]  15.8 us
    pallas_call x3, Pallas kernels, project(): pl.pallas_call(functools.partial(project_kernel, pieces), out_shape=(jax....  14.2 us
    ppermute x2, waiting for transfers between devices, local(): come[0][i] = lax.ppermute(part[0][i], 'tensor', inward)  9.81 us
    ppermute x4, waiting for transfers between devices, local(): come[k] = [lax.ppermute(p, 'tensor', inward) for p in part[k]]  8.09 us
    ppermute x2, waiting for transfers between devices, local(): lax.ppermute(added(f'add_3{i}', part[3][i], across), 'tensor', outward)  5.25 us
    pallas_call x2, Pallas kernels, finish(): pl.pallas_call(kernel, out_shape=(jax.ShapeDtypeStruct((rows_all, columns...  5.1 us
    ppermute x2, starting transfers between devices, local(): come[0][i] = lax.ppermute(part[0][i], 'tensor', inward)  5.09 us
  transfers between devices with their start and end apart: 15, of which 6 were waited for; matrix products, arithmetic and copies ran while one was open for 2% of the time, Pallas kernels for 32%

profile of v6, /device:TPU:0, one launch (start us, length us, event | category | flops | bytes accessed | tf_op | source)
XLA Modules:
  0.0 110.3 jit_solution(8835534803039836019)
XLA Ops:
  1.3 2.0 %pack.1.refs_0_ = bf16[2,1296,128]{2,1,0:T(8,128)(2,1)} custom-call(s32[1]{0:T(128)S(6)} %copy.14.len_ref, bf16[4,1024,128]{2,1,0:T(8,128)(2,1)} %k_ref.1, bf16[4,1024,128]{2,1,0:T(8,128)(2,1)} %v_ref.1, bf16[256,512]{1,0:T(8,128)(2,1)} %nk_ref.1, bf16[256,512]{1,0:T(8,128)(2,1)} %nv_ref.1), custom_call_target="tpu_custom_call" | custom-call | bytes 1327104 | tf_op jit(solution)/shard_map/pack/pallas_call | solution.py:66
  3.8 2.6 %collective-permute-start.1 = (bf16[2,1296,128]{2,1,0:T(8,128)(2,1)}, bf16[2,1296,128]{2,1,0:T(8,128)(2,1)S(1)}, u32[]{:S(2)}, u32[]{:S(2)}) collective-permute-start(bf16[2,1296,128]{2,1,0:T(8,128)(2,1)} %pack.1.refs_0_), channel_id=1, source_target_pairs={{0,2},{2,0},{1,3},{3,1},{4,6},{6,4},{5,7},{7,5},{8,10},{10,8},{9,1... | collective-permute-start | bytes 1990664 | tf_op jit(solution)/shard_map/ppermute | solution.py:375
  7.1 1.9 %fusion = (f32[1024,128]{1,0:T(8,128)S(1)}, f32[1024,128]{1,0:T(8,128)S(1)}) fusion(f32[128]{0:T(128)S(1)} %get-tuple-element.54, f32[128]{0:T(128)S(1)} %get-tuple-element.55, f32[1024]{0:T(1024)S(1)} %add_convert_fusion), kind=kLoop, calls=%fused_computation.2 | loop fusion | flops 262144 | bytes 1053696 | tf_op jit(solution)/shard_map/mul | solution.py:364
  11.2 8.9 %attend_near.1 = (f32[256,1024]{1,0:T(8,128)S(1)}, f32[256,128]{1,0:T(8,128)S(1)}, bf16[256,1024]{1,0:T(8,128)(2,1)S(1)}, bf16[1024,2048]{1,0:T(8,128)(2,1)S(1)}) custom-call(s32[6]{0:T(128)S(1)} %stack.20.place_ref, bf16[256,1024]{1,0:T(8,128)(2,1)S(1)} %copy-done.1, f32[1024,128]{1,0:T(8,128)S(1)} %get-tuple-element.53.cos_ref, ...), custom_call_target="tpu_custom_call" | custom-call | flops 335544320 | bytes 262144 | tf_op jit(solution)/shard_map/attend_near/pallas_call | solution.py:236
  20.1 1.9 %collective-permute-done.1.refs_0_ = bf16[2,1296,128]{2,1,0:T(8,128)(2,1)S(1)} collective-permute-done((bf16[2,1296,128]{2,1,0:T(8,128)(2,1)}, bf16[2,1296,128]{2,1,0:T(8,128)(2,1)S(1)}, u32[]{:S(2)}, u32[]{:S(2)}) %collective-permute-start.1) | collective-permute-done | bytes 663584 | tf_op jit(solution)/shard_map/ppermute | solution.py:375
  22.0 3.7 %attend_far.1 = (f32[128,1024]{1,0:T(8,128)S(1)}, f32[128,128]{1,0:T(8,128)S(1)}) custom-call(s32[6]{0:T(128)S(1)} %stack.20.place_ref, bf16[256,1024]{1,0:T(8,128)(2,1)S(1)} %get-tuple-element.27.q_ref, f32[1024,128]{1,0:T(8,128)S(1)} %get-tuple-element.53.cos_ref, f32[1024,128]{1,0:T(8,128)S(1)} %get-tuple-element.52.sin_ref, ...), custom_call_target="tpu_custom_call" | custom-call | flops 167772160 | bytes 262144 | tf_op jit(solution)/shard_map/attend_far/pallas_call | solution.py:236
  25.7 4.9 %attend_cross.1 = (bf16[128,1024]{1,0:T(8,128)(2,1)S(1)}, bf16[128,2048]{1,0:T(8,128)(2,1)S(1)}) custom-call(s32[6]{0:T(128)S(1)} %stack.20.place_ref, bf16[256,1024]{1,0:T(8,128)(2,1)S(1)} %get-tuple-element.27.q_ref, f32[1024,128]{1,0:T(8,128)S(1)} %get-tuple-element.53.cos_ref, f32[1024,128]{1,0:T(8,128)S(1)} %get-tuple-element.52.sin_ref, ...), custom_call_target="tpu_custom_call" | custom-call | flops 167772160 | bytes 262144 | tf_op jit(solution)/shard_map/attend_cross/pallas_call | solution.py:236
  30.6 3.8 %collective-permute-start.4 = (bf16[128,2048]{1,0:T(8,128)(2,1)S(1)}, bf16[128,2048]{1,0:T(8,128)(2,1)S(1)}, u32[]{:S(2)}, u32[]{:S(2)}) collective-permute-start(bf16[128,2048]{1,0:T(8,128)(2,1)S(1)} %get-tuple-element.35.a_ref), channel_id=1, source_target_pairs={{0,4},{12,8},{1,5},{13,9},{2,6},{14,10},{3,7},{15,11},{16,20},{28,... | collective-permute-start | bytes 1572872 | tf_op jit(solution)/shard_map/ppermute | solution.py:429
  34.3 5.6 %attend_rest.1 = (bf16[128,1024]{1,0:T(8,128)(2,1)S(1)}, bf16[128,2048]{1,0:T(8,128)(2,1)S(1)}) custom-call(s32[6]{0:T(128)S(1)} %stack.20.place_ref, bf16[256,1024]{1,0:T(8,128)(2,1)S(1)} %get-tuple-element.27.q_ref, f32[1024,128]{1,0:T(8,128)S(1)} %get-tuple-element.53.cos_ref, f32[1024,128]{1,0:T(8,128)S(1)} %get-tuple-element.52.sin_ref, ...), custom_call_target="tpu_custom_call" | custom-call | flops 335544320 | bytes 262144 | tf_op jit(solution)/shard_map/attend_rest/pallas_call | solution.py:236
  40.0 1.3 %collective-permute-start.7 = (bf16[128,2048]{1,0:T(8,128)(2,1)S(1)}, bf16[128,2048]{1,0:T(8,128)(2,1)S(1)}, u32[]{:S(2)}, u32[]{:S(2)}) collective-permute-start(bf16[128,2048]{1,0:T(8,128)(2,1)S(1)} %get-tuple-element.42.a_ref), channel_id=1, source_target_pairs={{0,4},{12,8},{1,5},{13,9},{2,6},{14,10},{3,7},{15,11},{16,20},{28,... | collective-permute-start | bytes 1572872 | tf_op jit(solution)/shard_map/ppermute | solution.py:429
  41.3 4.5 %project_1.1 = (bf16[128,2048]{1,0:T(8,128)(2,1)S(1)}, bf16[128,2048]{1,0:T(8,128)(2,1)S(1)}) custom-call(s32[4]{0:T(128)S(1)} %broadcast_select_fusion.order_ref, bf16[128,1024]{1,0:T(8,128)(2,1)S(1)} %get-tuple-element.34.refs_0_, bf16[128,1024]{1,0:T(8,128)(2,1)S(1)} %get-tuple-element.37.refs_1_, bf16[1024,8192]{1,0:T(8,128)(2,1)} %refs_2_.7), custom_call_target="tpu_custom_call" | custom-call | flops 1073741824 | bytes 4194304 | tf_op jit(solution)/shard_map/project_1/pallas_call | solution.py:263
  45.8 1.3 %collective-permute-start.11 = (bf16[128,2048]{1,0:T(8,128)(2,1)S(1)}, bf16[128,2048]{1,0:T(8,128)(2,1)S(1)}, u32[]{:S(2)}, u32[]{:S(2)}) collective-permute-start(bf16[128,2048]{1,0:T(8,128)(2,1)S(1)} %get-tuple-element.47.a_ref), channel_id=1, source_target_pairs={{0,4},{12,8},{1,5},{13,9},{2,6},{14,10},{3,7},{15,11},{16,20},{28,... | collective-permute-start | bytes 1572872 | tf_op jit(solution)/shard_map/ppermute | solution.py:432
  48.0 9.8 %collective-permute-done.7.b_ref = bf16[128,2048]{1,0:T(8,128)(2,1)S(1)} collective-permute-done((bf16[128,2048]{1,0:T(8,128)(2,1)S(1)}, bf16[128,2048]{1,0:T(8,128)(2,1)S(1)}, u32[]{:S(2)}, u32[]{:S(2)}) %collective-permute-start.7) | collective-permute-done | bytes 524320 | tf_op jit(solution)/shard_map/ppermute | solution.py:429
  58.6 7.2 %collective-permute-start.5 = (bf16[128,2048]{1,0:T(8,128)(2,1)S(1)}, bf16[128,2048]{1,0:T(8,128)(2,1)S(1)}, u32[]{:S(2)}, u32[]{:S(2)}) collective-permute-start(bf16[128,2048]{1,0:T(8,128)(2,1)S(1)} %get-tuple-element.41.a_ref), channel_id=1, source_target_pairs={{0,4},{12,8},{1,5},{13,9},{2,6},{14,10},{3,7},{15,11},{16,20},{28,... | collective-permute-start | bytes 1572872 | tf_op jit(solution)/shard_map/ppermute | solution.py:432
  65.8 5.3 %project_2.1 = (bf16[128,2048]{1,0:T(8,128)(2,1)S(1)}, bf16[128,2048]{1,0:T(8,128)(2,1)}) custom-call(s32[4]{0:T(128)S(1)} %broadcast_select_fusion.order_ref, bf16[128,1024]{1,0:T(8,128)(2,1)S(1)} %get-tuple-element.34.refs_0_, bf16[128,1024]{1,0:T(8,128)(2,1)S(1)} %get-tuple-element.37.refs_1_, bf16[1024,8192]{1,0:T(8,128)(2,1)} %refs_2_.7), custom_call_target="tpu_custom_call" | custom-call | flops 1073741824 | bytes 4194304 | tf_op jit(solution)/shard_map/project_2/pallas_call | solution.py:263
  72.5 4.5 %project_3.1 = (bf16[128,2048]{1,0:T(8,128)(2,1)S(1)}, bf16[128,2048]{1,0:T(8,128)(2,1)S(1)}) custom-call(s32[4]{0:T(128)S(1)} %broadcast_select_fusion.order_ref, bf16[128,1024]{1,0:T(8,128)(2,1)S(1)} %get-tuple-element.34.refs_0_, bf16[128,1024]{1,0:T(8,128)(2,1)S(1)} %get-tuple-element.37.refs_1_, bf16[1024,8192]{1,0:T(8,128)(2,1)} %refs_2_.7), custom_call_target="tpu_custom_call" | custom-call | flops 1073741824 | bytes 4194304 | tf_op jit(solution)/shard_map/project_3/pallas_call | solution.py:263
  77.1 1.5 %collective-permute-start.12 = (bf16[128,2048]{1,0:T(8,128)(2,1)S(1)}, bf16[128,2048]{1,0:T(8,128)(2,1)}, u32[]{:S(2)}, u32[]{:S(2)}) collective-permute-start(bf16[128,2048]{1,0:T(8,128)(2,1)S(1)} %add_10.1), channel_id=1, source_target_pairs={{4,8},{8,4},{5,9},{9,5},{6,10},{10,6},{7,11},{11,7},{20,24},{24,20... | collective-permute-start | bytes 1572872 | tf_op jit(solution)/shard_map/ppermute | solution.py:438
  80.2 5.9 %collective-permute-start.3 = (bf16[128,2048]{1,0:T(8,128)(2,1)}, bf16[128,2048]{1,0:T(8,128)(2,1)}, u32[]{:S(2)}, u32[]{:S(2)}) collective-permute-start(bf16[128,2048]{1,0:T(8,128)(2,1)} %get-tuple-element.39.refs_2_), channel_id=1, source_target_pairs={{0,4},{12,8},{1,5},{13,9},{2,6},{14,10},{3,7},{15,11},{16,20},{28,... | collective-permute-start | bytes 1572872 | tf_op jit(solution)/shard_map/ppermute | solution.py:432
  86.3 1.5 %collective-permute-start.6 = (bf16[128,2048]{1,0:T(8,128)(2,1)S(1)}, bf16[128,2048]{1,0:T(8,128)(2,1)}, u32[]{:S(2)}, u32[]{:S(2)}) collective-permute-start(bf16[128,2048]{1,0:T(8,128)(2,1)S(1)} %add_11.1), channel_id=1, source_target_pairs={{4,8},{8,4},{5,9},{9,5},{6,10},{10,6},{7,11},{11,7},{20,24},{24,20... | collective-permute-start | bytes 1572872 | tf_op jit(solution)/shard_map/ppermute | solution.py:438
  87.9 3.6 %collective-permute-done.10.refs_3_ = bf16[128,2048]{1,0:T(8,128)(2,1)S(1)} collective-permute-done((bf16[128,2048]{1,0:T(8,128)(2,1)S(1)}, bf16[128,2048]{1,0:T(8,128)(2,1)S(1)}, u32[]{:S(2)}, u32[]{:S(2)}) %collective-permute-start.10) | collective-permute-done | bytes 524320 | tf_op jit(solution)/shard_map/ppermute | solution.py:432
  95.7 2.5 %finish_0.1 = (bf16[256,2048]{1,0:T(8,128)(2,1)}, f32[16,256]{1,0:T(8,128)}) custom-call(s32[1]{0:T(128)} %bitcast.refs_0_, bf16[128,2048]{1,0:T(8,128)(2,1)S(1)} %get-tuple-element.45.a_ref.refs_1_, bf16[128,2048]{1,0:T(8,128)(2,1)S(1)} %copy-done.3, bf16[128,2048]{1,0:T(8,128)(2,1)S(1)} %copy-done.5, bf16[128,2048]{1,0:T(8,128)(2,1)} %collective-permute-done.12.refs_4_, ...), custom_call_target="tpu_custom_call" | custom-call | flops 1572864 | bytes 3145728 | tf_op jit(solution)/shard_map/finish_0/pallas_call | solution.py:323
  98.2 4.3 %collective-permute-done.3.refs_3_ = bf16[128,2048]{1,0:T(8,128)(2,1)} collective-permute-done((bf16[128,2048]{1,0:T(8,128)(2,1)}, bf16[128,2048]{1,0:T(8,128)(2,1)}, u32[]{:S(2)}, u32[]{:S(2)}) %collective-permute-start.3) | collective-permute-done | bytes 524320 | tf_op jit(solution)/shard_map/ppermute | solution.py:432
  102.5 5.2 %collective-permute-done.9.refs_5_ = bf16[128,2048]{1,0:T(8,128)(2,1)} collective-permute-done((bf16[128,2048]{1,0:T(8,128)(2,1)S(1)}, bf16[128,2048]{1,0:T(8,128)(2,1)}, u32[]{:S(2)}, u32[]{:S(2)}) %collective-permute-start.9) | collective-permute-done | bytes 524320 | tf_op jit(solution)/shard_map/ppermute | solution.py:439
  107.7 2.6 %finish_1.1 = (bf16[256,2048]{1,0:T(8,128)(2,1)}, f32[16,256]{1,0:T(8,128)}) custom-call(s32[1]{0:T(128)} %bitcast.refs_0_, bf16[128,2048]{1,0:T(8,128)(2,1)S(1)} %get-tuple-element.38.a_ref.refs_1_, bf16[128,2048]{1,0:T(8,128)(2,1)} %get-tuple-element.39.refs_2_, ...), custom_call_target="tpu_custom_call", output_to_operand_aliasing={{0}: (6, {}), {1}: (7, {})} | custom-call | flops 1572864 | bytes 3145728 | tf_op jit(solution)/shard_map/finish_1/pallas_call | solution.py:323
  (39 shorter events, 12.0 us)
Async XLA Ops:
  3.2 5.8 %collective-permute-start = (bf16[2,1296,128]{2,1,0:T(8,128)(2,1)}, bf16[2,1296,128]{2,1,0:T(8,128)(2,1)S(1)}, u32[]{:S(2)}, u32[]{:S(2)}) collective-permute-start(bf16[2,1296,128]{2,1,0:T(8,128)(2,1)} %pack.1.refs_0_), channel_id=1, source_target_pairs={{0,1},{1,0},{2,3},{3,2},{4,5},{5,4},{6,7},{7,6},{8,9},{9,8},{10,11... | collective-permute-start | bytes 1990664 | tf_op jit(solution)/shard_map/ppermute | solution.py:376
  3.8 18.3 %collective-permute-start.1 = (bf16[2,1296,128]{2,1,0:T(8,128)(2,1)}, bf16[2,1296,128]{2,1,0:T(8,128)(2,1)S(1)}, u32[]{:S(2)}, u32[]{:S(2)}) collective-permute-start(bf16[2,1296,128]{2,1,0:T(8,128)(2,1)} %pack.1.refs_0_), channel_id=1, source_target_pairs={{0,2},{2,0},{1,3},{3,1},{4,6},{6,4},{5,7},{7,5},{8,10},{10,8},{9,1... | collective-permute-start | bytes 1990664 | tf_op jit(solution)/shard_map/ppermute | solution.py:375
  9.0 1.1 copy-start
  10.1 1.0 copy-start.1
  22.0 3.7 %collective-permute-start.2 = (bf16[2,1296,128]{2,1,0:T(8,128)(2,1)S(1)}, bf16[2,1296,128]{2,1,0:T(8,128)(2,1)S(1)}, u32[]{:S(2)}, u32[]{:S(2)}) collective-permute-start(bf16[2,1296,128]{2,1,0:T(8,128)(2,1)S(1)} %collective-permute-done.1.refs_0_), channel_id=1, source_target_pairs={{0,1},{1,0},{2,3},{3,2},{4,5},{5,4},{6,7},{7,6},{8,9},{9,8},{10,11... | collective-permute-start | bytes 1990664 | tf_op jit(solution)/shard_map/ppermute | solution.py:391
  30.6 16.5 %collective-permute-start.4 = (bf16[128,2048]{1,0:T(8,128)(2,1)S(1)}, bf16[128,2048]{1,0:T(8,128)(2,1)S(1)}, u32[]{:S(2)}, u32[]{:S(2)}) collective-permute-start(bf16[128,2048]{1,0:T(8,128)(2,1)S(1)} %get-tuple-element.35.a_ref), channel_id=1, source_target_pairs={{0,4},{12,8},{1,5},{13,9},{2,6},{14,10},{3,7},{15,11},{16,20},{28,... | collective-permute-start | bytes 1572872 | tf_op jit(solution)/shard_map/ppermute | solution.py:429
  40.0 17.8 %collective-permute-start.7 = (bf16[128,2048]{1,0:T(8,128)(2,1)S(1)}, bf16[128,2048]{1,0:T(8,128)(2,1)S(1)}, u32[]{:S(2)}, u32[]{:S(2)}) collective-permute-start(bf16[128,2048]{1,0:T(8,128)(2,1)S(1)} %get-tuple-element.42.a_ref), channel_id=1, source_target_pairs={{0,4},{12,8},{1,5},{13,9},{2,6},{14,10},{3,7},{15,11},{16,20},{28,... | collective-permute-start | bytes 1572872 | tf_op jit(solution)/shard_map/ppermute | solution.py:429
  45.8 31.1 %collective-permute-start.11 = (bf16[128,2048]{1,0:T(8,128)(2,1)S(1)}, bf16[128,2048]{1,0:T(8,128)(2,1)S(1)}, u32[]{:S(2)}, u32[]{:S(2)}) collective-permute-start(bf16[128,2048]{1,0:T(8,128)(2,1)S(1)} %get-tuple-element.47.a_ref), channel_id=1, source_target_pairs={{0,4},{12,8},{1,5},{13,9},{2,6},{14,10},{3,7},{15,11},{16,20},{28,... | collective-permute-start | bytes 1572872 | tf_op jit(solution)/shard_map/ppermute | solution.py:432
  47.3 31.3 %collective-permute-start.13 = (bf16[128,2048]{1,0:T(8,128)(2,1)S(1)}, bf16[128,2048]{1,0:T(8,128)(2,1)S(1)}, u32[]{:S(2)}, u32[]{:S(2)}) collective-permute-start(bf16[128,2048]{1,0:T(8,128)(2,1)S(1)} %add_00.1), channel_id=1, source_target_pairs={{4,8},{8,4},{5,9},{9,5},{6,10},{10,6},{7,11},{11,7},{20,24},{24,20... | collective-permute-start | bytes 1572872 | tf_op jit(solution)/shard_map/ppermute | solution.py:437
  57.9 28.4 %collective-permute-start.8 = (bf16[128,2048]{1,0:T(8,128)(2,1)S(1)}, bf16[128,2048]{1,0:T(8,128)(2,1)S(1)}, u32[]{:S(2)}, u32[]{:S(2)}) collective-permute-start(bf16[128,2048]{1,0:T(8,128)(2,1)S(1)} %add_01.1), channel_id=1, source_target_pairs={{4,8},{8,4},{5,9},{9,5},{6,10},{10,6},{7,11},{11,7},{20,24},{24,20... | collective-permute-start | bytes 1572872 | tf_op jit(solution)/shard_map/ppermute | solution.py:437
  58.6 21.6 %collective-permute-start.5 = (bf16[128,2048]{1,0:T(8,128)(2,1)S(1)}, bf16[128,2048]{1,0:T(8,128)(2,1)S(1)}, u32[]{:S(2)}, u32[]{:S(2)}) collective-permute-start(bf16[128,2048]{1,0:T(8,128)(2,1)S(1)} %get-tuple-element.41.a_ref), channel_id=1, source_target_pairs={{0,4},{12,8},{1,5},{13,9},{2,6},{14,10},{3,7},{15,11},{16,20},{28,... | collective-permute-start | bytes 1572872 | tf_op jit(solution)/shard_map/ppermute | solution.py:432
  71.1 16.8 %copy-start.2 = (bf16[128,2048]{1,0:T(8,128)(2,1)}, bf16[128,2048]{1,0:T(8,128)(2,1)S(1)}, u32[]{:S(2)}) copy-start(bf16[128,2048]{1,0:T(8,128)(2,1)S(1)} %get-tuple-element.46.refs_2_) | copy-start | bytes 1572868
  71.1 20.3 %collective-permute-start.10 = (bf16[128,2048]{1,0:T(8,128)(2,1)S(1)}, bf16[128,2048]{1,0:T(8,128)(2,1)S(1)}, u32[]{:S(2)}, u32[]{:S(2)}) collective-permute-start(bf16[128,2048]{1,0:T(8,128)(2,1)S(1)} %get-tuple-element.46.refs_2_), channel_id=1, source_target_pairs={{0,4},{12,8},{1,5},{13,9},{2,6},{14,10},{3,7},{15,11},{16,20},{28,... | collective-permute-start | bytes 1572872 | tf_op jit(solution)/shard_map/ppermute | solution.py:432
  77.1 16.5 %collective-permute-start.12 = (bf16[128,2048]{1,0:T(8,128)(2,1)S(1)}, bf16[128,2048]{1,0:T(8,128)(2,1)}, u32[]{:S(2)}, u32[]{:S(2)}) collective-permute-start(bf16[128,2048]{1,0:T(8,128)(2,1)S(1)} %add_10.1), channel_id=1, source_target_pairs={{4,8},{8,4},{5,9},{9,5},{6,10},{10,6},{7,11},{11,7},{20,24},{24,20... | collective-permute-start | bytes 1572872 | tf_op jit(solution)/shard_map/ppermute | solution.py:438
  78.7 14.9 %collective-permute-start.14 = (bf16[128,2048]{1,0:T(8,128)(2,1)S(1)}, bf16[128,2048]{1,0:T(8,128)(2,1)}, u32[]{:S(2)}, u32[]{:S(2)}) collective-permute-start(bf16[128,2048]{1,0:T(8,128)(2,1)S(1)} %add_30.1), channel_id=1, source_target_pairs={{4,0},{8,12},{5,1},{9,13},{6,2},{10,14},{7,3},{11,15},{20,16},{24,... | collective-permute-start | bytes 1572872 | tf_op jit(solution)/shard_map/ppermute | solution.py:439
  80.2 22.2 %collective-permute-start.3 = (bf16[128,2048]{1,0:T(8,128)(2,1)}, bf16[128,2048]{1,0:T(8,128)(2,1)}, u32[]{:S(2)}, u32[]{:S(2)}) collective-permute-start(bf16[128,2048]{1,0:T(8,128)(2,1)} %get-tuple-element.39.refs_2_), channel_id=1, source_target_pairs={{0,4},{12,8},{1,5},{13,9},{2,6},{14,10},{3,7},{15,11},{16,20},{28,... | collective-permute-start | bytes 1572872 | tf_op jit(solution)/shard_map/ppermute | solution.py:432
  86.3 16.2 %collective-permute-start.6 = (bf16[128,2048]{1,0:T(8,128)(2,1)S(1)}, bf16[128,2048]{1,0:T(8,128)(2,1)}, u32[]{:S(2)}, u32[]{:S(2)}) collective-permute-start(bf16[128,2048]{1,0:T(8,128)(2,1)S(1)} %add_11.1), channel_id=1, source_target_pairs={{4,8},{8,4},{5,9},{9,5},{6,10},{10,6},{7,11},{11,7},{20,24},{24,20... | collective-permute-start | bytes 1572872 | tf_op jit(solution)/shard_map/ppermute | solution.py:438
  91.5 0.8 copy-start.4
  92.3 15.4 %collective-permute-start.9 = (bf16[128,2048]{1,0:T(8,128)(2,1)S(1)}, bf16[128,2048]{1,0:T(8,128)(2,1)}, u32[]{:S(2)}, u32[]{:S(2)}) collective-permute-start(bf16[128,2048]{1,0:T(8,128)(2,1)S(1)} %add_31.1), channel_id=1, source_target_pairs={{4,0},{8,12},{5,1},{9,13},{6,2},{10,14},{7,3},{11,15},{20,16},{24,... | collective-permute-start | bytes 1572872 | tf_op jit(solution)/shard_map/ppermute | solution.py:439
  93.6 1.0 copy-start.3
  94.7 1.0 copy-start.5

commit v7 on v6

--- a/solution.py
+++ b/solution.py
@@ -16,6 +16,7 @@
 LEN_ROWS = 16
 LOW = 32
 W_COPIES = 8
+HEADS_PER_STEP = 4
 NEG = -1e30
 VMEM_LIMIT = 44 * 1024 * 1024
 VMEM_MOST = 60 * 1024 * 1024
@@ -147,47 +148,64 @@
             query_out[:, at] = rotated(raw[:, at].astype(F32), cosine, sine).astype(BF16)
         q_ref = query_out
 
+    lane = lax.broadcasted_iota(jnp.int32, (n_rows, HD), 1)
+    per_step = heads if first else min(heads, HEADS_PER_STEP)
+
+    def columns_of(head):
+        return pl.ds(head * HD if first else pl.multiple_of(head * HD, HD), HD)
+
     def score(head):
-        query = q_ref[at_rows, head * HD : (head + 1) * HD]
+        query = q_ref[at_rows, columns_of(head)]
         scores = []
         for ref, keys, begin, count, mask in segments:
             keys = ref[0, begin : begin + count, :] if keys is None else keys
             scores.append(lax.dot_general(query, keys, NT, preferred_element_type=F32) + mask)
         return scores
 
-    lane = lax.broadcasted_iota(jnp.int32, (n_rows, HD), 1)
+    def step(index, stats):
+        head = index * per_step
+        following = score(head)
+        for i in range(per_step):
+            scores = following
+            if i + 1 < per_step:
+                following = score(head + 1)
+            at = columns_of(head)
+            peak = functools.reduce(jnp.maximum, [lane_max(x) for x in scores])
+            peak = jnp.max(peak, axis=1, keepdims=True)
+            if not first:
+                held_stats = stats_in[at_held, :]
+                before = jnp.max(jnp.where(lane == head, held_stats, -jnp.inf), axis=1, keepdims=True)
+                sums = jnp.where(lane == HD // 2 + head, held_stats, 0.0)
+                sums = jnp.sum(sums, axis=1, keepdims=True)
+                peak = jnp.maximum(before, peak)
+                shrink = jnp.exp2(before - peak)
+            total = None
+            out = None
+            for (ref, keys, begin, count, mask), part in zip(segments, scores):
+                weights = jnp.exp2(part - peak)
+                subtotal = lane_sum(weights)
+                total = subtotal if total is None else total + subtotal
+                values = ref[1, begin : begin + count, :]
+                update = jnp.dot(weights.astype(BF16), values, preferred_element_type=F32)
+                out = update if out is None else out + update
+            total = jnp.sum(total, axis=1, keepdims=True)
+            if not first:
+                total = total + sums * shrink
+                out = out + acc_in[at_held, at] * shrink
+            if last:
+                attended_out[:, at] = (out / total).astype(BF16)
+            else:
+                acc_out[:, at] = out
+                stats = jnp.where(lane == head, peak, stats)
+                stats = jnp.where(lane == HD // 2 + head, total, stats)
+            head = head + 1
+        return stats
+
     stats = jnp.zeros((n_rows, HD), F32)
-    following = score(0)
-    for head in range(heads):
-        scores = following
-        if head + 1 < heads:
-            following = score(head + 1)
-        at = slice(head * HD, (head + 1) * HD)
-        peak = functools.reduce(jnp.maximum, [lane_max(x) for x in scores])
-        peak = jnp.max(peak, axis=1, keepdims=True)
-        if not first:
-            before = stats_in[at_held, head : head + 1]
-            peak = jnp.maximum(before, peak)
-            shrink = jnp.exp2(before - peak)
-        total = None
-        out = None
-        for (ref, keys, begin, count, mask), part in zip(segments, scores):
-            weights = jnp.exp2(part - peak)
-            subtotal = lane_sum(weights)
-            total = subtotal if total is None else total + subtotal
-            values = ref[1, begin : begin + count, :]
-            update = jnp.dot(weights.astype(BF16), values, preferred_element_type=F32)
-            out = update if out is None else out + update
-        total = jnp.sum(total, axis=1, keepdims=True)
-        if not first:
-            total = total + stats_in[at_held, HD // 2 + head : HD // 2 + head + 1] * shrink
-            out = out + acc_in[at_held, at] * shrink
-        if last:
-            attended_out[:, at] = (out / total).astype(BF16)
-        else:
-            acc_out[:, at] = out
-            stats = jnp.where(lane == head, peak, stats)
-            stats = jnp.where(lane == HD // 2 + head, total, stats)
+    if per_step == heads:
+        stats = step(0, stats)
+    else:
+        stats = lax.fori_loop(0, heads // per_step, step, stats)
     if not last:
         stats_out[...] = stats
     if first:

time: 111 us -> 109 us (0.982)
  Pallas kernels: 45.1 us -> 43.5 us
    pallas_call x4, Pallas kernels: 23.1 us -> 21.5 us  [attend(): pl.pallas_call(functools.partial(attend_kernel, first, last, chunk, slots...]
where the time goes in v7:
time: 109 us
  Pallas kernels  43.5 us (40%)
  starting transfers between devices  30.8 us (28%)
  waiting for transfers between devices  25.1 us (23%)
  local copies, waits for them, and re-layouts  5.14 us (5%)
  between operations  2.2 us (2%)
  other arithmetic  1.92 us (2%)
    pallas_call x4, Pallas kernels, attend(): pl.pallas_call(functools.partial(attend_kernel, first, last, chunk, slots...  21.5 us
    ppermute x4, starting transfers between devices, local(): come[k] = [lax.ppermute(p, 'tensor', inward) for p in part[k]]  15.7 us
    pallas_call x3, Pallas kernels, project(): pl.pallas_call(functools.partial(project_kernel, pieces), out_shape=(jax....  14.2 us
    ppermute x2, waiting for transfers between devices, local(): come[0][i] = lax.ppermute(part[0][i], 'tensor', inward)  9.77 us
    ppermute x4, waiting for transfers between devices, local(): come[k] = [lax.ppermute(p, 'tensor', inward) for p in part[k]]  8.16 us
    ppermute x2, waiting for transfers between devices, local(): lax.ppermute(added(f'add_3{i}', part[3][i], across), 'tensor', outward)  5.25 us
    ppermute x2, starting transfers between devices, local(): come[0][i] = lax.ppermute(part[0][i], 'tensor', inward)  5.1 us
    pallas_call x2, Pallas kernels, finish(): pl.pallas_call(kernel, out_shape=(jax.ShapeDtypeStruct((rows_all, columns...  5.1 us
  transfers between devices with their start and end apart: 15, of which 6 were waited for; matrix products, arithmetic and copies ran while one was open for 2% of the time, Pallas kernels for 32%

profile of v7, /device:TPU:0, one launch (start us, length us, event | category | flops | bytes accessed | tf_op | source)
XLA Modules:
  0.0 108.7 jit_solution(17540113171581746565)
XLA Ops:
  1.3 2.0 %pack.1.refs_0_ = bf16[2,1296,128]{2,1,0:T(8,128)(2,1)} custom-call(s32[1]{0:T(128)S(6)} %copy.14.len_ref, bf16[4,1024,128]{2,1,0:T(8,128)(2,1)} %k_ref.1, bf16[4,1024,128]{2,1,0:T(8,128)(2,1)} %v_ref.1, bf16[256,512]{1,0:T(8,128)(2,1)} %nk_ref.1, bf16[256,512]{1,0:T(8,128)(2,1)} %nv_ref.1), custom_call_target="tpu_custom_call" | custom-call | bytes 1327104 | tf_op jit(solution)/shard_map/pack/pallas_call | solution.py:67
  3.8 2.6 %collective-permute-start.1 = (bf16[2,1296,128]{2,1,0:T(8,128)(2,1)}, bf16[2,1296,128]{2,1,0:T(8,128)(2,1)S(1)}, u32[]{:S(2)}, u32[]{:S(2)}) collective-permute-start(bf16[2,1296,128]{2,1,0:T(8,128)(2,1)} %pack.1.refs_0_), channel_id=1, source_target_pairs={{0,2},{2,0},{1,3},{3,1},{4,6},{6,4},{5,7},{7,5},{8,10},{10,8},{9,1... | collective-permute-start | bytes 1990664 | tf_op jit(solution)/shard_map/ppermute | solution.py:393
  7.1 1.9 %fusion = (f32[1024,128]{1,0:T(8,128)S(1)}, f32[1024,128]{1,0:T(8,128)S(1)}) fusion(f32[128]{0:T(128)S(1)} %get-tuple-element.54, f32[128]{0:T(128)S(1)} %get-tuple-element.55, f32[1024]{0:T(1024)S(1)} %add_convert_fusion), kind=kLoop, calls=%fused_computation.2 | loop fusion | flops 262144 | bytes 1053696 | tf_op jit(solution)/shard_map/mul | solution.py:382
  11.2 8.9 %attend_near.1 = (f32[256,1024]{1,0:T(8,128)S(1)}, f32[256,128]{1,0:T(8,128)S(1)}, bf16[256,1024]{1,0:T(8,128)(2,1)S(1)}, bf16[1024,2048]{1,0:T(8,128)(2,1)S(1)}) custom-call(s32[6]{0:T(128)S(1)} %stack.20.place_ref, bf16[256,1024]{1,0:T(8,128)(2,1)S(1)} %copy-done.1, f32[1024,128]{1,0:T(8,128)S(1)} %get-tuple-element.53.cos_ref, ...), custom_call_target="tpu_custom_call" | custom-call | flops 335544320 | bytes 262144 | tf_op jit(solution)/shard_map/attend_near/pallas_call | solution.py:254
  20.1 1.9 %collective-permute-done.1.refs_0_ = bf16[2,1296,128]{2,1,0:T(8,128)(2,1)S(1)} collective-permute-done((bf16[2,1296,128]{2,1,0:T(8,128)(2,1)}, bf16[2,1296,128]{2,1,0:T(8,128)(2,1)S(1)}, u32[]{:S(2)}, u32[]{:S(2)}) %collective-permute-start.1) | collective-permute-done | bytes 663584 | tf_op jit(solution)/shard_map/ppermute | solution.py:393
  22.0 3.1 %attend_far.1 = (f32[128,1024]{1,0:T(8,128)S(1)}, f32[128,128]{1,0:T(8,128)S(1)}) custom-call(s32[6]{0:T(128)S(1)} %stack.20.place_ref, bf16[256,1024]{1,0:T(8,128)(2,1)S(1)} %get-tuple-element.27.q_ref, f32[1024,128]{1,0:T(8,128)S(1)} %get-tuple-element.53.cos_ref, f32[1024,128]{1,0:T(8,128)S(1)} %get-tuple-element.52.sin_ref, ...), custom_call_target="tpu_custom_call" | custom-call | flops 167772160 | bytes 262144 | tf_op jit(solution)/shard_map/attend_far/pallas_call | solution.py:254
  25.1 3.8 %attend_cross.1 = (bf16[128,1024]{1,0:T(8,128)(2,1)S(1)}, bf16[128,2048]{1,0:T(8,128)(2,1)S(1)}) custom-call(s32[6]{0:T(128)S(1)} %stack.20.place_ref, bf16[256,1024]{1,0:T(8,128)(2,1)S(1)} %get-tuple-element.27.q_ref, f32[1024,128]{1,0:T(8,128)S(1)} %get-tuple-element.53.cos_ref, f32[1024,128]{1,0:T(8,128)S(1)} %get-tuple-element.52.sin_ref, ...), custom_call_target="tpu_custom_call" | custom-call | flops 167772160 | bytes 262144 | tf_op jit(solution)/shard_map/attend_cross/pallas_call | solution.py:254
  29.0 3.8 %collective-permute-start.4 = (bf16[128,2048]{1,0:T(8,128)(2,1)S(1)}, bf16[128,2048]{1,0:T(8,128)(2,1)S(1)}, u32[]{:S(2)}, u32[]{:S(2)}) collective-permute-start(bf16[128,2048]{1,0:T(8,128)(2,1)S(1)} %get-tuple-element.35.a_ref), channel_id=1, source_target_pairs={{0,4},{12,8},{1,5},{13,9},{2,6},{14,10},{3,7},{15,11},{16,20},{28,... | collective-permute-start | bytes 1572872 | tf_op jit(solution)/shard_map/ppermute | solution.py:447
  32.7 5.7 %attend_rest.1 = (bf16[128,1024]{1,0:T(8,128)(2,1)S(1)}, bf16[128,2048]{1,0:T(8,128)(2,1)S(1)}) custom-call(s32[6]{0:T(128)S(1)} %stack.20.place_ref, bf16[256,1024]{1,0:T(8,128)(2,1)S(1)} %get-tuple-element.27.q_ref, f32[1024,128]{1,0:T(8,128)S(1)} %get-tuple-element.53.cos_ref, f32[1024,128]{1,0:T(8,128)S(1)} %get-tuple-element.52.sin_ref, ...), custom_call_target="tpu_custom_call" | custom-call | flops 335544320 | bytes 262144 | tf_op jit(solution)/shard_map/attend_rest/pallas_call | solution.py:254
  38.4 1.3 %collective-permute-start.7 = (bf16[128,2048]{1,0:T(8,128)(2,1)S(1)}, bf16[128,2048]{1,0:T(8,128)(2,1)S(1)}, u32[]{:S(2)}, u32[]{:S(2)}) collective-permute-start(bf16[128,2048]{1,0:T(8,128)(2,1)S(1)} %get-tuple-element.42.a_ref), channel_id=1, source_target_pairs={{0,4},{12,8},{1,5},{13,9},{2,6},{14,10},{3,7},{15,11},{16,20},{28,... | collective-permute-start | bytes 1572872 | tf_op jit(solution)/shard_map/ppermute | solution.py:447
  39.7 4.5 %project_1.1 = (bf16[128,2048]{1,0:T(8,128)(2,1)S(1)}, bf16[128,2048]{1,0:T(8,128)(2,1)S(1)}) custom-call(s32[4]{0:T(128)S(1)} %broadcast_select_fusion.order_ref, bf16[128,1024]{1,0:T(8,128)(2,1)S(1)} %get-tuple-element.34.refs_0_, bf16[128,1024]{1,0:T(8,128)(2,1)S(1)} %get-tuple-element.37.refs_1_, bf16[1024,8192]{1,0:T(8,128)(2,1)} %refs_2_.7), custom_call_target="tpu_custom_call" | custom-call | flops 1073741824 | bytes 4194304 | tf_op jit(solution)/shard_map/project_1/pallas_call | solution.py:281
  44.2 1.3 %collective-permute-start.11 = (bf16[128,2048]{1,0:T(8,128)(2,1)S(1)}, bf16[128,2048]{1,0:T(8,128)(2,1)S(1)}, u32[]{:S(2)}, u32[]{:S(2)}) collective-permute-start(bf16[128,2048]{1,0:T(8,128)(2,1)S(1)} %get-tuple-element.47.a_ref), channel_id=1, source_target_pairs={{0,4},{12,8},{1,5},{13,9},{2,6},{14,10},{3,7},{15,11},{16,20},{28,... | collective-permute-start | bytes 1572872 | tf_op jit(solution)/shard_map/ppermute | solution.py:450
  46.4 9.8 %collective-permute-done.7.b_ref = bf16[128,2048]{1,0:T(8,128)(2,1)S(1)} collective-permute-done((bf16[128,2048]{1,0:T(8,128)(2,1)S(1)}, bf16[128,2048]{1,0:T(8,128)(2,1)S(1)}, u32[]{:S(2)}, u32[]{:S(2)}) %collective-permute-start.7) | collective-permute-done | bytes 524320 | tf_op jit(solution)/shard_map/ppermute | solution.py:447
  57.0 7.2 %collective-permute-start.5 = (bf16[128,2048]{1,0:T(8,128)(2,1)S(1)}, bf16[128,2048]{1,0:T(8,128)(2,1)S(1)}, u32[]{:S(2)}, u32[]{:S(2)}) collective-permute-start(bf16[128,2048]{1,0:T(8,128)(2,1)S(1)} %get-tuple-element.41.a_ref), channel_id=1, source_target_pairs={{0,4},{12,8},{1,5},{13,9},{2,6},{14,10},{3,7},{15,11},{16,20},{28,... | collective-permute-start | bytes 1572872 | tf_op jit(solution)/shard_map/ppermute | solution.py:450
  64.2 5.3 %project_2.1 = (bf16[128,2048]{1,0:T(8,128)(2,1)S(1)}, bf16[128,2048]{1,0:T(8,128)(2,1)}) custom-call(s32[4]{0:T(128)S(1)} %broadcast_select_fusion.order_ref, bf16[128,1024]{1,0:T(8,128)(2,1)S(1)} %get-tuple-element.34.refs_0_, bf16[128,1024]{1,0:T(8,128)(2,1)S(1)} %get-tuple-element.37.refs_1_, bf16[1024,8192]{1,0:T(8,128)(2,1)} %refs_2_.7), custom_call_target="tpu_custom_call" | custom-call | flops 1073741824 | bytes 4194304 | tf_op jit(solution)/shard_map/project_2/pallas_call | solution.py:281
  70.8 4.5 %project_3.1 = (bf16[128,2048]{1,0:T(8,128)(2,1)S(1)}, bf16[128,2048]{1,0:T(8,128)(2,1)S(1)}) custom-call(s32[4]{0:T(128)S(1)} %broadcast_select_fusion.order_ref, bf16[128,1024]{1,0:T(8,128)(2,1)S(1)} %get-tuple-element.34.refs_0_, bf16[128,1024]{1,0:T(8,128)(2,1)S(1)} %get-tuple-element.37.refs_1_, bf16[1024,8192]{1,0:T(8,128)(2,1)} %refs_2_.7), custom_call_target="tpu_custom_call" | custom-call | flops 1073741824 | bytes 4194304 | tf_op jit(solution)/shard_map/project_3/pallas_call | solution.py:281
  75.4 1.5 %collective-permute-start.12 = (bf16[128,2048]{1,0:T(8,128)(2,1)S(1)}, bf16[128,2048]{1,0:T(8,128)(2,1)}, u32[]{:S(2)}, u32[]{:S(2)}) collective-permute-start(bf16[128,2048]{1,0:T(8,128)(2,1)S(1)} %add_10.1), channel_id=1, source_target_pairs={{4,8},{8,4},{5,9},{9,5},{6,10},{10,6},{7,11},{11,7},{20,24},{24,20... | collective-permute-start | bytes 1572872 | tf_op jit(solution)/shard_map/ppermute | solution.py:456
  78.6 5.9 %collective-permute-start.3 = (bf16[128,2048]{1,0:T(8,128)(2,1)}, bf16[128,2048]{1,0:T(8,128)(2,1)}, u32[]{:S(2)}, u32[]{:S(2)}) collective-permute-start(bf16[128,2048]{1,0:T(8,128)(2,1)} %get-tuple-element.39.refs_2_), channel_id=1, source_target_pairs={{0,4},{12,8},{1,5},{13,9},{2,6},{14,10},{3,7},{15,11},{16,20},{28,... | collective-permute-start | bytes 1572872 | tf_op jit(solution)/shard_map/ppermute | solution.py:450
  84.6 1.5 %collective-permute-start.6 = (bf16[128,2048]{1,0:T(8,128)(2,1)S(1)}, bf16[128,2048]{1,0:T(8,128)(2,1)}, u32[]{:S(2)}, u32[]{:S(2)}) collective-permute-start(bf16[128,2048]{1,0:T(8,128)(2,1)S(1)} %add_11.1), channel_id=1, source_target_pairs={{4,8},{8,4},{5,9},{9,5},{6,10},{10,6},{7,11},{11,7},{20,24},{24,20... | collective-permute-start | bytes 1572872 | tf_op jit(solution)/shard_map/ppermute | solution.py:456
  86.3 3.6 %collective-permute-done.10.refs_3_ = bf16[128,2048]{1,0:T(8,128)(2,1)S(1)} collective-permute-done((bf16[128,2048]{1,0:T(8,128)(2,1)S(1)}, bf16[128,2048]{1,0:T(8,128)(2,1)S(1)}, u32[]{:S(2)}, u32[]{:S(2)}) %collective-permute-start.10) | collective-permute-done | bytes 524320 | tf_op jit(solution)/shard_map/ppermute | solution.py:450
  94.1 2.5 %finish_0.1 = (bf16[256,2048]{1,0:T(8,128)(2,1)}, f32[16,256]{1,0:T(8,128)}) custom-call(s32[1]{0:T(128)} %bitcast.refs_0_, bf16[128,2048]{1,0:T(8,128)(2,1)S(1)} %get-tuple-element.45.a_ref.refs_1_, bf16[128,2048]{1,0:T(8,128)(2,1)S(1)} %copy-done.3, bf16[128,2048]{1,0:T(8,128)(2,1)S(1)} %copy-done.5, bf16[128,2048]{1,0:T(8,128)(2,1)} %collective-permute-done.12.refs_4_, ...), custom_call_target="tpu_custom_call" | custom-call | flops 1572864 | bytes 3145728 | tf_op jit(solution)/shard_map/finish_0/pallas_call | solution.py:341
  96.6 4.3 %collective-permute-done.3.refs_3_ = bf16[128,2048]{1,0:T(8,128)(2,1)} collective-permute-done((bf16[128,2048]{1,0:T(8,128)(2,1)}, bf16[128,2048]{1,0:T(8,128)(2,1)}, u32[]{:S(2)}, u32[]{:S(2)}) %collective-permute-start.3) | collective-permute-done | bytes 524320 | tf_op jit(solution)/shard_map/ppermute | solution.py:450
  100.8 5.2 %collective-permute-done.9.refs_5_ = bf16[128,2048]{1,0:T(8,128)(2,1)} collective-permute-done((bf16[128,2048]{1,0:T(8,128)(2,1)S(1)}, bf16[128,2048]{1,0:T(8,128)(2,1)}, u32[]{:S(2)}, u32[]{:S(2)}) %collective-permute-start.9) | collective-permute-done | bytes 524320 | tf_op jit(solution)/shard_map/ppermute | solution.py:457
  106.1 2.6 %finish_1.1 = (bf16[256,2048]{1,0:T(8,128)(2,1)}, f32[16,256]{1,0:T(8,128)}) custom-call(s32[1]{0:T(128)} %bitcast.refs_0_, bf16[128,2048]{1,0:T(8,128)(2,1)S(1)} %get-tuple-element.38.a_ref.refs_1_, bf16[128,2048]{1,0:T(8,128)(2,1)} %get-tuple-element.39.refs_2_, ...), custom_call_target="tpu_custom_call", output_to_operand_aliasing={{0}: (6, {}), {1}: (7, {})} | custom-call | flops 1572864 | bytes 3145728 | tf_op jit(solution)/shard_map/finish_1/pallas_call | solution.py:341
  (39 shorter events, 12.0 us)
Async XLA Ops:
  3.2 5.8 %collective-permute-start = (bf16[2,1296,128]{2,1,0:T(8,128)(2,1)}, bf16[2,1296,128]{2,1,0:T(8,128)(2,1)S(1)}, u32[]{:S(2)}, u32[]{:S(2)}) collective-permute-start(bf16[2,1296,128]{2,1,0:T(8,128)(2,1)} %pack.1.refs_0_), channel_id=1, source_target_pairs={{0,1},{1,0},{2,3},{3,2},{4,5},{5,4},{6,7},{7,6},{8,9},{9,8},{10,11... | collective-permute-start | bytes 1990664 | tf_op jit(solution)/shard_map/ppermute | solution.py:394
  3.8 18.3 %collective-permute-start.1 = (bf16[2,1296,128]{2,1,0:T(8,128)(2,1)}, bf16[2,1296,128]{2,1,0:T(8,128)(2,1)S(1)}, u32[]{:S(2)}, u32[]{:S(2)}) collective-permute-start(bf16[2,1296,128]{2,1,0:T(8,128)(2,1)} %pack.1.refs_0_), channel_id=1, source_target_pairs={{0,2},{2,0},{1,3},{3,1},{4,6},{6,4},{5,7},{7,5},{8,10},{10,8},{9,1... | collective-permute-start | bytes 1990664 | tf_op jit(solution)/shard_map/ppermute | solution.py:393
  9.0 1.1 %copy-start = (bf16[2,1296,128]{2,1,0:T(8,128)(2,1)S(1)}, bf16[2,1296,128]{2,1,0:T(8,128)(2,1)}, u32[]{:S(2)}) copy-start(bf16[2,1296,128]{2,1,0:T(8,128)(2,1)} %pack.1.refs_0_) | copy-start | bytes 1990660
  10.1 1.0 copy-start.1
  22.0 3.1 %collective-permute-start.2 = (bf16[2,1296,128]{2,1,0:T(8,128)(2,1)S(1)}, bf16[2,1296,128]{2,1,0:T(8,128)(2,1)S(1)}, u32[]{:S(2)}, u32[]{:S(2)}) collective-permute-start(bf16[2,1296,128]{2,1,0:T(8,128)(2,1)S(1)} %collective-permute-done.1.refs_0_), channel_id=1, source_target_pairs={{0,1},{1,0},{2,3},{3,2},{4,5},{5,4},{6,7},{7,6},{8,9},{9,8},{10,11... | collective-permute-start | bytes 1990664 | tf_op jit(solution)/shard_map/ppermute | solution.py:409
  29.0 16.6 %collective-permute-start.4 = (bf16[128,2048]{1,0:T(8,128)(2,1)S(1)}, bf16[128,2048]{1,0:T(8,128)(2,1)S(1)}, u32[]{:S(2)}, u32[]{:S(2)}) collective-permute-start(bf16[128,2048]{1,0:T(8,128)(2,1)S(1)} %get-tuple-element.35.a_ref), channel_id=1, source_target_pairs={{0,4},{12,8},{1,5},{13,9},{2,6},{14,10},{3,7},{15,11},{16,20},{28,... | collective-permute-start | bytes 1572872 | tf_op jit(solution)/shard_map/ppermute | solution.py:447
  38.4 17.8 %collective-permute-start.7 = (bf16[128,2048]{1,0:T(8,128)(2,1)S(1)}, bf16[128,2048]{1,0:T(8,128)(2,1)S(1)}, u32[]{:S(2)}, u32[]{:S(2)}) collective-permute-start(bf16[128,2048]{1,0:T(8,128)(2,1)S(1)} %get-tuple-element.42.a_ref), channel_id=1, source_target_pairs={{0,4},{12,8},{1,5},{13,9},{2,6},{14,10},{3,7},{15,11},{16,20},{28,... | collective-permute-start | bytes 1572872 | tf_op jit(solution)/shard_map/ppermute | solution.py:447
  44.2 31.1 %collective-permute-start.11 = (bf16[128,2048]{1,0:T(8,128)(2,1)S(1)}, bf16[128,2048]{1,0:T(8,128)(2,1)S(1)}, u32[]{:S(2)}, u32[]{:S(2)}) collective-permute-start(bf16[128,2048]{1,0:T(8,128)(2,1)S(1)} %get-tuple-element.47.a_ref), channel_id=1, source_target_pairs={{0,4},{12,8},{1,5},{13,9},{2,6},{14,10},{3,7},{15,11},{16,20},{28,... | collective-permute-start | bytes 1572872 | tf_op jit(solution)/shard_map/ppermute | solution.py:450
  45.7 31.2 %collective-permute-start.13 = (bf16[128,2048]{1,0:T(8,128)(2,1)S(1)}, bf16[128,2048]{1,0:T(8,128)(2,1)S(1)}, u32[]{:S(2)}, u32[]{:S(2)}) collective-permute-start(bf16[128,2048]{1,0:T(8,128)(2,1)S(1)} %add_00.1), channel_id=1, source_target_pairs={{4,8},{8,4},{5,9},{9,5},{6,10},{10,6},{7,11},{11,7},{20,24},{24,20... | collective-permute-start | bytes 1572872 | tf_op jit(solution)/shard_map/ppermute | solution.py:455
  56.3 28.3 %collective-permute-start.8 = (bf16[128,2048]{1,0:T(8,128)(2,1)S(1)}, bf16[128,2048]{1,0:T(8,128)(2,1)S(1)}, u32[]{:S(2)}, u32[]{:S(2)}) collective-permute-start(bf16[128,2048]{1,0:T(8,128)(2,1)S(1)} %add_01.1), channel_id=1, source_target_pairs={{4,8},{8,4},{5,9},{9,5},{6,10},{10,6},{7,11},{11,7},{20,24},{24,20... | collective-permute-start | bytes 1572872 | tf_op jit(solution)/shard_map/ppermute | solution.py:455
  57.0 21.6 %collective-permute-start.5 = (bf16[128,2048]{1,0:T(8,128)(2,1)S(1)}, bf16[128,2048]{1,0:T(8,128)(2,1)S(1)}, u32[]{:S(2)}, u32[]{:S(2)}) collective-permute-start(bf16[128,2048]{1,0:T(8,128)(2,1)S(1)} %get-tuple-element.41.a_ref), channel_id=1, source_target_pairs={{0,4},{12,8},{1,5},{13,9},{2,6},{14,10},{3,7},{15,11},{16,20},{28,... | collective-permute-start | bytes 1572872 | tf_op jit(solution)/shard_map/ppermute | solution.py:450
  69.5 16.8 %copy-start.2 = (bf16[128,2048]{1,0:T(8,128)(2,1)}, bf16[128,2048]{1,0:T(8,128)(2,1)S(1)}, u32[]{:S(2)}) copy-start(bf16[128,2048]{1,0:T(8,128)(2,1)S(1)} %get-tuple-element.46.refs_2_) | copy-start | bytes 1572868
  69.5 20.4 %collective-permute-start.10 = (bf16[128,2048]{1,0:T(8,128)(2,1)S(1)}, bf16[128,2048]{1,0:T(8,128)(2,1)S(1)}, u32[]{:S(2)}, u32[]{:S(2)}) collective-permute-start(bf16[128,2048]{1,0:T(8,128)(2,1)S(1)} %get-tuple-element.46.refs_2_), channel_id=1, source_target_pairs={{0,4},{12,8},{1,5},{13,9},{2,6},{14,10},{3,7},{15,11},{16,20},{28,... | collective-permute-start | bytes 1572872 | tf_op jit(solution)/shard_map/ppermute | solution.py:450
  75.4 16.6 %collective-permute-start.12 = (bf16[128,2048]{1,0:T(8,128)(2,1)S(1)}, bf16[128,2048]{1,0:T(8,128)(2,1)}, u32[]{:S(2)}, u32[]{:S(2)}) collective-permute-start(bf16[128,2048]{1,0:T(8,128)(2,1)S(1)} %add_10.1), channel_id=1, source_target_pairs={{4,8},{8,4},{5,9},{9,5},{6,10},{10,6},{7,11},{11,7},{20,24},{24,20... | collective-permute-start | bytes 1572872 | tf_op jit(solution)/shard_map/ppermute | solution.py:456
  77.0 15.0 %collective-permute-start.14 = (bf16[128,2048]{1,0:T(8,128)(2,1)S(1)}, bf16[128,2048]{1,0:T(8,128)(2,1)}, u32[]{:S(2)}, u32[]{:S(2)}) collective-permute-start(bf16[128,2048]{1,0:T(8,128)(2,1)S(1)} %add_30.1), channel_id=1, source_target_pairs={{4,0},{8,12},{5,1},{9,13},{6,2},{10,14},{7,3},{11,15},{20,16},{24,... | collective-permute-start | bytes 1572872 | tf_op jit(solution)/shard_map/ppermute | solution.py:457
  78.6 22.2 %collective-permute-start.3 = (bf16[128,2048]{1,0:T(8,128)(2,1)}, bf16[128,2048]{1,0:T(8,128)(2,1)}, u32[]{:S(2)}, u32[]{:S(2)}) collective-permute-start(bf16[128,2048]{1,0:T(8,128)(2,1)} %get-tuple-element.39.refs_2_), channel_id=1, source_target_pairs={{0,4},{12,8},{1,5},{13,9},{2,6},{14,10},{3,7},{15,11},{16,20},{28,... | collective-permute-start | bytes 1572872 | tf_op jit(solution)/shard_map/ppermute | solution.py:450
  84.6 16.2 %collective-permute-start.6 = (bf16[128,2048]{1,0:T(8,128)(2,1)S(1)}, bf16[128,2048]{1,0:T(8,128)(2,1)}, u32[]{:S(2)}, u32[]{:S(2)}) collective-permute-start(bf16[128,2048]{1,0:T(8,128)(2,1)S(1)} %add_11.1), channel_id=1, source_target_pairs={{4,8},{8,4},{5,9},{9,5},{6,10},{10,6},{7,11},{11,7},{20,24},{24,20... | collective-permute-start | bytes 1572872 | tf_op jit(solution)/shard_map/ppermute | solution.py:456
  89.9 0.8 copy-start.4
  90.7 15.4 %collective-permute-start.9 = (bf16[128,2048]{1,0:T(8,128)(2,1)S(1)}, bf16[128,2048]{1,0:T(8,128)(2,1)}, u32[]{:S(2)}, u32[]{:S(2)}) collective-permute-start(bf16[128,2048]{1,0:T(8,128)(2,1)S(1)} %add_31.1), channel_id=1, source_target_pairs={{4,0},{8,12},{5,1},{9,13},{6,2},{10,14},{7,3},{11,15},{20,16},{24,... | collective-permute-start | bytes 1572872 | tf_op jit(solution)/shard_map/ppermute | solution.py:457
  92.0 1.0 copy-start.3
  93.1 1.0 copy-start.5

commit v8 on v7

--- a/solution.py
+++ b/solution.py
@@ -440,20 +440,23 @@
             held=cut,
         )
         part = [first_part]
-        for k in range(1, 4):
-            part.append(project(f"project_{k}", order, k, attended, out_weight, columns))
+        part.append(project("project_1", order, 1, attended, out_weight, columns))
+        third = project("project_3", order, 3, attended, out_weight, columns)
+        rest = [attended[0], after(attended[1], third[0])]
+        part += [project("project_2", order, 2, rest, out_weight, columns), third]
         come = [[None, None] for k in range(3)]
         for i in range(2):
             come[0][i] = lax.ppermute(part[0][i], "tensor", inward)
         part[1] = [part[1][0], after(part[1][1], come[0][0])]
-        for k in (1, 2):
-            come[k] = [lax.ppermute(p, "tensor", inward) for p in part[k]]
+        come[1] = [lax.ppermute(p, "tensor", inward) for p in part[1]]
+        part[2] = [part[2][0], after(part[2][1], come[1][0])]
+        come[2] = [lax.ppermute(p, "tensor", inward) for p in part[2]]
         done = None
-        previous = attended[1]
+        previous = part[1][0]
         for i in range(2):
             previous = added(f"add_0{i}", part[0][i], after(come[0][i], previous))
             across = lax.ppermute(previous, "tensor", middle)
-            second = lax.ppermute(added(f"add_1{i}", part[1][i], come[1][i]), "tensor", middle)
+            second = lax.ppermute(added(f"add_1{i}", part[1][i], come[1][i] if i == 0 else after(come[1][i], back)), "tensor", middle)
             back = lax.ppermute(added(f"add_3{i}", part[3][i], across), "tensor", outward)
             parts = [part[3][i], part[2][i], come[2][i], second, back]
             done = finish(f"finish_{i}", flag, parts, i * cut, rows, done)

time: 109 us -> 104 us (0.954)
  waiting for transfers between devices: 25.1 us -> 16 us
  starting transfers between devices: 30.8 us -> 35.8 us
  local copies, waits for them, and re-layouts: 5.14 us -> 3.93 us
    ppermute x2, waiting for transfers between devices: 9.77 us -> 0.71 us  [local(): come[0][i] = lax.ppermute(part[0][i], 'tensor', inward)]
    ppermute x2, waiting for transfers between devices: 5.25 us -> 0.01 us  [local(): lax.ppermute(added(f'add_3{i}', part[3][i], across), 'tensor', outward)]
    ppermute x6, waiting for transfers between devices: 8.16 us -> 13.4 us  [the longest x2 13.4 us: local(): come[2] = [lax.ppermute(p, 'tensor', inward) for p in part[2]]]
    ppermute x6, starting transfers between devices: 18.7 us -> 23.6 us  [the longest x2 13.1 us: local(): come[1] = [lax.ppermute(p, 'tensor', inward) for p in part[1]]]
    unnamed x12 -> x8, local copies, waits for them, and re-layouts: 5.02 us -> 3.82 us
  transfers between devices with their start and end apart: 15 -> 15, of which waited for: 6 -> 4; matrix products, arithmetic and copies ran while one was open for 2% -> 2% of each run, Pallas kernels for 32% -> 34%
where the time goes in v8:
time: 104 us; the launch traced here: 103 us
  Pallas kernels  43.5 us (42%)
  starting transfers between devices  35.8 us (34%)
  waiting for transfers between devices  16 us (15%)
  local copies, waits for them, and re-layouts  3.93 us (4%)
  between operations  2.17 us (2%)
  other arithmetic  1.92 us (2%)
    pallas_call x4, Pallas kernels, attend(): pl.pallas_call(functools.partial(attend_kernel, first, last, chunk, slots...  21.5 us
    pallas_call x3, Pallas kernels, project(): pl.pallas_call(functools.partial(project_kernel, pieces), out_shape=(jax....  14.2 us
    ppermute x2, waiting for transfers between devices, local(): come[2] = [lax.ppermute(p, 'tensor', inward) for p in part[2]]  13.4 us
    ppermute x2, starting transfers between devices, local(): come[1] = [lax.ppermute(p, 'tensor', inward) for p in part[1]]  13.1 us
    ppermute x2, starting transfers between devices, local(): come[2] = [lax.ppermute(p, 'tensor', inward) for p in part[2]]  7.61 us
    ppermute x2, starting transfers between devices, local(): come[0][i] = lax.ppermute(part[0][i], 'tensor', inward)  5.1 us
    pallas_call x2, Pallas kernels, finish(): pl.pallas_call(kernel, out_shape=(jax.ShapeDtypeStruct((rows_all, columns...  5.08 us
    unnamed x8, local copies, waits for them, and re-layouts  3.82 us
  transfers between devices with their start and end apart: 15, of which 4 were waited for; matrix products, arithmetic and copies ran while one was open for 2% of the time, Pallas kernels for 34%

profile of v8, /device:TPU:0, one launch (start us, length us, event | category | flops | bytes accessed | tf_op | source)
XLA Modules:
  0.0 103.3 jit_solution(9286687273306160422)
XLA Ops:
  1.3 2.0 %pack.1.refs_0_ = bf16[2,1296,128]{2,1,0:T(8,128)(2,1)} custom-call(s32[1]{0:T(128)S(6)} %copy.14.len_ref, bf16[4,1024,128]{2,1,0:T(8,128)(2,1)} %k_ref.1, bf16[4,1024,128]{2,1,0:T(8,128)(2,1)} %v_ref.1, bf16[256,512]{1,0:T(8,128)(2,1)} %nk_ref.1, bf16[256,512]{1,0:T(8,128)(2,1)} %nv_ref.1), custom_call_target="tpu_custom_call" | custom-call | bytes 1327104 | tf_op jit(solution)/shard_map/pack/pallas_call | solution.py:67
  3.8 2.6 %collective-permute-start.1 = (bf16[2,1296,128]{2,1,0:T(8,128)(2,1)}, bf16[2,1296,128]{2,1,0:T(8,128)(2,1)S(1)}, u32[]{:S(2)}, u32[]{:S(2)}) collective-permute-start(bf16[2,1296,128]{2,1,0:T(8,128)(2,1)} %pack.1.refs_0_), channel_id=1, source_target_pairs={{0,2},{2,0},{1,3},{3,1},{4,6},{6,4},{5,7},{7,5},{8,10},{10,8},{9,1... | collective-permute-start | bytes 1990664 | tf_op jit(solution)/shard_map/ppermute | solution.py:393
  7.1 1.9 %fusion = (f32[1024,128]{1,0:T(8,128)S(1)}, f32[1024,128]{1,0:T(8,128)S(1)}) fusion(f32[128]{0:T(128)S(1)} %get-tuple-element.60, f32[128]{0:T(128)S(1)} %get-tuple-element.61, f32[1024]{0:T(1024)S(1)} %add_convert_fusion), kind=kLoop, calls=%fused_computation.2 | loop fusion | flops 262144 | bytes 1053696 | tf_op jit(solution)/shard_map/mul | solution.py:382
  11.2 8.9 %attend_near.1 = (f32[256,1024]{1,0:T(8,128)S(1)}, f32[256,128]{1,0:T(8,128)S(1)}, bf16[256,1024]{1,0:T(8,128)(2,1)S(1)}, bf16[1024,2048]{1,0:T(8,128)(2,1)S(1)}) custom-call(s32[6]{0:T(128)S(1)} %stack.20.place_ref, bf16[256,1024]{1,0:T(8,128)(2,1)S(1)} %copy-done.1, f32[1024,128]{1,0:T(8,128)S(1)} %get-tuple-element.59.cos_ref, ...), custom_call_target="tpu_custom_call" | custom-call | flops 335544320 | bytes 262144 | tf_op jit(solution)/shard_map/attend_near/pallas_call | solution.py:254
  20.1 1.9 %collective-permute-done.1.refs_0_ = bf16[2,1296,128]{2,1,0:T(8,128)(2,1)S(1)} collective-permute-done((bf16[2,1296,128]{2,1,0:T(8,128)(2,1)}, bf16[2,1296,128]{2,1,0:T(8,128)(2,1)S(1)}, u32[]{:S(2)}, u32[]{:S(2)}) %collective-permute-start.1) | collective-permute-done | bytes 663584 | tf_op jit(solution)/shard_map/ppermute | solution.py:393
  22.0 3.1 %attend_far.1 = (f32[128,1024]{1,0:T(8,128)S(1)}, f32[128,128]{1,0:T(8,128)S(1)}) custom-call(s32[6]{0:T(128)S(1)} %stack.20.place_ref, bf16[256,1024]{1,0:T(8,128)(2,1)S(1)} %get-tuple-element.30.q_ref, f32[1024,128]{1,0:T(8,128)S(1)} %get-tuple-element.59.cos_ref, f32[1024,128]{1,0:T(8,128)S(1)} %get-tuple-element.58.sin_ref, ...), custom_call_target="tpu_custom_call" | custom-call | flops 167772160 | bytes 262144 | tf_op jit(solution)/shard_map/attend_far/pallas_call | solution.py:254
  25.1 3.8 %attend_cross.1 = (bf16[128,1024]{1,0:T(8,128)(2,1)S(1)}, bf16[128,2048]{1,0:T(8,128)(2,1)S(1)}) custom-call(s32[6]{0:T(128)S(1)} %stack.20.place_ref, bf16[256,1024]{1,0:T(8,128)(2,1)S(1)} %get-tuple-element.30.q_ref, f32[1024,128]{1,0:T(8,128)S(1)} %get-tuple-element.59.cos_ref, f32[1024,128]{1,0:T(8,128)S(1)} %get-tuple-element.58.sin_ref, ...), custom_call_target="tpu_custom_call" | custom-call | flops 167772160 | bytes 262144 | tf_op jit(solution)/shard_map/attend_cross/pallas_call | solution.py:254
  29.0 3.8 %collective-permute-start.5 = (bf16[128,2048]{1,0:T(8,128)(2,1)S(1)}, bf16[128,2048]{1,0:T(8,128)(2,1)S(1)}, u32[]{:S(2)}, u32[]{:S(2)}) collective-permute-start(bf16[128,2048]{1,0:T(8,128)(2,1)S(1)} %get-tuple-element.38.a_ref), channel_id=1, source_target_pairs={{0,4},{12,8},{1,5},{13,9},{2,6},{14,10},{3,7},{15,11},{16,20},{28,... | collective-permute-start | bytes 1572872 | tf_op jit(solution)/shard_map/ppermute | solution.py:449
  32.7 5.7 %attend_rest.1 = (bf16[128,1024]{1,0:T(8,128)(2,1)S(1)}, bf16[128,2048]{1,0:T(8,128)(2,1)S(1)}) custom-call(s32[6]{0:T(128)S(1)} %stack.20.place_ref, bf16[256,1024]{1,0:T(8,128)(2,1)S(1)} %get-tuple-element.30.q_ref, f32[1024,128]{1,0:T(8,128)S(1)} %get-tuple-element.59.cos_ref, f32[1024,128]{1,0:T(8,128)S(1)} %get-tuple-element.58.sin_ref, ...), custom_call_target="tpu_custom_call" | custom-call | flops 335544320 | bytes 262144 | tf_op jit(solution)/shard_map/attend_rest/pallas_call | solution.py:254
  38.4 1.3 %collective-permute-start.10 = (bf16[128,2048]{1,0:T(8,128)(2,1)S(1)}, bf16[128,2048]{1,0:T(8,128)(2,1)S(1)}, u32[]{:S(2)}, u32[]{:S(2)}) collective-permute-start(bf16[128,2048]{1,0:T(8,128)(2,1)S(1)} %get-tuple-element.51.a_ref), channel_id=1, source_target_pairs={{0,4},{12,8},{1,5},{13,9},{2,6},{14,10},{3,7},{15,11},{16,20},{28,... | collective-permute-start | bytes 1572872 | tf_op jit(solution)/shard_map/ppermute | solution.py:449
  39.7 4.5 %project_1.1 = (bf16[128,2048]{1,0:T(8,128)(2,1)S(1)}, bf16[128,2048]{1,0:T(8,128)(2,1)S(1)}) custom-call(s32[4]{0:T(128)S(1)} %broadcast_select_fusion.order_ref, bf16[128,1024]{1,0:T(8,128)(2,1)S(1)} %get-tuple-element.37.refs_0_, bf16[128,1024]{1,0:T(8,128)(2,1)S(1)} %get-tuple-element.43.refs_1_, bf16[1024,8192]{1,0:T(8,128)(2,1)} %refs_2_.7), custom_call_target="tpu_custom_call" | custom-call | flops 1073741824 | bytes 4194304 | tf_op jit(solution)/shard_map/project_1/pallas_call | solution.py:281
  45.8 7.2 %collective-permute-start.3 = (bf16[128,2048]{1,0:T(8,128)(2,1)S(1)}, bf16[128,2048]{1,0:T(8,128)(2,1)S(1)}, u32[]{:S(2)}, u32[]{:S(2)}) collective-permute-start(bf16[128,2048]{1,0:T(8,128)(2,1)S(1)} %get-tuple-element.45.a_ref), channel_id=1, source_target_pairs={{0,4},{12,8},{1,5},{13,9},{2,6},{14,10},{3,7},{15,11},{16,20},{28,... | collective-permute-start | bytes 1572872 | tf_op jit(solution)/shard_map/ppermute | solution.py:451
  53.0 4.5 %project_3.1 = (bf16[128,2048]{1,0:T(8,128)(2,1)S(1)}, bf16[128,2048]{1,0:T(8,128)(2,1)S(1)}) custom-call(s32[4]{0:T(128)S(1)} %broadcast_select_fusion.order_ref, bf16[128,1024]{1,0:T(8,128)(2,1)S(1)} %get-tuple-element.37.refs_0_, bf16[128,1024]{1,0:T(8,128)(2,1)S(1)} %get-tuple-element.43.refs_1_, bf16[1024,8192]{1,0:T(8,128)(2,1)} %refs_2_.7), custom_call_target="tpu_custom_call" | custom-call | flops 1073741824 | bytes 4194304 | tf_op jit(solution)/shard_map/project_3/pallas_call | solution.py:281
  58.3 5.9 %collective-permute-start.6 = (bf16[128,2048]{1,0:T(8,128)(2,1)S(1)}, bf16[128,2048]{1,0:T(8,128)(2,1)S(1)}, u32[]{:S(2)}, u32[]{:S(2)}) collective-permute-start(bf16[128,2048]{1,0:T(8,128)(2,1)S(1)} %get-tuple-element.48.a_ref), channel_id=1, source_target_pairs={{0,4},{12,8},{1,5},{13,9},{2,6},{14,10},{3,7},{15,11},{16,20},{28,... | collective-permute-start | bytes 1572872 | tf_op jit(solution)/shard_map/ppermute | solution.py:451
  64.3 1.3 %collective-permute-start.8 = (bf16[128,2048]{1,0:T(8,128)(2,1)S(1)}, bf16[128,2048]{1,0:T(8,128)(2,1)S(1)}, u32[]{:S(2)}, u32[]{:S(2)}) collective-permute-start(bf16[128,2048]{1,0:T(8,128)(2,1)S(1)} %add_30.1), channel_id=1, source_target_pairs={{4,0},{8,12},{5,1},{9,13},{6,2},{10,14},{7,3},{11,15},{20,16},{24,... | collective-permute-start | bytes 1572872 | tf_op jit(solution)/shard_map/ppermute | solution.py:460
  65.7 5.2 %project_2.1 = (bf16[128,2048]{1,0:T(8,128)(2,1)}, bf16[128,2048]{1,0:T(8,128)(2,1)S(1)}) custom-call(s32[4]{0:T(128)S(1)} %broadcast_select_fusion.order_ref, bf16[128,1024]{1,0:T(8,128)(2,1)S(1)} %get-tuple-element.37.refs_0_, bf16[128,1024]{1,0:T(8,128)(2,1)S(1)} %get-tuple-element.43.refs_1_, bf16[1024,8192]{1,0:T(8,128)(2,1)} %refs_2_.7), custom_call_target="tpu_custom_call" | custom-call | flops 1073741824 | bytes 4194304 | tf_op jit(solution)/shard_map/project_2/pallas_call | solution.py:281
  70.9 5.4 %collective-permute-start.13 = (bf16[128,2048]{1,0:T(8,128)(2,1)}, bf16[128,2048]{1,0:T(8,128)(2,1)}, u32[]{:S(2)}, u32[]{:S(2)}) collective-permute-start(bf16[128,2048]{1,0:T(8,128)(2,1)} %get-tuple-element.53.refs_2_), channel_id=1, source_target_pairs={{0,4},{12,8},{1,5},{13,9},{2,6},{14,10},{3,7},{15,11},{16,20},{28,... | collective-permute-start | bytes 1572872 | tf_op jit(solution)/shard_map/ppermute | solution.py:453
  76.4 1.5 %collective-permute-start.14 = (bf16[128,2048]{1,0:T(8,128)(2,1)S(1)}, bf16[128,2048]{1,0:T(8,128)(2,1)}, u32[]{:S(2)}, u32[]{:S(2)}) collective-permute-start(bf16[128,2048]{1,0:T(8,128)(2,1)S(1)} %add_10.1), channel_id=1, source_target_pairs={{4,8},{8,4},{5,9},{9,5},{6,10},{10,6},{7,11},{11,7},{20,24},{24,20... | collective-permute-start | bytes 1572872 | tf_op jit(solution)/shard_map/ppermute | solution.py:459
  77.9 2.2 %collective-permute-start.4 = (bf16[128,2048]{1,0:T(8,128)(2,1)S(1)}, bf16[128,2048]{1,0:T(8,128)(2,1)}, u32[]{:S(2)}, u32[]{:S(2)}) collective-permute-start(bf16[128,2048]{1,0:T(8,128)(2,1)S(1)} %get-tuple-element.46.refs_2_), channel_id=1, source_target_pairs={{0,4},{12,8},{1,5},{13,9},{2,6},{14,10},{3,7},{15,11},{16,20},{28,... | collective-permute-start | bytes 1572872 | tf_op jit(solution)/shard_map/ppermute | solution.py:453
  82.3 1.5 %collective-permute-start.9 = (bf16[128,2048]{1,0:T(8,128)(2,1)S(1)}, bf16[128,2048]{1,0:T(8,128)(2,1)}, u32[]{:S(2)}, u32[]{:S(2)}) collective-permute-start(bf16[128,2048]{1,0:T(8,128)(2,1)S(1)} %add_11.1), channel_id=1, source_target_pairs={{4,8},{8,4},{5,9},{9,5},{6,10},{10,6},{7,11},{11,7},{20,24},{24,20... | collective-permute-start | bytes 1572872 | tf_op jit(solution)/shard_map/ppermute | solution.py:459
  83.8 6.2 %collective-permute-done.13.refs_3_ = bf16[128,2048]{1,0:T(8,128)(2,1)} collective-permute-done((bf16[128,2048]{1,0:T(8,128)(2,1)}, bf16[128,2048]{1,0:T(8,128)(2,1)}, u32[]{:S(2)}, u32[]{:S(2)}) %collective-permute-start.13) | collective-permute-done | bytes 524320 | tf_op jit(solution)/shard_map/ppermute | solution.py:453
  91.0 2.5 %finish_0.1 = (bf16[256,2048]{1,0:T(8,128)(2,1)}, f32[16,256]{1,0:T(8,128)}) custom-call(s32[1]{0:T(128)} %bitcast.refs_0_, bf16[128,2048]{1,0:T(8,128)(2,1)S(1)} %get-tuple-element.42.a_ref.refs_1_, bf16[128,2048]{1,0:T(8,128)(2,1)} %get-tuple-element.53.refs_2_, bf16[128,2048]{1,0:T(8,128)(2,1)} %collective-permute-done.13.refs_3_, ...), custom_call_target="tpu_custom_call" | custom-call | flops 1572864 | bytes 3145728 | tf_op jit(solution)/shard_map/finish_0/pallas_call | solution.py:341
  93.6 7.2 %collective-permute-done.4.refs_3_ = bf16[128,2048]{1,0:T(8,128)(2,1)} collective-permute-done((bf16[128,2048]{1,0:T(8,128)(2,1)S(1)}, bf16[128,2048]{1,0:T(8,128)(2,1)}, u32[]{:S(2)}, u32[]{:S(2)}) %collective-permute-start.4) | collective-permute-done | bytes 524320 | tf_op jit(solution)/shard_map/ppermute | solution.py:453
  100.7 2.6 %finish_1.1 = (bf16[256,2048]{1,0:T(8,128)(2,1)}, f32[16,256]{1,0:T(8,128)}) custom-call(s32[1]{0:T(128)} %bitcast.refs_0_, bf16[128,2048]{1,0:T(8,128)(2,1)S(1)} %get-tuple-element.41.a_ref.refs_1_, bf16[128,2048]{1,0:T(8,128)(2,1)S(1)} %get-tuple-element.46.refs_2_, ...), custom_call_target="tpu_custom_call", output_to_operand_aliasing={{0}: (6, {}), {1}: (7, {})} | custom-call | flops 1572864 | bytes 3145728 | tf_op jit(solution)/shard_map/finish_1/pallas_call | solution.py:341
  (35 shorter events, 8.7 us)
Async XLA Ops:
  3.2 5.8 %collective-permute-start = (bf16[2,1296,128]{2,1,0:T(8,128)(2,1)}, bf16[2,1296,128]{2,1,0:T(8,128)(2,1)S(1)}, u32[]{:S(2)}, u32[]{:S(2)}) collective-permute-start(bf16[2,1296,128]{2,1,0:T(8,128)(2,1)} %pack.1.refs_0_), channel_id=1, source_target_pairs={{0,1},{1,0},{2,3},{3,2},{4,5},{5,4},{6,7},{7,6},{8,9},{9,8},{10,11... | collective-permute-start | bytes 1990664 | tf_op jit(solution)/shard_map/ppermute | solution.py:394
  3.8 18.3 %collective-permute-start.1 = (bf16[2,1296,128]{2,1,0:T(8,128)(2,1)}, bf16[2,1296,128]{2,1,0:T(8,128)(2,1)S(1)}, u32[]{:S(2)}, u32[]{:S(2)}) collective-permute-start(bf16[2,1296,128]{2,1,0:T(8,128)(2,1)} %pack.1.refs_0_), channel_id=1, source_target_pairs={{0,2},{2,0},{1,3},{3,1},{4,6},{6,4},{5,7},{7,5},{8,10},{10,8},{9,1... | collective-permute-start | bytes 1990664 | tf_op jit(solution)/shard_map/ppermute | solution.py:393
  9.0 1.1 %copy-start = (bf16[2,1296,128]{2,1,0:T(8,128)(2,1)S(1)}, bf16[2,1296,128]{2,1,0:T(8,128)(2,1)}, u32[]{:S(2)}) copy-start(bf16[2,1296,128]{2,1,0:T(8,128)(2,1)} %pack.1.refs_0_) | copy-start | bytes 1990660
  10.1 1.0 %copy-start.1 = (bf16[256,1024]{1,0:T(8,128)(2,1)S(1)}, bf16[256,1024]{1,0:T(8,128)(2,1)}, u32[]{:S(2)}) copy-start(bf16[256,1024]{1,0:T(8,128)(2,1)} %q_ref.1) | copy-start | bytes 1572868
  22.0 3.1 %collective-permute-start.2 = (bf16[2,1296,128]{2,1,0:T(8,128)(2,1)S(1)}, bf16[2,1296,128]{2,1,0:T(8,128)(2,1)S(1)}, u32[]{:S(2)}, u32[]{:S(2)}) collective-permute-start(bf16[2,1296,128]{2,1,0:T(8,128)(2,1)S(1)} %collective-permute-done.1.refs_0_), channel_id=1, source_target_pairs={{0,1},{1,0},{2,3},{3,2},{4,5},{5,4},{6,7},{7,6},{8,9},{9,8},{10,11... | collective-permute-start | bytes 1990664 | tf_op jit(solution)/shard_map/ppermute | solution.py:409
  29.0 16.0 %collective-permute-start.5 = (bf16[128,2048]{1,0:T(8,128)(2,1)S(1)}, bf16[128,2048]{1,0:T(8,128)(2,1)S(1)}, u32[]{:S(2)}, u32[]{:S(2)}) collective-permute-start(bf16[128,2048]{1,0:T(8,128)(2,1)S(1)} %get-tuple-element.38.a_ref), channel_id=1, source_target_pairs={{0,4},{12,8},{1,5},{13,9},{2,6},{14,10},{3,7},{15,11},{16,20},{28,... | collective-permute-start | bytes 1572872 | tf_op jit(solution)/shard_map/ppermute | solution.py:449
  38.4 19.0 %collective-permute-start.10 = (bf16[128,2048]{1,0:T(8,128)(2,1)S(1)}, bf16[128,2048]{1,0:T(8,128)(2,1)S(1)}, u32[]{:S(2)}, u32[]{:S(2)}) collective-permute-start(bf16[128,2048]{1,0:T(8,128)(2,1)S(1)} %get-tuple-element.51.a_ref), channel_id=1, source_target_pairs={{0,4},{12,8},{1,5},{13,9},{2,6},{14,10},{3,7},{15,11},{16,20},{28,... | collective-permute-start | bytes 1572872 | tf_op jit(solution)/shard_map/ppermute | solution.py:449
  45.1 19.2 %collective-permute-start.7 = (bf16[128,2048]{1,0:T(8,128)(2,1)S(1)}, bf16[128,2048]{1,0:T(8,128)(2,1)S(1)}, u32[]{:S(2)}, u32[]{:S(2)}) collective-permute-start(bf16[128,2048]{1,0:T(8,128)(2,1)S(1)} %add_00.1), channel_id=1, source_target_pairs={{4,8},{8,4},{5,9},{9,5},{6,10},{10,6},{7,11},{11,7},{20,24},{24,20... | collective-permute-start | bytes 1572872 | tf_op jit(solution)/shard_map/ppermute | solution.py:458
  45.8 30.5 %collective-permute-start.3 = (bf16[128,2048]{1,0:T(8,128)(2,1)S(1)}, bf16[128,2048]{1,0:T(8,128)(2,1)S(1)}, u32[]{:S(2)}, u32[]{:S(2)}) collective-permute-start(bf16[128,2048]{1,0:T(8,128)(2,1)S(1)} %get-tuple-element.45.a_ref), channel_id=1, source_target_pairs={{0,4},{12,8},{1,5},{13,9},{2,6},{14,10},{3,7},{15,11},{16,20},{28,... | collective-permute-start | bytes 1572872 | tf_op jit(solution)/shard_map/ppermute | solution.py:451
  57.6 20.3 %collective-permute-start.11 = (bf16[128,2048]{1,0:T(8,128)(2,1)S(1)}, bf16[128,2048]{1,0:T(8,128)(2,1)S(1)}, u32[]{:S(2)}, u32[]{:S(2)}) collective-permute-start(bf16[128,2048]{1,0:T(8,128)(2,1)S(1)} %add_01.1), channel_id=1, source_target_pairs={{4,8},{8,4},{5,9},{9,5},{6,10},{10,6},{7,11},{11,7},{20,24},{24,20... | collective-permute-start | bytes 1572872 | tf_op jit(solution)/shard_map/ppermute | solution.py:458
  58.3 21.9 %collective-permute-start.6 = (bf16[128,2048]{1,0:T(8,128)(2,1)S(1)}, bf16[128,2048]{1,0:T(8,128)(2,1)S(1)}, u32[]{:S(2)}, u32[]{:S(2)}) collective-permute-start(bf16[128,2048]{1,0:T(8,128)(2,1)S(1)} %get-tuple-element.48.a_ref), channel_id=1, source_target_pairs={{0,4},{12,8},{1,5},{13,9},{2,6},{14,10},{3,7},{15,11},{16,20},{28,... | collective-permute-start | bytes 1572872 | tf_op jit(solution)/shard_map/ppermute | solution.py:451
  64.3 17.2 %collective-permute-start.8 = (bf16[128,2048]{1,0:T(8,128)(2,1)S(1)}, bf16[128,2048]{1,0:T(8,128)(2,1)S(1)}, u32[]{:S(2)}, u32[]{:S(2)}) collective-permute-start(bf16[128,2048]{1,0:T(8,128)(2,1)S(1)} %add_30.1), channel_id=1, source_target_pairs={{4,0},{8,12},{5,1},{9,13},{6,2},{10,14},{7,3},{11,15},{20,16},{24,... | collective-permute-start | bytes 1572872 | tf_op jit(solution)/shard_map/ppermute | solution.py:460
  70.9 19.1 %collective-permute-start.13 = (bf16[128,2048]{1,0:T(8,128)(2,1)}, bf16[128,2048]{1,0:T(8,128)(2,1)}, u32[]{:S(2)}, u32[]{:S(2)}) collective-permute-start(bf16[128,2048]{1,0:T(8,128)(2,1)} %get-tuple-element.53.refs_2_), channel_id=1, source_target_pairs={{0,4},{12,8},{1,5},{13,9},{2,6},{14,10},{3,7},{15,11},{16,20},{28,... | collective-permute-start | bytes 1572872 | tf_op jit(solution)/shard_map/ppermute | solution.py:453
  76.4 13.6 %collective-permute-start.14 = (bf16[128,2048]{1,0:T(8,128)(2,1)S(1)}, bf16[128,2048]{1,0:T(8,128)(2,1)}, u32[]{:S(2)}, u32[]{:S(2)}) collective-permute-start(bf16[128,2048]{1,0:T(8,128)(2,1)S(1)} %add_10.1), channel_id=1, source_target_pairs={{4,8},{8,4},{5,9},{9,5},{6,10},{10,6},{7,11},{11,7},{20,24},{24,20... | collective-permute-start | bytes 1572872 | tf_op jit(solution)/shard_map/ppermute | solution.py:459
  77.9 22.9 %collective-permute-start.4 = (bf16[128,2048]{1,0:T(8,128)(2,1)S(1)}, bf16[128,2048]{1,0:T(8,128)(2,1)}, u32[]{:S(2)}, u32[]{:S(2)}) collective-permute-start(bf16[128,2048]{1,0:T(8,128)(2,1)S(1)} %get-tuple-element.46.refs_2_), channel_id=1, source_target_pairs={{0,4},{12,8},{1,5},{13,9},{2,6},{14,10},{3,7},{15,11},{16,20},{28,... | collective-permute-start | bytes 1572872 | tf_op jit(solution)/shard_map/ppermute | solution.py:453
  80.2 20.5 %collective-permute-start.12 = (bf16[128,2048]{1,0:T(8,128)(2,1)S(1)}, bf16[128,2048]{1,0:T(8,128)(2,1)}, u32[]{:S(2)}, u32[]{:S(2)}) collective-permute-start(bf16[128,2048]{1,0:T(8,128)(2,1)S(1)} %add_31.1), channel_id=1, source_target_pairs={{4,0},{8,12},{5,1},{9,13},{6,2},{10,14},{7,3},{11,15},{20,16},{24,... | collective-permute-start | bytes 1572872 | tf_op jit(solution)/shard_map/ppermute | solution.py:460
  81.5 0.8 copy-start.2
  82.3 18.4 %collective-permute-start.9 = (bf16[128,2048]{1,0:T(8,128)(2,1)S(1)}, bf16[128,2048]{1,0:T(8,128)(2,1)}, u32[]{:S(2)}, u32[]{:S(2)}) collective-permute-start(bf16[128,2048]{1,0:T(8,128)(2,1)S(1)} %add_11.1), channel_id=1, source_target_pairs={{4,8},{8,4},{5,9},{9,5},{6,10},{10,6},{7,11},{11,7},{20,24},{24,20... | collective-permute-start | bytes 1572872 | tf_op jit(solution)/shard_map/ppermute | solution.py:459
  90.0 1.0 %copy-start.3 = (bf16[128,2048]{1,0:T(8,128)(2,1)S(1)}, bf16[128,2048]{1,0:T(8,128)(2,1)}, u32[]{:S(2)}) copy-start(bf16[128,2048]{1,0:T(8,128)(2,1)} %copy-done.2) | copy-start | bytes 1572868

commit v9 on v8

--- a/solution.py
+++ b/solution.py
@@ -308,6 +308,23 @@
         cost_estimate=cost(a.size, a.size * 6),
         name=name,
     )(a, b)
+
+
+def gather_kernel(flag_ref, first_ref, second_ref, a_ref, b_ref, out_ref):
+    own = jnp.where(flag_ref[0] == 1, first_ref[...].astype(F32), second_ref[...].astype(F32))
+    out_ref[...] = own + (a_ref[...].astype(F32) + b_ref[...].astype(F32))
+
+
+def gathered(name, flag, first, second, a, b):
+    return pl.pallas_call(
+        gather_kernel,
+        out_shape=jax.ShapeDtypeStruct(a.shape, F32),
+        in_specs=[SMEM] + [VMEM] * 4,
+        out_specs=VMEM,
+        compiler_params=PARAMS_LESS,
+        cost_estimate=cost(a.size * 3, a.size * 12),
+        name=name,
+    )(flag, first, second, a, b)
 
 
 def finish(name, flag, parts, begin, rows_all, into=None):
@@ -459,7 +476,11 @@
             second = lax.ppermute(added(f"add_1{i}", part[1][i], come[1][i] if i == 0 else after(come[1][i], back)), "tensor", middle)
             back = lax.ppermute(added(f"add_3{i}", part[3][i], across), "tensor", outward)
             parts = [part[3][i], part[2][i], come[2][i], second, back]
-            done = finish(f"finish_{i}", flag, parts, i * cut, rows, done)
+            if i == 1:
+                most = gathered("gather", flag, *parts[:2], *parts[3:])
+                done = finish("finish_1", None, [most, after(come[2][1], most)], cut, rows, done)
+            else:
+                done = finish("finish_0", flag, parts, 0, rows, done)
         return done[0], done[1].T
     every = lax.all_gather(own, ("seq", "pipe"), axis=0)
     place = jnp.concatenate([jnp.stack([me, me]), jnp.arange(shards)]).astype(jnp.int32)

time: 104 us -> 103 us (level)
  waiting for transfers between devices: 16 us -> 11 us
  starting transfers between devices: 35.8 us -> 39.8 us
    ppermute x2, waiting for transfers between devices: 13.4 us -> 8.32 us  [local(): come[2] = [lax.ppermute(p, 'tensor', inward) for p in part[2]]]
    ppermute x2, starting transfers between devices: 7.61 us -> 11.6 us  [local(): come[2] = [lax.ppermute(p, 'tensor', inward) for p in part[2]]]
    pallas_call x0 -> x1, Pallas kernels: none -> 1.6 us  [gathered(): pl.pallas_call(gather_kernel, out_shape=jax.ShapeDtypeStruct(a.shape, F32...]
    pallas_call x2, Pallas kernels: 5.08 us -> 3.84 us  [finish(): pl.pallas_call(kernel, out_shape=(jax.ShapeDtypeStruct((rows_all, columns...]
  transfers between devices with their start and end apart: 15 -> 15, of which waited for: 4 -> 4; matrix products, arithmetic and copies ran while one was open for 2% -> 2% of each run, Pallas kernels for 34% -> 36%
where the time goes in v9:
time: 103 us; the launch traced here: 102 us
  Pallas kernels  43.9 us (43%)
  starting transfers between devices  39.8 us (39%)
  waiting for transfers between devices  11 us (11%)
  local copies, waits for them, and re-layouts  3.29 us (3%)
  between operations  2.19 us (2%)
  other arithmetic  1.92 us (2%)
    pallas_call x4, Pallas kernels, attend(): pl.pallas_call(functools.partial(attend_kernel, first, last, chunk, slots...  21.5 us
    pallas_call x3, Pallas kernels, project(): pl.pallas_call(functools.partial(project_kernel, pieces), out_shape=(jax....  14.3 us
    ppermute x2, starting transfers between devices, local(): come[1] = [lax.ppermute(p, 'tensor', inward) for p in part[1]]  13.1 us
    ppermute x2, starting transfers between devices, local(): come[2] = [lax.ppermute(p, 'tensor', inward) for p in part[2]]  11.6 us
    ppermute x2, waiting for transfers between devices, local(): come[2] = [lax.ppermute(p, 'tensor', inward) for p in part[2]]  8.32 us
    ppermute x2, starting transfers between devices, local(): come[0][i] = lax.ppermute(part[0][i], 'tensor', inward)  5.1 us
    pallas_call x2, Pallas kernels, finish(): pl.pallas_call(kernel, out_shape=(jax.ShapeDtypeStruct((rows_all, columns...  3.84 us
    unnamed x8, local copies, waits for them, and re-layouts  3.17 us
  transfers between devices with their start and end apart: 15, of which 4 were waited for; matrix products, arithmetic and copies ran while one was open for 2% of the time, Pallas kernels for 36%

profile of v9, /device:TPU:0, one launch (start us, length us, event | category | flops | bytes accessed | tf_op | source)
XLA Modules:
  0.0 102.2 jit_solution(4838683643596153116)
XLA Ops:
  1.3 2.0 %pack.1.refs_0_ = bf16[2,1296,128]{2,1,0:T(8,128)(2,1)} custom-call(s32[1]{0:T(128)S(6)} %copy.14.len_ref, bf16[4,1024,128]{2,1,0:T(8,128)(2,1)} %k_ref.1, bf16[4,1024,128]{2,1,0:T(8,128)(2,1)} %v_ref.1, bf16[256,512]{1,0:T(8,128)(2,1)} %nk_ref.1, bf16[256,512]{1,0:T(8,128)(2,1)} %nv_ref.1), custom_call_target="tpu_custom_call" | custom-call | bytes 1327104 | tf_op jit(solution)/shard_map/pack/pallas_call | solution.py:67
  3.8 2.6 %collective-permute-start.1 = (bf16[2,1296,128]{2,1,0:T(8,128)(2,1)}, bf16[2,1296,128]{2,1,0:T(8,128)(2,1)S(1)}, u32[]{:S(2)}, u32[]{:S(2)}) collective-permute-start(bf16[2,1296,128]{2,1,0:T(8,128)(2,1)} %pack.1.refs_0_), channel_id=1, source_target_pairs={{0,2},{2,0},{1,3},{3,1},{4,6},{6,4},{5,7},{7,5},{8,10},{10,8},{9,1... | collective-permute-start | bytes 1990664 | tf_op jit(solution)/shard_map/ppermute | solution.py:410
  7.1 1.9 %fusion = (f32[1024,128]{1,0:T(8,128)S(1)}, f32[1024,128]{1,0:T(8,128)S(1)}) fusion(f32[128]{0:T(128)S(1)} %get-tuple-element.62, f32[128]{0:T(128)S(1)} %get-tuple-element.63, f32[1024]{0:T(1024)S(1)} %add_convert_fusion), kind=kLoop, calls=%fused_computation.2 | loop fusion | flops 262144 | bytes 1053696 | tf_op jit(solution)/shard_map/mul | solution.py:399
  11.2 8.9 %attend_near.1 = (f32[256,1024]{1,0:T(8,128)S(1)}, f32[256,128]{1,0:T(8,128)S(1)}, bf16[256,1024]{1,0:T(8,128)(2,1)S(1)}, bf16[1024,2048]{1,0:T(8,128)(2,1)S(1)}) custom-call(s32[6]{0:T(128)S(1)} %stack.20.place_ref, bf16[256,1024]{1,0:T(8,128)(2,1)S(1)} %copy-done.1, f32[1024,128]{1,0:T(8,128)S(1)} %get-tuple-element.61.cos_ref, ...), custom_call_target="tpu_custom_call" | custom-call | flops 335544320 | bytes 262144 | tf_op jit(solution)/shard_map/attend_near/pallas_call | solution.py:254
  20.1 1.9 %collective-permute-done.1.refs_0_ = bf16[2,1296,128]{2,1,0:T(8,128)(2,1)S(1)} collective-permute-done((bf16[2,1296,128]{2,1,0:T(8,128)(2,1)}, bf16[2,1296,128]{2,1,0:T(8,128)(2,1)S(1)}, u32[]{:S(2)}, u32[]{:S(2)}) %collective-permute-start.1) | collective-permute-done | bytes 663584 | tf_op jit(solution)/shard_map/ppermute | solution.py:410
  22.0 3.1 %attend_far.1 = (f32[128,1024]{1,0:T(8,128)S(1)}, f32[128,128]{1,0:T(8,128)S(1)}) custom-call(s32[6]{0:T(128)S(1)} %stack.20.place_ref, bf16[256,1024]{1,0:T(8,128)(2,1)S(1)} %get-tuple-element.31.q_ref, f32[1024,128]{1,0:T(8,128)S(1)} %get-tuple-element.61.cos_ref, f32[1024,128]{1,0:T(8,128)S(1)} %get-tuple-element.60.sin_ref, ...), custom_call_target="tpu_custom_call" | custom-call | flops 167772160 | bytes 262144 | tf_op jit(solution)/shard_map/attend_far/pallas_call | solution.py:254
  25.1 3.8 %attend_cross.1 = (bf16[128,1024]{1,0:T(8,128)(2,1)S(1)}, bf16[128,2048]{1,0:T(8,128)(2,1)S(1)}) custom-call(s32[6]{0:T(128)S(1)} %stack.20.place_ref, bf16[256,1024]{1,0:T(8,128)(2,1)S(1)} %get-tuple-element.31.q_ref, f32[1024,128]{1,0:T(8,128)S(1)} %get-tuple-element.61.cos_ref, f32[1024,128]{1,0:T(8,128)S(1)} %get-tuple-element.60.sin_ref, ...), custom_call_target="tpu_custom_call" | custom-call | flops 167772160 | bytes 262144 | tf_op jit(solution)/shard_map/attend_cross/pallas_call | solution.py:254
  29.0 3.8 %collective-permute-start.4 = (bf16[128,2048]{1,0:T(8,128)(2,1)S(1)}, bf16[128,2048]{1,0:T(8,128)(2,1)S(1)}, u32[]{:S(2)}, u32[]{:S(2)}) collective-permute-start(bf16[128,2048]{1,0:T(8,128)(2,1)S(1)} %get-tuple-element.39.a_ref), channel_id=1, source_target_pairs={{0,4},{12,8},{1,5},{13,9},{2,6},{14,10},{3,7},{15,11},{16,20},{28,... | collective-permute-start | bytes 1572872 | tf_op jit(solution)/shard_map/ppermute | solution.py:466
  32.7 5.7 %attend_rest.1 = (bf16[128,1024]{1,0:T(8,128)(2,1)S(1)}, bf16[128,2048]{1,0:T(8,128)(2,1)S(1)}) custom-call(s32[6]{0:T(128)S(1)} %stack.20.place_ref, bf16[256,1024]{1,0:T(8,128)(2,1)S(1)} %get-tuple-element.31.q_ref, f32[1024,128]{1,0:T(8,128)S(1)} %get-tuple-element.61.cos_ref, f32[1024,128]{1,0:T(8,128)S(1)} %get-tuple-element.60.sin_ref, ...), custom_call_target="tpu_custom_call" | custom-call | flops 335544320 | bytes 262144 | tf_op jit(solution)/shard_map/attend_rest/pallas_call | solution.py:254
  38.4 1.3 %collective-permute-start.9 = (bf16[128,2048]{1,0:T(8,128)(2,1)S(1)}, bf16[128,2048]{1,0:T(8,128)(2,1)S(1)}, u32[]{:S(2)}, u32[]{:S(2)}) collective-permute-start(bf16[128,2048]{1,0:T(8,128)(2,1)S(1)} %get-tuple-element.52.a_ref), channel_id=1, source_target_pairs={{0,4},{12,8},{1,5},{13,9},{2,6},{14,10},{3,7},{15,11},{16,20},{28,... | collective-permute-start | bytes 1572872 | tf_op jit(solution)/shard_map/ppermute | solution.py:466
  39.7 4.5 %project_1.1 = (bf16[128,2048]{1,0:T(8,128)(2,1)S(1)}, bf16[128,2048]{1,0:T(8,128)(2,1)S(1)}) custom-call(s32[4]{0:T(128)S(1)} %broadcast_select_fusion.order_ref, bf16[128,1024]{1,0:T(8,128)(2,1)S(1)} %get-tuple-element.38.refs_0_, bf16[128,1024]{1,0:T(8,128)(2,1)S(1)} %get-tuple-element.44.refs_1_, bf16[1024,8192]{1,0:T(8,128)(2,1)} %refs_2_.7), custom_call_target="tpu_custom_call" | custom-call | flops 1073741824 | bytes 4194304 | tf_op jit(solution)/shard_map/project_1/pallas_call | solution.py:281
  45.8 7.2 %collective-permute-start.3 = (bf16[128,2048]{1,0:T(8,128)(2,1)S(1)}, bf16[128,2048]{1,0:T(8,128)(2,1)S(1)}, u32[]{:S(2)}, u32[]{:S(2)}) collective-permute-start(bf16[128,2048]{1,0:T(8,128)(2,1)S(1)} %get-tuple-element.46.a_ref), channel_id=1, source_target_pairs={{0,4},{12,8},{1,5},{13,9},{2,6},{14,10},{3,7},{15,11},{16,20},{28,... | collective-permute-start | bytes 1572872 | tf_op jit(solution)/shard_map/ppermute | solution.py:468
  53.0 4.5 %project_3.1 = (bf16[128,2048]{1,0:T(8,128)(2,1)S(1)}, bf16[128,2048]{1,0:T(8,128)(2,1)S(1)}) custom-call(s32[4]{0:T(128)S(1)} %broadcast_select_fusion.order_ref, bf16[128,1024]{1,0:T(8,128)(2,1)S(1)} %get-tuple-element.38.refs_0_, bf16[128,1024]{1,0:T(8,128)(2,1)S(1)} %get-tuple-element.44.refs_1_, bf16[1024,8192]{1,0:T(8,128)(2,1)} %refs_2_.7), custom_call_target="tpu_custom_call" | custom-call | flops 1073741824 | bytes 4194304 | tf_op jit(solution)/shard_map/project_3/pallas_call | solution.py:281
  58.3 5.9 %collective-permute-start.5 = (bf16[128,2048]{1,0:T(8,128)(2,1)S(1)}, bf16[128,2048]{1,0:T(8,128)(2,1)S(1)}, u32[]{:S(2)}, u32[]{:S(2)}) collective-permute-start(bf16[128,2048]{1,0:T(8,128)(2,1)S(1)} %get-tuple-element.49.a_ref), channel_id=1, source_target_pairs={{0,4},{12,8},{1,5},{13,9},{2,6},{14,10},{3,7},{15,11},{16,20},{28,... | collective-permute-start | bytes 1572872 | tf_op jit(solution)/shard_map/ppermute | solution.py:468
  65.7 5.3 %project_2.1 = (bf16[128,2048]{1,0:T(8,128)(2,1)}, bf16[128,2048]{1,0:T(8,128)(2,1)}) custom-call(s32[4]{0:T(128)S(1)} %broadcast_select_fusion.order_ref, bf16[128,1024]{1,0:T(8,128)(2,1)S(1)} %get-tuple-element.38.refs_0_, bf16[128,1024]{1,0:T(8,128)(2,1)S(1)} %get-tuple-element.44.refs_1_, bf16[1024,8192]{1,0:T(8,128)(2,1)} %refs_2_.7), custom_call_target="tpu_custom_call" | custom-call | flops 1073741824 | bytes 4194304 | tf_op jit(solution)/shard_map/project_2/pallas_call | solution.py:281
  71.0 5.4 %collective-permute-start.13 = (bf16[128,2048]{1,0:T(8,128)(2,1)}, bf16[128,2048]{1,0:T(8,128)(2,1)}, u32[]{:S(2)}, u32[]{:S(2)}) collective-permute-start(bf16[128,2048]{1,0:T(8,128)(2,1)} %get-tuple-element.55.refs_2_), channel_id=1, source_target_pairs={{0,4},{12,8},{1,5},{13,9},{2,6},{14,10},{3,7},{15,11},{16,20},{28,... | collective-permute-start | bytes 1572872 | tf_op jit(solution)/shard_map/ppermute | solution.py:470
  76.5 1.5 %collective-permute-start.14 = (bf16[128,2048]{1,0:T(8,128)(2,1)S(1)}, bf16[128,2048]{1,0:T(8,128)(2,1)}, u32[]{:S(2)}, u32[]{:S(2)}) collective-permute-start(bf16[128,2048]{1,0:T(8,128)(2,1)S(1)} %add_10.1), channel_id=1, source_target_pairs={{4,8},{8,4},{5,9},{9,5},{6,10},{10,6},{7,11},{11,7},{20,24},{24,20... | collective-permute-start | bytes 1572872 | tf_op jit(solution)/shard_map/ppermute | solution.py:476
  79.6 1.5 %collective-permute-start.8 = (bf16[128,2048]{1,0:T(8,128)(2,1)S(1)}, bf16[128,2048]{1,0:T(8,128)(2,1)}, u32[]{:S(2)}, u32[]{:S(2)}) collective-permute-start(bf16[128,2048]{1,0:T(8,128)(2,1)S(1)} %add_11.1), channel_id=1, source_target_pairs={{4,8},{8,4},{5,9},{9,5},{6,10},{10,6},{7,11},{11,7},{20,24},{24,20... | collective-permute-start | bytes 1572872 | tf_op jit(solution)/shard_map/ppermute | solution.py:476
  81.1 6.3 %collective-permute-start.12 = (bf16[128,2048]{1,0:T(8,128)(2,1)}, bf16[128,2048]{1,0:T(8,128)(2,1)S(1)}, u32[]{:S(2)}, u32[]{:S(2)}) collective-permute-start(bf16[128,2048]{1,0:T(8,128)(2,1)} %get-tuple-element.47.second_ref), channel_id=1, source_target_pairs={{0,4},{12,8},{1,5},{13,9},{2,6},{14,10},{3,7},{15,11},{16,20},{28,... | collective-permute-start | bytes 1572872 | tf_op jit(solution)/shard_map/ppermute | solution.py:470
  87.3 2.6 %collective-permute-done.13.refs_3_ = bf16[128,2048]{1,0:T(8,128)(2,1)} collective-permute-done((bf16[128,2048]{1,0:T(8,128)(2,1)}, bf16[128,2048]{1,0:T(8,128)(2,1)}, u32[]{:S(2)}, u32[]{:S(2)}) %collective-permute-start.13) | collective-permute-done | bytes 524320 | tf_op jit(solution)/shard_map/ppermute | solution.py:470
  91.0 2.5 %finish_0.1 = (bf16[256,2048]{1,0:T(8,128)(2,1)}, f32[16,256]{1,0:T(8,128)}) custom-call(s32[1]{0:T(128)} %bitcast.flag_ref.refs_0_, bf16[128,2048]{1,0:T(8,128)(2,1)S(1)} %get-tuple-element.43.a_ref.refs_1_, bf16[128,2048]{1,0:T(8,128)(2,1)} %get-tuple-element.55.refs_2_, bf16[128,2048]{1,0:T(8,128)(2,1)} %collective-permute-done.13.refs_3_, ...), custom_call_target="tpu_custom_call" | custom-call | flops 1572864 | bytes 3145728 | tf_op jit(solution)/shard_map/finish_0/pallas_call | solution.py:358
  93.6 1.6 %gather.1.refs_0_ = f32[128,2048]{1,0:T(8,128)S(1)} custom-call(s32[1]{0:T(128)} %bitcast.flag_ref.refs_0_, bf16[128,2048]{1,0:T(8,128)(2,1)S(1)} %get-tuple-element.42.a_ref.first_ref, bf16[128,2048]{1,0:T(8,128)(2,1)} %get-tuple-element.47.second_ref, bf16[128,2048]{1,0:T(8,128)(2,1)} %collective-permute-done.8.a_ref, ...), custom_call_target="tpu_custom_call" | custom-call | flops 786432 | bytes 3145728 | tf_op jit(solution)/shard_map/gather/pallas_call | solution.py:319
  95.2 5.7 %collective-permute-done.12.refs_1_ = bf16[128,2048]{1,0:T(8,128)(2,1)S(1)} collective-permute-done((bf16[128,2048]{1,0:T(8,128)(2,1)}, bf16[128,2048]{1,0:T(8,128)(2,1)S(1)}, u32[]{:S(2)}, u32[]{:S(2)}) %collective-permute-start.12) | collective-permute-done | bytes 524320 | tf_op jit(solution)/shard_map/ppermute | solution.py:470
  100.8 1.3 %finish_1.1 = (bf16[256,2048]{1,0:T(8,128)(2,1)}, f32[16,256]{1,0:T(8,128)}) custom-call(f32[128,2048]{1,0:T(8,128)S(1)} %gather.1.refs_0_, bf16[128,2048]{1,0:T(8,128)(2,1)S(1)} %collective-permute-done.12.refs_1_, bf16[256,2048]{1,0:T(8,128)(2,1)} %get-tuple-element.56.refs_2_, ...), custom_call_target="tpu_custom_call", output_to_operand_aliasing={{0}: (2, {}), {1}: (3, {})} | custom-call | flops 1572864 | bytes 1572864 | tf_op jit(solution)/shard_map/finish_1/pallas_call | solution.py:358
  (36 shorter events, 9.3 us)
Async XLA Ops:
  3.2 5.8 %collective-permute-start = (bf16[2,1296,128]{2,1,0:T(8,128)(2,1)}, bf16[2,1296,128]{2,1,0:T(8,128)(2,1)S(1)}, u32[]{:S(2)}, u32[]{:S(2)}) collective-permute-start(bf16[2,1296,128]{2,1,0:T(8,128)(2,1)} %pack.1.refs_0_), channel_id=1, source_target_pairs={{0,1},{1,0},{2,3},{3,2},{4,5},{5,4},{6,7},{7,6},{8,9},{9,8},{10,11... | collective-permute-start | bytes 1990664 | tf_op jit(solution)/shard_map/ppermute | solution.py:411
  3.8 18.3 %collective-permute-start.1 = (bf16[2,1296,128]{2,1,0:T(8,128)(2,1)}, bf16[2,1296,128]{2,1,0:T(8,128)(2,1)S(1)}, u32[]{:S(2)}, u32[]{:S(2)}) collective-permute-start(bf16[2,1296,128]{2,1,0:T(8,128)(2,1)} %pack.1.refs_0_), channel_id=1, source_target_pairs={{0,2},{2,0},{1,3},{3,1},{4,6},{6,4},{5,7},{7,5},{8,10},{10,8},{9,1... | collective-permute-start | bytes 1990664 | tf_op jit(solution)/shard_map/ppermute | solution.py:410
  9.0 1.1 %copy-start = (bf16[2,1296,128]{2,1,0:T(8,128)(2,1)S(1)}, bf16[2,1296,128]{2,1,0:T(8,128)(2,1)}, u32[]{:S(2)}) copy-start(bf16[2,1296,128]{2,1,0:T(8,128)(2,1)} %pack.1.refs_0_) | copy-start | bytes 1990660
  10.1 1.0 %copy-start.1 = (bf16[256,1024]{1,0:T(8,128)(2,1)S(1)}, bf16[256,1024]{1,0:T(8,128)(2,1)}, u32[]{:S(2)}) copy-start(bf16[256,1024]{1,0:T(8,128)(2,1)} %q_ref.1) | copy-start | bytes 1572868
  22.0 3.1 %collective-permute-start.2 = (bf16[2,1296,128]{2,1,0:T(8,128)(2,1)S(1)}, bf16[2,1296,128]{2,1,0:T(8,128)(2,1)S(1)}, u32[]{:S(2)}, u32[]{:S(2)}) collective-permute-start(bf16[2,1296,128]{2,1,0:T(8,128)(2,1)S(1)} %collective-permute-done.1.refs_0_), channel_id=1, source_target_pairs={{0,1},{1,0},{2,3},{3,2},{4,5},{5,4},{6,7},{7,6},{8,9},{9,8},{10,11... | collective-permute-start | bytes 1990664 | tf_op jit(solution)/shard_map/ppermute | solution.py:426
  29.0 16.0 %collective-permute-start.4 = (bf16[128,2048]{1,0:T(8,128)(2,1)S(1)}, bf16[128,2048]{1,0:T(8,128)(2,1)S(1)}, u32[]{:S(2)}, u32[]{:S(2)}) collective-permute-start(bf16[128,2048]{1,0:T(8,128)(2,1)S(1)} %get-tuple-element.39.a_ref), channel_id=1, source_target_pairs={{0,4},{12,8},{1,5},{13,9},{2,6},{14,10},{3,7},{15,11},{16,20},{28,... | collective-permute-start | bytes 1572872 | tf_op jit(solution)/shard_map/ppermute | solution.py:466
  38.4 19.0 %collective-permute-start.9 = (bf16[128,2048]{1,0:T(8,128)(2,1)S(1)}, bf16[128,2048]{1,0:T(8,128)(2,1)S(1)}, u32[]{:S(2)}, u32[]{:S(2)}) collective-permute-start(bf16[128,2048]{1,0:T(8,128)(2,1)S(1)} %get-tuple-element.52.a_ref), channel_id=1, source_target_pairs={{0,4},{12,8},{1,5},{13,9},{2,6},{14,10},{3,7},{15,11},{16,20},{28,... | collective-permute-start | bytes 1572872 | tf_op jit(solution)/shard_map/ppermute | solution.py:466
  45.1 19.2 %collective-permute-start.6 = (bf16[128,2048]{1,0:T(8,128)(2,1)S(1)}, bf16[128,2048]{1,0:T(8,128)(2,1)S(1)}, u32[]{:S(2)}, u32[]{:S(2)}) collective-permute-start(bf16[128,2048]{1,0:T(8,128)(2,1)S(1)} %add_00.1), channel_id=1, source_target_pairs={{4,8},{8,4},{5,9},{9,5},{6,10},{10,6},{7,11},{11,7},{20,24},{24,20... | collective-permute-start | bytes 1572872 | tf_op jit(solution)/shard_map/ppermute | solution.py:475
  45.8 30.6 %collective-permute-start.3 = (bf16[128,2048]{1,0:T(8,128)(2,1)S(1)}, bf16[128,2048]{1,0:T(8,128)(2,1)S(1)}, u32[]{:S(2)}, u32[]{:S(2)}) collective-permute-start(bf16[128,2048]{1,0:T(8,128)(2,1)S(1)} %get-tuple-element.46.a_ref), channel_id=1, source_target_pairs={{0,4},{12,8},{1,5},{13,9},{2,6},{14,10},{3,7},{15,11},{16,20},{28,... | collective-permute-start | bytes 1572872 | tf_op jit(solution)/shard_map/ppermute | solution.py:468
  57.6 20.4 %collective-permute-start.10 = (bf16[128,2048]{1,0:T(8,128)(2,1)S(1)}, bf16[128,2048]{1,0:T(8,128)(2,1)S(1)}, u32[]{:S(2)}, u32[]{:S(2)}) collective-permute-start(bf16[128,2048]{1,0:T(8,128)(2,1)S(1)} %add_01.1), channel_id=1, source_target_pairs={{4,8},{8,4},{5,9},{9,5},{6,10},{10,6},{7,11},{11,7},{20,24},{24,20... | collective-permute-start | bytes 1572872 | tf_op jit(solution)/shard_map/ppermute | solution.py:475
  58.3 21.1 %collective-permute-start.5 = (bf16[128,2048]{1,0:T(8,128)(2,1)S(1)}, bf16[128,2048]{1,0:T(8,128)(2,1)S(1)}, u32[]{:S(2)}, u32[]{:S(2)}) collective-permute-start(bf16[128,2048]{1,0:T(8,128)(2,1)S(1)} %get-tuple-element.49.a_ref), channel_id=1, source_target_pairs={{0,4},{12,8},{1,5},{13,9},{2,6},{14,10},{3,7},{15,11},{16,20},{28,... | collective-permute-start | bytes 1572872 | tf_op jit(solution)/shard_map/ppermute | solution.py:468
  64.4 15.1 %collective-permute-start.7 = (bf16[128,2048]{1,0:T(8,128)(2,1)S(1)}, bf16[128,2048]{1,0:T(8,128)(2,1)S(1)}, u32[]{:S(2)}, u32[]{:S(2)}) collective-permute-start(bf16[128,2048]{1,0:T(8,128)(2,1)S(1)} %add_30.1), channel_id=1, source_target_pairs={{4,0},{8,12},{5,1},{9,13},{6,2},{10,14},{7,3},{11,15},{20,16},{24,... | collective-permute-start | bytes 1572872 | tf_op jit(solution)/shard_map/ppermute | solution.py:477
  71.0 19.0 %collective-permute-start.13 = (bf16[128,2048]{1,0:T(8,128)(2,1)}, bf16[128,2048]{1,0:T(8,128)(2,1)}, u32[]{:S(2)}, u32[]{:S(2)}) collective-permute-start(bf16[128,2048]{1,0:T(8,128)(2,1)} %get-tuple-element.55.refs_2_), channel_id=1, source_target_pairs={{0,4},{12,8},{1,5},{13,9},{2,6},{14,10},{3,7},{15,11},{16,20},{28,... | collective-permute-start | bytes 1572872 | tf_op jit(solution)/shard_map/ppermute | solution.py:470
  76.5 13.5 %collective-permute-start.14 = (bf16[128,2048]{1,0:T(8,128)(2,1)S(1)}, bf16[128,2048]{1,0:T(8,128)(2,1)}, u32[]{:S(2)}, u32[]{:S(2)}) collective-permute-start(bf16[128,2048]{1,0:T(8,128)(2,1)S(1)} %add_10.1), channel_id=1, source_target_pairs={{4,8},{8,4},{5,9},{9,5},{6,10},{10,6},{7,11},{11,7},{20,24},{24,20... | collective-permute-start | bytes 1572872 | tf_op jit(solution)/shard_map/ppermute | solution.py:476
  78.1 15.4 %collective-permute-start.11 = (bf16[128,2048]{1,0:T(8,128)(2,1)S(1)}, bf16[128,2048]{1,0:T(8,128)(2,1)}, u32[]{:S(2)}, u32[]{:S(2)}) collective-permute-start(bf16[128,2048]{1,0:T(8,128)(2,1)S(1)} %add_31.1), channel_id=1, source_target_pairs={{4,0},{8,12},{5,1},{9,13},{6,2},{10,14},{7,3},{11,15},{20,16},{24,... | collective-permute-start | bytes 1572872 | tf_op jit(solution)/shard_map/ppermute | solution.py:477
  79.4 1.6 %copy-start.2 = (bf16[128,2048]{1,0:T(8,128)(2,1)}, bf16[128,2048]{1,0:T(8,128)(2,1)S(1)}, u32[]{:S(2)}) copy-start(bf16[128,2048]{1,0:T(8,128)(2,1)S(1)} %collective-permute-done.7.refs_5_) | copy-start | bytes 1572868
  79.6 14.0 %collective-permute-start.8 = (bf16[128,2048]{1,0:T(8,128)(2,1)S(1)}, bf16[128,2048]{1,0:T(8,128)(2,1)}, u32[]{:S(2)}, u32[]{:S(2)}) collective-permute-start(bf16[128,2048]{1,0:T(8,128)(2,1)S(1)} %add_11.1), channel_id=1, source_target_pairs={{4,8},{8,4},{5,9},{9,5},{6,10},{10,6},{7,11},{11,7},{20,24},{24,20... | collective-permute-start | bytes 1572872 | tf_op jit(solution)/shard_map/ppermute | solution.py:476
  81.1 19.8 %collective-permute-start.12 = (bf16[128,2048]{1,0:T(8,128)(2,1)}, bf16[128,2048]{1,0:T(8,128)(2,1)S(1)}, u32[]{:S(2)}, u32[]{:S(2)}) collective-permute-start(bf16[128,2048]{1,0:T(8,128)(2,1)} %get-tuple-element.47.second_ref), channel_id=1, source_target_pairs={{0,4},{12,8},{1,5},{13,9},{2,6},{14,10},{3,7},{15,11},{16,20},{28,... | collective-permute-start | bytes 1572872 | tf_op jit(solution)/shard_map/ppermute | solution.py:470
  90.0 1.0 %copy-start.3 = (bf16[128,2048]{1,0:T(8,128)(2,1)S(1)}, bf16[128,2048]{1,0:T(8,128)(2,1)}, u32[]{:S(2)}) copy-start(bf16[128,2048]{1,0:T(8,128)(2,1)} %copy-done.2) | copy-start | bytes 1572868

commit v10 on v9

--- a/solution.py
+++ b/solution.py
@@ -330,7 +330,7 @@
 def finish(name, flag, parts, begin, rows_all, into=None):
     rows, columns = parts[0].shape
     blocks = columns // BLOCK
-    steps = 2 if blocks % 16 == 0 else 1
+    steps = 2 if blocks % 16 == 0 and flag is not None else 1
     per = blocks // steps
     count = len(parts)
     flags = () if flag is None else (flag,)

time: 103 us -> 103 us (level)
  no operation moved by 1% of the time
where the time goes in v10:
time: 103 us; the launch traced here: 102 us
  Pallas kernels  43.8 us (43%)
  starting transfers between devices  39.8 us (39%)
  waiting for transfers between devices  11 us (11%)
  local copies, waits for them, and re-layouts  3.29 us (3%)
  between operations  2.19 us (2%)
  other arithmetic  1.92 us (2%)
    pallas_call x4, Pallas kernels, attend(): pl.pallas_call(functools.partial(attend_kernel, first, last, chunk, slots...  21.5 us
    pallas_call x3, Pallas kernels, project(): pl.pallas_call(functools.partial(project_kernel, pieces), out_shape=(jax....  14.3 us
    ppermute x2, starting transfers between devices, local(): come[1] = [lax.ppermute(p, 'tensor', inward) for p in part[1]]  13.1 us
    ppermute x2, starting transfers between devices, local(): come[2] = [lax.ppermute(p, 'tensor', inward) for p in part[2]]  11.6 us
    ppermute x2, waiting for transfers between devices, local(): come[2] = [lax.ppermute(p, 'tensor', inward) for p in part[2]]  8.32 us
    ppermute x2, starting transfers between devices, local(): come[0][i] = lax.ppermute(part[0][i], 'tensor', inward)  5.1 us
    pallas_call x2, Pallas kernels, finish(): pl.pallas_call(kernel, out_shape=(jax.ShapeDtypeStruct((rows_all, columns...  3.68 us
    unnamed x8, local copies, waits for them, and re-layouts  3.17 us
  transfers between devices with their start and end apart: 15, of which 4 were waited for; matrix products, arithmetic and copies ran while one was open for 2% of the time, Pallas kernels for 36%

profile of v10, /device:TPU:0, one launch (start us, length us, event | category | flops | bytes accessed | tf_op | source)
XLA Modules:
  0.0 102.0 jit_solution(7570004836379734724)
XLA Ops:
  1.3 2.0 %pack.1.refs_0_ = bf16[2,1296,128]{2,1,0:T(8,128)(2,1)} custom-call(s32[1]{0:T(128)S(6)} %copy.14.len_ref, bf16[4,1024,128]{2,1,0:T(8,128)(2,1)} %k_ref.1, bf16[4,1024,128]{2,1,0:T(8,128)(2,1)} %v_ref.1, bf16[256,512]{1,0:T(8,128)(2,1)} %nk_ref.1, bf16[256,512]{1,0:T(8,128)(2,1)} %nv_ref.1), custom_call_target="tpu_custom_call" | custom-call | bytes 1327104 | tf_op jit(solution)/shard_map/pack/pallas_call | solution.py:67
  3.8 2.6 %collective-permute-start.1 = (bf16[2,1296,128]{2,1,0:T(8,128)(2,1)}, bf16[2,1296,128]{2,1,0:T(8,128)(2,1)S(1)}, u32[]{:S(2)}, u32[]{:S(2)}) collective-permute-start(bf16[2,1296,128]{2,1,0:T(8,128)(2,1)} %pack.1.refs_0_), channel_id=1, source_target_pairs={{0,2},{2,0},{1,3},{3,1},{4,6},{6,4},{5,7},{7,5},{8,10},{10,8},{9,1... | collective-permute-start | bytes 1990664 | tf_op jit(solution)/shard_map/ppermute | solution.py:410
  7.1 1.9 %fusion = (f32[1024,128]{1,0:T(8,128)S(1)}, f32[1024,128]{1,0:T(8,128)S(1)}) fusion(f32[128]{0:T(128)S(1)} %get-tuple-element.62, f32[128]{0:T(128)S(1)} %get-tuple-element.63, f32[1024]{0:T(1024)S(1)} %add_convert_fusion), kind=kLoop, calls=%fused_computation.2 | loop fusion | flops 262144 | bytes 1053696 | tf_op jit(solution)/shard_map/mul | solution.py:399
  11.2 8.9 %attend_near.1 = (f32[256,1024]{1,0:T(8,128)S(1)}, f32[256,128]{1,0:T(8,128)S(1)}, bf16[256,1024]{1,0:T(8,128)(2,1)S(1)}, bf16[1024,2048]{1,0:T(8,128)(2,1)S(1)}) custom-call(s32[6]{0:T(128)S(1)} %stack.20.place_ref, bf16[256,1024]{1,0:T(8,128)(2,1)S(1)} %copy-done.1, f32[1024,128]{1,0:T(8,128)S(1)} %get-tuple-element.61.cos_ref, ...), custom_call_target="tpu_custom_call" | custom-call | flops 335544320 | bytes 262144 | tf_op jit(solution)/shard_map/attend_near/pallas_call | solution.py:254
  20.1 1.9 %collective-permute-done.1.refs_0_ = bf16[2,1296,128]{2,1,0:T(8,128)(2,1)S(1)} collective-permute-done((bf16[2,1296,128]{2,1,0:T(8,128)(2,1)}, bf16[2,1296,128]{2,1,0:T(8,128)(2,1)S(1)}, u32[]{:S(2)}, u32[]{:S(2)}) %collective-permute-start.1) | collective-permute-done | bytes 663584 | tf_op jit(solution)/shard_map/ppermute | solution.py:410
  22.0 3.1 %attend_far.1 = (f32[128,1024]{1,0:T(8,128)S(1)}, f32[128,128]{1,0:T(8,128)S(1)}) custom-call(s32[6]{0:T(128)S(1)} %stack.20.place_ref, bf16[256,1024]{1,0:T(8,128)(2,1)S(1)} %get-tuple-element.31.q_ref, f32[1024,128]{1,0:T(8,128)S(1)} %get-tuple-element.61.cos_ref, f32[1024,128]{1,0:T(8,128)S(1)} %get-tuple-element.60.sin_ref, ...), custom_call_target="tpu_custom_call" | custom-call | flops 167772160 | bytes 262144 | tf_op jit(solution)/shard_map/attend_far/pallas_call | solution.py:254
  25.1 3.8 %attend_cross.1 = (bf16[128,1024]{1,0:T(8,128)(2,1)S(1)}, bf16[128,2048]{1,0:T(8,128)(2,1)S(1)}) custom-call(s32[6]{0:T(128)S(1)} %stack.20.place_ref, bf16[256,1024]{1,0:T(8,128)(2,1)S(1)} %get-tuple-element.31.q_ref, f32[1024,128]{1,0:T(8,128)S(1)} %get-tuple-element.61.cos_ref, f32[1024,128]{1,0:T(8,128)S(1)} %get-tuple-element.60.sin_ref, ...), custom_call_target="tpu_custom_call" | custom-call | flops 167772160 | bytes 262144 | tf_op jit(solution)/shard_map/attend_cross/pallas_call | solution.py:254
  29.0 3.8 %collective-permute-start.4 = (bf16[128,2048]{1,0:T(8,128)(2,1)S(1)}, bf16[128,2048]{1,0:T(8,128)(2,1)S(1)}, u32[]{:S(2)}, u32[]{:S(2)}) collective-permute-start(bf16[128,2048]{1,0:T(8,128)(2,1)S(1)} %get-tuple-element.39.a_ref), channel_id=1, source_target_pairs={{0,4},{12,8},{1,5},{13,9},{2,6},{14,10},{3,7},{15,11},{16,20},{28,... | collective-permute-start | bytes 1572872 | tf_op jit(solution)/shard_map/ppermute | solution.py:466
  32.7 5.7 %attend_rest.1 = (bf16[128,1024]{1,0:T(8,128)(2,1)S(1)}, bf16[128,2048]{1,0:T(8,128)(2,1)S(1)}) custom-call(s32[6]{0:T(128)S(1)} %stack.20.place_ref, bf16[256,1024]{1,0:T(8,128)(2,1)S(1)} %get-tuple-element.31.q_ref, f32[1024,128]{1,0:T(8,128)S(1)} %get-tuple-element.61.cos_ref, f32[1024,128]{1,0:T(8,128)S(1)} %get-tuple-element.60.sin_ref, ...), custom_call_target="tpu_custom_call" | custom-call | flops 335544320 | bytes 262144 | tf_op jit(solution)/shard_map/attend_rest/pallas_call | solution.py:254
  38.4 1.3 %collective-permute-start.9 = (bf16[128,2048]{1,0:T(8,128)(2,1)S(1)}, bf16[128,2048]{1,0:T(8,128)(2,1)S(1)}, u32[]{:S(2)}, u32[]{:S(2)}) collective-permute-start(bf16[128,2048]{1,0:T(8,128)(2,1)S(1)} %get-tuple-element.52.a_ref), channel_id=1, source_target_pairs={{0,4},{12,8},{1,5},{13,9},{2,6},{14,10},{3,7},{15,11},{16,20},{28,... | collective-permute-start | bytes 1572872 | tf_op jit(solution)/shard_map/ppermute | solution.py:466
  39.7 4.5 %project_1.1 = (bf16[128,2048]{1,0:T(8,128)(2,1)S(1)}, bf16[128,2048]{1,0:T(8,128)(2,1)S(1)}) custom-call(s32[4]{0:T(128)S(1)} %broadcast_select_fusion.order_ref, bf16[128,1024]{1,0:T(8,128)(2,1)S(1)} %get-tuple-element.38.refs_0_, bf16[128,1024]{1,0:T(8,128)(2,1)S(1)} %get-tuple-element.44.refs_1_, bf16[1024,8192]{1,0:T(8,128)(2,1)} %refs_2_.7), custom_call_target="tpu_custom_call" | custom-call | flops 1073741824 | bytes 4194304 | tf_op jit(solution)/shard_map/project_1/pallas_call | solution.py:281
  45.8 7.2 %collective-permute-start.3 = (bf16[128,2048]{1,0:T(8,128)(2,1)S(1)}, bf16[128,2048]{1,0:T(8,128)(2,1)S(1)}, u32[]{:S(2)}, u32[]{:S(2)}) collective-permute-start(bf16[128,2048]{1,0:T(8,128)(2,1)S(1)} %get-tuple-element.46.a_ref), channel_id=1, source_target_pairs={{0,4},{12,8},{1,5},{13,9},{2,6},{14,10},{3,7},{15,11},{16,20},{28,... | collective-permute-start | bytes 1572872 | tf_op jit(solution)/shard_map/ppermute | solution.py:468
  53.0 4.5 %project_3.1 = (bf16[128,2048]{1,0:T(8,128)(2,1)S(1)}, bf16[128,2048]{1,0:T(8,128)(2,1)S(1)}) custom-call(s32[4]{0:T(128)S(1)} %broadcast_select_fusion.order_ref, bf16[128,1024]{1,0:T(8,128)(2,1)S(1)} %get-tuple-element.38.refs_0_, bf16[128,1024]{1,0:T(8,128)(2,1)S(1)} %get-tuple-element.44.refs_1_, bf16[1024,8192]{1,0:T(8,128)(2,1)} %refs_2_.7), custom_call_target="tpu_custom_call" | custom-call | flops 1073741824 | bytes 4194304 | tf_op jit(solution)/shard_map/project_3/pallas_call | solution.py:281
  58.3 5.9 %collective-permute-start.5 = (bf16[128,2048]{1,0:T(8,128)(2,1)S(1)}, bf16[128,2048]{1,0:T(8,128)(2,1)S(1)}, u32[]{:S(2)}, u32[]{:S(2)}) collective-permute-start(bf16[128,2048]{1,0:T(8,128)(2,1)S(1)} %get-tuple-element.49.a_ref), channel_id=1, source_target_pairs={{0,4},{12,8},{1,5},{13,9},{2,6},{14,10},{3,7},{15,11},{16,20},{28,... | collective-permute-start | bytes 1572872 | tf_op jit(solution)/shard_map/ppermute | solution.py:468
  65.7 5.3 %project_2.1 = (bf16[128,2048]{1,0:T(8,128)(2,1)}, bf16[128,2048]{1,0:T(8,128)(2,1)}) custom-call(s32[4]{0:T(128)S(1)} %broadcast_select_fusion.order_ref, bf16[128,1024]{1,0:T(8,128)(2,1)S(1)} %get-tuple-element.38.refs_0_, bf16[128,1024]{1,0:T(8,128)(2,1)S(1)} %get-tuple-element.44.refs_1_, bf16[1024,8192]{1,0:T(8,128)(2,1)} %refs_2_.7), custom_call_target="tpu_custom_call" | custom-call | flops 1073741824 | bytes 4194304 | tf_op jit(solution)/shard_map/project_2/pallas_call | solution.py:281
  71.0 5.4 %collective-permute-start.13 = (bf16[128,2048]{1,0:T(8,128)(2,1)}, bf16[128,2048]{1,0:T(8,128)(2,1)}, u32[]{:S(2)}, u32[]{:S(2)}) collective-permute-start(bf16[128,2048]{1,0:T(8,128)(2,1)} %get-tuple-element.55.refs_2_), channel_id=1, source_target_pairs={{0,4},{12,8},{1,5},{13,9},{2,6},{14,10},{3,7},{15,11},{16,20},{28,... | collective-permute-start | bytes 1572872 | tf_op jit(solution)/shard_map/ppermute | solution.py:470
  76.5 1.5 %collective-permute-start.14 = (bf16[128,2048]{1,0:T(8,128)(2,1)S(1)}, bf16[128,2048]{1,0:T(8,128)(2,1)}, u32[]{:S(2)}, u32[]{:S(2)}) collective-permute-start(bf16[128,2048]{1,0:T(8,128)(2,1)S(1)} %add_10.1), channel_id=1, source_target_pairs={{4,8},{8,4},{5,9},{9,5},{6,10},{10,6},{7,11},{11,7},{20,24},{24,20... | collective-permute-start | bytes 1572872 | tf_op jit(solution)/shard_map/ppermute | solution.py:476
  78.1 1.3 %collective-permute-start.11 = (bf16[128,2048]{1,0:T(8,128)(2,1)S(1)}, bf16[128,2048]{1,0:T(8,128)(2,1)}, u32[]{:S(2)}, u32[]{:S(2)}) collective-permute-start(bf16[128,2048]{1,0:T(8,128)(2,1)S(1)} %add_31.1), channel_id=1, source_target_pairs={{4,0},{8,12},{5,1},{9,13},{6,2},{10,14},{7,3},{11,15},{20,16},{24,... | collective-permute-start | bytes 1572872 | tf_op jit(solution)/shard_map/ppermute | solution.py:477
  79.6 1.5 %collective-permute-start.8 = (bf16[128,2048]{1,0:T(8,128)(2,1)S(1)}, bf16[128,2048]{1,0:T(8,128)(2,1)}, u32[]{:S(2)}, u32[]{:S(2)}) collective-permute-start(bf16[128,2048]{1,0:T(8,128)(2,1)S(1)} %add_11.1), channel_id=1, source_target_pairs={{4,8},{8,4},{5,9},{9,5},{6,10},{10,6},{7,11},{11,7},{20,24},{24,20... | collective-permute-start | bytes 1572872 | tf_op jit(solution)/shard_map/ppermute | solution.py:476
  81.1 6.3 %collective-permute-start.12 = (bf16[128,2048]{1,0:T(8,128)(2,1)}, bf16[128,2048]{1,0:T(8,128)(2,1)S(1)}, u32[]{:S(2)}, u32[]{:S(2)}) collective-permute-start(bf16[128,2048]{1,0:T(8,128)(2,1)} %get-tuple-element.47.second_ref), channel_id=1, source_target_pairs={{0,4},{12,8},{1,5},{13,9},{2,6},{14,10},{3,7},{15,11},{16,20},{28,... | collective-permute-start | bytes 1572872 | tf_op jit(solution)/shard_map/ppermute | solution.py:470
  87.3 2.6 %collective-permute-done.13.refs_3_ = bf16[128,2048]{1,0:T(8,128)(2,1)} collective-permute-done((bf16[128,2048]{1,0:T(8,128)(2,1)}, bf16[128,2048]{1,0:T(8,128)(2,1)}, u32[]{:S(2)}, u32[]{:S(2)}) %collective-permute-start.13) | collective-permute-done | bytes 524320 | tf_op jit(solution)/shard_map/ppermute | solution.py:470
  91.0 2.5 %finish_0.1 = (bf16[256,2048]{1,0:T(8,128)(2,1)}, f32[16,256]{1,0:T(8,128)}) custom-call(s32[1]{0:T(128)} %bitcast.flag_ref.refs_0_, bf16[128,2048]{1,0:T(8,128)(2,1)S(1)} %get-tuple-element.43.a_ref.refs_1_, bf16[128,2048]{1,0:T(8,128)(2,1)} %get-tuple-element.55.refs_2_, bf16[128,2048]{1,0:T(8,128)(2,1)} %collective-permute-done.13.refs_3_, ...), custom_call_target="tpu_custom_call" | custom-call | flops 1572864 | bytes 3145728 | tf_op jit(solution)/shard_map/finish_0/pallas_call | solution.py:358
  93.6 1.6 %gather.1.refs_0_ = f32[128,2048]{1,0:T(8,128)S(1)} custom-call(s32[1]{0:T(128)} %bitcast.flag_ref.refs_0_, bf16[128,2048]{1,0:T(8,128)(2,1)S(1)} %get-tuple-element.42.a_ref.first_ref, bf16[128,2048]{1,0:T(8,128)(2,1)} %get-tuple-element.47.second_ref, bf16[128,2048]{1,0:T(8,128)(2,1)} %collective-permute-done.8.a_ref, ...), custom_call_target="tpu_custom_call" | custom-call | flops 786432 | bytes 3145728 | tf_op jit(solution)/shard_map/gather/pallas_call | solution.py:319
  95.2 5.7 %collective-permute-done.12.refs_1_ = bf16[128,2048]{1,0:T(8,128)(2,1)S(1)} collective-permute-done((bf16[128,2048]{1,0:T(8,128)(2,1)}, bf16[128,2048]{1,0:T(8,128)(2,1)S(1)}, u32[]{:S(2)}, u32[]{:S(2)}) %collective-permute-start.12) | collective-permute-done | bytes 524320 | tf_op jit(solution)/shard_map/ppermute | solution.py:470
  (36 shorter events, 9.2 us)
Async XLA Ops:
  3.2 5.8 %collective-permute-start = (bf16[2,1296,128]{2,1,0:T(8,128)(2,1)}, bf16[2,1296,128]{2,1,0:T(8,128)(2,1)S(1)}, u32[]{:S(2)}, u32[]{:S(2)}) collective-permute-start(bf16[2,1296,128]{2,1,0:T(8,128)(2,1)} %pack.1.refs_0_), channel_id=1, source_target_pairs={{0,1},{1,0},{2,3},{3,2},{4,5},{5,4},{6,7},{7,6},{8,9},{9,8},{10,11... | collective-permute-start | bytes 1990664 | tf_op jit(solution)/shard_map/ppermute | solution.py:411
  3.8 18.3 %collective-permute-start.1 = (bf16[2,1296,128]{2,1,0:T(8,128)(2,1)}, bf16[2,1296,128]{2,1,0:T(8,128)(2,1)S(1)}, u32[]{:S(2)}, u32[]{:S(2)}) collective-permute-start(bf16[2,1296,128]{2,1,0:T(8,128)(2,1)} %pack.1.refs_0_), channel_id=1, source_target_pairs={{0,2},{2,0},{1,3},{3,1},{4,6},{6,4},{5,7},{7,5},{8,10},{10,8},{9,1... | collective-permute-start | bytes 1990664 | tf_op jit(solution)/shard_map/ppermute | solution.py:410
  9.0 1.1 %copy-start = (bf16[2,1296,128]{2,1,0:T(8,128)(2,1)S(1)}, bf16[2,1296,128]{2,1,0:T(8,128)(2,1)}, u32[]{:S(2)}) copy-start(bf16[2,1296,128]{2,1,0:T(8,128)(2,1)} %pack.1.refs_0_) | copy-start | bytes 1990660
  10.1 1.0 %copy-start.1 = (bf16[256,1024]{1,0:T(8,128)(2,1)S(1)}, bf16[256,1024]{1,0:T(8,128)(2,1)}, u32[]{:S(2)}) copy-start(bf16[256,1024]{1,0:T(8,128)(2,1)} %q_ref.1) | copy-start | bytes 1572868
  22.0 3.1 %collective-permute-start.2 = (bf16[2,1296,128]{2,1,0:T(8,128)(2,1)S(1)}, bf16[2,1296,128]{2,1,0:T(8,128)(2,1)S(1)}, u32[]{:S(2)}, u32[]{:S(2)}) collective-permute-start(bf16[2,1296,128]{2,1,0:T(8,128)(2,1)S(1)} %collective-permute-done.1.refs_0_), channel_id=1, source_target_pairs={{0,1},{1,0},{2,3},{3,2},{4,5},{5,4},{6,7},{7,6},{8,9},{9,8},{10,11... | collective-permute-start | bytes 1990664 | tf_op jit(solution)/shard_map/ppermute | solution.py:426
  29.0 16.0 %collective-permute-start.4 = (bf16[128,2048]{1,0:T(8,128)(2,1)S(1)}, bf16[128,2048]{1,0:T(8,128)(2,1)S(1)}, u32[]{:S(2)}, u32[]{:S(2)}) collective-permute-start(bf16[128,2048]{1,0:T(8,128)(2,1)S(1)} %get-tuple-element.39.a_ref), channel_id=1, source_target_pairs={{0,4},{12,8},{1,5},{13,9},{2,6},{14,10},{3,7},{15,11},{16,20},{28,... | collective-permute-start | bytes 1572872 | tf_op jit(solution)/shard_map/ppermute | solution.py:466
  38.4 19.0 %collective-permute-start.9 = (bf16[128,2048]{1,0:T(8,128)(2,1)S(1)}, bf16[128,2048]{1,0:T(8,128)(2,1)S(1)}, u32[]{:S(2)}, u32[]{:S(2)}) collective-permute-start(bf16[128,2048]{1,0:T(8,128)(2,1)S(1)} %get-tuple-element.52.a_ref), channel_id=1, source_target_pairs={{0,4},{12,8},{1,5},{13,9},{2,6},{14,10},{3,7},{15,11},{16,20},{28,... | collective-permute-start | bytes 1572872 | tf_op jit(solution)/shard_map/ppermute | solution.py:466
  45.1 19.2 %collective-permute-start.6 = (bf16[128,2048]{1,0:T(8,128)(2,1)S(1)}, bf16[128,2048]{1,0:T(8,128)(2,1)S(1)}, u32[]{:S(2)}, u32[]{:S(2)}) collective-permute-start(bf16[128,2048]{1,0:T(8,128)(2,1)S(1)} %add_00.1), channel_id=1, source_target_pairs={{4,8},{8,4},{5,9},{9,5},{6,10},{10,6},{7,11},{11,7},{20,24},{24,20... | collective-permute-start | bytes 1572872 | tf_op jit(solution)/shard_map/ppermute | solution.py:475
  45.8 30.6 %collective-permute-start.3 = (bf16[128,2048]{1,0:T(8,128)(2,1)S(1)}, bf16[128,2048]{1,0:T(8,128)(2,1)S(1)}, u32[]{:S(2)}, u32[]{:S(2)}) collective-permute-start(bf16[128,2048]{1,0:T(8,128)(2,1)S(1)} %get-tuple-element.46.a_ref), channel_id=1, source_target_pairs={{0,4},{12,8},{1,5},{13,9},{2,6},{14,10},{3,7},{15,11},{16,20},{28,... | collective-permute-start | bytes 1572872 | tf_op jit(solution)/shard_map/ppermute | solution.py:468
  57.6 20.4 %collective-permute-start.10 = (bf16[128,2048]{1,0:T(8,128)(2,1)S(1)}, bf16[128,2048]{1,0:T(8,128)(2,1)S(1)}, u32[]{:S(2)}, u32[]{:S(2)}) collective-permute-start(bf16[128,2048]{1,0:T(8,128)(2,1)S(1)} %add_01.1), channel_id=1, source_target_pairs={{4,8},{8,4},{5,9},{9,5},{6,10},{10,6},{7,11},{11,7},{20,24},{24,20... | collective-permute-start | bytes 1572872 | tf_op jit(solution)/shard_map/ppermute | solution.py:475
  58.3 21.1 %collective-permute-start.5 = (bf16[128,2048]{1,0:T(8,128)(2,1)S(1)}, bf16[128,2048]{1,0:T(8,128)(2,1)S(1)}, u32[]{:S(2)}, u32[]{:S(2)}) collective-permute-start(bf16[128,2048]{1,0:T(8,128)(2,1)S(1)} %get-tuple-element.49.a_ref), channel_id=1, source_target_pairs={{0,4},{12,8},{1,5},{13,9},{2,6},{14,10},{3,7},{15,11},{16,20},{28,... | collective-permute-start | bytes 1572872 | tf_op jit(solution)/shard_map/ppermute | solution.py:468
  64.4 15.1 %collective-permute-start.7 = (bf16[128,2048]{1,0:T(8,128)(2,1)S(1)}, bf16[128,2048]{1,0:T(8,128)(2,1)S(1)}, u32[]{:S(2)}, u32[]{:S(2)}) collective-permute-start(bf16[128,2048]{1,0:T(8,128)(2,1)S(1)} %add_30.1), channel_id=1, source_target_pairs={{4,0},{8,12},{5,1},{9,13},{6,2},{10,14},{7,3},{11,15},{20,16},{24,... | collective-permute-start | bytes 1572872 | tf_op jit(solution)/shard_map/ppermute | solution.py:477
  71.0 19.0 %collective-permute-start.13 = (bf16[128,2048]{1,0:T(8,128)(2,1)}, bf16[128,2048]{1,0:T(8,128)(2,1)}, u32[]{:S(2)}, u32[]{:S(2)}) collective-permute-start(bf16[128,2048]{1,0:T(8,128)(2,1)} %get-tuple-element.55.refs_2_), channel_id=1, source_target_pairs={{0,4},{12,8},{1,5},{13,9},{2,6},{14,10},{3,7},{15,11},{16,20},{28,... | collective-permute-start | bytes 1572872 | tf_op jit(solution)/shard_map/ppermute | solution.py:470
  76.5 13.5 %collective-permute-start.14 = (bf16[128,2048]{1,0:T(8,128)(2,1)S(1)}, bf16[128,2048]{1,0:T(8,128)(2,1)}, u32[]{:S(2)}, u32[]{:S(2)}) collective-permute-start(bf16[128,2048]{1,0:T(8,128)(2,1)S(1)} %add_10.1), channel_id=1, source_target_pairs={{4,8},{8,4},{5,9},{9,5},{6,10},{10,6},{7,11},{11,7},{20,24},{24,20... | collective-permute-start | bytes 1572872 | tf_op jit(solution)/shard_map/ppermute | solution.py:476
  78.1 15.4 %collective-permute-start.11 = (bf16[128,2048]{1,0:T(8,128)(2,1)S(1)}, bf16[128,2048]{1,0:T(8,128)(2,1)}, u32[]{:S(2)}, u32[]{:S(2)}) collective-permute-start(bf16[128,2048]{1,0:T(8,128)(2,1)S(1)} %add_31.1), channel_id=1, source_target_pairs={{4,0},{8,12},{5,1},{9,13},{6,2},{10,14},{7,3},{11,15},{20,16},{24,... | collective-permute-start | bytes 1572872 | tf_op jit(solution)/shard_map/ppermute | solution.py:477
  79.4 1.6 %copy-start.2 = (bf16[128,2048]{1,0:T(8,128)(2,1)}, bf16[128,2048]{1,0:T(8,128)(2,1)S(1)}, u32[]{:S(2)}) copy-start(bf16[128,2048]{1,0:T(8,128)(2,1)S(1)} %collective-permute-done.7.refs_5_) | copy-start | bytes 1572868
  79.6 14.0 %collective-permute-start.8 = (bf16[128,2048]{1,0:T(8,128)(2,1)S(1)}, bf16[128,2048]{1,0:T(8,128)(2,1)}, u32[]{:S(2)}, u32[]{:S(2)}) collective-permute-start(bf16[128,2048]{1,0:T(8,128)(2,1)S(1)} %add_11.1), channel_id=1, source_target_pairs={{4,8},{8,4},{5,9},{9,5},{6,10},{10,6},{7,11},{11,7},{20,24},{24,20... | collective-permute-start | bytes 1572872 | tf_op jit(solution)/shard_map/ppermute | solution.py:476
  81.1 19.8 %collective-permute-start.12 = (bf16[128,2048]{1,0:T(8,128)(2,1)}, bf16[128,2048]{1,0:T(8,128)(2,1)S(1)}, u32[]{:S(2)}, u32[]{:S(2)}) collective-permute-start(bf16[128,2048]{1,0:T(8,128)(2,1)} %get-tuple-element.47.second_ref), channel_id=1, source_target_pairs={{0,4},{12,8},{1,5},{13,9},{2,6},{14,10},{3,7},{15,11},{16,20},{28,... | collective-permute-start | bytes 1572872 | tf_op jit(solution)/shard_map/ppermute | solution.py:470
  90.0 1.0 %copy-start.3 = (bf16[128,2048]{1,0:T(8,128)(2,1)S(1)}, bf16[128,2048]{1,0:T(8,128)(2,1)}, u32[]{:S(2)}) copy-start(bf16[128,2048]{1,0:T(8,128)(2,1)} %copy-done.2) | copy-start | bytes 1572868
